TPU v7x, 256 devices: a whole 4x4x8 slice. The times are simulated.
256 devices in a mesh: dp: 4 (over z_lo, core), expert: 16 (over y, z_hi), tensor: 4 (over x).
Axes of the slice: x: 4, y: 4, z: 8 (z_hi: 4, z_lo: 2; z = z_hi * 2 + z_lo), core: 2. Of those that a mesh axis runs over, the one named last changes fastest.
Arguments:
- master: float32 [64, 2048, 1024], P('expert', ('dp', 'tensor')), may hold values from -0.125 to 0.125
- first_moment: float32 [64, 2048, 1024], P('expert', ('dp', 'tensor')), may hold values from -0.03 to 0.03
- second_moment: float32 [64, 2048, 1024], P('expert', ('dp', 'tensor')), may hold values from 1e-05 to 0.001
- gradient: bfloat16 [64, 2048, 1024], P('expert', ('dp', 'tensor')), may hold values from -0.119628906 to 0.119628906
- tokens: bfloat16 [2, 8192, 2048], P(None, ('dp', 'expert')), may hold values from -6 to 6
- expert_ids: int32 [2, 8192, 8], P(None, ('dp', 'expert')), may hold values from 0 to 63, all different within a row; in each aligned block of 128 rows (0 to 127, 128 to 255, ..., all dimensions but the last counted through in order) at most 32 rows name the same one
- router_scores: float32 [2, 8192, 8], P(None, ('dp', 'expert')), may hold values from 0.1 to 1
Outputs:
- new_master: float32 [64, 2048, 1024], P('expert', ('dp', 'tensor'))
- mixed: bfloat16 [2, 8192, 1024], P(None, ('dp', 'expert'), 'tensor')
Inputs may be any that keep to these rules, and one draw needn't show every extreme that they name: `expert_ids`: each token names 8 different experts. Within the tokens of one step that lie on one token group (aligned blocks of 128 rows), no expert is named more than 32 times, a bound that some block reaches.
All inputs are finite; a program needn't handle non-finite values.
Results may differ from a plain program's by a relative error of at most 0.0053.
Values may be sent and summed in bfloat16 or wider, within the bound.
No kernel may reach another device: no remote copies, remote signals or barrier semaphores. Data moves between devices by JAX's collectives and lax.ppermute only.
A program may use at most 128 MiB of HBM per device.

v0:
```python
import jax
import jax.numpy as jnp
from jax import lax
from jax.sharding import PartitionSpec as P

learn_rate = 0.01
decay_rate = 0.1
beta_one = 0.9
beta_two = 0.95
epsilon = 1e-08
correct_one = 1.0 - 0.9**4
correct_two = 1.0 - 0.95**4


def adam_update(master, first_moment, second_moment, gradient):
    grad_full = gradient.astype(jnp.float32)
    new_first = beta_one * first_moment + (1.0 - beta_one) * grad_full
    new_second = beta_two * second_moment + (1.0 - beta_two) * grad_full * grad_full
    update = new_first / correct_one / (jnp.sqrt(new_second / correct_two) + epsilon)
    return master * (1.0 - learn_rate * decay_rate) - learn_rate * update


def expert_apply(arrived, weight):
    product = jnp.einsum("gnd,df->gnf", arrived, weight, preferred_element_type=jnp.float32)
    return jax.nn.silu(product).astype(jnp.bfloat16)


def send_back(activations):
    return lax.all_to_all(activations, ("dp", "expert"), split_axis=0, concat_axis=0, tiled=True)


def per_device(master, first_moment, second_moment, gradient, tokens, expert_ids, router_scores):
    new_master = adam_update(master, first_moment, second_moment, gradient)
    lowered = new_master.astype(jnp.bfloat16)
    dp_count = lax.axis_size("dp")
    owner_count = lax.axis_size("expert")
    tensor_count = lax.axis_size("tensor")
    local_experts, local_rows, width = lowered.shape
    hidden_part = width // tensor_count
    blocks = lowered.reshape(local_experts, local_rows, tensor_count, hidden_part)
    blocks = blocks.transpose(0, 2, 1, 3).reshape(
        local_experts * tensor_count, local_rows, hidden_part
    )
    moved = lax.all_to_all(blocks, ("dp", "tensor"), split_axis=0, concat_axis=1, tiled=True)
    weight = moved.reshape(-1, hidden_part)
    group_count = dp_count * owner_count
    results = []
    for decode_step in range(tokens.shape[0]):
        features = tokens[decode_step]
        chosen = expert_ids[decode_step]
        weights_raw = router_scores[decode_step]
        token_count, choice_count = chosen.shape
        capacity = min(token_count, 2 * token_count * choice_count // group_count)
        flat = chosen.reshape(-1)
        route_count = flat.shape[0]
        onehot = (flat[:, None] == jnp.arange(group_count, dtype=jnp.int32)[None, :]).astype(
            jnp.int32
        )
        position = jnp.sum((jnp.cumsum(onehot, axis=0) - 1) * onehot, axis=1)
        owner = flat % dp_count * owner_count + flat // dp_count
        slot = owner * capacity + position
        source = jnp.arange(route_count, dtype=jnp.int32) // choice_count
        outgoing = jnp.zeros((group_count * capacity, features.shape[1]), jnp.bfloat16)
        outgoing = outgoing.at[slot].set(features[source]).reshape(group_count, capacity, -1)
        returned = (lambda arrived: send_back(expert_apply(arrived, weight)))(
            lax.all_to_all(outgoing, ("dp", "expert"), split_axis=0, concat_axis=0, tiled=True)
        )
        values = returned.reshape(group_count * capacity, -1)[slot]
        values = values.astype(jnp.float32).reshape(token_count, choice_count, -1)
        shares = weights_raw / jnp.sum(weights_raw, axis=1, keepdims=True)
        results.append(jnp.sum(shares[:, :, None] * values, axis=1).astype(jnp.bfloat16))
    return (new_master, jnp.stack(results))


def solution(mesh):
    placed = (
        P("expert", ("dp", "tensor"), None),
        P("expert", ("dp", "tensor"), None),
        P("expert", ("dp", "tensor"), None),
        P("expert", ("dp", "tensor"), None),
        P(None, ("dp", "expert"), None),
        P(None, ("dp", "expert"), None),
        P(None, ("dp", "expert"), None),
    )
    return jax.shard_map(
        per_device,
        mesh=mesh,
        in_specs=placed,
        out_specs=(P("expert", ("dp", "tensor"), None), P(None, ("dp", "expert"), "tensor")),
        check_vma=False,
    )
```

profile of v0, /device:TPU:1, one launch (start us, length us, event | category | flops | bytes accessed | tf_op | source)
XLA Modules:
  0.0 537.0 jit_solution(1433320626011595901)
XLA Ops:
  0.6 6.1 %fusion.27 = (bf16[4,128,1024]{2,1,0:T(8,128)(2,1)S(1)}, f32[4,128,1024]{2,1,0:T(8,128)}) fusion(f32[4,128,1024]{2,1,0:T(8,128)} %param.9, bf16[4,128,1024]{2,1,0:T(8,128)(2,1)} %param.10, f32[4,128,1024]{2,1,0:T(8,128)} %param.8, f32[4,128,1024]{2,1,0:T(8,128)} %param.7), kind=kLoop, calls=%fused_computation.77 | loop fusion | flops 8388608 | bytes 10485760 | tf_op jit(solution)/shard_map/convert_element_type | solution.py:34
  6.9 1.1 pad_maximum_fusion
  7.9 7.3 %all-to-all-start.1 = ((bf16[16,128,256]{2,1,0:T(8,128)(2,1)}), bf16[16,128,256]{2,1,0:T(8,128)(2,1)S(1)}, u32[]{:S(2)}, u32[]{:S(2)}) async-start(bf16[16,128,256]{2,1,0:T(8,128)(2,1)} %bitcast.8), calls=%async_computation.1 | async-start | bytes 2097152 | tf_op jit(solution)/shard_map/all_to_all | solution.py:44
  15.6 18.0 %reduce-window.14 = s32[64,8,128]{2,1,0:T(8,128)S(1)} reduce-window(s32[64,8,128]{2,1,0:T(8,128)S(1)} %fusion.21, s32[]{:T(128)} %constant.89.clone.1), window={size=1x1x128 pad=0_0x0_0x127_0}, to_apply=%region_1.2 | reduce-window | flops 8323072 | bytes 524292 | tf_op jit(solution)/shard_map/reduce-window
  33.8 0.1 copy.15
  34.5 35.9 %scatter_custom_fusion = bf16[2048,2048]{1,0:T(8,128)(2,1)} fusion(s32[1024]{0:T(1024)S(1)} %bitcast.79, bf16[128,2048]{1,0:T(8,128)(2,1)S(1)} %get-tuple-element.6, s32[1024]{0:T(1024)S(1)} %broadcast_clamp_fusion.2, bf16[]{:T(256)} %constant.88.clone.1), kind=kCustom, calls=%fused_computation.8 | custom fusion | bytes 8388610 | tf_op jit(solution)/shard_map/scatter | solution.py:64
  70.4 11.5 %all-to-all-start = ((bf16[64,32,2048]{2,1,0:T(8,128)(2,1)}), bf16[64,32,2048]{2,1,0:T(8,128)(2,1)}, u32[]{:S(2)}, u32[]{:S(2)}) async-start(bf16[64,32,2048]{2,1,0:T(8,128)(2,1)} %bitcast.65), calls=%async_computation | async-start | bytes 16777216 | tf_op jit(solution)/shard_map/all_to_all | solution.py:66
  82.3 18.0 %reduce-window.16 = s32[64,8,128]{2,1,0:T(8,128)S(1)} reduce-window(s32[64,8,128]{2,1,0:T(8,128)S(1)} %fusion.22, s32[]{:T(128)} %constant.89.clone.1), window={size=1x1x128 pad=0_0x0_0x127_0}, to_apply=%region_7.8 | reduce-window | flops 8323072 | bytes 524292 | tf_op jit(solution)/shard_map/reduce-window.2
  100.5 0.1 copy.21
  101.0 24.9 %scatter_custom_fusion.1 = bf16[2048,2048]{1,0:T(8,128)(2,1)} fusion(s32[1024]{0:T(1024)S(1)} %bitcast.81, bf16[128,2048]{1,0:T(8,128)(2,1)S(1)} %get-tuple-element.7, s32[1024]{0:T(1024)S(1)} %broadcast_clamp_fusion.2, bf16[]{:T(256)} %constant.88.clone.1), kind=kCustom, calls=%fused_computation.6 | custom fusion | bytes 8388610 | tf_op jit(solution)/shard_map/scatter | solution.py:64
  125.9 137.0 %all-to-all-done = bf16[64,32,2048]{2,1,0:T(8,128)(2,1)} async-done(((bf16[64,32,2048]{2,1,0:T(8,128)(2,1)}), bf16[64,32,2048]{2,1,0:T(8,128)(2,1)}, u32[]{:S(2)}, u32[]{:S(2)}) %all-to-all-start) | async-done | bytes 8388640 | tf_op jit(solution)/shard_map/all_to_all | solution.py:66
  262.9 12.5 %all-to-all-start.3 = ((bf16[64,32,2048]{2,1,0:T(8,128)(2,1)}), bf16[64,32,2048]{2,1,0:T(8,128)(2,1)}, u32[]{:S(2)}, u32[]{:S(2)}) async-start(bf16[64,32,2048]{2,1,0:T(8,128)(2,1)} %bitcast.66), calls=%async_computation.3 | async-start | bytes 16777216 | tf_op jit(solution)/shard_map/all_to_all | solution.py:66
  275.4 7.0 %multiply_convert_fusion.1 = bf16[64,32,256]{2,1,0:T(8,128)(2,1)} fusion(bf16[64,32,2048]{2,1,0:T(8,128)(2,1)} %all-to-all-done, bf16[2048,256,1]{1,0,2:T(8,128)(2,1)S(1)} %bitcast.69), kind=kOutput, calls=%fused_computation.24 | convolution fusion | flops 2150105088 | bytes 10485760 | tf_op jit(solution)/shard_map/gnd,df->gnf/dot_general | solution.py:24
  282.4 174.0 %all-to-all-done.3 = bf16[64,32,2048]{2,1,0:T(8,128)(2,1)} async-done(((bf16[64,32,2048]{2,1,0:T(8,128)(2,1)}), bf16[64,32,2048]{2,1,0:T(8,128)(2,1)}, u32[]{:S(2)}, u32[]{:S(2)}) %all-to-all-start.3) | async-done | bytes 8388640 | tf_op jit(solution)/shard_map/all_to_all | solution.py:66
  456.4 12.3 %all-to-all-start.2 = ((bf16[64,32,256]{2,1,0:T(8,128)(2,1)}), bf16[64,32,256]{2,1,0:T(8,128)(2,1)S(1)}, u32[]{:S(2)}, u32[]{:S(2)}) async-start(bf16[64,32,256]{2,1,0:T(8,128)(2,1)} %multiply_convert_fusion.1), calls=%async_computation.2 | async-start | bytes 2097152 | tf_op jit(solution)/shard_map/all_to_all | solution.py:29
  468.8 6.9 %multiply_convert_fusion = bf16[64,32,256]{2,1,0:T(8,128)(2,1)} fusion(bf16[64,32,2048]{2,1,0:T(8,128)(2,1)} %all-to-all-done.3, bf16[2048,256,1]{1,0,2:T(8,128)(2,1)S(1)} %bitcast.70), kind=kOutput, calls=%fused_computation.23 | convolution fusion | flops 2150105088 | bytes 10485760 | tf_op jit(solution)/shard_map/gnd,df->gnf/dot_general | solution.py:24
  475.7 21.7 %all-to-all-done.2 = bf16[64,32,256]{2,1,0:T(8,128)(2,1)S(1)} async-done(((bf16[64,32,256]{2,1,0:T(8,128)(2,1)}), bf16[64,32,256]{2,1,0:T(8,128)(2,1)S(1)}, u32[]{:S(2)}, u32[]{:S(2)}) %all-to-all-start.2) | async-done | bytes 1048608 | tf_op jit(solution)/shard_map/all_to_all | solution.py:29
  497.4 5.8 %all-to-all-start.4 = ((bf16[64,32,256]{2,1,0:T(8,128)(2,1)}), bf16[64,32,256]{2,1,0:T(8,128)(2,1)S(1)}, u32[]{:S(2)}, u32[]{:S(2)}) async-start(bf16[64,32,256]{2,1,0:T(8,128)(2,1)} %multiply_convert_fusion), calls=%async_computation.4 | async-start | bytes 2097152 | tf_op jit(solution)/shard_map/all_to_all | solution.py:29
  503.4 3.9 gather_fusion
  507.4 0.4 fusion.16
  507.8 23.9 %all-to-all-done.4 = bf16[64,32,256]{2,1,0:T(8,128)(2,1)S(1)} async-done(((bf16[64,32,256]{2,1,0:T(8,128)(2,1)}), bf16[64,32,256]{2,1,0:T(8,128)(2,1)S(1)}, u32[]{:S(2)}, u32[]{:S(2)}) %all-to-all-start.4) | async-done | bytes 1048608 | tf_op jit(solution)/shard_map/all_to_all | solution.py:29
  531.6 3.9 gather_fusion.1
  535.6 0.4 fusion.15
  536.0 0.7 pad_maximum_fusion.1
  (42 shorter events, 2.2 us)
Async XLA Ops:
  6.8 8.4 %copy-start.2 = (s32[2,128,8]{1,2,0:T(8,128)S(1)}, s32[2,128,8]{1,2,0:T(8,128)}, u32[]{:S(2)}) copy-start(s32[2,128,8]{1,2,0:T(8,128)} %param.12) | copy-start | bytes 24580
  7.9 26.4 %copy-start = (bf16[2,128,2048]{2,1,0:T(8,128)(2,1)S(1)}, bf16[2,128,2048]{2,1,0:T(8,128)(2,1)}, u32[]{:S(2)}) copy-start(bf16[2,128,2048]{2,1,0:T(8,128)(2,1)} %param.11) | copy-start | bytes 3145732
  7.9 62.5 %all-to-all-start.1 = ((bf16[16,128,256]{2,1,0:T(8,128)(2,1)}), bf16[16,128,256]{2,1,0:T(8,128)(2,1)S(1)}, u32[]{:S(2)}, u32[]{:S(2)}) async-start(bf16[16,128,256]{2,1,0:T(8,128)(2,1)} %bitcast.8), calls=%async_computation.1 | async-start | bytes 2097152 | tf_op jit(solution)/shard_map/all_to_all | solution.py:44
  70.4 192.5 %all-to-all-start = ((bf16[64,32,2048]{2,1,0:T(8,128)(2,1)}), bf16[64,32,2048]{2,1,0:T(8,128)(2,1)}, u32[]{:S(2)}, u32[]{:S(2)}) async-start(bf16[64,32,2048]{2,1,0:T(8,128)(2,1)} %bitcast.65), calls=%async_computation | async-start | bytes 16777216 | tf_op jit(solution)/shard_map/all_to_all | solution.py:66
  262.9 193.5 %all-to-all-start.3 = ((bf16[64,32,2048]{2,1,0:T(8,128)(2,1)}), bf16[64,32,2048]{2,1,0:T(8,128)(2,1)}, u32[]{:S(2)}, u32[]{:S(2)}) async-start(bf16[64,32,2048]{2,1,0:T(8,128)(2,1)} %bitcast.66), calls=%async_computation.3 | async-start | bytes 16777216 | tf_op jit(solution)/shard_map/all_to_all | solution.py:66
  456.4 41.0 %all-to-all-start.2 = ((bf16[64,32,256]{2,1,0:T(8,128)(2,1)}), bf16[64,32,256]{2,1,0:T(8,128)(2,1)S(1)}, u32[]{:S(2)}, u32[]{:S(2)}) async-start(bf16[64,32,256]{2,1,0:T(8,128)(2,1)} %multiply_convert_fusion.1), calls=%async_computation.2 | async-start | bytes 2097152 | tf_op jit(solution)/shard_map/all_to_all | solution.py:29
  475.7 27.5 %copy-start.1 = (f32[2,128,8]{1,2,0:T(8,128)S(1)}, f32[2,128,8]{1,2,0:T(8,128)}, u32[]{:S(2)}) copy-start(f32[2,128,8]{1,2,0:T(8,128)} %param.13) | copy-start | bytes 24580
  497.4 34.3 %all-to-all-start.4 = ((bf16[64,32,256]{2,1,0:T(8,128)(2,1)}), bf16[64,32,256]{2,1,0:T(8,128)(2,1)S(1)}, u32[]{:S(2)}, u32[]{:S(2)}) async-start(bf16[64,32,256]{2,1,0:T(8,128)(2,1)} %multiply_convert_fusion), calls=%async_computation.4 | async-start | bytes 2097152 | tf_op jit(solution)/shard_map/all_to_all | solution.py:29
where the time goes:
time: 547 us; the launch traced here: 537 us
  waiting for transfers between devices  357 us (65%)
  local copies, waits for them, and re-layouts  70.6 us (13%)
  starting transfers between devices  49.5 us (9%)
  other arithmetic  45.3 us (8%)
  matrix products  13.9 us (3%)
    all_to_all x2, waiting for transfers between devices, per_device(): lax.all_to_all(outgoing, ('dp', 'expert'), split_axis=0, concat_axis=0, t...  311 us
    scatter x2, local copies, waits for them, and re-layouts, per_device(): outgoing.at[slot].set(features[source]).reshape(group_count, capacity, -1)  60.8 us
    all_to_all x2, waiting for transfers between devices, send_back(): lax.all_to_all(activations, ('dp', 'expert'), split_axis=0, concat_axis=0...  45.6 us
    another operation x4, other arithmetic  36.1 us
    all_to_all x2, starting transfers between devices, per_device(): lax.all_to_all(outgoing, ('dp', 'expert'), split_axis=0, concat_axis=0, t...  24.1 us
    all_to_all x2, starting transfers between devices, send_back(): lax.all_to_all(activations, ('dp', 'expert'), split_axis=0, concat_axis=0...  18.1 us
    dot_general x2, matrix products, expert_apply(): jnp.einsum('gnd,df->gnf', arrived, weight, preferred_element_type=jnp.flo...  13.9 us
  transfers between devices with their start and end apart: 5, of which 4 were waited for; matrix products, arithmetic and copies ran while one was open for 22% of the time, Pallas kernels for 0%

commit v1 on v0

v1 whole, which is shorter than its diff:
```python
import jax
import jax.numpy as jnp
from jax import lax
from jax.experimental import pallas as pl
from jax.experimental.pallas import tpu as pltpu
from jax.sharding import Mesh, PartitionSpec as P

learn_rate = 0.01
decay_rate = 0.1
beta_one = 0.9
beta_two = 0.95
epsilon = 1e-08
correct_one = 1.0 - 0.9**4
correct_two = 1.0 - 0.95**4

TILE = 512


def adam_update(master, first_moment, second_moment, gradient):
    grad_full = gradient.astype(jnp.float32)
    new_first = beta_one * first_moment + (1.0 - beta_one) * grad_full
    new_second = beta_two * second_moment + (1.0 - beta_two) * grad_full * grad_full
    update = new_first / correct_one / (jnp.sqrt(new_second / correct_two) + epsilon)
    return master * (1.0 - learn_rate * decay_rate) - learn_rate * update


def expert_kernel(parts, which, first, last, *refs):
    tokens_ref, share_ref = refs[0], refs[1]
    weights = refs[2 : 2 + parts]
    total_ref = None if first else refs[2 + parts]
    out_ref = refs[-1]
    at = 0
    product = None
    for weight in weights:
        depth = weight.shape[0]
        piece = jnp.dot(
            tokens_ref[:, at : at + depth], weight[...], preferred_element_type=jnp.float32
        )
        product = piece if product is None else product + piece
        at += depth
    value = share_ref[:, which : which + 1] * (product * jax.nn.sigmoid(product))
    if not first:
        value = value + total_ref[...]
    if not last:
        out_ref[...] = value
        return
    groups, quarters, rows, width = out_ref.shape
    for group in range(groups):
        for quarter in range(quarters):
            out_ref[group, quarter] = value[
                group * rows : (group + 1) * rows, quarter * width : (quarter + 1) * width
            ].astype(out_ref.dtype)


def add_expert(tokens, shares, weights, which, total, out_shape, rows):
    count, depth = tokens.shape
    width = weights[0].shape[1]
    first, last = total is None, out_shape is not None
    in_specs = [
        pl.BlockSpec((TILE, depth), lambda i: (i, 0)),
        pl.BlockSpec((TILE, shares.shape[1]), lambda i: (i, 0)),
    ]
    in_specs += [pl.BlockSpec(w.shape, lambda i: (0, 0)) for w in weights]
    operands = [tokens, shares, *weights]
    if not first:
        in_specs.append(pl.BlockSpec((TILE, width), lambda i: (i, 0)))
        operands.append(total)
    if last:
        out = jax.ShapeDtypeStruct(out_shape, jnp.bfloat16)
        out_spec = pl.BlockSpec((TILE // rows,) + out_shape[1:], lambda i: (i, 0, 0, 0))
    else:
        out = jax.ShapeDtypeStruct((count, width), jnp.float32)
        out_spec = pl.BlockSpec((TILE, width), lambda i: (i, 0))

    def body(*refs):
        expert_kernel(len(weights), which, first, last, *refs)

    return pl.pallas_call(
        body,
        grid=(count // TILE,),
        in_specs=in_specs,
        out_specs=out_spec,
        out_shape=out,
        compiler_params=pltpu.CompilerParams(vmem_limit_bytes=40 * 2**20),
        cost_estimate=pl.CostEstimate(
            flops=2 * count * depth * width,
            bytes_accessed=2 * count * depth + 2 * depth * width + 8 * count * width,
            transcendentals=count * width,
        ),
    )(*operands)


def swap(value, offset):
    high, low = lax.axis_size("zh"), lax.axis_size("zl")
    pairs = []
    for z in range(offset, high * low + offset, low):
        a, b = [(at % low) * high + at // low % high for at in (z, z + 1)]
        pairs += [(a, b), (b, a)]
    return lax.ppermute(value, ("zl", "zh"), pairs)


def per_device(master, first_moment, second_moment, gradient, tokens, expert_ids, router_scores):
    steps, token_count, depth = tokens.shape
    quarters = lax.axis_size("x")
    cores = lax.axis_size("core")
    owners = lax.axis_size("zh")
    groups = cores * lax.axis_size("y")
    z_low, z_high = lax.axis_index("zl"), lax.axis_index("zh")
    y_at, x_at = lax.axis_index("y"), lax.axis_index("x")

    half = depth // 2
    flat = tokens.reshape(steps * token_count, depth)
    turned = jnp.where(
        z_low == 0, flat, jnp.concatenate([flat[:, half:], flat[:, :half]], axis=1)
    )
    all_tokens = lax.all_gather(turned, ("core", "y"), axis=0, tiled=True)

    ids = expert_ids.reshape(steps * token_count, -1)
    raw = router_scores.reshape(steps * token_count, -1)
    both = jnp.concatenate(
        [ids.astype(jnp.float32), raw / jnp.sum(raw, axis=1, keepdims=True)], axis=1
    )
    both = lax.all_gather(both, ("core", "y"), axis=0, tiled=True)
    choices = ids.shape[1]
    turn = jnp.where(z_low == 0, 1, -1)
    order = jnp.stack([z_high, z_high - turn, z_high + turn, z_high + 2])
    names = (quarters * (y_at * owners + jnp.mod(order, owners)) + x_at).astype(jnp.float32)
    shares = jnp.stack(
        [
            jnp.sum(jnp.where(both[:, :choices] == names[p], both[:, choices:], 0.0), axis=1)
            for p in range(4)
        ],
        axis=1,
    )

    new_master = adam_update(master, first_moment, second_moment, gradient)
    lowered = new_master.astype(jnp.bfloat16)
    experts, rows, width = lowered.shape
    strip = width // (quarters * cores)
    blocks = lowered.reshape(experts, rows, quarters, cores, strip)
    blocks = blocks.transpose(3, 0, 1, 2, 4).reshape(cores * experts, rows, quarters * strip)
    own = lax.all_to_all(blocks, ("core", "x"), split_axis=0, concat_axis=0, tiled=True)
    own = own.reshape(-1, quarters * strip)

    cut = own.shape[0] // 2
    a1, c1 = swap(own, 0), swap(own, 1)
    a2, c2 = swap(c1, 0), swap(a1, 1)
    a3, c3 = swap(c2, 0), swap(a2, 1)
    a4, c4 = swap(c3[:cut], 0), swap(a3[cut:], 1)

    total = add_expert(all_tokens, shares, [own, a1], 0, None, None, 0)
    total = add_expert(all_tokens, shares, [c2, c1], 1, total, None, 0)
    total = add_expert(all_tokens, shares, [a2, a3], 2, total, None, 0)
    out_shape = (groups, quarters, steps * token_count, strip)
    total = add_expert(
        all_tokens, shares, [a4, c4, c3], 3, total, out_shape, steps * token_count
    )
    total = total.reshape(groups * quarters, steps * token_count, strip)
    back = lax.all_to_all(total, ("core", "y", "x"), split_axis=0, concat_axis=0, tiled=True)
    back = back.reshape(cores, -1, steps, token_count, strip).astype(jnp.float32)
    mixed = jnp.sum(back, axis=1).astype(jnp.bfloat16)
    mixed = mixed.transpose(1, 2, 0, 3).reshape(steps, token_count, cores * strip)
    return (new_master, mixed)


def solution(mesh):
    grid = Mesh(mesh.devices.reshape(2, 2, 4, 4, 4), ("zl", "core", "y", "zh", "x"))
    owner, part, group = ("y", "zh"), ("zl", "core", "x"), ("zl", "core", "y", "zh")
    weights = P(owner, part, None)
    routed = P(None, group, None)
    return jax.shard_map(
        per_device,
        mesh=grid,
        in_specs=(weights,) * 4 + (routed,) * 3,
        out_specs=(weights, P(None, group, "x")),
        check_vma=False,
    )
```

time: 547 us -> 202 us (0.37); the launches traced: 537 us -> 202 us
  waiting for transfers between devices: 357 us -> 40.6 us
  blocking collectives: 0 us -> 78 us
  local copies, waits for them, and re-layouts: 70.6 us -> 12.9 us
  starting transfers between devices: 49.5 us -> 14.7 us
  other arithmetic: 45.3 us -> 11.5 us
  Pallas kernels: 0 us -> 29.9 us
  matrix products: 13.9 us -> 0 us
  between operations: 1.25 us -> 14.2 us
    all_to_all x5 -> x0, waiting for transfers between devices: 357 us -> none  [the longest x2 311 us: per_device(): lax.all_to_all(outgoing, ('dp', 'expert'), split_axis=0, concat_axis=0, t...]
    scatter x2 -> x0, local copies, waits for them, and re-layouts: 60.8 us -> none  [per_device(): outgoing.at[slot].set(features[source]).reshape(group_count, capacity, -1)]
    all_to_all x0 -> x2, blocking collectives: none -> 53.5 us  [the longest x1 32.4 us: per_device(): lax.all_to_all(total, ('core', 'y', 'x'), split_axis=0, concat_axis=0, ti...]
    all_to_all x5 -> x0, starting transfers between devices: 49.5 us -> none  [the longest x2 24.1 us: per_device(): lax.all_to_all(outgoing, ('dp', 'expert'), split_axis=0, concat_axis=0, t...]
    ppermute x0 -> x8, waiting for transfers between devices: none -> 40.6 us  [swap(): return lax.ppermute(value, ('zl', 'zh'), pairs)]
    another operation x5 -> x1, other arithmetic: 36.8 us -> 0.04 us  [per_device(): jnp.stack([jnp.sum(jnp.where(both[:, :choices] == names[p], both[:, choic...]
    pallas_call x0 -> x4, Pallas kernels: none -> 29.9 us  [add_expert(): pl.pallas_call(body, grid=(count // TILE,), in_specs=in_specs, out_specs=...]
    all_gather x0 -> x1, blocking collectives: none -> 24.5 us  [per_device(): both = lax.all_gather(both, ('core', 'y'), axis=0, tiled=True)]
  transfers between devices with their start and end apart: 5 -> 9, of which waited for: 4 -> 3; matrix products, arithmetic and copies ran while one was open for 22% -> 6% of each run, Pallas kernels for 0% -> 11%
where the time goes in v1:
time: 202 us
  blocking collectives  78 us (39%)
  waiting for transfers between devices  40.6 us (20%)
  Pallas kernels  29.9 us (15%)
  starting transfers between devices  14.7 us (7%)
  between operations  14.2 us (7%)
  local copies, waits for them, and re-layouts  12.9 us (6%)
  other arithmetic  11.5 us (6%)
    ppermute x8, waiting for transfers between devices, swap(): return lax.ppermute(value, ('zl', 'zh'), pairs)  40.6 us
    all_to_all x1, blocking collectives, per_device(): lax.all_to_all(total, ('core', 'y', 'x'), split_axis=0, concat_axis=0, ti...  32.4 us
    pallas_call x4, Pallas kernels, add_expert(): pl.pallas_call(body, grid=(count // TILE,), in_specs=in_specs, out_specs=...  29.9 us
    all_gather x1, blocking collectives, per_device(): both = lax.all_gather(both, ('core', 'y'), axis=0, tiled=True)  24.5 us
    all_to_all x1, blocking collectives, per_device(): lax.all_to_all(blocks, ('core', 'x'), split_axis=0, concat_axis=0, tiled=...  21 us
    ppermute x8, starting transfers between devices, swap(): return lax.ppermute(value, ('zl', 'zh'), pairs)  14.7 us
    unnamed x21, local copies, waits for them, and re-layouts  6.27 us
    convert_element_type x1, other arithmetic, per_device(): lowered = new_master.astype(jnp.bfloat16)  5.46 us
  transfers between devices with their start and end apart: 9, of which 3 were waited for; matrix products, arithmetic and copies ran while one was open for 6% of the time, Pallas kernels for 11%

profile of v1, /device:TPU:1, one launch (start us, length us, event | category | flops | bytes accessed | tf_op | source)
XLA Modules:
  0.0 201.7 jit_solution(3837700033566814266)
XLA Ops:
  7.2 2.3 %fusion.16 = (bf16[256,1024]{1,0:T(8,128)(2,1)}, bf16[256,1024]{1,0:T(8,128)(2,1)}) fusion(bf16[256,2048]{1,0:T(8,128)(2,1)} %bitcast.30), kind=kLoop, calls=%fused_computation.29 | loop fusion | bytes 2097152 | tf_op jit(solution)/shard_map/slice | solution.py:114
  9.5 2.8 %maximum_select_fusion = bf16[256,2048]{1,0:T(8,128)(2,1)} fusion(bf16[256,1024]{1,0:T(8,128)(2,1)} %get-tuple-element.11, bf16[256,1024]{1,0:T(8,128)(2,1)} %get-tuple-element.10, pred[]{:T(512)S(6)} %eq.30, bf16[2,128,2048]{2,1,0:T(8,128)(2,1)S(1)} %copy-done.6), kind=kLoop, calls=%fused_computation.11 | loop fusion | flops 2621440 | bytes 3145729 | tf_op jit(solution)/shard_map/jit(_where)/select_n | solution.py:113
  12.4 5.5 %fusion.14 = (bf16[4,128,1024]{2,1,0:T(8,128)(2,1)S(1)}, f32[4,128,1024]{2,1,0:T(8,128)}) fusion(f32[4,128,1024]{2,1,0:T(8,128)S(1)} %copy-done.7, bf16[4,128,1024]{2,1,0:T(8,128)(2,1)} %param.10, f32[4,128,1024]{2,1,0:T(8,128)} %param.8, f32[4,128,1024]{2,1,0:T(8,128)} %param.7), kind=kLoop, calls=%fused_computation.28 | loop fusion | flops 8388608 | bytes 10485760 | tf_op jit(solution)/shard_map/convert_element_type | solution.py:137
  19.3 21.0 %all_to_all.10 = bf16[8,128,512]{2,1,0:T(8,128)(2,1)S(1)} all-to-all(bf16[8,128,512]{2,1,0:T(8,128)(2,1)S(1)} %reshape.36), channel_id=1, replica_groups=mesh['zl'=2,'core'=2,'y'=4,'zh'=4,'x'=4] {'core','x'}, dimensions={0} | all-to-all | bytes 2097152 | tf_op jit(solution)/shard_map/all_to_all | solution.py:142
  40.4 1.6 collective-permute-start.4
  42.0 4.7 %collective-permute-start = (bf16[1024,512]{1,0:T(8,128)(2,1)S(1)}, bf16[1024,512]{1,0:T(8,128)(2,1)S(1)}, u32[]{:S(2)}, u32[]{:S(2)}) collective-permute-start(bf16[1024,512]{1,0:T(8,128)(2,1)S(1)} %bitcast.27), channel_id=1, source_target_pairs={{128,4},{4,128},{132,8},{8,132},{136,12},{12,136},{140,0},{0,140},... | collective-permute-start | bytes 3145736 | tf_op jit(solution)/shard_map/ppermute | solution.py:99
  46.6 1.0 copy-done.2
  47.6 17.8 %collective-permute-done.4.refs_3_ = bf16[1024,512]{1,0:T(8,128)(2,1)S(1)} collective-permute-done((bf16[1024,512]{1,0:T(8,128)(2,1)S(1)}, bf16[1024,512]{1,0:T(8,128)(2,1)S(1)}, u32[]{:S(2)}, u32[]{:S(2)}) %collective-permute-start.4) | collective-permute-done | bytes 1048608 | tf_op jit(solution)/shard_map/ppermute | solution.py:99
  65.5 5.3 %collective-permute-start.5 = (bf16[1024,512]{1,0:T(8,128)(2,1)S(1)}, bf16[1024,512]{1,0:T(8,128)(2,1)}, u32[]{:S(2)}, u32[]{:S(2)}) collective-permute-start(bf16[1024,512]{1,0:T(8,128)(2,1)S(1)} %collective-permute-done.4.refs_3_), channel_id=1, source_target_pairs={{128,4},{4,128},{132,8},{8,132},{136,12},{12,136},{140,0},{0,140},... | collective-permute-start | bytes 3145736 | tf_op jit(solution)/shard_map/ppermute | solution.py:99
  70.7 1.0 copy-done.4
  71.8 1.0 copy-done
  72.8 20.9 %collective-permute-done.5.refs_2_ = bf16[1024,512]{1,0:T(8,128)(2,1)} collective-permute-done((bf16[1024,512]{1,0:T(8,128)(2,1)S(1)}, bf16[1024,512]{1,0:T(8,128)(2,1)}, u32[]{:S(2)}, u32[]{:S(2)}) %collective-permute-start.5) | collective-permute-done | bytes 1048608 | tf_op jit(solution)/shard_map/ppermute | solution.py:99
  93.7 1.9 collective-permute-done.1.refs_2_
  96.1 24.5 %all_gather.7 = f32[2048,16]{0,1:T(8,128)S(1)} all-gather(f32[256,16]{0,1:T(8,128)S(1)} %pad_maximum_fusion.1), channel_id=1, replica_groups=mesh['zl'=2,'core'=2,'y'=4,'zh'=4,'x'=4] {'core','y'}, dimensions={0}, use_global_device_ids=true | all-gather | bytes 147456 | tf_op jit(solution)/shard_map/all_gather | solution.py:123
  121.4 2.7 %select_reduce_fusion.3 = (f32[2048]{0:T(1024)S(1)}, f32[2048]{0:T(1024)S(1)}, f32[2048]{0:T(1024)S(1)}, f32[2048]{0:T(1024)S(1)}) fusion(f32[2048,16]{0,1:T(8,128)S(1)} %all_gather.7, f32[]{:T(128)} %bitcast.8, f32[]{:T(128)} %bitcast.12, f32[]{:T(128)} %bitcast.14, f32[]{:T(128)} %bitcast.10), kind=kLoop, calls=%fused_computation.15 | loop fusion | flops 188416 | bytes 163856 | tf_op jit(solution)/shard_map/reduce_sum | solution.py:130
  125.3 0.8 slice.51
  126.2 2.6 %collective-permute-start.7 = (bf16[512,512]{1,0:T(8,128)(2,1)}, bf16[512,512]{1,0:T(8,128)(2,1)}, u32[]{:S(2)}, u32[]{:S(2)}) collective-permute-start(bf16[512,512]{1,0:T(8,128)(2,1)} %slice.51), channel_id=1, source_target_pairs={{128,4},{4,128},{132,8},{8,132},{136,12},{12,136},{140,0},{0,140},... | collective-permute-start | bytes 1572872 | tf_op jit(solution)/shard_map/ppermute | solution.py:99
  128.8 1.2 copy-done.3
  130.0 1.2 copy-done.5
  131.2 7.2 %shard_map.86.refs_4_ = f32[2048,512]{1,0:T(8,128)S(1)} custom-call(bf16[2048,2048]{1,0:T(8,128)(2,1)} %all-gather.2.cloned.1.call-done.refs_0_, f32[2048,4]{1,0:T(8,128)S(1)} %copy.24.refs_1_, bf16[1024,512]{1,0:T(8,128)(2,1)S(1)} %bitcast.28, bf16[1024,512]{1,0:T(8,128)(2,1)S(1)} %copy-done.5), custom_call_target="tpu_custom_call" | custom-call | flops 4294967296 | bytes 18874368 | tf_op jit(solution)/shard_map/pallas_call | solution.py:78
  138.5 7.6 %shard_map.87.refs_4_ = f32[2048,512]{1,0:T(8,128)S(1)} custom-call(bf16[2048,2048]{1,0:T(8,128)(2,1)} %all-gather.2.cloned.1.call-done.refs_0_, f32[2048,4]{1,0:T(8,128)S(1)} %copy.24.refs_1_, bf16[1024,512]{1,0:T(8,128)(2,1)} %collective-permute-done.5.refs_2_, bf16[1024,512]{1,0:T(8,128)(2,1)S(1)} %copy-done.1, f32[2048,512]{1,0:T(8,128)S(1)} %shard_map.86.refs_4_), custom_call_target="tpu_custom_call" | custom-call | flops 4294967296 | bytes 18874368 | tf_op jit(solution)/shard_map/pallas_call | solution.py:78
  146.0 7.6 %shard_map.88.refs_5_ = f32[2048,512]{1,0:T(8,128)S(1)} custom-call(bf16[2048,2048]{1,0:T(8,128)(2,1)} %all-gather.2.cloned.1.call-done.refs_0_, f32[2048,4]{1,0:T(8,128)S(1)} %copy.24.refs_1_, bf16[1024,512]{1,0:T(8,128)(2,1)} %collective-permute-done.1.refs_2_, bf16[1024,512]{1,0:T(8,128)(2,1)S(1)} %collective-permute-done.6.refs_3_, ...), custom_call_target="tpu_custom_call" | custom-call | flops 4294967296 | bytes 18874368 | tf_op jit(solution)/shard_map/pallas_call | solution.py:78
  153.6 7.6 %shard_map.89 = bf16[8,4,256,128]{3,2,1,0:T(8,128)(2,1)S(1)} custom-call(bf16[2048,2048]{1,0:T(8,128)(2,1)} %all-gather.2.cloned.1.call-done.refs_0_, f32[2048,4]{1,0:T(8,128)S(1)} %copy.24.refs_1_, bf16[512,512]{1,0:T(8,128)(2,1)} %collective-permute-done.3.refs_2_, bf16[512,512]{1,0:T(8,128)(2,1)} %collective-permute-done.7.refs_3_, ...), custom_call_target="tpu_custom_call" | custom-call | flops 4294967296 | bytes 18874368 | tf_op jit(solution)/shard_map/pallas_call | solution.py:78
  161.2 32.4 %all_to_all.11 = bf16[32,256,128]{2,1,0:T(8,128)(2,1)S(1)} all-to-all(bf16[32,256,128]{2,1,0:T(8,128)(2,1)S(1)} %bitcast.25), channel_id=1, replica_groups=mesh['zl'=2,'core'=2,'y'=4,'zh'=4,'x'=4] {'core','y','x'}, dimensions={0} | all-to-all | bytes 4194304 | tf_op jit(solution)/shard_map/all_to_all | solution.py:159
  (42 shorter events, 5.4 us)
Async XLA Ops:
  7.2 2.4 %copy-start.6 = (bf16[2,128,2048]{2,1,0:T(8,128)(2,1)S(1)}, bf16[2,128,2048]{2,1,0:T(8,128)(2,1)}, u32[]{:S(2)}) copy-start(bf16[2,128,2048]{2,1,0:T(8,128)(2,1)} %param.11) | copy-start | bytes 3145732
  7.2 121.6 %all-gather.2.cloned.1.call-start = ((), (), s32[]{:S(2)}) async-start(), calls=%async_computation.2 | async-start | bytes 9437184 | tf_op jit(solution)/shard_map/all_gather | solution.py:116
  9.5 2.8 %copy-start.7 = (f32[4,128,1024]{2,1,0:T(8,128)S(1)}, f32[4,128,1024]{2,1,0:T(8,128)}, u32[]{:S(2)}) copy-start(f32[4,128,1024]{2,1,0:T(8,128)} %param.9) | copy-start | bytes 6291460
  18.9 77.2 %copy-start.9 = (s32[2,128,8]{1,2,0:T(8,128)S(1)}, s32[2,128,8]{1,2,0:T(8,128)}, u32[]{:S(2)}) copy-start(s32[2,128,8]{1,2,0:T(8,128)} %param.12) | copy-start | bytes 24580
  18.9 77.2 %copy-start.8 = (f32[2,128,8]{1,2,0:T(8,128)S(1)}, f32[2,128,8]{1,2,0:T(8,128)}, u32[]{:S(2)}) copy-start(f32[2,128,8]{1,2,0:T(8,128)} %param.13) | copy-start | bytes 24580
  40.4 25.1 %collective-permute-start.4 = (bf16[1024,512]{1,0:T(8,128)(2,1)S(1)}, bf16[1024,512]{1,0:T(8,128)(2,1)S(1)}, u32[]{:S(2)}, u32[]{:S(2)}) collective-permute-start(bf16[1024,512]{1,0:T(8,128)(2,1)S(1)} %bitcast.26), channel_id=1, source_target_pairs={{0,128},{128,0},{4,132},{132,4},{8,136},{136,8},{12,140},{140,12},... | collective-permute-start | bytes 3145736 | tf_op jit(solution)/shard_map/ppermute | solution.py:99
  42.0 29.8 %collective-permute-start = (bf16[1024,512]{1,0:T(8,128)(2,1)S(1)}, bf16[1024,512]{1,0:T(8,128)(2,1)S(1)}, u32[]{:S(2)}, u32[]{:S(2)}) collective-permute-start(bf16[1024,512]{1,0:T(8,128)(2,1)S(1)} %bitcast.27), channel_id=1, source_target_pairs={{128,4},{4,128},{132,8},{8,132},{136,12},{12,136},{140,0},{0,140},... | collective-permute-start | bytes 3145736 | tf_op jit(solution)/shard_map/ppermute | solution.py:99
  46.6 1.0 copy-start.2
  65.5 28.2 %collective-permute-start.5 = (bf16[1024,512]{1,0:T(8,128)(2,1)S(1)}, bf16[1024,512]{1,0:T(8,128)(2,1)}, u32[]{:S(2)}, u32[]{:S(2)}) collective-permute-start(bf16[1024,512]{1,0:T(8,128)(2,1)S(1)} %collective-permute-done.4.refs_3_), channel_id=1, source_target_pairs={{128,4},{4,128},{132,8},{8,132},{136,12},{12,136},{140,0},{0,140},... | collective-permute-start | bytes 3145736 | tf_op jit(solution)/shard_map/ppermute | solution.py:99
  70.7 1.0 copy-start.4
  71.8 23.7 %collective-permute-start.1 = (bf16[1024,512]{1,0:T(8,128)(2,1)S(1)}, bf16[1024,512]{1,0:T(8,128)(2,1)}, u32[]{:S(2)}, u32[]{:S(2)}) collective-permute-start(bf16[1024,512]{1,0:T(8,128)(2,1)S(1)} %collective-permute-done.refs_3_), channel_id=1, source_target_pairs={{0,128},{128,0},{4,132},{132,4},{8,136},{136,8},{12,140},{140,12},... | collective-permute-start | bytes 3145736 | tf_op jit(solution)/shard_map/ppermute | solution.py:99
  71.8 1.0 copy-start
  93.7 31.7 %collective-permute-start.6 = (bf16[1024,512]{1,0:T(8,128)(2,1)}, bf16[1024,512]{1,0:T(8,128)(2,1)S(1)}, u32[]{:S(2)}, u32[]{:S(2)}) collective-permute-start(bf16[1024,512]{1,0:T(8,128)(2,1)} %collective-permute-done.5.refs_2_), channel_id=1, source_target_pairs={{0,128},{128,0},{4,132},{132,4},{8,136},{136,8},{12,140},{140,12},... | collective-permute-start | bytes 3145736 | tf_op jit(solution)/shard_map/ppermute | solution.py:99
  95.5 29.0 %collective-permute-start.2 = (bf16[1024,512]{1,0:T(8,128)(2,1)}, bf16[1024,512]{1,0:T(8,128)(2,1)S(1)}, u32[]{:S(2)}, u32[]{:S(2)}) collective-permute-start(bf16[1024,512]{1,0:T(8,128)(2,1)} %collective-permute-done.1.refs_2_), channel_id=1, source_target_pairs={{128,4},{4,128},{132,8},{8,132},{136,12},{12,136},{140,0},{0,140},... | collective-permute-start | bytes 3145736 | tf_op jit(solution)/shard_map/ppermute | solution.py:99
  125.3 28.2 %collective-permute-start.3 = (bf16[512,512]{1,0:T(8,128)(2,1)}, bf16[512,512]{1,0:T(8,128)(2,1)}, u32[]{:S(2)}, u32[]{:S(2)}) collective-permute-start(bf16[512,512]{1,0:T(8,128)(2,1)} %slice.50), channel_id=1, source_target_pairs={{0,128},{128,0},{4,132},{132,4},{8,136},{136,8},{12,140},{140,12},... | collective-permute-start | bytes 1572872 | tf_op jit(solution)/shard_map/ppermute | solution.py:99
  126.2 27.4 %collective-permute-start.7 = (bf16[512,512]{1,0:T(8,128)(2,1)}, bf16[512,512]{1,0:T(8,128)(2,1)}, u32[]{:S(2)}, u32[]{:S(2)}) collective-permute-start(bf16[512,512]{1,0:T(8,128)(2,1)} %slice.51), channel_id=1, source_target_pairs={{128,4},{4,128},{132,8},{8,132},{136,12},{12,136},{140,0},{0,140},... | collective-permute-start | bytes 1572872 | tf_op jit(solution)/shard_map/ppermute | solution.py:99
  128.8 1.2 copy-start.3
  130.0 1.2 copy-start.5
  131.2 7.2 %copy-start.1 = (bf16[1024,512]{1,0:T(8,128)(2,1)S(1)}, bf16[1024,512]{1,0:T(8,128)(2,1)}, u32[]{:S(2)}) copy-start(bf16[1024,512]{1,0:T(8,128)(2,1)} %copy-done) | copy-start | bytes 3145732
Sparse Core Ops, SparseCore 0:
  12.5 56.5 all-gather.1

commit v2 on v1

v2 whole, which is shorter than its diff:
```python
import jax
import jax.numpy as jnp
from jax import lax
from jax.experimental import pallas as pl
from jax.experimental.pallas import tpu as pltpu
from jax.sharding import Mesh, PartitionSpec as P

learn_rate = 0.01
decay_rate = 0.1
beta_one = 0.9
beta_two = 0.95
epsilon = 1e-08
correct_one = 1.0 - 0.9**4
correct_two = 1.0 - 0.95**4

CAP = 32
PARTS = 4
BIG = 40 * 2**20


def adam_update(master, first_moment, second_moment, gradient):
    grad_full = gradient.astype(jnp.float32)
    new_first = beta_one * first_moment + (1.0 - beta_one) * grad_full
    new_second = beta_two * second_moment + (1.0 - beta_two) * grad_full * grad_full
    update = new_first / correct_one / (jnp.sqrt(new_second / correct_two) + epsilon)
    return master * (1.0 - learn_rate * decay_rate) - learn_rate * update


def pick_kernel(where_ref, ids_ref, low_ref, high_ref, out_ref):
    steps, _, count = ids_ref.shape[2:]
    half = low_ref.shape[1]
    earlier = lax.broadcasted_iota(jnp.int32, (count, count), 0)
    later = lax.broadcasted_iota(jnp.int32, (count, count), 1)
    before = jnp.where(earlier < later, 1.0, 0.0).astype(jnp.bfloat16)
    slot = lax.broadcasted_iota(jnp.int32, (CAP, count), 0).astype(jnp.float32)
    for step in range(steps):
        ids = ids_ref[0, 0, step]
        masks = []
        for part in range(PARTS):
            hit = jnp.where(ids == where_ref[1 + part], 1.0, 0.0)
            masks.append(jnp.max(hit, axis=0, keepdims=True))
        mask = jnp.concatenate(masks * 2, axis=0)
        place = jnp.dot(
            mask.astype(jnp.bfloat16), before, preferred_element_type=jnp.float32
        )
        chosen = [
            jnp.where(slot == place[part : part + 1], mask[part : part + 1], 0.0)
            for part in range(PARTS)
        ]
        chosen = jnp.concatenate(chosen, axis=0).astype(jnp.bfloat16)
        rows = slice(step * count, (step + 1) * count)
        for at, ref in ((0, low_ref), (half, high_ref)):
            picked = jnp.dot(chosen, ref[rows, :], preferred_element_type=jnp.float32)
            picked = picked.astype(jnp.bfloat16)
            for part in range(PARTS):
                out_ref[part, step * CAP : (step + 1) * CAP, at : at + half] = picked[
                    part * CAP : (part + 1) * CAP
                ]


def pick_rows(where, all_ids, all_tokens, group_rows):
    ys, cores, steps, choices, count = all_ids.shape
    total, depth = all_tokens.shape
    half = depth // 2
    groups = total // group_rows
    return pl.pallas_call(
        pick_kernel,
        grid_spec=pltpu.PrefetchScalarGridSpec(
            num_scalar_prefetch=1,
            grid=(groups,),
            in_specs=[
                pl.BlockSpec(
                    (1, 1, steps, choices, count), lambda i, w: (i % ys, i // ys, 0, 0, 0)
                ),
                pl.BlockSpec((group_rows, half), lambda i, w: (i, w[0])),
                pl.BlockSpec((group_rows, half), lambda i, w: (i, 1 - w[0])),
            ],
            out_specs=pl.BlockSpec((PARTS, steps * CAP, depth), lambda i, w: (0, i, 0)),
        ),
        out_shape=jax.ShapeDtypeStruct((PARTS, groups * steps * CAP, depth), jnp.bfloat16),
        compiler_params=pltpu.CompilerParams(vmem_limit_bytes=BIG),
        cost_estimate=pl.CostEstimate(
            flops=8 * total * 128 * depth, bytes_accessed=4 * total * depth, transcendentals=0
        ),
    )(where, all_ids, all_tokens, all_tokens)


def expert_kernel(rows_ref, *refs):
    weights, out_ref = refs[:-1], refs[-1]
    at, product = 0, None
    for weight in weights:
        depth = weight.shape[0]
        piece = jnp.dot(
            rows_ref[0, :, at : at + depth], weight[...], preferred_element_type=jnp.float32
        )
        product = piece if product is None else product + piece
        at += depth
    value = (product * jax.nn.sigmoid(product)).astype(out_ref.dtype)
    groups, quarters, rows, width = out_ref.shape
    for group in range(groups):
        for quarter in range(quarters):
            out_ref[group, quarter] = value[
                group * rows : (group + 1) * rows, quarter * width : (quarter + 1) * width
            ]


def run_expert(picked, part, weights, groups, quarters):
    _, count, depth = picked.shape
    width = weights[0].shape[1]
    strip = width // quarters
    cuts = 2
    return pl.pallas_call(
        expert_kernel,
        grid=(cuts,),
        in_specs=[pl.BlockSpec((1, count, depth), lambda i: (part, 0, 0))]
        + [pl.BlockSpec((w.shape[0], width // cuts), lambda i: (0, i)) for w in weights],
        out_specs=pl.BlockSpec(
            (groups, quarters // cuts, count // groups, strip), lambda i: (0, i, 0, 0)
        ),
        out_shape=jax.ShapeDtypeStruct((groups, quarters, count // groups, strip), jnp.bfloat16),
        compiler_params=pltpu.CompilerParams(vmem_limit_bytes=BIG),
        cost_estimate=pl.CostEstimate(
            flops=2 * count * depth * width,
            bytes_accessed=2 * count * depth + 2 * depth * width + 2 * count * width,
            transcendentals=count * width,
        ),
    )(picked, *weights)


def place_kernel(order_ref, ids_ref, raw_ref, out_ref):
    count, choices = ids_ref.shape[1:]
    lanes = out_ref.shape[2]
    names = 128
    ids = ids_ref[0]
    raw = raw_ref[0]
    shares = raw / jnp.sum(raw, axis=1, keepdims=True)
    name = lax.broadcasted_iota(jnp.int32, (count, names), 1)
    mask = jnp.zeros((count, names), jnp.float32)
    weight = jnp.zeros((count, names), jnp.float32)
    for choice in range(choices):
        hit = ids[:, choice : choice + 1] == name
        mask = mask + jnp.where(hit, 1.0, 0.0)
        weight = weight + jnp.where(hit, shares[:, choice : choice + 1], 0.0)
    row = lax.broadcasted_iota(jnp.int32, (count, count), 0)
    column = lax.broadcasted_iota(jnp.int32, (count, count), 1)
    before = jnp.where(column < row, 1.0, 0.0).astype(jnp.bfloat16)
    place = jnp.dot(before, mask.astype(jnp.bfloat16), preferred_element_type=jnp.float32)
    place = jnp.where(mask > 0.0, place, 255.0).astype(jnp.bfloat16)
    high = weight.astype(jnp.bfloat16)
    low = (weight - high.astype(jnp.float32)).astype(jnp.bfloat16)
    stacked = jnp.concatenate([place, high, low], axis=0)
    span = lanes // PARTS
    for part in range(PARTS):
        lane = lax.broadcasted_iota(jnp.int32, (names, span), 1)
        device = lane // CAP
        expert = (device // 4 * 4 + order_ref[part]) * 4 + device % 4
        spread = jnp.where(
            lax.broadcasted_iota(jnp.int32, (names, span), 0) == expert, 1.0, 0.0
        ).astype(jnp.bfloat16)
        wide = jnp.dot(stacked, spread, preferred_element_type=jnp.float32)
        slot = (lax.broadcasted_iota(jnp.int32, (count, span), 1) % CAP).astype(jnp.float32)
        here = wide[:count] == slot
        at = slice(part * span, (part + 1) * span)
        out_ref[0, :count, at] = jnp.where(here, wide[count : 2 * count], 0.0).astype(jnp.bfloat16)
        out_ref[0, count:, at] = jnp.where(here, wide[2 * count :], 0.0).astype(jnp.bfloat16)


def place_rows(order, ids, raw, lanes):
    steps, count, choices = ids.shape
    return pl.pallas_call(
        place_kernel,
        grid_spec=pltpu.PrefetchScalarGridSpec(
            num_scalar_prefetch=1,
            grid=(steps,),
            in_specs=[pl.BlockSpec((1, count, choices), lambda i, w: (i, 0, 0))] * 2,
            out_specs=pl.BlockSpec((1, 2 * count, lanes), lambda i, w: (i, 0, 0)),
        ),
        out_shape=jax.ShapeDtypeStruct((steps, 2 * count, lanes), jnp.bfloat16),
        compiler_params=pltpu.CompilerParams(vmem_limit_bytes=BIG),
        cost_estimate=pl.CostEstimate(
            flops=2 * steps * 3 * count * 128 * lanes,
            bytes_accessed=4 * steps * count * lanes,
            transcendentals=0,
        ),
    )(order, ids, raw)


def mix_kernel(place_ref, *refs):
    returned, out_ref = refs[:-1], refs[-1]
    steps, count, width = out_ref.shape
    for step in range(steps):
        total = None
        for part, ref in enumerate(returned):
            cores, devices, _, slots, strip = ref.shape
            span = devices * slots
            rows = jnp.concatenate(
                [ref[core, :, step].reshape(span, strip) for core in range(cores)], axis=1
            )
            piece = jnp.dot(
                place_ref[step, :, part * span : (part + 1) * span],
                rows,
                preferred_element_type=jnp.float32,
            )
            total = piece if total is None else total + piece
        out_ref[step] = (total[:count] + total[count:]).astype(out_ref.dtype)


def mix_rows(placed, returned, count, width):
    steps = placed.shape[0]
    return pl.pallas_call(
        mix_kernel,
        in_specs=[pl.BlockSpec(memory_space=pltpu.VMEM)] * (1 + len(returned)),
        out_specs=pl.BlockSpec(memory_space=pltpu.VMEM),
        out_shape=jax.ShapeDtypeStruct((steps, count, width), jnp.bfloat16),
        compiler_params=pltpu.CompilerParams(vmem_limit_bytes=BIG),
        cost_estimate=pl.CostEstimate(
            flops=4 * placed.size * width // 2, bytes_accessed=2 * placed.size, transcendentals=0
        ),
    )(placed, *returned)


def swap(value, offset):
    high, low = lax.axis_size("zh"), lax.axis_size("zl")
    pairs = []
    for z in range(offset, high * low + offset, low):
        a, b = [(at % low) * high + at // low % high for at in (z, z + 1)]
        pairs += [(a, b), (b, a)]
    return lax.ppermute(value, ("zl", "zh"), pairs)


def gather_ids(expert_ids):
    own = expert_ids.transpose(0, 2, 1)
    other = lax.ppermute(own, "core", [(0, 1), (1, 0)])
    first = lax.axis_index("core") == 0
    pair = jnp.stack([jnp.where(first, own, other), jnp.where(first, other, own)])
    size = lax.axis_size("y")
    ring = [pair]
    for away in range(1, size):
        ring.append(lax.ppermute(pair, "y", [((at + away) % size, at) for at in range(size)]))
    ring = jnp.stack(ring + ring)
    return lax.dynamic_slice_in_dim(ring, size - lax.axis_index("y"), size, axis=0)


def per_device(master, first_moment, second_moment, gradient, tokens, expert_ids, router_scores):
    steps, token_count, depth = tokens.shape
    quarters = lax.axis_size("x")
    cores = lax.axis_size("core")
    owners = lax.axis_size("zh")
    ys = lax.axis_size("y")
    groups = cores * ys
    z_low, z_high = lax.axis_index("zl"), lax.axis_index("zh")
    y_at, x_at = lax.axis_index("y"), lax.axis_index("x")

    all_tokens = lax.all_gather(
        tokens.reshape(steps * token_count, depth), ("core", "y"), axis=0, tiled=True
    )
    all_ids = gather_ids(expert_ids)

    turn = jnp.where(z_low == 0, 1, -1)
    order = jnp.mod(jnp.stack([z_high, z_high - turn, z_high + turn, z_high + 2]), owners)
    names = quarters * (y_at * owners + order) + x_at
    where = jnp.concatenate([z_low[None], names]).astype(jnp.int32)

    new_master = adam_update(master, first_moment, second_moment, gradient)
    lowered = new_master.astype(jnp.bfloat16)
    experts, rows, width = lowered.shape
    strip = width // (quarters * cores)
    blocks = lowered.reshape(experts, rows, quarters, cores, strip)
    blocks = blocks.transpose(3, 0, 1, 2, 4).reshape(cores * experts, rows, quarters * strip)
    blocks, all_ids = lax.optimization_barrier((blocks, all_ids))
    own = lax.all_to_all(blocks, ("core", "x"), split_axis=0, concat_axis=0, tiled=True)
    own = own.reshape(-1, quarters * strip)

    def expert(part, weights):
        acted = run_expert(picked, part, weights, groups, quarters)
        acted = acted.reshape(groups * quarters, steps * CAP, strip)
        back = lax.all_to_all(acted, ("core", "y", "x"), split_axis=0, concat_axis=0, tiled=True)
        return back.reshape(cores, ys * quarters, steps, CAP, strip)

    hold = lax.optimization_barrier
    a1, c1 = swap(own, 0), swap(own, 1)
    placed = place_rows(
        order.astype(jnp.int32), expert_ids, router_scores, PARTS * quarters * ys * CAP
    )
    a1, c1, placed = hold((a1, c1, placed))
    a2, c2 = swap(c1, 0), swap(a1, 1)
    picked = pick_rows(where, all_ids, all_tokens, steps * token_count)
    a2, c2, picked = hold((a2, c2, picked))
    a3, c3 = swap(c2, 0), swap(a2, 1)
    back1, back2 = expert(0, [own, a1]), expert(1, [c2, c1])
    a3, c3, back1, back2 = hold((a3, c3, back1, back2))
    cut = own.shape[0] // 2
    a4, c4 = swap(c3[:cut], 0), swap(a3[cut:], 1)
    back3 = expert(2, [a2, a3])
    a4, c4, back3 = hold((a4, c4, back3))
    returned = [back1, back2, back3, expert(3, [a4, c4, c3])]
    mixed = mix_rows(placed, returned, token_count, cores * strip)
    return (new_master, mixed)


def solution(mesh):
    grid = Mesh(mesh.devices.reshape(2, 2, 4, 4, 4), ("zl", "core", "y", "zh", "x"))
    owner, part, group = ("y", "zh"), ("zl", "core", "x"), ("zl", "core", "y", "zh")
    weights = P(owner, part, None)
    routed = P(None, group, None)
    return jax.shard_map(
        per_device,
        mesh=grid,
        in_specs=(weights,) * 4 + (routed,) * 3,
        out_specs=(weights, P(None, group, "x")),
        check_vma=False,
    )
```

time: 202 us -> 194 us (0.960)
  starting transfers between devices: 14.7 us -> 25.3 us
  blocking collectives: 78 us -> 67.6 us
  other arithmetic: 11.5 us -> 6.28 us
  Pallas kernels: 29.9 us -> 25 us
    all_gather x1 -> x0, blocking collectives: 24.5 us -> none  [per_device(): both = lax.all_gather(both, ('core', 'y'), axis=0, tiled=True)]
    all_to_all x1 -> x3, blocking collectives: 32.4 us -> 46.6 us  [expert(): lax.all_to_all(acted, ('core', 'y', 'x'), split_axis=0, concat_axis=0, ti...]
    all_to_all x0 -> x1, starting transfers between devices: none -> 7.1 us  [expert(): lax.all_to_all(acted, ('core', 'y', 'x'), split_axis=0, concat_axis=0, ti...]
    ppermute x8, waiting for transfers between devices: 40.6 us -> 34 us  [swap(): return lax.ppermute(value, ('zl', 'zh'), pairs)]
    ppermute x0 -> x4, starting transfers between devices: none -> 5.44 us  [the longest x1 3.33 us: gather_ids(): other = lax.ppermute(own, 'core', [(0, 1), (1, 0)])]
    pallas_call x4 -> x7, Pallas kernels: 29.9 us -> 25 us  [the longest x4 10.5 us: run_expert(): pl.pallas_call(expert_kernel, grid=(cuts,), in_specs=[pl.BlockSpec((1, co...]
    all_to_all x0 -> x1, waiting for transfers between devices: none -> 4.35 us  [expert(): lax.all_to_all(acted, ('core', 'y', 'x'), split_axis=0, concat_axis=0, ti...]
    ppermute x0 -> x4, waiting for transfers between devices: none -> 3.22 us  [the longest x3 3.22 us: gather_ids(): lax.ppermute(pair, 'y', [((at + away) % size, at) for at in range(size)])]
  transfers between devices with their start and end apart: 9 -> 14, of which waited for: 3 -> 8; matrix products, arithmetic and copies ran while one was open for 6% -> 5% of each run, Pallas kernels for 11% -> 10%
where the time goes in v2:
time: 194 us; the launch traced here: 193 us
  blocking collectives  67.6 us (35%)
  waiting for transfers between devices  42.3 us (22%)
  starting transfers between devices  25.3 us (13%)
  Pallas kernels  25 us (13%)
  between operations  14.3 us (7%)
  local copies, waits for them, and re-layouts  12.3 us (6%)
  other arithmetic  6.28 us (3%)
    all_to_all x3, blocking collectives, expert(): lax.all_to_all(acted, ('core', 'y', 'x'), split_axis=0, concat_axis=0, ti...  46.6 us
    ppermute x8, waiting for transfers between devices, swap(): return lax.ppermute(value, ('zl', 'zh'), pairs)  34 us
    all_to_all x1, blocking collectives, per_device(): lax.all_to_all(blocks, ('core', 'x'), split_axis=0, concat_axis=0, tiled=...  21.1 us
    ppermute x8, starting transfers between devices, swap(): return lax.ppermute(value, ('zl', 'zh'), pairs)  12.8 us
    pallas_call x4, Pallas kernels, run_expert(): pl.pallas_call(expert_kernel, grid=(cuts,), in_specs=[pl.BlockSpec((1, co...  10.5 us
    pallas_call x1, Pallas kernels, pick_rows(): pl.pallas_call(pick_kernel, grid_spec=pltpu.PrefetchScalarGridSpec(num_sc...  9.33 us
    unnamed x21, local copies, waits for them, and re-layouts  8.67 us
    all_to_all x1, starting transfers between devices, expert(): lax.all_to_all(acted, ('core', 'y', 'x'), split_axis=0, concat_axis=0, ti...  7.1 us
  transfers between devices with their start and end apart: 14, of which 8 were waited for; matrix products, arithmetic and copies ran while one was open for 5% of the time, Pallas kernels for 10%

profile of v2, /device:TPU:1, one launch (start us, length us, event | category | flops | bytes accessed | tf_op | source)
XLA Modules:
  0.0 193.2 jit_solution(1027368627865091048)
XLA Ops:
  7.9 3.3 %collective-permute-start = (s32[2,8,128]{2,1,0:T(8,128)}, s32[2,8,128]{2,1,0:T(8,128)S(1)}, u32[]{:S(2)}, u32[]{:S(2)}) collective-permute-start(s32[2,8,128]{2,1,0:T(8,128)} %bitcast.47), channel_id=1, source_target_pairs={{0,64},{64,0},{1,65},{65,1},{2,66},{66,2},{3,67},{67,3},{4,68},{68... | collective-permute-start | bytes 24584 | tf_op jit(solution)/shard_map/ppermute | solution.py:233
  11.2 6.1 %fusion.10 = (bf16[4,128,1024]{2,1,0:T(8,128)(2,1)S(1)}, f32[4,128,1024]{2,1,0:T(8,128)}) fusion(f32[4,128,1024]{2,1,0:T(8,128)} %param.9, bf16[4,128,1024]{2,1,0:T(8,128)(2,1)} %param.10, f32[4,128,1024]{2,1,0:T(8,128)} %param.8, f32[4,128,1024]{2,1,0:T(8,128)} %param.7), kind=kLoop, calls=%fused_computation.29 | loop fusion | flops 8388608 | bytes 10485760 | tf_op jit(solution)/shard_map/convert_element_type | solution.py:265
  21.6 2.5 %collective-permute-done.2 = s32[2,2,8,128]{3,2,1,0:T(8,128)S(1)} collective-permute-done((s32[2,2,8,128]{3,2,1,0:T(8,128)S(1)}, s32[2,2,8,128]{3,2,1,0:T(8,128)S(1)}, u32[]{:S(2)}, u32[]{:S(2)}) %collective-permute-start.2) | collective-permute-done | bytes 16416 | tf_op jit(solution)/shard_map/ppermute | solution.py:239
  24.3 21.1 %all_to_all.25 = bf16[8,128,512]{2,1,0:T(8,128)(2,1)S(1)} all-to-all(bf16[8,128,512]{2,1,0:T(8,128)(2,1)S(1)} %reshape.41), channel_id=1, replica_groups=mesh['zl'=2,'core'=2,'y'=4,'zh'=4,'x'=4] {'core','x'}, dimensions={0} | all-to-all | bytes 2097152 | tf_op jit(solution)/shard_map/all_to_all | solution.py:271
  47.0 4.7 %collective-permute-start.5 = (bf16[1024,512]{1,0:T(8,128)(2,1)S(1)}, bf16[1024,512]{1,0:T(8,128)(2,1)}, u32[]{:S(2)}, u32[]{:S(2)}) collective-permute-start(bf16[1024,512]{1,0:T(8,128)(2,1)S(1)} %bitcast.36), channel_id=1, source_target_pairs={{128,4},{4,128},{132,8},{8,132},{136,12},{12,136},{140,0},{0,140},... | collective-permute-start | bytes 3145736 | tf_op jit(solution)/shard_map/ppermute | solution.py:228
  52.0 2.8 %shard_map.86.place_ref = bf16[2,256,2048]{2,1,0:T(8,128)(2,1)S(1)} custom-call(s32[4]{0:T(128)S(1)} %get-tuple-element.33.order_ref, s32[2,128,8]{2,1,0:T(8,128)S(1)} %copy.10.ids_ref, f32[2,128,8]{2,1,0:T(8,128)S(1)} %copy.11.raw_ref), custom_call_target="tpu_custom_call" | custom-call | flops 402653184 | bytes 2097152 | tf_op jit(solution)/shard_map/pallas_call | solution.py:170
  54.9 15.7 %collective-permute-done.4.refs_1_ = bf16[1024,512]{1,0:T(8,128)(2,1)} collective-permute-done((bf16[1024,512]{1,0:T(8,128)(2,1)S(1)}, bf16[1024,512]{1,0:T(8,128)(2,1)}, u32[]{:S(2)}, u32[]{:S(2)}) %collective-permute-start.4) | collective-permute-done | bytes 1048608 | tf_op jit(solution)/shard_map/ppermute | solution.py:228
  70.6 4.6 %collective-permute-done.5.refs_1_ = bf16[1024,512]{1,0:T(8,128)(2,1)} collective-permute-done((bf16[1024,512]{1,0:T(8,128)(2,1)S(1)}, bf16[1024,512]{1,0:T(8,128)(2,1)}, u32[]{:S(2)}, u32[]{:S(2)}) %collective-permute-start.5) | collective-permute-done | bytes 1048608 | tf_op jit(solution)/shard_map/ppermute | solution.py:228
  75.2 2.4 %collective-permute-start.7 = (bf16[1024,512]{1,0:T(8,128)(2,1)}, bf16[1024,512]{1,0:T(8,128)(2,1)}, u32[]{:S(2)}, u32[]{:S(2)}) collective-permute-start(bf16[1024,512]{1,0:T(8,128)(2,1)} %collective-permute-done.4.refs_1_), channel_id=1, source_target_pairs={{128,4},{4,128},{132,8},{8,132},{136,12},{12,136},{140,0},{0,140},... | collective-permute-start | bytes 3145736 | tf_op jit(solution)/shard_map/ppermute | solution.py:228
  77.6 9.3 %shard_map.87.rows_ref = bf16[4,512,2048]{2,1,0:T(8,128)(2,1)S(1)} custom-call(s32[5]{0:T(128)S(1)} %pad_add_fusion.1.where_ref, s32[4,2,2,8,128]{4,3,2,1,0:T(8,128)S(1)} %constant_dynamic-slice_fusion.ids_ref, bf16[2048,2048]{1,0:T(8,128)(2,1)} %all-gather.2.cloned.1.call-done.low_ref.high_ref, bf16[2048,2048]{1,0:T(8,128)(2,1)} %all-gather.2.cloned.1.call-done.low_ref.high_ref), custom_call_target="tpu_custom_call" | custom-call | flops 4294967296 | bytes 16777216 | tf_op jit(solution)/shard_map/pallas_call | solution.py:66
  87.0 12.5 %collective-permute-done.6.refs_0_ = bf16[1024,512]{1,0:T(8,128)(2,1)} collective-permute-done((bf16[1024,512]{1,0:T(8,128)(2,1)}, bf16[1024,512]{1,0:T(8,128)(2,1)}, u32[]{:S(2)}, u32[]{:S(2)}) %collective-permute-start.6) | collective-permute-done | bytes 1048608 | tf_op jit(solution)/shard_map/ppermute | solution.py:228
  102.7 2.7 %shard_map.89 = bf16[8,4,64,128]{3,2,1,0:T(8,128)(2,1)S(1)} custom-call(bf16[4,512,2048]{2,1,0:T(8,128)(2,1)S(1)} %shard_map.87.rows_ref, bf16[1024,512]{1,0:T(8,128)(2,1)} %collective-permute-done.7.refs_0_, bf16[1024,512]{1,0:T(8,128)(2,1)} %collective-permute-done.5.refs_1_), custom_call_target="tpu_custom_call" | custom-call | flops 1073741824 | bytes 4718592 | tf_op jit(solution)/shard_map/pallas_call | solution.py:112
  106.2 7.1 %all-to-all-start.2 = ((bf16[32,64,128]{2,1,0:T(8,128)(2,1)}), bf16[32,64,128]{2,1,0:T(8,128)(2,1)}, u32[]{:S(2)}, u32[]{:S(2)}) async-start(bf16[32,64,128]{2,1,0:T(8,128)(2,1)} %bitcast.41), calls=%async_computation.2 | async-start | bytes 1048576 | tf_op jit(solution)/shard_map/all_to_all | solution.py:277
  113.3 3.4 %copy-done.1 = bf16[4,512,2048]{2,1,0:T(8,128)(2,1)S(1)} copy-done((bf16[4,512,2048]{2,1,0:T(8,128)(2,1)S(1)}, bf16[4,512,2048]{2,1,0:T(8,128)(2,1)}, u32[]{:S(2)}) %copy-start.1) | copy-done | bytes 8388632
  116.6 2.6 %shard_map.88 = bf16[8,4,64,128]{3,2,1,0:T(8,128)(2,1)S(1)} custom-call(bf16[4,512,2048]{2,1,0:T(8,128)(2,1)S(1)} %copy-done.1, bf16[1024,512]{1,0:T(8,128)(2,1)S(1)} %bitcast.37, bf16[1024,512]{1,0:T(8,128)(2,1)} %collective-permute-done.4.refs_1_), custom_call_target="tpu_custom_call" | custom-call | flops 1073741824 | bytes 4718592 | tf_op jit(solution)/shard_map/pallas_call | solution.py:112
  120.1 4.3 %all-to-all-done.2 = bf16[32,64,128]{2,1,0:T(8,128)(2,1)} async-done(((bf16[32,64,128]{2,1,0:T(8,128)(2,1)}), bf16[32,64,128]{2,1,0:T(8,128)(2,1)}, u32[]{:S(2)}, u32[]{:S(2)}) %all-to-all-start.2) | async-done | bytes 524320 | tf_op jit(solution)/shard_map/all_to_all | solution.py:277
  124.4 15.9 %all_to_all.26 = bf16[32,64,128]{2,1,0:T(8,128)(2,1)S(1)} all-to-all(bf16[32,64,128]{2,1,0:T(8,128)(2,1)} %bitcast.42), channel_id=1, replica_groups=mesh['zl'=2,'core'=2,'y'=4,'zh'=4,'x'=4] {'core','y','x'}, dimensions={0} | all-to-all | bytes 1048576 | tf_op jit(solution)/shard_map/all_to_all | solution.py:277
  142.5 2.0 %collective-permute-start.11 = (bf16[512,512]{1,0:T(8,128)(2,1)S(1)}, bf16[512,512]{1,0:T(8,128)(2,1)S(1)}, u32[]{:S(2)}, u32[]{:S(2)}) collective-permute-start(bf16[512,512]{1,0:T(8,128)(2,1)S(1)} %slice.7), channel_id=1, source_target_pairs={{128,4},{4,128},{132,8},{8,132},{136,12},{12,136},{140,0},{0,140},... | collective-permute-start | bytes 1572872 | tf_op jit(solution)/shard_map/ppermute | solution.py:228
  144.6 3.4 %copy-done.2 = bf16[4,512,2048]{2,1,0:T(8,128)(2,1)S(1)} copy-done((bf16[4,512,2048]{2,1,0:T(8,128)(2,1)S(1)}, bf16[4,512,2048]{2,1,0:T(8,128)(2,1)}, u32[]{:S(2)}) %copy-start.2) | copy-done | bytes 8388632
  147.9 2.7 %shard_map.90 = bf16[8,4,64,128]{3,2,1,0:T(8,128)(2,1)S(1)} custom-call(bf16[4,512,2048]{2,1,0:T(8,128)(2,1)S(1)} %copy-done.2, bf16[1024,512]{1,0:T(8,128)(2,1)} %collective-permute-done.6.refs_0_, bf16[1024,512]{1,0:T(8,128)(2,1)} %collective-permute-done.8.refs_1_), custom_call_target="tpu_custom_call" | custom-call | flops 1073741824 | bytes 4718592 | tf_op jit(solution)/shard_map/pallas_call | solution.py:112
  150.6 15.6 %all_to_all.27 = bf16[32,64,128]{2,1,0:T(8,128)(2,1)S(1)} all-to-all(bf16[32,64,128]{2,1,0:T(8,128)(2,1)S(1)} %bitcast.44), channel_id=1, replica_groups=mesh['zl'=2,'core'=2,'y'=4,'zh'=4,'x'=4] {'core','y','x'}, dimensions={0} | all-to-all | bytes 1048576 | tf_op jit(solution)/shard_map/all_to_all | solution.py:277
  166.3 2.6 %shard_map.91 = bf16[8,4,64,128]{3,2,1,0:T(8,128)(2,1)S(1)} custom-call(bf16[4,512,2048]{2,1,0:T(8,128)(2,1)S(1)} %copy-done.2, bf16[512,512]{1,0:T(8,128)(2,1)S(1)} %collective-permute-done.10.refs_0_, bf16[512,512]{1,0:T(8,128)(2,1)S(1)} %collective-permute-done.11.refs_1_, bf16[1024,512]{1,0:T(8,128)(2,1)} %collective-permute-done.9.refs_2_), custom_call_target="tpu_custom_call" | custom-call | flops 1073741824 | bytes 4718592 | tf_op jit(solution)/shard_map/pallas_call | solution.py:112
  168.8 15.1 %all_to_all.28 = bf16[32,64,128]{2,1,0:T(8,128)(2,1)S(1)} all-to-all(bf16[32,64,128]{2,1,0:T(8,128)(2,1)S(1)} %bitcast.43), channel_id=1, replica_groups=mesh['zl'=2,'core'=2,'y'=4,'zh'=4,'x'=4] {'core','y','x'}, dimensions={0} | all-to-all | bytes 1048576 | tf_op jit(solution)/shard_map/all_to_all | solution.py:277
  183.9 2.4 %shard_map.92 = bf16[2,128,256]{2,1,0:T(8,128)(2,1)} custom-call(bf16[2,256,2048]{2,1,0:T(8,128)(2,1)S(1)} %shard_map.86.place_ref, bf16[2,16,2,32,128]{4,3,2,1,0:T(8,128)(2,1)S(1)} %bitcast.38, bf16[2,16,2,32,128]{4,3,2,1,0:T(8,128)(2,1)} %bitcast.18.refs_1_, bf16[2,16,2,32,128]{4,3,2,1,0:T(8,128)(2,1)S(1)} %bitcast.39, ...), custom_call_target="tpu_custom_call" | custom-call | flops 536870912 | bytes 2097152 | tf_op jit(solution)/shard_map/pallas_call | solution.py:210
  (51 shorter events, 14.2 us)
Async XLA Ops:
  7.2 70.4 %all-gather.2.cloned.1.call-start = ((), (), s32[]{:S(2)}) async-start(), calls=%async_computation.5 | async-start | bytes 9437184 | tf_op jit(solution)/shard_map/all_gather | solution.py:254
  7.9 10.9 %collective-permute-start = (s32[2,8,128]{2,1,0:T(8,128)}, s32[2,8,128]{2,1,0:T(8,128)S(1)}, u32[]{:S(2)}, u32[]{:S(2)}) collective-permute-start(s32[2,8,128]{2,1,0:T(8,128)} %bitcast.47), channel_id=1, source_target_pairs={{0,64},{64,0},{1,65},{65,1},{2,66},{66,2},{3,67},{67,3},{4,68},{68... | collective-permute-start | bytes 24584 | tf_op jit(solution)/shard_map/ppermute | solution.py:233
  18.1 0.8 copy-start.5
  18.4 33.4 %copy-start.6 = (f32[2,128,8]{1,2,0:T(8,128)S(1)}, f32[2,128,8]{1,2,0:T(8,128)}, u32[]{:S(2)}) copy-start(f32[2,128,8]{1,2,0:T(8,128)} %param.13) | copy-start | bytes 24580
  18.9 2.7 %collective-permute-start.1 = (s32[2,2,8,128]{3,2,1,0:T(8,128)S(1)}, s32[2,2,8,128]{3,2,1,0:T(8,128)S(1)}, u32[]{:S(2)}, u32[]{:S(2)}) collective-permute-start(s32[2,2,8,128]{3,2,1,0:T(8,128)S(1)} %pad_add_fusion), channel_id=1, source_target_pairs={{16,0},{32,16},{48,32},{0,48},{17,1},{33,17},{49,33},{1,49},{18,2}... | collective-permute-start | bytes 49160 | tf_op jit(solution)/shard_map/ppermute | solution.py:239
  20.0 4.1 %collective-permute-start.2 = (s32[2,2,8,128]{3,2,1,0:T(8,128)S(1)}, s32[2,2,8,128]{3,2,1,0:T(8,128)S(1)}, u32[]{:S(2)}, u32[]{:S(2)}) collective-permute-start(s32[2,2,8,128]{3,2,1,0:T(8,128)S(1)} %pad_add_fusion), channel_id=1, source_target_pairs={{32,0},{48,16},{0,32},{16,48},{33,1},{49,17},{1,33},{17,49},{34,2}... | collective-permute-start | bytes 49160 | tf_op jit(solution)/shard_map/ppermute | solution.py:239
  20.3 3.9 %collective-permute-start.3 = (s32[2,2,8,128]{3,2,1,0:T(8,128)S(1)}, s32[2,2,8,128]{3,2,1,0:T(8,128)S(1)}, u32[]{:S(2)}, u32[]{:S(2)}) collective-permute-start(s32[2,2,8,128]{3,2,1,0:T(8,128)S(1)} %pad_add_fusion), channel_id=1, source_target_pairs={{48,0},{0,16},{16,32},{32,48},{49,1},{1,17},{17,33},{33,49},{50,2}... | collective-permute-start | bytes 49160 | tf_op jit(solution)/shard_map/ppermute | solution.py:239
  45.4 25.2 %collective-permute-start.4 = (bf16[1024,512]{1,0:T(8,128)(2,1)S(1)}, bf16[1024,512]{1,0:T(8,128)(2,1)}, u32[]{:S(2)}, u32[]{:S(2)}) collective-permute-start(bf16[1024,512]{1,0:T(8,128)(2,1)S(1)} %bitcast.35), channel_id=1, source_target_pairs={{0,128},{128,0},{4,132},{132,4},{8,136},{136,8},{12,140},{140,12},... | collective-permute-start | bytes 3145736 | tf_op jit(solution)/shard_map/ppermute | solution.py:228
  47.0 28.1 %collective-permute-start.5 = (bf16[1024,512]{1,0:T(8,128)(2,1)S(1)}, bf16[1024,512]{1,0:T(8,128)(2,1)}, u32[]{:S(2)}, u32[]{:S(2)}) collective-permute-start(bf16[1024,512]{1,0:T(8,128)(2,1)S(1)} %bitcast.36), channel_id=1, source_target_pairs={{128,4},{4,128},{132,8},{8,132},{136,12},{12,136},{140,0},{0,140},... | collective-permute-start | bytes 3145736 | tf_op jit(solution)/shard_map/ppermute | solution.py:228
  75.2 24.3 %collective-permute-start.6 = (bf16[1024,512]{1,0:T(8,128)(2,1)}, bf16[1024,512]{1,0:T(8,128)(2,1)}, u32[]{:S(2)}, u32[]{:S(2)}) collective-permute-start(bf16[1024,512]{1,0:T(8,128)(2,1)} %collective-permute-done.5.refs_1_), channel_id=1, source_target_pairs={{0,128},{128,0},{4,132},{132,4},{8,136},{136,8},{12,140},{140,12},... | collective-permute-start | bytes 3145736 | tf_op jit(solution)/shard_map/ppermute | solution.py:228
  75.2 25.5 %collective-permute-start.7 = (bf16[1024,512]{1,0:T(8,128)(2,1)}, bf16[1024,512]{1,0:T(8,128)(2,1)}, u32[]{:S(2)}, u32[]{:S(2)}) collective-permute-start(bf16[1024,512]{1,0:T(8,128)(2,1)} %collective-permute-done.4.refs_1_), channel_id=1, source_target_pairs={{128,4},{4,128},{132,8},{8,132},{136,12},{12,136},{140,0},{0,140},... | collective-permute-start | bytes 3145736 | tf_op jit(solution)/shard_map/ppermute | solution.py:228
  86.9 18.4 %copy-start = (bf16[4,512,2048]{2,1,0:T(8,128)(2,1)}, bf16[4,512,2048]{2,1,0:T(8,128)(2,1)S(1)}, u32[]{:S(2)}) copy-start(bf16[4,512,2048]{2,1,0:T(8,128)(2,1)S(1)} %shard_map.87.rows_ref) | copy-start | bytes 25165828
  100.6 39.6 %collective-permute-start.8 = (bf16[1024,512]{1,0:T(8,128)(2,1)}, bf16[1024,512]{1,0:T(8,128)(2,1)}, u32[]{:S(2)}, u32[]{:S(2)}) collective-permute-start(bf16[1024,512]{1,0:T(8,128)(2,1)} %collective-permute-done.7.refs_0_), channel_id=1, source_target_pairs={{0,128},{128,0},{4,132},{132,4},{8,136},{136,8},{12,140},{140,12},... | collective-permute-start | bytes 3145736 | tf_op jit(solution)/shard_map/ppermute | solution.py:228
  100.7 39.6 %collective-permute-start.9 = (bf16[1024,512]{1,0:T(8,128)(2,1)}, bf16[1024,512]{1,0:T(8,128)(2,1)}, u32[]{:S(2)}, u32[]{:S(2)}) collective-permute-start(bf16[1024,512]{1,0:T(8,128)(2,1)} %collective-permute-done.6.refs_0_), channel_id=1, source_target_pairs={{128,4},{4,128},{132,8},{8,132},{136,12},{12,136},{140,0},{0,140},... | collective-permute-start | bytes 3145736 | tf_op jit(solution)/shard_map/ppermute | solution.py:228
  105.4 0.8 copy-start.3
  106.2 18.3 %all-to-all-start.2 = ((bf16[32,64,128]{2,1,0:T(8,128)(2,1)}), bf16[32,64,128]{2,1,0:T(8,128)(2,1)}, u32[]{:S(2)}, u32[]{:S(2)}) async-start(bf16[32,64,128]{2,1,0:T(8,128)(2,1)} %bitcast.41), calls=%async_computation.2 | async-start | bytes 1048576 | tf_op jit(solution)/shard_map/all_to_all | solution.py:277
  113.3 3.4 %copy-start.1 = (bf16[4,512,2048]{2,1,0:T(8,128)(2,1)S(1)}, bf16[4,512,2048]{2,1,0:T(8,128)(2,1)}, u32[]{:S(2)}) copy-start(bf16[4,512,2048]{2,1,0:T(8,128)(2,1)} %copy-done) | copy-start | bytes 25165828
  119.2 0.9 copy-start.4
  141.4 24.9 %collective-permute-start.10 = (bf16[512,512]{1,0:T(8,128)(2,1)S(1)}, bf16[512,512]{1,0:T(8,128)(2,1)S(1)}, u32[]{:S(2)}, u32[]{:S(2)}) collective-permute-start(bf16[512,512]{1,0:T(8,128)(2,1)S(1)} %slice.6), channel_id=1, source_target_pairs={{0,128},{128,0},{4,132},{132,4},{8,136},{136,8},{12,140},{140,12},... | collective-permute-start | bytes 1572872 | tf_op jit(solution)/shard_map/ppermute | solution.py:228
  142.5 23.7 %collective-permute-start.11 = (bf16[512,512]{1,0:T(8,128)(2,1)S(1)}, bf16[512,512]{1,0:T(8,128)(2,1)S(1)}, u32[]{:S(2)}, u32[]{:S(2)}) collective-permute-start(bf16[512,512]{1,0:T(8,128)(2,1)S(1)} %slice.7), channel_id=1, source_target_pairs={{128,4},{4,128},{132,8},{8,132},{136,12},{12,136},{140,0},{0,140},... | collective-permute-start | bytes 1572872 | tf_op jit(solution)/shard_map/ppermute | solution.py:228
  144.6 3.4 %copy-start.2 = (bf16[4,512,2048]{2,1,0:T(8,128)(2,1)S(1)}, bf16[4,512,2048]{2,1,0:T(8,128)(2,1)}, u32[]{:S(2)}) copy-start(bf16[4,512,2048]{2,1,0:T(8,128)(2,1)} %copy-done) | copy-start | bytes 25165828
Sparse Core Ops, SparseCore 0:
  9.9 56.5 all-gather.1

commit v3 on v2

v3 whole, which is shorter than its diff:
```python
import functools

import jax
import jax.numpy as jnp
from jax import lax
from jax.experimental import pallas as pl
from jax.experimental.pallas import tpu as pltpu
from jax.sharding import Mesh, PartitionSpec as P

learn_rate = 0.01
decay_rate = 0.1
beta_one = 0.9
beta_two = 0.95
epsilon = 1e-08
correct_one = 1.0 - 0.9**4
correct_two = 1.0 - 0.95**4

CAP = 32
PARTS = 4
CHUNKS = 2
STRIP = 128
ROOM = 20 * 2**20


def adam_kernel(master_ref, first_ref, second_ref, gradient_ref, new_ref, *chunk_refs):
    grad_full = gradient_ref[0].astype(jnp.float32)
    new_first = beta_one * first_ref[0] + (1.0 - beta_one) * grad_full
    new_second = beta_two * second_ref[0] + (1.0 - beta_two) * grad_full * grad_full
    update = new_first / correct_one / (jnp.sqrt(new_second / correct_two) + epsilon)
    updated = master_ref[0] * (1.0 - learn_rate * decay_rate) - learn_rate * update
    new_ref[0] = updated
    lowered = updated.astype(jnp.bfloat16)
    cores, _, _, part = chunk_refs[0].shape
    at = 0
    for ref in chunk_refs:
        for start in range(0, part, STRIP):
            for core in range(cores):
                ref[core, 0, :, start : start + STRIP] = lowered[:, at : at + STRIP]
                at += STRIP


def adam(master, first_moment, second_moment, gradient, cores):
    experts, rows, width = master.shape
    part = width // (cores * CHUNKS)
    whole = pl.BlockSpec((1, rows, width), lambda i: (i, 0, 0))
    block = pl.BlockSpec((cores, 1, rows, part), lambda i: (0, i, 0, 0))
    chunk = jax.ShapeDtypeStruct((cores, experts, rows, part), jnp.bfloat16)
    return pl.pallas_call(
        adam_kernel,
        grid=(experts,),
        in_specs=[whole] * 4,
        out_specs=[whole] + [block] * CHUNKS,
        out_shape=[jax.ShapeDtypeStruct(master.shape, jnp.float32)] + [chunk] * CHUNKS,
        compiler_params=pltpu.CompilerParams(vmem_limit_bytes=ROOM),
        cost_estimate=pl.CostEstimate(
            flops=16 * master.size, bytes_accessed=20 * master.size, transcendentals=master.size
        ),
    )(master, first_moment, second_moment, gradient)


def pick_kernel(where_ref, ids_ref, low_ref, high_ref, out_ref):
    steps, _, count = ids_ref.shape[2:]
    half = low_ref.shape[1]
    earlier = lax.broadcasted_iota(jnp.int32, (count, count), 0)
    later = lax.broadcasted_iota(jnp.int32, (count, count), 1)
    before = jnp.where(earlier < later, 1.0, 0.0).astype(jnp.bfloat16)
    slot = lax.broadcasted_iota(jnp.int32, (CAP, count), 0).astype(jnp.float32)
    for step in range(steps):
        ids = ids_ref[0, 0, step]
        masks = []
        for part in range(PARTS):
            hit = jnp.where(ids == where_ref[3 + part], 1.0, 0.0)
            masks.append(jnp.max(hit, axis=0, keepdims=True))
        mask = jnp.concatenate(masks * 2, axis=0)
        place = jnp.dot(
            mask.astype(jnp.bfloat16), before, preferred_element_type=jnp.float32
        )
        chosen = [
            jnp.where(slot == place[part : part + 1], mask[part : part + 1], 0.0)
            for part in range(PARTS)
        ]
        chosen = jnp.concatenate(chosen, axis=0).astype(jnp.bfloat16)
        rows = slice(step * count, (step + 1) * count)
        for at, ref in ((0, low_ref), (half, high_ref)):
            picked = jnp.dot(chosen, ref[rows, :], preferred_element_type=jnp.float32)
            picked = picked.astype(jnp.bfloat16)
            for part in range(PARTS):
                out_ref[part, step * CAP : (step + 1) * CAP, at : at + half] = picked[
                    part * CAP : (part + 1) * CAP
                ]


def pick_rows(where, all_ids, all_tokens, group_rows):
    _, ys, steps, choices, count = all_ids.shape
    total, depth = all_tokens.shape
    half = depth // 2
    groups = total // group_rows
    return pl.pallas_call(
        pick_kernel,
        grid_spec=pltpu.PrefetchScalarGridSpec(
            num_scalar_prefetch=1,
            grid=(groups,),
            in_specs=[
                pl.BlockSpec(
                    (1, 1, steps, choices, count),
                    lambda i, w: ((i // ys + w[1]) % 2, (i % ys + ys - w[2]) % ys, 0, 0, 0),
                ),
                pl.BlockSpec((group_rows, half), lambda i, w: (i, w[0])),
                pl.BlockSpec((group_rows, half), lambda i, w: (i, 1 - w[0])),
            ],
            out_specs=pl.BlockSpec((PARTS, steps * CAP, depth), lambda i, w: (0, i, 0)),
        ),
        out_shape=jax.ShapeDtypeStruct((PARTS, groups * steps * CAP, depth), jnp.bfloat16),
        compiler_params=pltpu.CompilerParams(vmem_limit_bytes=ROOM),
        cost_estimate=pl.CostEstimate(
            flops=8 * total * 128 * depth, bytes_accessed=4 * total * depth, transcendentals=0
        ),
    )(where, all_ids, all_tokens, all_tokens)


def halves(picked_ref, part, even, odd):
    half = picked_ref.shape[2] // 2
    total = None
    for at, weight in ((0, even), (half, odd)):
        if weight is not None:
            rows = picked_ref[part, :, at : at + half]
            piece = jnp.dot(rows, weight[...], preferred_element_type=jnp.float32)
            total = piece if total is None else total + piece
    return total


def act(out_ref, slot, chunk, product):
    value = (product * jax.nn.sigmoid(product)).astype(out_ref.dtype)
    groups, _, _, rows, strip = out_ref.shape
    wide = value.shape[1] // strip
    for group in range(groups):
        for column in range(wide):
            out_ref[group, chunk * wide + column, slot] = value[
                group * rows : (group + 1) * rows, column * strip : (column + 1) * strip
            ]


def early_kernel(picked_ref, own_a, own_b, a1_a, a1_b, c2_a, c2_b, c1_a, c1_b, out_ref):
    for chunk, (even, odd) in enumerate(((own_a, a1_a), (own_b, a1_b))):
        act(out_ref, 0, chunk, halves(picked_ref, 0, even, odd))
    for chunk, (even, odd) in enumerate(((c2_a, c1_a), (c2_b, c1_b))):
        act(out_ref, 1, chunk, halves(picked_ref, 1, even, odd))


def later_kernel(picked_ref, a2_a, a2_b, a3_a, a3_b, c3_a, c3_b, out_ref, start_ref):
    for chunk, (even, odd) in enumerate(((a2_a, a3_a), (a2_b, a3_b))):
        act(out_ref, 0, chunk, halves(picked_ref, 2, even, odd))
    for chunk, odd in enumerate((c3_a, c3_b)):
        start_ref[chunk] = halves(picked_ref, 3, None, odd)


def last_kernel(picked_ref, z4_a, z4_b, acted_ref, start_ref, out_ref):
    out_ref[:, :, :1] = acted_ref[...]
    for chunk, even in enumerate((z4_a, z4_b)):
        act(out_ref, 1, chunk, start_ref[chunk] + halves(picked_ref, 3, even, None))


def run(body, operands, out_shape, flops):
    spec = pl.BlockSpec(memory_space=pltpu.VMEM)
    return pl.pallas_call(
        body,
        in_specs=[spec] * len(operands),
        out_specs=jax.tree.map(lambda _: spec, out_shape),
        out_shape=out_shape,
        compiler_params=pltpu.CompilerParams(vmem_limit_bytes=ROOM),
        cost_estimate=pl.CostEstimate(
            flops=flops,
            bytes_accessed=sum(2 * x.size for x in operands),
            transcendentals=0,
        ),
    )(*operands)


def place_kernel(order_ref, ids_ref, raw_ref, out_ref):
    count, choices = ids_ref.shape[1:]
    lanes = out_ref.shape[2]
    names = 128
    ids = ids_ref[0]
    raw = raw_ref[0]
    shares = raw / jnp.sum(raw, axis=1, keepdims=True)
    name = lax.broadcasted_iota(jnp.int32, (count, names), 1)
    mask = jnp.zeros((count, names), jnp.float32)
    weight = jnp.zeros((count, names), jnp.float32)
    for choice in range(choices):
        hit = ids[:, choice : choice + 1] == name
        mask = mask + jnp.where(hit, 1.0, 0.0)
        weight = weight + jnp.where(hit, shares[:, choice : choice + 1], 0.0)
    row = lax.broadcasted_iota(jnp.int32, (count, count), 0)
    column = lax.broadcasted_iota(jnp.int32, (count, count), 1)
    before = jnp.where(column < row, 1.0, 0.0).astype(jnp.bfloat16)
    place = jnp.dot(before, mask.astype(jnp.bfloat16), preferred_element_type=jnp.float32)
    place = jnp.where(mask > 0.0, place, 255.0).astype(jnp.bfloat16)
    high = weight.astype(jnp.bfloat16)
    low = (weight - high.astype(jnp.float32)).astype(jnp.bfloat16)
    stacked = jnp.concatenate([place, high, low], axis=0)
    span = lanes // PARTS
    for part in range(PARTS):
        lane = lax.broadcasted_iota(jnp.int32, (names, span), 1)
        device = lane // CAP
        expert = (device // 4 * 4 + order_ref[part]) * 4 + device % 4
        spread = jnp.where(
            lax.broadcasted_iota(jnp.int32, (names, span), 0) == expert, 1.0, 0.0
        ).astype(jnp.bfloat16)
        wide = jnp.dot(stacked, spread, preferred_element_type=jnp.float32)
        slot = (lax.broadcasted_iota(jnp.int32, (count, span), 1) % CAP).astype(jnp.float32)
        here = wide[:count] == slot
        at = slice(part * span, (part + 1) * span)
        out_ref[0, :count, at] = jnp.where(here, wide[count : 2 * count], 0.0).astype(jnp.bfloat16)
        out_ref[0, count:, at] = jnp.where(here, wide[2 * count :], 0.0).astype(jnp.bfloat16)


def place_rows(order, ids, raw, lanes):
    steps, count, choices = ids.shape
    return pl.pallas_call(
        place_kernel,
        grid_spec=pltpu.PrefetchScalarGridSpec(
            num_scalar_prefetch=1,
            grid=(steps,),
            in_specs=[pl.BlockSpec((1, count, choices), lambda i, w: (i, 0, 0))] * 2,
            out_specs=pl.BlockSpec((1, 2 * count, lanes), lambda i, w: (i, 0, 0)),
        ),
        out_shape=jax.ShapeDtypeStruct((steps, 2 * count, lanes), jnp.bfloat16),
        compiler_params=pltpu.CompilerParams(vmem_limit_bytes=ROOM),
        cost_estimate=pl.CostEstimate(
            flops=2 * steps * 3 * count * 128 * lanes,
            bytes_accessed=4 * steps * count * lanes,
            transcendentals=0,
        ),
    )(order, ids, raw)


def mix_kernel(first, final, place_ref, returned_ref, *refs):
    out_ref = refs[-1]
    steps, count, _ = out_ref.shape
    cores, devices, slots, _, rows, strip = returned_ref.shape
    span = devices * rows
    for step in range(steps):
        total = None
        for slot in range(slots):
            part = first + slot
            arrived = jnp.concatenate(
                [returned_ref[c, :, slot, step].reshape(span, strip) for c in range(cores)], axis=1
            )
            piece = jnp.dot(
                place_ref[step, :, part * span : (part + 1) * span],
                arrived,
                preferred_element_type=jnp.float32,
            )
            total = piece if total is None else total + piece
        total = total[:count] + total[count:]
        if final:
            total = total + refs[0][step]
        out_ref[step] = total.astype(out_ref.dtype)


def swap(value, offset):
    high, low = lax.axis_size("zh"), lax.axis_size("zl")
    pairs = []
    for z in range(offset, high * low + offset, low):
        a, b = [(at % low) * high + at // low % high for at in (z, z + 1)]
        pairs += [(a, b), (b, a)]
    return lax.ppermute(value, ("zl", "zh"), pairs)


def along_y(expert_ids):
    own = expert_ids.transpose(0, 2, 1)
    size = lax.axis_size("y")
    ring = [own]
    for away in range(1, size):
        ring.append(lax.ppermute(own, "y", [((at + away) % size, at) for at in range(size)]))
    return jnp.stack(ring)


def per_device(master, first_moment, second_moment, gradient, tokens, expert_ids, router_scores):
    steps, token_count, depth = tokens.shape
    quarters = lax.axis_size("x")
    cores = lax.axis_size("core")
    owners = lax.axis_size("zh")
    ys = lax.axis_size("y")
    groups = cores * ys
    z_low, z_high = lax.axis_index("zl"), lax.axis_index("zh")
    y_at, x_at = lax.axis_index("y"), lax.axis_index("x")

    all_tokens = lax.all_gather(
        tokens.reshape(steps * token_count, depth), ("core", "y"), axis=0, tiled=True
    )
    near_ids = along_y(expert_ids)

    turn = jnp.where(z_low == 0, 1, -1)
    order = jnp.mod(jnp.stack([z_high, z_high - turn, z_high + turn, z_high + 2]), owners)
    names = quarters * (y_at * owners + order) + x_at
    here = jnp.stack([z_low, lax.axis_index("core"), y_at])
    where = jnp.concatenate([here, names]).astype(jnp.int32)

    new_master, *chunks = adam(master, first_moment, second_moment, gradient, cores)
    rows, width = master.shape[1:]
    part = width // (cores * CHUNKS)
    strip = width // (quarters * cores)
    chunks = [chunk.reshape(-1, rows, part) for chunk in chunks]

    def share_out(chunk):
        moved = lax.all_to_all(chunk, ("core", "x"), split_axis=0, concat_axis=0, tiled=True)
        return moved.reshape(-1, part)

    hold = lax.optimization_barrier
    first_chunk, near_ids = hold((chunks[0], near_ids))
    own_a = share_out(first_chunk)
    far_ids = lax.ppermute(near_ids, "core", [(0, 1), (1, 0)])
    own_a, all_ids = hold((own_a, jnp.stack([near_ids, far_ids])))
    a1_a, c1_a = swap(own_a, 0), swap(own_a, 1)
    own_b = share_out(chunks[1])
    a1_b, c1_b = swap(own_b, 0), swap(own_b, 1)
    placed = place_rows(
        order.astype(jnp.int32), expert_ids, router_scores, PARTS * quarters * ys * CAP
    )
    a1_a, c1_a = hold((a1_a, c1_a))
    a2_a, c2_a = swap(c1_a, 0), swap(a1_a, 1)
    a1_b, c1_b, placed = hold((a1_b, c1_b, placed))
    a2_b, c2_b = swap(c1_b, 0), swap(a1_b, 1)
    picked = pick_rows(where, all_ids, all_tokens, steps * token_count)
    a2_a, c2_a = hold((a2_a, c2_a))
    a3_a, c3_a = swap(c2_a, 0), swap(a2_a, 1)
    a2_b, c2_b, picked = hold((a2_b, c2_b, picked))
    a3_b, c3_b = swap(c2_b, 0), swap(a2_b, 1)
    flops = 2 * picked.shape[1] * depth * width // cores
    acted = jax.ShapeDtypeStruct((groups, quarters, 2, steps * CAP, strip), jnp.bfloat16)
    single = jax.ShapeDtypeStruct((groups, quarters, 1, steps * CAP, strip), jnp.bfloat16)
    start = jax.ShapeDtypeStruct((CHUNKS, picked.shape[1], part), jnp.float32)

    def send_back(value):
        value = value.reshape(groups * quarters, 2 * steps * CAP, strip)
        back = lax.all_to_all(value, ("core", "y", "x"), split_axis=0, concat_axis=0, tiled=True)
        return back.reshape(cores, ys * quarters, 2, steps, CAP, strip)

    early = run(
        early_kernel, [picked, own_a, own_b, a1_a, a1_b, c2_a, c2_b, c1_a, c1_b], acted, 2 * flops
    )
    a3_a, c3_a = hold((a3_a, c3_a))
    z4_a = swap(c3_a, 0)
    a3_b, c3_b, early = hold((a3_b, c3_b, early))
    early = send_back(early)
    z4_b = swap(a3_b, 1)
    later, begun = run(
        later_kernel, [picked, a2_a, a2_b, a3_a, a3_b, c3_a, c3_b], [single, start], 3 * flops // 2
    )
    mixed_shape = (steps, token_count, cores * strip)
    half_mixed = run(
        functools.partial(mix_kernel, 0, False),
        [placed, early],
        jax.ShapeDtypeStruct(mixed_shape, jnp.float32),
        2 * placed.size * cores * strip // 2,
    )
    z4_a, z4_b, later, begun, half_mixed = hold((z4_a, z4_b, later, begun, half_mixed))
    final = send_back(run(last_kernel, [picked, z4_a, z4_b, later, begun], acted, flops // 2))
    mixed = run(
        functools.partial(mix_kernel, 2, True),
        [placed, final, half_mixed],
        jax.ShapeDtypeStruct(mixed_shape, jnp.bfloat16),
        2 * placed.size * cores * strip // 2,
    )
    return (new_master, mixed)


def solution(mesh):
    grid = Mesh(mesh.devices.reshape(2, 2, 4, 4, 4), ("zl", "core", "y", "zh", "x"))
    owner, part, group = ("y", "zh"), ("zl", "core", "x"), ("zl", "core", "y", "zh")
    weights = P(owner, part, None)
    routed = P(None, group, None)
    return jax.shard_map(
        per_device,
        mesh=grid,
        in_specs=(weights,) * 4 + (routed,) * 3,
        out_specs=(weights, P(None, group, "x")),
        check_vma=False,
    )
```

time: 194 us -> 164 us (0.85)
  blocking collectives: 67.6 us -> 23.3 us
  starting transfers between devices: 25.3 us -> 45.5 us
  local copies, waits for them, and re-layouts: 12.3 us -> 21.8 us
  waiting for transfers between devices: 42.3 us -> 34.3 us
  other arithmetic: 6.28 us -> 0.18 us
    all_to_all x4 -> x1, blocking collectives: 67.6 us -> 23.3 us  [send_back(): lax.all_to_all(value, ('core', 'y', 'x'), split_axis=0, concat_axis=0, ti...]
    ppermute x8 -> x14, waiting for transfers between devices: 34 us -> 19.7 us  [swap(): return lax.ppermute(value, ('zl', 'zh'), pairs)]
    unnamed x21 -> x36, local copies, waits for them, and re-layouts: 8.67 us -> 21.8 us
    all_to_all x1 -> x3, starting transfers between devices: 7.1 us -> 19.4 us  [the longest x2 10.2 us: share_out(): lax.all_to_all(chunk, ('core', 'x'), split_axis=0, concat_axis=0, tiled=T...]
    ppermute x8 -> x14, starting transfers between devices: 12.8 us -> 23 us  [swap(): return lax.ppermute(value, ('zl', 'zh'), pairs)]
    all_to_all x1 -> x3, waiting for transfers between devices: 4.35 us -> 10.6 us  [the longest x2 7.47 us: share_out(): lax.all_to_all(chunk, ('core', 'x'), split_axis=0, concat_axis=0, tiled=T...]
    convert_element_type x1 -> x0, other arithmetic: 6.1 us -> none  [per_device(): lowered = new_master.astype(jnp.bfloat16)]
    ppermute x4, starting transfers between devices: 5.44 us -> 3.04 us  [the longest x3 2.94 us: along_y(): lax.ppermute(own, 'y', [((at + away) % size, at) for at in range(size)])]
  transfers between devices with their start and end apart: 14 -> 22, of which waited for: 8 -> 11; matrix products, arithmetic and copies ran while one was open for 5% -> 0% of each run, Pallas kernels for 10% -> 13%
where the time goes in v3:
time: 164 us
  starting transfers between devices  45.5 us (28%)
  waiting for transfers between devices  34.3 us (21%)
  Pallas kernels  24.2 us (15%)
  blocking collectives  23.3 us (14%)
  local copies, waits for them, and re-layouts  21.8 us (13%)
  between operations  14.3 us (9%)
    all_to_all x1, blocking collectives, send_back(): lax.all_to_all(value, ('core', 'y', 'x'), split_axis=0, concat_axis=0, ti...  23.3 us
    ppermute x14, starting transfers between devices, swap(): return lax.ppermute(value, ('zl', 'zh'), pairs)  23 us
    unnamed x36, local copies, waits for them, and re-layouts  21.8 us
    ppermute x14, waiting for transfers between devices, swap(): return lax.ppermute(value, ('zl', 'zh'), pairs)  19.7 us
    pallas_call x5, Pallas kernels, run(): pl.pallas_call(body, in_specs=[spec] * len(operands), out_specs=jax.tree....  11.1 us
    all_to_all x2, starting transfers between devices, share_out(): lax.all_to_all(chunk, ('core', 'x'), split_axis=0, concat_axis=0, tiled=T...  10.2 us
    all_to_all x1, starting transfers between devices, send_back(): lax.all_to_all(value, ('core', 'y', 'x'), split_axis=0, concat_axis=0, ti...  9.18 us
    all_to_all x2, waiting for transfers between devices, share_out(): lax.all_to_all(chunk, ('core', 'x'), split_axis=0, concat_axis=0, tiled=T...  7.47 us
  transfers between devices with their start and end apart: 22, of which 11 were waited for; matrix products, arithmetic and copies ran while one was open for 0% of the time, Pallas kernels for 13%

profile of v3, /device:TPU:1, one launch (start us, length us, event | category | flops | bytes accessed | tf_op | source)
XLA Modules:
  0.0 163.6 jit_solution(5458009157073504785)
XLA Ops:
  13.9 3.1 %shard_map.86 = (f32[4,128,1024]{2,1,0:T(8,128)}, bf16[2,4,128,256]{3,2,1,0:T(8,128)(2,1)}, bf16[2,4,128,256]{3,2,1,0:T(8,128)(2,1)}) custom-call(f32[4,128,1024]{2,1,0:T(8,128)S(1)} %copy-done.5, f32[4,128,1024]{2,1,0:T(8,128)S(1)} %copy-done.6, f32[4,128,1024]{2,1,0:T(8,128)S(1)} %copy-done.7, bf16[4,128,1024]{2,1,0:T(8,128)(2,1)S(1)} %copy-done.8), custom_call_target="tpu_custom_call" | custom-call | flops 8388608 | bytes 10485760 | tf_op jit(solution)/shard_map/pallas_call | solution.py:48
  17.0 6.8 %all-to-all-start = ((bf16[8,128,256]{2,1,0:T(8,128)(2,1)}), bf16[8,128,256]{2,1,0:T(8,128)(2,1)S(1)}, u32[]{:S(2)}, u32[]{:S(2)}) async-start(bf16[8,128,256]{2,1,0:T(8,128)(2,1)} %bitcast), calls=%async_computation | async-start | bytes 1048576 | tf_op jit(solution)/shard_map/all_to_all | solution.py:307
  26.7 3.3 %collective-permute-done.5 = s32[2,8,128]{2,1,0:T(8,128)S(1)} collective-permute-done((s32[2,8,128]{2,1,0:T(8,128)S(1)}, s32[2,8,128]{2,1,0:T(8,128)S(1)}, u32[]{:S(2)}, u32[]{:S(2)}) %collective-permute-start.5) | collective-permute-done | bytes 8224 | tf_op jit(solution)/shard_map/ppermute | solution.py:275
  30.0 3.5 %all-to-all-done = bf16[8,128,256]{2,1,0:T(8,128)(2,1)S(1)} async-done(((bf16[8,128,256]{2,1,0:T(8,128)(2,1)}), bf16[8,128,256]{2,1,0:T(8,128)(2,1)S(1)}, u32[]{:S(2)}, u32[]{:S(2)}) %all-to-all-start) | async-done | bytes 524320 | tf_op jit(solution)/shard_map/all_to_all | solution.py:307
  33.5 3.4 %all-to-all-start.1 = ((bf16[8,128,256]{2,1,0:T(8,128)(2,1)}), bf16[8,128,256]{2,1,0:T(8,128)(2,1)S(1)}, u32[]{:S(2)}, u32[]{:S(2)}) async-start(bf16[8,128,256]{2,1,0:T(8,128)(2,1)} %bitcast.9), calls=%async_computation.1 | async-start | bytes 1048576 | tf_op jit(solution)/shard_map/all_to_all | solution.py:307
  37.9 4.7 %collective-permute-start.1 = (bf16[1024,256]{1,0:T(8,128)(2,1)S(1)}, bf16[1024,256]{1,0:T(8,128)(2,1)}, u32[]{:S(2)}, u32[]{:S(2)}) collective-permute-start(bf16[1024,256]{1,0:T(8,128)(2,1)S(1)} %bitcast.29), channel_id=1, source_target_pairs={{128,4},{4,128},{132,8},{8,132},{136,12},{12,136},{140,0},{0,140},... | collective-permute-start | bytes 1572872 | tf_op jit(solution)/shard_map/ppermute | solution.py:267
  42.7 4.0 %all-to-all-done.1 = bf16[8,128,256]{2,1,0:T(8,128)(2,1)S(1)} async-done(((bf16[8,128,256]{2,1,0:T(8,128)(2,1)}), bf16[8,128,256]{2,1,0:T(8,128)(2,1)S(1)}, u32[]{:S(2)}, u32[]{:S(2)}) %all-to-all-start.1) | async-done | bytes 524320 | tf_op jit(solution)/shard_map/all_to_all | solution.py:307
  47.6 4.8 %collective-permute-start.9 = (bf16[1024,256]{1,0:T(8,128)(2,1)S(1)}, bf16[1024,256]{1,0:T(8,128)(2,1)}, u32[]{:S(2)}, u32[]{:S(2)}) collective-permute-start(bf16[1024,256]{1,0:T(8,128)(2,1)S(1)} %bitcast.32), channel_id=1, source_target_pairs={{128,4},{4,128},{132,8},{8,132},{136,12},{12,136},{140,0},{0,140},... | collective-permute-start | bytes 1572872 | tf_op jit(solution)/shard_map/ppermute | solution.py:267
  52.8 2.8 %shard_map.87.place_ref = bf16[2,256,2048]{2,1,0:T(8,128)(2,1)S(1)} custom-call(s32[4]{0:T(128)S(1)} %get-tuple-element.61.order_ref, s32[2,128,8]{2,1,0:T(8,128)S(1)} %copy.9.ids_ref, f32[2,128,8]{2,1,0:T(8,128)S(1)} %copy.10.raw_ref), custom_call_target="tpu_custom_call" | custom-call | flops 402653184 | bytes 2097152 | tf_op jit(solution)/shard_map/pallas_call | solution.py:219
  57.3 4.3 %collective-permute-done.8.a1_a = bf16[1024,256]{1,0:T(8,128)(2,1)} collective-permute-done((bf16[1024,256]{1,0:T(8,128)(2,1)S(1)}, bf16[1024,256]{1,0:T(8,128)(2,1)}, u32[]{:S(2)}, u32[]{:S(2)}) %collective-permute-start.8) | collective-permute-done | bytes 524320 | tf_op jit(solution)/shard_map/ppermute | solution.py:267
  61.6 3.9 %collective-permute-done.9.c1_a = bf16[1024,256]{1,0:T(8,128)(2,1)} collective-permute-done((bf16[1024,256]{1,0:T(8,128)(2,1)S(1)}, bf16[1024,256]{1,0:T(8,128)(2,1)}, u32[]{:S(2)}, u32[]{:S(2)}) %collective-permute-start.9) | collective-permute-done | bytes 524320 | tf_op jit(solution)/shard_map/ppermute | solution.py:267
  67.9 3.4 %copy-done.3 = bf16[2048,2048]{1,0:T(8,128)(2,1)S(1)} copy-done((bf16[2048,2048]{1,0:T(8,128)(2,1)S(1)}, bf16[2048,2048]{1,0:T(8,128)(2,1)}, u32[]{:S(2)}) %copy-start.3) | copy-done | bytes 8388632
  71.3 7.2 %shard_map.88.picked_ref = bf16[4,512,2048]{2,1,0:T(8,128)(2,1)S(1)} custom-call(s32[7]{0:T(128)S(1)} %pad_add_fusion.2.where_ref, s32[2,4,2,8,128]{4,3,2,1,0:T(8,128)S(1)} %pad_add_fusion.ids_ref, bf16[2048,2048]{1,0:T(8,128)(2,1)S(1)} %copy-done.3, bf16[2048,2048]{1,0:T(8,128)(2,1)S(1)} %copy-done.3), custom_call_target="tpu_custom_call" | custom-call | flops 4294967296 | bytes 16777216 | tf_op jit(solution)/shard_map/pallas_call | solution.py:98
  78.6 3.0 %collective-permute-start.16 = (bf16[1024,256]{1,0:T(8,128)(2,1)}, bf16[1024,256]{1,0:T(8,128)(2,1)S(1)}, u32[]{:S(2)}, u32[]{:S(2)}) collective-permute-start(bf16[1024,256]{1,0:T(8,128)(2,1)} %collective-permute-done.2.a2_b), channel_id=1, source_target_pairs={{128,4},{4,128},{132,8},{8,132},{136,12},{12,136},{140,0},{0,140},... | collective-permute-start | bytes 1572872 | tf_op jit(solution)/shard_map/ppermute | solution.py:267
  81.6 2.5 %collective-permute-done.10.a2_a = bf16[1024,256]{1,0:T(8,128)(2,1)} collective-permute-done((bf16[1024,256]{1,0:T(8,128)(2,1)}, bf16[1024,256]{1,0:T(8,128)(2,1)}, u32[]{:S(2)}, u32[]{:S(2)}) %collective-permute-start.10) | collective-permute-done | bytes 524320 | tf_op jit(solution)/shard_map/ppermute | solution.py:267
  84.1 3.9 %collective-permute-done.11.c2_a = bf16[1024,256]{1,0:T(8,128)(2,1)} collective-permute-done((bf16[1024,256]{1,0:T(8,128)(2,1)}, bf16[1024,256]{1,0:T(8,128)(2,1)}, u32[]{:S(2)}, u32[]{:S(2)}) %collective-permute-start.11) | collective-permute-done | bytes 524320 | tf_op jit(solution)/shard_map/ppermute | solution.py:267
  90.4 4.2 %shard_map.89 = bf16[8,4,2,64,128]{4,3,2,1,0:T(8,128)(2,1)S(1)} custom-call(bf16[4,512,2048]{2,1,0:T(8,128)(2,1)S(1)} %shard_map.88.picked_ref, bf16[1024,256]{1,0:T(8,128)(2,1)S(1)} %bitcast.33, bf16[1024,256]{1,0:T(8,128)(2,1)S(1)} %bitcast.30, bf16[1024,256]{1,0:T(8,128)(2,1)} %collective-permute-done.8.a1_a, ...), custom_call_target="tpu_custom_call" | custom-call | flops 2147483648 | bytes 12582912 | tf_op jit(solution)/shard_map/pallas_call | solution.py:165
  95.5 3.6 %collective-permute-done.16.c3_b = bf16[1024,256]{1,0:T(8,128)(2,1)S(1)} collective-permute-done((bf16[1024,256]{1,0:T(8,128)(2,1)}, bf16[1024,256]{1,0:T(8,128)(2,1)S(1)}, u32[]{:S(2)}, u32[]{:S(2)}) %collective-permute-start.16) | collective-permute-done | bytes 524320 | tf_op jit(solution)/shard_map/ppermute | solution.py:267
  99.9 9.2 %all-to-all-start.2 = ((bf16[32,128,128]{2,1,0:T(8,128)(2,1)}), bf16[32,128,128]{2,1,0:T(8,128)(2,1)S(1)}, u32[]{:S(2)}, u32[]{:S(2)}) async-start(bf16[32,128,128]{2,1,0:T(8,128)(2,1)} %bitcast.27), calls=%async_computation.2 | async-start | bytes 2097152 | tf_op jit(solution)/shard_map/all_to_all | solution.py:337
  112.8 3.4 %copy-done.1 = bf16[4,512,2048]{2,1,0:T(8,128)(2,1)S(1)} copy-done((bf16[4,512,2048]{2,1,0:T(8,128)(2,1)S(1)}, bf16[4,512,2048]{2,1,0:T(8,128)(2,1)}, u32[]{:S(2)}) %copy-start.1) | copy-done | bytes 8388632
  117.3 3.5 %shard_map.90 = (bf16[8,4,1,64,128]{4,3,2,1,0:T(8,128)(2,1)S(1)}, f32[2,512,256]{2,1,0:T(8,128)S(1)}) custom-call(bf16[4,512,2048]{2,1,0:T(8,128)(2,1)S(1)} %copy-done.1, bf16[1024,256]{1,0:T(8,128)(2,1)} %collective-permute-done.10.a2_a, bf16[1024,256]{1,0:T(8,128)(2,1)} %collective-permute-done.2.a2_b, bf16[1024,256]{1,0:T(8,128)(2,1)} %collective-permute-done.12.a3_a, ...), custom_call_target="tpu_custom_call" | custom-call | flops 1610612736 | bytes 11534336 | tf_op jit(solution)/shard_map/pallas_call | solution.py:165
  122.5 3.2 %all-to-all-done.2 = bf16[32,128,128]{2,1,0:T(8,128)(2,1)S(1)} async-done(((bf16[32,128,128]{2,1,0:T(8,128)(2,1)}), bf16[32,128,128]{2,1,0:T(8,128)(2,1)S(1)}, u32[]{:S(2)}, u32[]{:S(2)}) %all-to-all-start.2) | async-done | bytes 1048608 | tf_op jit(solution)/shard_map/all_to_all | solution.py:337
  127.0 3.4 %copy-done.2 = bf16[4,512,2048]{2,1,0:T(8,128)(2,1)S(1)} copy-done((bf16[4,512,2048]{2,1,0:T(8,128)(2,1)S(1)}, bf16[4,512,2048]{2,1,0:T(8,128)(2,1)}, u32[]{:S(2)}) %copy-start.2) | copy-done | bytes 8388632
  132.4 23.3 %all_to_all.20 = bf16[32,128,128]{2,1,0:T(8,128)(2,1)S(1)} all-to-all(bf16[32,128,128]{2,1,0:T(8,128)(2,1)S(1)} %bitcast.24), channel_id=1, replica_groups=mesh['zl'=2,'core'=2,'y'=4,'zh'=4,'x'=4] {'core','y','x'}, dimensions={0} | all-to-all | bytes 2097152 | tf_op jit(solution)/shard_map/all_to_all | solution.py:337
  (70 shorter events, 31.1 us)
Async XLA Ops:
  7.2 60.7 %all-gather.2.cloned.1.call-start = ((), (), s32[]{:S(2)}) async-start(), calls=%async_computation.4 | async-start | bytes 9437184 | tf_op jit(solution)/shard_map/all_gather | solution.py:289
  17.0 35.6 %copy-start.16 = (f32[2,128,8]{1,2,0:T(8,128)S(1)}, f32[2,128,8]{1,2,0:T(8,128)}, u32[]{:S(2)}) copy-start(f32[2,128,8]{1,2,0:T(8,128)} %param.13) | copy-start | bytes 24580
  17.0 16.6 %all-to-all-start = ((bf16[8,128,256]{2,1,0:T(8,128)(2,1)}), bf16[8,128,256]{2,1,0:T(8,128)(2,1)S(1)}, u32[]{:S(2)}, u32[]{:S(2)}) async-start(bf16[8,128,256]{2,1,0:T(8,128)(2,1)} %bitcast), calls=%async_computation | async-start | bytes 1048576 | tf_op jit(solution)/shard_map/all_to_all | solution.py:307
  23.8 2.9 %collective-permute-start.4 = (s32[2,8,128]{2,1,0:T(8,128)S(1)}, s32[2,8,128]{2,1,0:T(8,128)S(1)}, u32[]{:S(2)}, u32[]{:S(2)}) collective-permute-start(s32[2,8,128]{2,1,0:T(8,128)S(1)} %bitcast.37), channel_id=1, source_target_pairs={{16,0},{32,16},{48,32},{0,48},{17,1},{33,17},{49,33},{1,49},{18,2}... | collective-permute-start | bytes 24584 | tf_op jit(solution)/shard_map/ppermute | solution.py:275
  25.7 4.3 %collective-permute-start.5 = (s32[2,8,128]{2,1,0:T(8,128)S(1)}, s32[2,8,128]{2,1,0:T(8,128)S(1)}, u32[]{:S(2)}, u32[]{:S(2)}) collective-permute-start(s32[2,8,128]{2,1,0:T(8,128)S(1)} %bitcast.38), channel_id=1, source_target_pairs={{32,0},{48,16},{0,32},{16,48},{33,1},{49,17},{1,33},{17,49},{34,2}... | collective-permute-start | bytes 24584 | tf_op jit(solution)/shard_map/ppermute | solution.py:275
  26.0 4.0 %collective-permute-start.6 = (s32[2,8,128]{2,1,0:T(8,128)S(1)}, s32[2,8,128]{2,1,0:T(8,128)S(1)}, u32[]{:S(2)}, u32[]{:S(2)}) collective-permute-start(s32[2,8,128]{2,1,0:T(8,128)S(1)} %bitcast.39), channel_id=1, source_target_pairs={{48,0},{0,16},{16,32},{32,48},{49,1},{1,17},{17,33},{33,49},{50,2}... | collective-permute-start | bytes 24584 | tf_op jit(solution)/shard_map/ppermute | solution.py:275
  33.5 13.2 %all-to-all-start.1 = ((bf16[8,128,256]{2,1,0:T(8,128)(2,1)}), bf16[8,128,256]{2,1,0:T(8,128)(2,1)S(1)}, u32[]{:S(2)}, u32[]{:S(2)}) async-start(bf16[8,128,256]{2,1,0:T(8,128)(2,1)} %bitcast.9), calls=%async_computation.1 | async-start | bytes 1048576 | tf_op jit(solution)/shard_map/all_to_all | solution.py:307
  37.0 5.7 %collective-permute-start.7 = (s32[4,2,8,128]{3,2,1,0:T(8,128)S(1)}, s32[4,2,8,128]{3,2,1,0:T(8,128)S(1)}, u32[]{:S(2)}, u32[]{:S(2)}) collective-permute-start(s32[4,2,8,128]{3,2,1,0:T(8,128)S(1)} %pad_add_fusion.1), channel_id=1, source_target_pairs={{0,64},{64,0},{1,65},{65,1},{2,66},{66,2},{3,67},{67,3},{4,68},{68... | collective-permute-start | bytes 98312 | tf_op jit(solution)/shard_map/ppermute | solution.py:313
  37.1 18.5 %collective-permute-start = (bf16[1024,256]{1,0:T(8,128)(2,1)S(1)}, bf16[1024,256]{1,0:T(8,128)(2,1)}, u32[]{:S(2)}, u32[]{:S(2)}) collective-permute-start(bf16[1024,256]{1,0:T(8,128)(2,1)S(1)} %bitcast.28), channel_id=1, source_target_pairs={{0,128},{128,0},{4,132},{132,4},{8,136},{136,8},{12,140},{140,12},... | collective-permute-start | bytes 1572872 | tf_op jit(solution)/shard_map/ppermute | solution.py:267
  37.9 17.7 %collective-permute-start.1 = (bf16[1024,256]{1,0:T(8,128)(2,1)S(1)}, bf16[1024,256]{1,0:T(8,128)(2,1)}, u32[]{:S(2)}, u32[]{:S(2)}) collective-permute-start(bf16[1024,256]{1,0:T(8,128)(2,1)S(1)} %bitcast.29), channel_id=1, source_target_pairs={{128,4},{4,128},{132,8},{8,132},{136,12},{12,136},{140,0},{0,140},... | collective-permute-start | bytes 1572872 | tf_op jit(solution)/shard_map/ppermute | solution.py:267
  46.7 14.9 %collective-permute-start.8 = (bf16[1024,256]{1,0:T(8,128)(2,1)S(1)}, bf16[1024,256]{1,0:T(8,128)(2,1)}, u32[]{:S(2)}, u32[]{:S(2)}) collective-permute-start(bf16[1024,256]{1,0:T(8,128)(2,1)S(1)} %bitcast.31), channel_id=1, source_target_pairs={{0,128},{128,0},{4,132},{132,4},{8,136},{136,8},{12,140},{140,12},... | collective-permute-start | bytes 1572872 | tf_op jit(solution)/shard_map/ppermute | solution.py:267
  47.6 17.9 %collective-permute-start.9 = (bf16[1024,256]{1,0:T(8,128)(2,1)S(1)}, bf16[1024,256]{1,0:T(8,128)(2,1)}, u32[]{:S(2)}, u32[]{:S(2)}) collective-permute-start(bf16[1024,256]{1,0:T(8,128)(2,1)S(1)} %bitcast.32), channel_id=1, source_target_pairs={{128,4},{4,128},{132,8},{8,132},{136,12},{12,136},{140,0},{0,140},... | collective-permute-start | bytes 1572872 | tf_op jit(solution)/shard_map/ppermute | solution.py:267
  55.6 22.9 %collective-permute-start.2 = (bf16[1024,256]{1,0:T(8,128)(2,1)}, bf16[1024,256]{1,0:T(8,128)(2,1)}, u32[]{:S(2)}, u32[]{:S(2)}) collective-permute-start(bf16[1024,256]{1,0:T(8,128)(2,1)} %collective-permute-done.1.c1_b), channel_id=1, source_target_pairs={{0,128},{128,0},{4,132},{132,4},{8,136},{136,8},{12,140},{140,12},... | collective-permute-start | bytes 1572872 | tf_op jit(solution)/shard_map/ppermute | solution.py:267
  55.7 22.8 %collective-permute-start.3 = (bf16[1024,256]{1,0:T(8,128)(2,1)}, bf16[1024,256]{1,0:T(8,128)(2,1)}, u32[]{:S(2)}, u32[]{:S(2)}) collective-permute-start(bf16[1024,256]{1,0:T(8,128)(2,1)} %collective-permute-done.a1_b), channel_id=1, source_target_pairs={{128,4},{4,128},{132,8},{8,132},{136,12},{12,136},{140,0},{0,140},... | collective-permute-start | bytes 1572872 | tf_op jit(solution)/shard_map/ppermute | solution.py:267
  65.5 18.5 %collective-permute-start.10 = (bf16[1024,256]{1,0:T(8,128)(2,1)}, bf16[1024,256]{1,0:T(8,128)(2,1)}, u32[]{:S(2)}, u32[]{:S(2)}) collective-permute-start(bf16[1024,256]{1,0:T(8,128)(2,1)} %collective-permute-done.9.c1_a), channel_id=1, source_target_pairs={{0,128},{128,0},{4,132},{132,4},{8,136},{136,8},{12,140},{140,12},... | collective-permute-start | bytes 1572872 | tf_op jit(solution)/shard_map/ppermute | solution.py:267
  65.5 22.5 %collective-permute-start.11 = (bf16[1024,256]{1,0:T(8,128)(2,1)}, bf16[1024,256]{1,0:T(8,128)(2,1)}, u32[]{:S(2)}, u32[]{:S(2)}) collective-permute-start(bf16[1024,256]{1,0:T(8,128)(2,1)} %collective-permute-done.8.a1_a), channel_id=1, source_target_pairs={{128,4},{4,128},{132,8},{8,132},{136,12},{12,136},{140,0},{0,140},... | collective-permute-start | bytes 1572872 | tf_op jit(solution)/shard_map/ppermute | solution.py:267
  78.5 16.1 %copy-start = (bf16[4,512,2048]{2,1,0:T(8,128)(2,1)}, bf16[4,512,2048]{2,1,0:T(8,128)(2,1)S(1)}, u32[]{:S(2)}) copy-start(bf16[4,512,2048]{2,1,0:T(8,128)(2,1)S(1)} %shard_map.88.picked_ref) | copy-start | bytes 25165828
  78.5 17.0 %collective-permute-start.15 = (bf16[1024,256]{1,0:T(8,128)(2,1)}, bf16[1024,256]{1,0:T(8,128)(2,1)}, u32[]{:S(2)}, u32[]{:S(2)}) collective-permute-start(bf16[1024,256]{1,0:T(8,128)(2,1)} %collective-permute-done.3.c2_b), channel_id=1, source_target_pairs={{0,128},{128,0},{4,132},{132,4},{8,136},{136,8},{12,140},{140,12},... | collective-permute-start | bytes 1572872 | tf_op jit(solution)/shard_map/ppermute | solution.py:267
  78.6 20.5 %collective-permute-start.16 = (bf16[1024,256]{1,0:T(8,128)(2,1)}, bf16[1024,256]{1,0:T(8,128)(2,1)S(1)}, u32[]{:S(2)}, u32[]{:S(2)}) collective-permute-start(bf16[1024,256]{1,0:T(8,128)(2,1)} %collective-permute-done.2.a2_b), channel_id=1, source_target_pairs={{128,4},{4,128},{132,8},{8,132},{136,12},{12,136},{140,0},{0,140},... | collective-permute-start | bytes 1572872 | tf_op jit(solution)/shard_map/ppermute | solution.py:267
  88.0 21.1 %collective-permute-start.12 = (bf16[1024,256]{1,0:T(8,128)(2,1)}, bf16[1024,256]{1,0:T(8,128)(2,1)}, u32[]{:S(2)}, u32[]{:S(2)}) collective-permute-start(bf16[1024,256]{1,0:T(8,128)(2,1)} %collective-permute-done.11.c2_a), channel_id=1, source_target_pairs={{0,128},{128,0},{4,132},{132,4},{8,136},{136,8},{12,140},{140,12},... | collective-permute-start | bytes 1572872 | tf_op jit(solution)/shard_map/ppermute | solution.py:267
  88.0 22.5 %collective-permute-start.13 = (bf16[1024,256]{1,0:T(8,128)(2,1)}, bf16[1024,256]{1,0:T(8,128)(2,1)}, u32[]{:S(2)}, u32[]{:S(2)}) collective-permute-start(bf16[1024,256]{1,0:T(8,128)(2,1)} %collective-permute-done.10.a2_a), channel_id=1, source_target_pairs={{128,4},{4,128},{132,8},{8,132},{136,12},{12,136},{140,0},{0,140},... | collective-permute-start | bytes 1572872 | tf_op jit(solution)/shard_map/ppermute | solution.py:267
  99.9 25.7 %all-to-all-start.2 = ((bf16[32,128,128]{2,1,0:T(8,128)(2,1)}), bf16[32,128,128]{2,1,0:T(8,128)(2,1)S(1)}, u32[]{:S(2)}, u32[]{:S(2)}) async-start(bf16[32,128,128]{2,1,0:T(8,128)(2,1)} %bitcast.27), calls=%async_computation.2 | async-start | bytes 2097152 | tf_op jit(solution)/shard_map/all_to_all | solution.py:337
  110.5 15.6 %collective-permute-start.14 = (bf16[1024,256]{1,0:T(8,128)(2,1)}, bf16[1024,256]{1,0:T(8,128)(2,1)}, u32[]{:S(2)}, u32[]{:S(2)}) collective-permute-start(bf16[1024,256]{1,0:T(8,128)(2,1)} %collective-permute-done.13.c3_a), channel_id=1, source_target_pairs={{0,128},{128,0},{4,132},{132,4},{8,136},{136,8},{12,140},{140,12},... | collective-permute-start | bytes 1572872 | tf_op jit(solution)/shard_map/ppermute | solution.py:267
  110.5 15.6 %collective-permute-start.17 = (bf16[1024,256]{1,0:T(8,128)(2,1)}, bf16[1024,256]{1,0:T(8,128)(2,1)}, u32[]{:S(2)}, u32[]{:S(2)}) collective-permute-start(bf16[1024,256]{1,0:T(8,128)(2,1)} %collective-permute-done.15.a3_b), channel_id=1, source_target_pairs={{128,4},{4,128},{132,8},{8,132},{136,12},{12,136},{140,0},{0,140},... | collective-permute-start | bytes 1572872 | tf_op jit(solution)/shard_map/ppermute | solution.py:267
  (15 other events, 33.2 us)
Sparse Core Ops, SparseCore 0:
  9.9 56.6 all-gather.1

commit v4 on v3

v4 whole, which is shorter than its diff:
```python
import functools

import jax
import jax.numpy as jnp
from jax import lax
from jax.experimental import pallas as pl
from jax.experimental.pallas import tpu as pltpu
from jax.sharding import Mesh, PartitionSpec as P

learn_rate = 0.01
decay_rate = 0.1
beta_one = 0.9
beta_two = 0.95
epsilon = 1e-08
correct_one = 1.0 - 0.9**4
correct_two = 1.0 - 0.95**4

CAP = 32
PARTS = 4
CHUNKS = 2
STRIP = 128
ROOM = 12 * 2**20
WIDE = 56 * 2**20
SMALL = pl.CostEstimate(flops=1, bytes_accessed=1, transcendentals=0)


def adam_kernel(master_ref, first_ref, second_ref, gradient_ref, new_ref, *chunk_refs):
    grad_full = gradient_ref[0].astype(jnp.float32)
    new_first = beta_one * first_ref[0] + (1.0 - beta_one) * grad_full
    new_second = beta_two * second_ref[0] + (1.0 - beta_two) * grad_full * grad_full
    update = new_first / correct_one / (jnp.sqrt(new_second / correct_two) + epsilon)
    updated = master_ref[0] * (1.0 - learn_rate * decay_rate) - learn_rate * update
    new_ref[0] = updated
    lowered = updated.astype(jnp.bfloat16)
    cores, _, _, part = chunk_refs[0].shape
    at = 0
    for ref in chunk_refs:
        for start in range(0, part, STRIP):
            for core in range(cores):
                ref[core, 0, :, start : start + STRIP] = lowered[:, at : at + STRIP]
                at += STRIP


def adam(master, first_moment, second_moment, gradient, cores):
    experts, rows, width = master.shape
    part = width // (cores * CHUNKS)
    whole = pl.BlockSpec((1, rows, width), lambda i: (i, 0, 0))
    block = pl.BlockSpec((cores, 1, rows, part), lambda i: (0, i, 0, 0))
    chunk = jax.ShapeDtypeStruct((cores, experts, rows, part), jnp.bfloat16)
    return pl.pallas_call(
        adam_kernel,
        grid=(experts,),
        in_specs=[whole] * 4,
        out_specs=[whole] + [block] * CHUNKS,
        out_shape=[jax.ShapeDtypeStruct(master.shape, jnp.float32)] + [chunk] * CHUNKS,
        compiler_params=pltpu.CompilerParams(vmem_limit_bytes=WIDE),
        cost_estimate=pl.CostEstimate(
            flops=16 * master.size, bytes_accessed=20 * master.size, transcendentals=master.size
        ),
    )(master, first_moment, second_moment, gradient)


def pick_kernel(where_ref, ids_ref, *refs):
    sides, ys, _, _, count = ids_ref.shape
    token_refs, out_refs = refs[: sides * ys], refs[sides * ys :]
    parts = len(out_refs)
    earlier = lax.broadcasted_iota(jnp.int32, (count, count), 0)
    later = lax.broadcasted_iota(jnp.int32, (count, count), 1)
    before = jnp.where(earlier < later, 1.0, 0.0).astype(jnp.bfloat16)
    slot = lax.broadcasted_iota(jnp.int32, (CAP, count), 0).astype(jnp.float32)
    masks = []
    groups = [(side, away) for side in range(sides) for away in range(ys)]
    for side, away in groups:
        ids = ids_ref[side, away, 0]
        for part in range(parts):
            hit = jnp.where(ids == where_ref[1 + part], 1.0, 0.0)
            masks.append(jnp.max(hit, axis=0, keepdims=True))
    mask = jnp.concatenate(masks, axis=0)
    place = jnp.dot(mask.astype(jnp.bfloat16), before, preferred_element_type=jnp.float32)
    for at, (side, away) in enumerate(groups):
        lines = [slice(at * parts + part, at * parts + part + 1) for part in range(parts)]
        chosen = [jnp.where(slot == place[line], mask[line], 0.0) for line in lines]
        chosen = jnp.concatenate(chosen, axis=0).astype(jnp.bfloat16)
        picked = jnp.dot(chosen, token_refs[at][0], preferred_element_type=jnp.float32)
        picked = picked.astype(jnp.bfloat16)
        for part in range(parts):
            out_refs[part][side, away] = picked[part * CAP : (part + 1) * CAP]


def pick_rows(where, ids, tokens):
    sides, ys, steps, choices, count = ids.shape
    depth = tokens[0].shape[2]
    half = depth // 2
    out = jax.ShapeDtypeStruct((sides, ys, steps * CAP, depth), jnp.bfloat16)
    return pl.pallas_call(
        pick_kernel,
        grid_spec=pltpu.PrefetchScalarGridSpec(
            num_scalar_prefetch=1,
            grid=(steps, 2),
            in_specs=[pl.BlockSpec((sides, ys, 1, choices, count), lambda i, j, w: (0, 0, i, 0, 0))]
            + [pl.BlockSpec((1, count, half), lambda i, j, w: (i, 0, (j + w[0]) % 2))]
            * (sides * ys),
            out_specs=[pl.BlockSpec((sides, ys, CAP, half), lambda i, j, w: (0, 0, i, j))] * PARTS,
        ),
        out_shape=[out] * PARTS,
        compiler_params=pltpu.CompilerParams(vmem_limit_bytes=2 * ROOM),
        cost_estimate=SMALL,
    )(where, ids, *tokens)


def halves(rows_ref, even, odd):
    sides, ys, count, depth = rows_ref.shape
    half = depth // 2
    total = None
    for at, weight in ((0, even), (half, odd)):
        if weight is not None:
            rows = rows_ref[:, :, :, at : at + half].reshape(sides * ys * count, half)
            piece = jnp.dot(rows, weight[...], preferred_element_type=jnp.float32)
            total = piece if total is None else total + piece
    return total


def act(out_ref, places, slot, chunk, product):
    value = (product * jax.nn.sigmoid(product)).astype(out_ref.dtype)
    _, _, _, rows, strip = out_ref.shape
    wide = value.shape[1] // strip
    for away, place in enumerate(places):
        for column in range(wide):
            out_ref[place, chunk * wide + column, slot] = value[
                away * rows : (away + 1) * rows, column * strip : (column + 1) * strip
            ]


def around(at_ref, rows_ref):
    cores, ys = rows_ref.shape[:2]
    core, y = at_ref[0], at_ref[1]
    return [
        lax.rem(core + side, cores) * ys + lax.rem(y + away, ys)
        for side in range(cores)
        for away in range(ys)
    ]


def early_kernel(at_ref, rows_0, rows_1, own_a, own_b, a1_a, a1_b, c2_a, c2_b, c1_a, c1_b, out_ref):
    places = around(at_ref, rows_0)
    for chunk, (even, odd) in enumerate(((own_a, a1_a), (own_b, a1_b))):
        act(out_ref, places, 0, chunk, halves(rows_0, even, odd))
    for chunk, (even, odd) in enumerate(((c2_a, c1_a), (c2_b, c1_b))):
        act(out_ref, places, 1, chunk, halves(rows_1, even, odd))


def later_kernel(at_ref, rows_2, a2_a, a2_b, a3_a, a3_b, out_ref):
    places = around(at_ref, rows_2)
    for chunk, (even, odd) in enumerate(((a2_a, a3_a), (a2_b, a3_b))):
        act(out_ref, places, 0, chunk, halves(rows_2, even, odd))


def begin_kernel(rows_3, c3_a, c3_b, start_ref):
    for chunk, odd in enumerate((c3_a, c3_b)):
        start_ref[chunk] = halves(rows_3, None, odd)


def last_kernel(at_ref, rows_3, z4_a, z4_b, start_ref, out_ref):
    places = around(at_ref, rows_3)
    for chunk, even in enumerate((z4_a, z4_b)):
        act(out_ref, places, 0, chunk, start_ref[chunk] + halves(rows_3, even, None))


def run(body, operands, out_shape, scalars=None):
    spec = pl.BlockSpec(memory_space=pltpu.VMEM)
    in_specs = [spec] * len(operands)
    if scalars is not None:
        in_specs = [pl.BlockSpec(memory_space=pltpu.SMEM)] + in_specs
        operands = [scalars] + operands
    return pl.pallas_call(
        body,
        in_specs=in_specs,
        out_specs=spec,
        out_shape=out_shape,
        compiler_params=pltpu.CompilerParams(vmem_limit_bytes=ROOM),
        cost_estimate=SMALL,
    )(*operands)


def place_kernel(order_ref, ids_ref, raw_ref, out_ref):
    count, choices = ids_ref.shape[1:]
    lanes = out_ref.shape[2]
    names = 128
    ids = ids_ref[0]
    raw = raw_ref[0]
    shares = raw / jnp.sum(raw, axis=1, keepdims=True)
    name = lax.broadcasted_iota(jnp.int32, (count, names), 1)
    mask = jnp.zeros((count, names), jnp.float32)
    weight = jnp.zeros((count, names), jnp.float32)
    for choice in range(choices):
        hit = ids[:, choice : choice + 1] == name
        mask = mask + jnp.where(hit, 1.0, 0.0)
        weight = weight + jnp.where(hit, shares[:, choice : choice + 1], 0.0)
    row = lax.broadcasted_iota(jnp.int32, (count, count), 0)
    column = lax.broadcasted_iota(jnp.int32, (count, count), 1)
    before = jnp.where(column < row, 1.0, 0.0).astype(jnp.bfloat16)
    place = jnp.dot(before, mask.astype(jnp.bfloat16), preferred_element_type=jnp.float32)
    place = jnp.where(mask > 0.0, place, 255.0).astype(jnp.bfloat16)
    high = weight.astype(jnp.bfloat16)
    low = (weight - high.astype(jnp.float32)).astype(jnp.bfloat16)
    stacked = jnp.concatenate([place, high, low], axis=0)
    span = lanes // PARTS
    for part in range(PARTS):
        lane = lax.broadcasted_iota(jnp.int32, (names, span), 1)
        device = lane // CAP
        expert = (device // 4 * 4 + order_ref[part]) * 4 + device % 4
        spread = jnp.where(
            lax.broadcasted_iota(jnp.int32, (names, span), 0) == expert, 1.0, 0.0
        ).astype(jnp.bfloat16)
        wide = jnp.dot(stacked, spread, preferred_element_type=jnp.float32)
        slot = (lax.broadcasted_iota(jnp.int32, (count, span), 1) % CAP).astype(jnp.float32)
        here = wide[:count] == slot
        at = slice(part * span, (part + 1) * span)
        out_ref[0, :count, at] = jnp.where(here, wide[count : 2 * count], 0.0).astype(jnp.bfloat16)
        out_ref[0, count:, at] = jnp.where(here, wide[2 * count :], 0.0).astype(jnp.bfloat16)


def place_rows(order, ids, raw, lanes):
    steps, count, choices = ids.shape
    return pl.pallas_call(
        place_kernel,
        grid_spec=pltpu.PrefetchScalarGridSpec(
            num_scalar_prefetch=1,
            grid=(steps,),
            in_specs=[pl.BlockSpec((1, count, choices), lambda i, w: (i, 0, 0))] * 2,
            out_specs=pl.BlockSpec((1, 2 * count, lanes), lambda i, w: (i, 0, 0)),
        ),
        out_shape=jax.ShapeDtypeStruct((steps, 2 * count, lanes), jnp.bfloat16),
        compiler_params=pltpu.CompilerParams(vmem_limit_bytes=ROOM),
        cost_estimate=SMALL,
    )(order, ids, raw)


def mix_kernel(first, place_ref, *refs):
    out_ref = refs[-1]
    steps, count, _ = out_ref.shape
    for step in range(steps):
        part, total = first, None
        for ref in refs[:-1]:
            if len(ref.shape) == len(out_ref.shape):
                total = total + ref[step]
                continue
            cores, devices, slots, _, rows, strip = ref.shape
            span = devices * rows
            for slot in range(slots):
                arrived = jnp.concatenate(
                    [ref[core, :, slot, step].reshape(span, strip) for core in range(cores)], axis=1
                )
                piece = jnp.dot(
                    place_ref[step, :, part * span : (part + 1) * span],
                    arrived,
                    preferred_element_type=jnp.float32,
                )
                piece = piece[:count] + piece[count:]
                total = piece if total is None else total + piece
                part += 1
        out_ref[step] = total.astype(out_ref.dtype)


def swap(value, offset):
    high, low = lax.axis_size("zh"), lax.axis_size("zl")
    pairs = []
    for z in range(offset, high * low + offset, low):
        a, b = [(at % low) * high + at // low % high for at in (z, z + 1)]
        pairs += [(a, b), (b, a)]
    return lax.ppermute(value, ("zl", "zh"), pairs)


def from_y(value, away):
    size = lax.axis_size("y")
    return lax.ppermute(value, "y", [((at + away) % size, at) for at in range(size)])


def swap_cores(value):
    return lax.ppermute(value, "core", [(0, 1), (1, 0)])


def per_device(master, first_moment, second_moment, gradient, tokens, expert_ids, router_scores):
    steps, token_count, depth = tokens.shape
    quarters = lax.axis_size("x")
    cores = lax.axis_size("core")
    owners = lax.axis_size("zh")
    ys = lax.axis_size("y")
    groups = cores * ys
    z_low, z_high = lax.axis_index("zl"), lax.axis_index("zh")
    y_at, x_at = lax.axis_index("y"), lax.axis_index("x")

    turn = jnp.where(z_low == 0, 1, -1)
    order = jnp.mod(jnp.stack([z_high, z_high - turn, z_high + turn, z_high + 2]), owners)
    names = quarters * (y_at * owners + order) + x_at
    where = jnp.concatenate([z_low[None], names]).astype(jnp.int32)
    order = order.astype(jnp.int32)
    here = jnp.stack([lax.axis_index("core"), y_at]).astype(jnp.int32)

    next_up, next_down = from_y(tokens, 1), from_y(tokens, -1)
    ids = expert_ids.transpose(0, 2, 1)
    near_ids = jnp.stack([ids] + [from_y(ids, away) for away in range(1, ys)])
    new_master, *chunks = adam(master, first_moment, second_moment, gradient, cores)
    rows, width = master.shape[1:]
    part = width // (cores * CHUNKS)
    strip = width // (quarters * cores)
    chunks = [chunk.reshape(-1, rows, part) for chunk in chunks]

    def share_out(chunk):
        moved = lax.all_to_all(chunk, ("core", "x"), split_axis=0, concat_axis=0, tiled=True)
        return moved.reshape(-1, part)

    def send_back(value):
        slots = value.shape[2]
        value = value.reshape(groups * quarters, slots * steps * CAP, strip)
        back = lax.all_to_all(value, ("core", "y", "x"), split_axis=0, concat_axis=0, tiled=True)
        return back.reshape(cores, ys * quarters, slots, steps, CAP, strip)

    hold = lax.optimization_barrier
    first_chunk, near_ids = hold((chunks[0], near_ids))
    own_a = share_out(first_chunk)
    own_a, all_ids = hold((own_a, jnp.stack([near_ids, swap_cores(near_ids)])))
    a1_a, c1_a = swap(own_a, 0), swap(own_a, 1)
    own_b, next_up, next_down = hold((share_out(chunks[1]), next_up, next_down))
    near = [tokens, next_up, from_y(next_down, -1), next_down]
    a1_b, c1_b = swap(own_b, 0), swap(own_b, 1)
    placed = place_rows(order, expert_ids, router_scores, PARTS * quarters * ys * CAP)
    a1_a, c1_a = hold((a1_a, c1_a))
    a2_a, c2_a = swap(c1_a, 0), swap(a1_a, 1)
    a1_b, c1_b, placed = hold((a1_b, c1_b, placed))
    a2_b, c2_b = swap(c1_b, 0), swap(a1_b, 1)
    far = [swap_cores(value) for value in near]
    rows = pick_rows(where, all_ids, near + far)
    a2_a, c2_a = hold((a2_a, c2_a))
    a3_a, c3_a = swap(c2_a, 0), swap(a2_a, 1)
    a2_b, c2_b, *rows = hold((a2_b, c2_b, *rows))
    a3_b, c3_b = swap(c2_b, 0), swap(a2_b, 1)
    double = jax.ShapeDtypeStruct((groups, quarters, 2, steps * CAP, strip), jnp.bfloat16)
    single = jax.ShapeDtypeStruct((groups, quarters, 1, steps * CAP, strip), jnp.bfloat16)
    start = jax.ShapeDtypeStruct((CHUNKS, groups * steps * CAP, part), jnp.float32)
    early = [rows[0], rows[1], own_a, own_b, a1_a, a1_b, c2_a, c2_b, c1_a, c1_b]
    early = run(early_kernel, early, double, here)
    a3_a, c3_a = hold((a3_a, c3_a))
    z4_a = swap(c3_a, 0)
    a3_b, c3_b, early = hold((a3_b, c3_b, early))
    early = send_back(early)
    z4_b = swap(a3_b, 1)
    later = send_back(run(later_kernel, [rows[2], a2_a, a2_b, a3_a, a3_b], single, here))
    begun = run(begin_kernel, [rows[3], c3_a, c3_b], start)
    mixed_shape = (steps, token_count, cores * strip)
    half_mixed = jax.ShapeDtypeStruct(mixed_shape, jnp.float32)
    half_mixed = run(functools.partial(mix_kernel, 0), [placed, early], half_mixed)
    z4_a, z4_b, begun, half_mixed = hold((z4_a, z4_b, begun, half_mixed))
    final = send_back(run(last_kernel, [rows[3], z4_a, z4_b, begun], single, here))
    mixed = jax.ShapeDtypeStruct(mixed_shape, jnp.bfloat16)
    mixed = run(functools.partial(mix_kernel, 2), [placed, later, final, half_mixed], mixed)
    return (new_master, mixed)


def solution(mesh):
    grid = Mesh(mesh.devices.reshape(2, 2, 4, 4, 4), ("zl", "core", "y", "zh", "x"))
    owner, part, group = ("y", "zh"), ("zl", "core", "x"), ("zl", "core", "y", "zh")
    weights = P(owner, part, None)
    routed = P(None, group, None)
    return jax.shard_map(
        per_device,
        mesh=grid,
        in_specs=(weights,) * 4 + (routed,) * 3,
        out_specs=(weights, P(None, group, "x")),
        check_vma=False,
    )
```

time: 164 us -> 195 us (1.19)
  waiting for transfers between devices: 34.3 us -> 68.5 us
  starting transfers between devices: 45.5 us -> 62.7 us
  between operations: 14.3 us -> 0.87 us
  blocking collectives: 23.3 us -> 15.9 us
  local copies, waits for them, and re-layouts: 21.8 us -> 15.8 us
  Pallas kernels: 24.2 us -> 29.6 us
    ppermute x14, waiting for transfers between devices: 19.7 us -> 43.6 us  [swap(): return lax.ppermute(value, ('zl', 'zh'), pairs)]
    all_to_all x1 -> x2, starting transfers between devices: 9.18 us -> 16.9 us  [send_back(): lax.all_to_all(value, ('core', 'y', 'x'), split_axis=0, concat_axis=0, ti...]
    ppermute x4 -> x11, starting transfers between devices: 3.04 us -> 10.6 us  [the longest x6 7.28 us: from_y(): lax.ppermute(value, 'y', [((at + away) % size, at) for at in range(size)])]
    all_to_all x1, blocking collectives: 23.3 us -> 15.9 us  [send_back(): lax.all_to_all(value, ('core', 'y', 'x'), split_axis=0, concat_axis=0, ti...]
    all_to_all x2, waiting for transfers between devices: 7.47 us -> 14.7 us  [share_out(): lax.all_to_all(chunk, ('core', 'x'), split_axis=0, concat_axis=0, tiled=T...]
    unnamed x36 -> x38, local copies, waits for them, and re-layouts: 21.8 us -> 15.8 us
    pallas_call x5 -> x6, Pallas kernels: 11.1 us -> 14 us  [run(): pl.pallas_call(body, in_specs=in_specs, out_specs=spec, out_shape=out_sha...]
    pallas_call x1, Pallas kernels: 3.06 us -> 5.77 us  [adam(): pl.pallas_call(adam_kernel, grid=(experts,), in_specs=[whole] * 4, out_sp...]
  transfers between devices with their start and end apart: 22 -> 29, of which waited for: 11 -> 15; matrix products, arithmetic and copies ran while one was open for 0% -> 0% of each run, Pallas kernels for 13% -> 14%
where the time goes in v4:
time: 195 us; the launch traced here: 194 us
  waiting for transfers between devices  68.5 us (35%)
  starting transfers between devices  62.7 us (32%)
  Pallas kernels  29.6 us (15%)
  blocking collectives  15.9 us (8%)
  local copies, waits for them, and re-layouts  15.8 us (8%)
    ppermute x14, waiting for transfers between devices, swap(): return lax.ppermute(value, ('zl', 'zh'), pairs)  43.6 us
    ppermute x14, starting transfers between devices, swap(): return lax.ppermute(value, ('zl', 'zh'), pairs)  23.5 us
    all_to_all x2, starting transfers between devices, send_back(): lax.all_to_all(value, ('core', 'y', 'x'), split_axis=0, concat_axis=0, ti...  16.9 us
    all_to_all x1, blocking collectives, send_back(): lax.all_to_all(value, ('core', 'y', 'x'), split_axis=0, concat_axis=0, ti...  15.9 us
    unnamed x38, local copies, waits for them, and re-layouts  15.8 us
    all_to_all x2, waiting for transfers between devices, share_out(): lax.all_to_all(chunk, ('core', 'x'), split_axis=0, concat_axis=0, tiled=T...  14.7 us
    pallas_call x6, Pallas kernels, run(): pl.pallas_call(body, in_specs=in_specs, out_specs=spec, out_shape=out_sha...  14 us
    all_to_all x2, starting transfers between devices, share_out(): lax.all_to_all(chunk, ('core', 'x'), split_axis=0, concat_axis=0, tiled=T...  11.6 us
  transfers between devices with their start and end apart: 29, of which 15 were waited for; matrix products, arithmetic and copies ran while one was open for 0% of the time, Pallas kernels for 14%

profile of v4, /device:TPU:1, one launch (start us, length us, event | category | flops | bytes accessed | tf_op | source)
XLA Modules:
  0.0 193.6 jit_solution(2914469341440925793)
XLA Ops:
  0.6 3.6 %collective-permute-start = (bf16[2,128,2048]{2,1,0:T(8,128)(2,1)}, bf16[2,128,2048]{2,1,0:T(8,128)(2,1)}, u32[]{:S(2)}, u32[]{:S(2)}) collective-permute-start(bf16[2,128,2048]{2,1,0:T(8,128)(2,1)} %refs_0_.1), channel_id=1, source_target_pairs={{16,0},{32,16},{48,32},{0,48},{17,1},{33,17},{49,33},{1,49},{18,2}... | collective-permute-start | bytes 3145736 | tf_op jit(solution)/shard_map/ppermute | solution.py:276
  4.3 5.8 %shard_map.86 = (f32[4,128,1024]{2,1,0:T(8,128)}, bf16[2,4,128,256]{3,2,1,0:T(8,128)(2,1)}, bf16[2,4,128,256]{3,2,1,0:T(8,128)(2,1)}) custom-call(f32[4,128,1024]{2,1,0:T(8,128)} %master_ref.1, f32[4,128,1024]{2,1,0:T(8,128)} %first_ref.1, f32[4,128,1024]{2,1,0:T(8,128)} %second_ref.1, bf16[4,128,1024]{2,1,0:T(8,128)(2,1)} %gradient_ref.1), custom_call_target="tpu_custom_call" | custom-call | flops 8388608 | bytes 10485760 | tf_op jit(solution)/shard_map/pallas_call | solution.py:50
  10.1 5.4 %all-to-all-start = ((bf16[8,128,256]{2,1,0:T(8,128)(2,1)}), bf16[8,128,256]{2,1,0:T(8,128)(2,1)S(1)}, u32[]{:S(2)}, u32[]{:S(2)}) async-start(bf16[8,128,256]{2,1,0:T(8,128)(2,1)} %bitcast.36), calls=%async_computation | async-start | bytes 1048576 | tf_op jit(solution)/shard_map/all_to_all | solution.py:310
  15.4 3.0 %collective-permute-start.6 = (s32[2,8,128]{2,1,0:T(8,128)S(1)}, s32[2,8,128]{2,1,0:T(8,128)S(1)}, u32[]{:S(2)}, u32[]{:S(2)}) collective-permute-start(s32[2,8,128]{2,1,0:T(8,128)S(1)} %bitcast.39), channel_id=1, source_target_pairs={{16,0},{32,16},{48,32},{0,48},{17,1},{33,17},{49,33},{1,49},{18,2}... | collective-permute-start | bytes 24584 | tf_op jit(solution)/shard_map/ppermute | solution.py:276
  19.1 6.1 %all-to-all-done = bf16[8,128,256]{2,1,0:T(8,128)(2,1)S(1)} async-done(((bf16[8,128,256]{2,1,0:T(8,128)(2,1)}), bf16[8,128,256]{2,1,0:T(8,128)(2,1)S(1)}, u32[]{:S(2)}, u32[]{:S(2)}) %all-to-all-start) | async-done | bytes 524320 | tf_op jit(solution)/shard_map/all_to_all | solution.py:310
  26.4 3.2 %collective-permute-done.1.refs_3_ = bf16[2,128,2048]{2,1,0:T(8,128)(2,1)} collective-permute-done((bf16[2,128,2048]{2,1,0:T(8,128)(2,1)}, bf16[2,128,2048]{2,1,0:T(8,128)(2,1)}, u32[]{:S(2)}, u32[]{:S(2)}) %collective-permute-start.1) | collective-permute-done | bytes 1048608 | tf_op jit(solution)/shard_map/ppermute | solution.py:276
  29.8 6.2 %all-to-all-start.1 = ((bf16[8,128,256]{2,1,0:T(8,128)(2,1)}), bf16[8,128,256]{2,1,0:T(8,128)(2,1)S(1)}, u32[]{:S(2)}, u32[]{:S(2)}) async-start(bf16[8,128,256]{2,1,0:T(8,128)(2,1)} %bitcast.35), calls=%async_computation.1 | async-start | bytes 1048576 | tf_op jit(solution)/shard_map/all_to_all | solution.py:310
  37.2 8.6 %all-to-all-done.1 = bf16[8,128,256]{2,1,0:T(8,128)(2,1)S(1)} async-done(((bf16[8,128,256]{2,1,0:T(8,128)(2,1)}), bf16[8,128,256]{2,1,0:T(8,128)(2,1)S(1)}, u32[]{:S(2)}, u32[]{:S(2)}) %all-to-all-start.1) | async-done | bytes 524320 | tf_op jit(solution)/shard_map/all_to_all | solution.py:310
  47.4 5.4 %collective-permute-start.3 = (bf16[1024,256]{1,0:T(8,128)(2,1)S(1)}, bf16[1024,256]{1,0:T(8,128)(2,1)S(1)}, u32[]{:S(2)}, u32[]{:S(2)}) collective-permute-start(bf16[1024,256]{1,0:T(8,128)(2,1)S(1)} %bitcast.27), channel_id=1, source_target_pairs={{128,4},{4,128},{132,8},{8,132},{136,12},{12,136},{140,0},{0,140},... | collective-permute-start | bytes 1572872 | tf_op jit(solution)/shard_map/ppermute | solution.py:271
  53.6 6.1 %collective-permute-done.15.a1_a = bf16[1024,256]{1,0:T(8,128)(2,1)} collective-permute-done((bf16[1024,256]{1,0:T(8,128)(2,1)S(1)}, bf16[1024,256]{1,0:T(8,128)(2,1)}, u32[]{:S(2)}, u32[]{:S(2)}) %collective-permute-start.15) | collective-permute-done | bytes 524320 | tf_op jit(solution)/shard_map/ppermute | solution.py:271
  60.6 10.2 %collective-permute-done.2.a1_b = bf16[1024,256]{1,0:T(8,128)(2,1)S(1)} collective-permute-done((bf16[1024,256]{1,0:T(8,128)(2,1)S(1)}, bf16[1024,256]{1,0:T(8,128)(2,1)S(1)}, u32[]{:S(2)}, u32[]{:S(2)}) %collective-permute-start.2) | collective-permute-done | bytes 524320 | tf_op jit(solution)/shard_map/ppermute | solution.py:271
  71.7 5.3 %collective-permute-start.16 = (bf16[1024,256]{1,0:T(8,128)(2,1)S(1)}, bf16[1024,256]{1,0:T(8,128)(2,1)}, u32[]{:S(2)}, u32[]{:S(2)}) collective-permute-start(bf16[1024,256]{1,0:T(8,128)(2,1)S(1)} %bitcast.30), channel_id=1, source_target_pairs={{128,4},{4,128},{132,8},{8,132},{136,12},{12,136},{140,0},{0,140},... | collective-permute-start | bytes 1572872 | tf_op jit(solution)/shard_map/ppermute | solution.py:271
  78.4 2.8 %shard_map.87.place_ref = bf16[2,256,2048]{2,1,0:T(8,128)(2,1)S(1)} custom-call(s32[4]{0:T(128)S(1)} %get-tuple-element.75.order_ref, s32[2,128,8]{2,1,0:T(8,128)S(1)} %copy.9.ids_ref, f32[2,128,8]{2,1,0:T(8,128)S(1)} %copy.10.raw_ref), custom_call_target="tpu_custom_call" | custom-call | flops 1 | bytes 1 | tf_op jit(solution)/shard_map/pallas_call | solution.py:225
  81.2 7.5 %collective-permute-done.16.c1_a = bf16[1024,256]{1,0:T(8,128)(2,1)} collective-permute-done((bf16[1024,256]{1,0:T(8,128)(2,1)S(1)}, bf16[1024,256]{1,0:T(8,128)(2,1)}, u32[]{:S(2)}, u32[]{:S(2)}) %collective-permute-start.16) | collective-permute-done | bytes 524320 | tf_op jit(solution)/shard_map/ppermute | solution.py:271
  93.4 7.0 %shard_map.88 = (bf16[2,4,64,2048]{3,2,1,0:T(8,128)(2,1)S(1)}, bf16[2,4,64,2048]{3,2,1,0:T(8,128)(2,1)S(1)}, bf16[2,4,64,2048]{3,2,1,0:T(8,128)(2,1)S(1)}, bf16[2,4,64,2048]{3,2,1,0:T(8,128)(2,1)S(1)}) custom-call(s32[5]{0:T(128)S(1)} %pad_add_fusion.3.where_ref, s32[2,4,2,8,128]{4,3,2,1,0:T(8,128)S(1)} %pad_add_fusion.ids_ref, ...), custom_call_target="tpu_custom_call" | custom-call | flops 1 | bytes 1 | tf_op jit(solution)/shard_map/pallas_call | solution.py:95
  106.9 5.3 %collective-permute-done.17.a2_a = bf16[1024,256]{1,0:T(8,128)(2,1)} collective-permute-done((bf16[1024,256]{1,0:T(8,128)(2,1)}, bf16[1024,256]{1,0:T(8,128)(2,1)}, u32[]{:S(2)}, u32[]{:S(2)}) %collective-permute-start.17) | collective-permute-done | bytes 524320 | tf_op jit(solution)/shard_map/ppermute | solution.py:271
  118.9 4.9 %shard_map.89 = bf16[8,4,2,64,128]{4,3,2,1,0:T(8,128)(2,1)} custom-call(s32[2]{0:T(128)S(1)} %pad_add_fusion.2.at_ref, bf16[2,4,64,2048]{3,2,1,0:T(8,128)(2,1)S(1)} %copy-done.3, bf16[2,4,64,2048]{3,2,1,0:T(8,128)(2,1)S(1)} %copy-done.5, bf16[1024,256]{1,0:T(8,128)(2,1)S(1)} %bitcast.31, bf16[1024,256]{1,0:T(8,128)(2,1)S(1)} %bitcast.28, ...), custom_call_target="tpu_custom_call" | custom-call | flops 1 | bytes 1 | tf_op jit(solution)/shard_map/pallas_call | solution.py:175
  124.9 7.9 %all-to-all-start.3 = ((bf16[32,128,128]{2,1,0:T(8,128)(2,1)}), bf16[32,128,128]{2,1,0:T(8,128)(2,1)S(1)}, u32[]{:S(2)}, u32[]{:S(2)}) async-start(bf16[32,128,128]{2,1,0:T(8,128)(2,1)} %bitcast.20), calls=%async_computation.3 | async-start | bytes 2097152 | tf_op jit(solution)/shard_map/all_to_all | solution.py:316
  133.2 2.7 %collective-permute-start.20 = (bf16[1024,256]{1,0:T(8,128)(2,1)}, bf16[1024,256]{1,0:T(8,128)(2,1)}, u32[]{:S(2)}, u32[]{:S(2)}) collective-permute-start(bf16[1024,256]{1,0:T(8,128)(2,1)} %collective-permute-done.17.a2_a), channel_id=1, source_target_pairs={{128,4},{4,128},{132,8},{8,132},{136,12},{12,136},{140,0},{0,140},... | collective-permute-start | bytes 1572872 | tf_op jit(solution)/shard_map/ppermute | solution.py:271
  135.9 10.7 %collective-permute-done.19.a3_a = bf16[1024,256]{1,0:T(8,128)(2,1)S(1)} collective-permute-done((bf16[1024,256]{1,0:T(8,128)(2,1)}, bf16[1024,256]{1,0:T(8,128)(2,1)S(1)}, u32[]{:S(2)}, u32[]{:S(2)}) %collective-permute-start.19) | collective-permute-done | bytes 524320 | tf_op jit(solution)/shard_map/ppermute | solution.py:271
  147.7 2.7 %collective-permute-start.24 = (bf16[1024,256]{1,0:T(8,128)(2,1)}, bf16[1024,256]{1,0:T(8,128)(2,1)}, u32[]{:S(2)}, u32[]{:S(2)}) collective-permute-start(bf16[1024,256]{1,0:T(8,128)(2,1)} %collective-permute-done.21.a3_b), channel_id=1, source_target_pairs={{128,4},{4,128},{132,8},{8,132},{136,12},{12,136},{140,0},{0,140},... | collective-permute-start | bytes 1572872 | tf_op jit(solution)/shard_map/ppermute | solution.py:271
  155.4 9.0 %all-to-all-start.2 = ((bf16[32,64,128]{2,1,0:T(8,128)(2,1)}), bf16[32,64,128]{2,1,0:T(8,128)(2,1)}, u32[]{:S(2)}, u32[]{:S(2)}) async-start(bf16[32,64,128]{2,1,0:T(8,128)(2,1)} %bitcast.32), calls=%async_computation.2 | async-start | bytes 1048576 | tf_op jit(solution)/shard_map/all_to_all | solution.py:316
  171.1 4.4 %all-to-all-done.2 = bf16[32,64,128]{2,1,0:T(8,128)(2,1)} async-done(((bf16[32,64,128]{2,1,0:T(8,128)(2,1)}), bf16[32,64,128]{2,1,0:T(8,128)(2,1)}, u32[]{:S(2)}, u32[]{:S(2)}) %all-to-all-start.2) | async-done | bytes 524320 | tf_op jit(solution)/shard_map/all_to_all | solution.py:316
  175.6 15.9 %all_to_all.25 = bf16[32,64,128]{2,1,0:T(8,128)(2,1)S(1)} all-to-all(bf16[32,64,128]{2,1,0:T(8,128)(2,1)} %bitcast.33), channel_id=1, replica_groups=mesh['zl'=2,'core'=2,'y'=4,'zh'=4,'x'=4] {'core','y','x'}, dimensions={0} | all-to-all | bytes 1048576 | tf_op jit(solution)/shard_map/all_to_all | solution.py:316
  (87 shorter events, 43.0 us)
Async XLA Ops:
  0.6 25.7 %collective-permute-start = (bf16[2,128,2048]{2,1,0:T(8,128)(2,1)}, bf16[2,128,2048]{2,1,0:T(8,128)(2,1)}, u32[]{:S(2)}, u32[]{:S(2)}) collective-permute-start(bf16[2,128,2048]{2,1,0:T(8,128)(2,1)} %refs_0_.1), channel_id=1, source_target_pairs={{16,0},{32,16},{48,32},{0,48},{17,1},{33,17},{49,33},{1,49},{18,2}... | collective-permute-start | bytes 3145736 | tf_op jit(solution)/shard_map/ppermute | solution.py:276
  4.3 25.3 %collective-permute-start.1 = (bf16[2,128,2048]{2,1,0:T(8,128)(2,1)}, bf16[2,128,2048]{2,1,0:T(8,128)(2,1)}, u32[]{:S(2)}, u32[]{:S(2)}) collective-permute-start(bf16[2,128,2048]{2,1,0:T(8,128)(2,1)} %refs_0_.1), channel_id=1, source_target_pairs={{48,0},{0,16},{16,32},{32,48},{49,1},{1,17},{17,33},{33,49},{50,2}... | collective-permute-start | bytes 3145736 | tf_op jit(solution)/shard_map/ppermute | solution.py:276
  10.1 15.2 %all-to-all-start = ((bf16[8,128,256]{2,1,0:T(8,128)(2,1)}), bf16[8,128,256]{2,1,0:T(8,128)(2,1)S(1)}, u32[]{:S(2)}, u32[]{:S(2)}) async-start(bf16[8,128,256]{2,1,0:T(8,128)(2,1)} %bitcast.36), calls=%async_computation | async-start | bytes 1048576 | tf_op jit(solution)/shard_map/all_to_all | solution.py:310
  15.4 14.2 %collective-permute-start.6 = (s32[2,8,128]{2,1,0:T(8,128)S(1)}, s32[2,8,128]{2,1,0:T(8,128)S(1)}, u32[]{:S(2)}, u32[]{:S(2)}) collective-permute-start(s32[2,8,128]{2,1,0:T(8,128)S(1)} %bitcast.39), channel_id=1, source_target_pairs={{16,0},{32,16},{48,32},{0,48},{17,1},{33,17},{49,33},{1,49},{18,2}... | collective-permute-start | bytes 24584 | tf_op jit(solution)/shard_map/ppermute | solution.py:276
  29.6 47.4 %collective-permute-start.10 = (bf16[2,128,2048]{2,1,0:T(8,128)(2,1)}, bf16[2,128,2048]{2,1,0:T(8,128)(2,1)}, u32[]{:S(2)}, u32[]{:S(2)}) collective-permute-start(bf16[2,128,2048]{2,1,0:T(8,128)(2,1)} %collective-permute-done.1.refs_3_), channel_id=1, source_target_pairs={{48,0},{0,16},{16,32},{32,48},{49,1},{1,17},{17,33},{33,49},{50,2}... | collective-permute-start | bytes 3145736 | tf_op jit(solution)/shard_map/ppermute | solution.py:276
  29.8 16.0 %all-to-all-start.1 = ((bf16[8,128,256]{2,1,0:T(8,128)(2,1)}), bf16[8,128,256]{2,1,0:T(8,128)(2,1)S(1)}, u32[]{:S(2)}, u32[]{:S(2)}) async-start(bf16[8,128,256]{2,1,0:T(8,128)(2,1)} %bitcast.35), calls=%async_computation.1 | async-start | bytes 1048576 | tf_op jit(solution)/shard_map/all_to_all | solution.py:310
  47.4 23.5 %collective-permute-start.2 = (bf16[1024,256]{1,0:T(8,128)(2,1)S(1)}, bf16[1024,256]{1,0:T(8,128)(2,1)S(1)}, u32[]{:S(2)}, u32[]{:S(2)}) collective-permute-start(bf16[1024,256]{1,0:T(8,128)(2,1)S(1)} %bitcast.26), channel_id=1, source_target_pairs={{0,128},{128,0},{4,132},{132,4},{8,136},{136,8},{12,140},{140,12},... | collective-permute-start | bytes 1572872 | tf_op jit(solution)/shard_map/ppermute | solution.py:271
  47.4 24.1 %collective-permute-start.3 = (bf16[1024,256]{1,0:T(8,128)(2,1)S(1)}, bf16[1024,256]{1,0:T(8,128)(2,1)S(1)}, u32[]{:S(2)}, u32[]{:S(2)}) collective-permute-start(bf16[1024,256]{1,0:T(8,128)(2,1)S(1)} %bitcast.27), channel_id=1, source_target_pairs={{128,4},{4,128},{132,8},{8,132},{136,12},{12,136},{140,0},{0,140},... | collective-permute-start | bytes 1572872 | tf_op jit(solution)/shard_map/ppermute | solution.py:271
  52.8 35.9 %collective-permute-start.11 = (bf16[2,128,2048]{2,1,0:T(8,128)(2,1)}, bf16[2,128,2048]{2,1,0:T(8,128)(2,1)}, u32[]{:S(2)}, u32[]{:S(2)}) collective-permute-start(bf16[2,128,2048]{2,1,0:T(8,128)(2,1)} %refs_0_.1), channel_id=1, source_target_pairs={{0,64},{64,0},{1,65},{65,1},{2,66},{66,2},{3,67},{67,3},{4,68},{68... | collective-permute-start | bytes 3145736 | tf_op jit(solution)/shard_map/ppermute | solution.py:280
  59.7 31.7 %collective-permute-start.14 = (bf16[2,128,2048]{2,1,0:T(8,128)(2,1)}, bf16[2,128,2048]{2,1,0:T(8,128)(2,1)}, u32[]{:S(2)}, u32[]{:S(2)}) collective-permute-start(bf16[2,128,2048]{2,1,0:T(8,128)(2,1)} %collective-permute-done.1.refs_3_), channel_id=1, source_target_pairs={{0,64},{64,0},{1,65},{65,1},{2,66},{66,2},{3,67},{67,3},{4,68},{68... | collective-permute-start | bytes 3145736 | tf_op jit(solution)/shard_map/ppermute | solution.py:280
  70.9 20.6 %collective-permute-start.12 = (bf16[2,128,2048]{2,1,0:T(8,128)(2,1)}, bf16[2,128,2048]{2,1,0:T(8,128)(2,1)}, u32[]{:S(2)}, u32[]{:S(2)}) collective-permute-start(bf16[2,128,2048]{2,1,0:T(8,128)(2,1)} %collective-permute-done.refs_1_), channel_id=1, source_target_pairs={{0,64},{64,0},{1,65},{65,1},{2,66},{66,2},{3,67},{67,3},{4,68},{68... | collective-permute-start | bytes 3145736 | tf_op jit(solution)/shard_map/ppermute | solution.py:280
  71.7 17.0 %collective-permute-start.16 = (bf16[1024,256]{1,0:T(8,128)(2,1)S(1)}, bf16[1024,256]{1,0:T(8,128)(2,1)}, u32[]{:S(2)}, u32[]{:S(2)}) collective-permute-start(bf16[1024,256]{1,0:T(8,128)(2,1)S(1)} %bitcast.30), channel_id=1, source_target_pairs={{128,4},{4,128},{132,8},{8,132},{136,12},{12,136},{140,0},{0,140},... | collective-permute-start | bytes 1572872 | tf_op jit(solution)/shard_map/ppermute | solution.py:271
  77.0 16.3 %collective-permute-start.13 = (bf16[2,128,2048]{2,1,0:T(8,128)(2,1)}, bf16[2,128,2048]{2,1,0:T(8,128)(2,1)}, u32[]{:S(2)}, u32[]{:S(2)}) collective-permute-start(bf16[2,128,2048]{2,1,0:T(8,128)(2,1)} %collective-permute-done.10.refs_2_), channel_id=1, source_target_pairs={{0,64},{64,0},{1,65},{65,1},{2,66},{66,2},{3,67},{67,3},{4,68},{68... | collective-permute-start | bytes 3145736 | tf_op jit(solution)/shard_map/ppermute | solution.py:280
  88.7 17.1 %collective-permute-start.4 = (bf16[1024,256]{1,0:T(8,128)(2,1)S(1)}, bf16[1024,256]{1,0:T(8,128)(2,1)}, u32[]{:S(2)}, u32[]{:S(2)}) collective-permute-start(bf16[1024,256]{1,0:T(8,128)(2,1)S(1)} %copy-done.14), channel_id=1, source_target_pairs={{0,128},{128,0},{4,132},{132,4},{8,136},{136,8},{12,140},{140,12},... | collective-permute-start | bytes 1572872 | tf_op jit(solution)/shard_map/ppermute | solution.py:271
  88.7 17.1 %collective-permute-start.5 = (bf16[1024,256]{1,0:T(8,128)(2,1)S(1)}, bf16[1024,256]{1,0:T(8,128)(2,1)}, u32[]{:S(2)}, u32[]{:S(2)}) collective-permute-start(bf16[1024,256]{1,0:T(8,128)(2,1)S(1)} %copy-done.11), channel_id=1, source_target_pairs={{128,4},{4,128},{132,8},{8,132},{136,12},{12,136},{140,0},{0,140},... | collective-permute-start | bytes 1572872 | tf_op jit(solution)/shard_map/ppermute | solution.py:271
  91.4 20.8 %collective-permute-start.17 = (bf16[1024,256]{1,0:T(8,128)(2,1)}, bf16[1024,256]{1,0:T(8,128)(2,1)}, u32[]{:S(2)}, u32[]{:S(2)}) collective-permute-start(bf16[1024,256]{1,0:T(8,128)(2,1)} %collective-permute-done.16.c1_a), channel_id=1, source_target_pairs={{0,128},{128,0},{4,132},{132,4},{8,136},{136,8},{12,140},{140,12},... | collective-permute-start | bytes 1572872 | tf_op jit(solution)/shard_map/ppermute | solution.py:271
  91.5 22.2 %collective-permute-start.18 = (bf16[1024,256]{1,0:T(8,128)(2,1)}, bf16[1024,256]{1,0:T(8,128)(2,1)}, u32[]{:S(2)}, u32[]{:S(2)}) collective-permute-start(bf16[1024,256]{1,0:T(8,128)(2,1)} %collective-permute-done.15.a1_a), channel_id=1, source_target_pairs={{128,4},{4,128},{132,8},{8,132},{136,12},{12,136},{140,0},{0,140},... | collective-permute-start | bytes 1572872 | tf_op jit(solution)/shard_map/ppermute | solution.py:271
  105.8 18.0 %collective-permute-start.21 = (bf16[1024,256]{1,0:T(8,128)(2,1)}, bf16[1024,256]{1,0:T(8,128)(2,1)}, u32[]{:S(2)}, u32[]{:S(2)}) collective-permute-start(bf16[1024,256]{1,0:T(8,128)(2,1)} %collective-permute-done.5.c2_b), channel_id=1, source_target_pairs={{0,128},{128,0},{4,132},{132,4},{8,136},{136,8},{12,140},{140,12},... | collective-permute-start | bytes 1572872 | tf_op jit(solution)/shard_map/ppermute | solution.py:271
  106.1 18.8 %collective-permute-start.22 = (bf16[1024,256]{1,0:T(8,128)(2,1)}, bf16[1024,256]{1,0:T(8,128)(2,1)}, u32[]{:S(2)}, u32[]{:S(2)}) collective-permute-start(bf16[1024,256]{1,0:T(8,128)(2,1)} %collective-permute-done.4.a2_b), channel_id=1, source_target_pairs={{128,4},{4,128},{132,8},{8,132},{136,12},{12,136},{140,0},{0,140},... | collective-permute-start | bytes 1572872 | tf_op jit(solution)/shard_map/ppermute | solution.py:271
  124.9 30.5 %all-to-all-start.3 = ((bf16[32,128,128]{2,1,0:T(8,128)(2,1)}), bf16[32,128,128]{2,1,0:T(8,128)(2,1)S(1)}, u32[]{:S(2)}, u32[]{:S(2)}) async-start(bf16[32,128,128]{2,1,0:T(8,128)(2,1)} %bitcast.20), calls=%async_computation.3 | async-start | bytes 2097152 | tf_op jit(solution)/shard_map/all_to_all | solution.py:316
  133.2 14.5 %collective-permute-start.20 = (bf16[1024,256]{1,0:T(8,128)(2,1)}, bf16[1024,256]{1,0:T(8,128)(2,1)}, u32[]{:S(2)}, u32[]{:S(2)}) collective-permute-start(bf16[1024,256]{1,0:T(8,128)(2,1)} %collective-permute-done.17.a2_a), channel_id=1, source_target_pairs={{128,4},{4,128},{132,8},{8,132},{136,12},{12,136},{140,0},{0,140},... | collective-permute-start | bytes 1572872 | tf_op jit(solution)/shard_map/ppermute | solution.py:271
  147.7 20.6 %collective-permute-start.23 = (bf16[1024,256]{1,0:T(8,128)(2,1)}, bf16[1024,256]{1,0:T(8,128)(2,1)}, u32[]{:S(2)}, u32[]{:S(2)}) collective-permute-start(bf16[1024,256]{1,0:T(8,128)(2,1)} %collective-permute-done.20.c3_a), channel_id=1, source_target_pairs={{0,128},{128,0},{4,132},{132,4},{8,136},{136,8},{12,140},{140,12},... | collective-permute-start | bytes 1572872 | tf_op jit(solution)/shard_map/ppermute | solution.py:271
  147.7 20.7 %collective-permute-start.24 = (bf16[1024,256]{1,0:T(8,128)(2,1)}, bf16[1024,256]{1,0:T(8,128)(2,1)}, u32[]{:S(2)}, u32[]{:S(2)}) collective-permute-start(bf16[1024,256]{1,0:T(8,128)(2,1)} %collective-permute-done.21.a3_b), channel_id=1, source_target_pairs={{128,4},{4,128},{132,8},{8,132},{136,12},{12,136},{140,0},{0,140},... | collective-permute-start | bytes 1572872 | tf_op jit(solution)/shard_map/ppermute | solution.py:271
  155.4 20.2 %all-to-all-start.2 = ((bf16[32,64,128]{2,1,0:T(8,128)(2,1)}), bf16[32,64,128]{2,1,0:T(8,128)(2,1)}, u32[]{:S(2)}, u32[]{:S(2)}) async-start(bf16[32,64,128]{2,1,0:T(8,128)(2,1)} %bitcast.32), calls=%async_computation.2 | async-start | bytes 1048576 | tf_op jit(solution)/shard_map/all_to_all | solution.py:316
  (23 other events, 176.8 us)

commit v5 on v4

v5 whole, which is shorter than its diff:
```python
import functools

import jax
import jax.numpy as jnp
from jax import lax
from jax.experimental import pallas as pl
from jax.experimental.pallas import tpu as pltpu
from jax.sharding import Mesh, PartitionSpec as P

learn_rate = 0.01
decay_rate = 0.1
beta_one = 0.9
beta_two = 0.95
epsilon = 1e-08
correct_one = 1.0 - 0.9**4
correct_two = 1.0 - 0.95**4

CAP = 32
PARTS = 4
STRIP = 128
ROOM = 20 * 2**20
WIDE = 56 * 2**20
SMALL = pl.CostEstimate(flops=1, bytes_accessed=1, transcendentals=0)


def adam_kernel(master_ref, first_ref, second_ref, gradient_ref, new_ref, block_ref):
    grad_full = gradient_ref[0].astype(jnp.float32)
    new_first = beta_one * first_ref[0] + (1.0 - beta_one) * grad_full
    new_second = beta_two * second_ref[0] + (1.0 - beta_two) * grad_full * grad_full
    update = new_first / correct_one / (jnp.sqrt(new_second / correct_two) + epsilon)
    updated = master_ref[0] * (1.0 - learn_rate * decay_rate) - learn_rate * update
    new_ref[0] = updated
    lowered = updated.astype(jnp.bfloat16)
    cores, _, _, part = block_ref.shape
    at = 0
    for start in range(0, part, STRIP):
        for core in range(cores):
            block_ref[core, 0, :, start : start + STRIP] = lowered[:, at : at + STRIP]
            at += STRIP


def adam(master, first_moment, second_moment, gradient, cores):
    experts, rows, width = master.shape
    part = width // cores
    whole = pl.BlockSpec((1, rows, width), lambda i: (i, 0, 0))
    block = pl.BlockSpec((cores, 1, rows, part), lambda i: (0, i, 0, 0))
    chunk = jax.ShapeDtypeStruct((cores, experts, rows, part), jnp.bfloat16)
    return pl.pallas_call(
        adam_kernel,
        grid=(experts,),
        in_specs=[whole] * 4,
        out_specs=[whole, block],
        out_shape=[jax.ShapeDtypeStruct(master.shape, jnp.float32)] + [chunk],
        compiler_params=pltpu.CompilerParams(vmem_limit_bytes=WIDE),
        cost_estimate=pl.CostEstimate(
            flops=16 * master.size, bytes_accessed=20 * master.size, transcendentals=master.size
        ),
    )(master, first_moment, second_moment, gradient)


def pick_kernel(where_ref, ids_ref, tokens_ref, out_ref):
    count = ids_ref.shape[2]
    ys, parts = out_ref.shape[:2]
    earlier = lax.broadcasted_iota(jnp.int32, (count, count), 0)
    later = lax.broadcasted_iota(jnp.int32, (count, count), 1)
    before = jnp.where(earlier < later, 1.0, 0.0).astype(jnp.bfloat16)
    slot = lax.broadcasted_iota(jnp.int32, (CAP, count), 0).astype(jnp.float32)
    ids = ids_ref[0]
    masks = []
    for at in range(ys * parts):
        hit = jnp.where(ids == where_ref[1 + at], 1.0, 0.0)
        masks.append(jnp.max(hit, axis=0, keepdims=True))
    mask = jnp.concatenate(masks, axis=0)
    place = jnp.dot(mask.astype(jnp.bfloat16), before, preferred_element_type=jnp.float32)
    chosen = [
        jnp.where(slot == place[at : at + 1], mask[at : at + 1], 0.0) for at in range(ys * parts)
    ]
    chosen = jnp.concatenate(chosen, axis=0).astype(jnp.bfloat16)
    picked = jnp.dot(chosen, tokens_ref[0], preferred_element_type=jnp.float32)
    picked = picked.astype(jnp.bfloat16)
    for y in range(ys):
        for part in range(parts):
            at = (y * parts + part) * CAP
            out_ref[y, part] = picked[at : at + CAP]


def pick_rows(where, ids, tokens, ys):
    steps, choices, count = ids.shape
    depth = tokens.shape[2]
    half = depth // 2
    out = jax.ShapeDtypeStruct((ys, PARTS, steps * CAP, depth), jnp.bfloat16)
    return pl.pallas_call(
        pick_kernel,
        grid_spec=pltpu.PrefetchScalarGridSpec(
            num_scalar_prefetch=1,
            grid=(steps, 2),
            in_specs=[
                pl.BlockSpec((1, choices, count), lambda i, j, w: (i, 0, 0)),
                pl.BlockSpec((1, count, half), lambda i, j, w: (i, 0, (j + w[0]) % 2)),
            ],
            out_specs=pl.BlockSpec((ys, PARTS, CAP, half), lambda i, j, w: (0, 0, i, j)),
        ),
        out_shape=out,
        compiler_params=pltpu.CompilerParams(vmem_limit_bytes=ROOM),
        cost_estimate=SMALL,
    )(where, ids, tokens)


def multiply(rows_ref, weights, at=0):
    sides, ys, count, _ = rows_ref.shape
    total = None
    for weight in weights:
        depth = weight.shape[0]
        rows = rows_ref[:, :, :, at : at + depth].reshape(sides * ys * count, depth)
        piece = jnp.dot(rows, weight[...], preferred_element_type=jnp.float32)
        total = piece if total is None else total + piece
        at += depth
    return total


def fetch(near, far, part, held, sems, slot=0):
    copies = []
    for side, ref in enumerate((near, far)):
        copy = pltpu.make_async_copy(ref.at[:, part], held.at[slot, side], sems.at[slot, side])
        copy.start()
        copies.append(copy)
    return copies


def wait(copies):
    for copy in copies:
        copy.wait()


def act(out_ref, places, slot, product):
    value = (product * jax.nn.sigmoid(product)).astype(out_ref.dtype)
    _, _, _, rows, strip = out_ref.shape
    for away, place in enumerate(places):
        for column in range(value.shape[1] // strip):
            out_ref[place, column, slot] = value[
                away * rows : (away + 1) * rows, column * strip : (column + 1) * strip
            ]


def around(core_ref, ys):
    return [lax.rem(core_ref[0] + side, 2) * ys + y for side in range(2) for y in range(ys)]


def early_kernel(core_ref, near, far, *refs):
    weights, (out_ref, held, sems) = refs[:-3], refs[-3:]
    first, second = [fetch(near, far, part, held, sems, part) for part in range(2)]
    places = around(core_ref, near.shape[0])
    wait(first)
    act(out_ref, places, 0, multiply(held.at[0], weights[:4]))
    wait(second)
    act(out_ref, places, 1, multiply(held.at[1], weights[4:]))


def later_kernel(core_ref, near, far, *refs):
    weights, (out_ref, held, sems) = refs[:-3], refs[-3:]
    wait(fetch(near, far, 2, held, sems))
    act(out_ref, around(core_ref, near.shape[0]), 0, multiply(held.at[0], weights))


def begin_kernel(core_ref, near, far, c3_a, c3_b, start_ref, held, sems):
    wait(fetch(near, far, 3, held, sems))
    start_ref[...] = multiply(held.at[0], [c3_a, c3_b], near.shape[3] // 2)


def last_kernel(core_ref, near, far, z4_a, z4_b, start_ref, out_ref, held, sems):
    wait(fetch(near, far, 3, held, sems))
    product = start_ref[...] + multiply(held.at[0], [z4_a, z4_b])
    act(out_ref, around(core_ref, near.shape[0]), 0, product)


def run(body, operands, out_shape, rows=None, core=None, slots=1):
    spec = pl.BlockSpec(memory_space=pltpu.VMEM)
    in_specs = [spec] * len(operands)
    scratch = []
    if rows is not None:
        in_specs = [
            pl.BlockSpec(memory_space=pltpu.SMEM),
            pl.BlockSpec(memory_space=pl.ANY),
            pl.BlockSpec(memory_space=pl.ANY),
        ] + in_specs
        operands = [core, *rows, *operands]
        ys, _, count, depth = rows[0].shape
        scratch = [
            pltpu.VMEM((slots, 2, ys, count, depth), jnp.bfloat16),
            pltpu.SemaphoreType.DMA((slots, 2)),
        ]
    return pl.pallas_call(
        body,
        in_specs=in_specs,
        out_specs=spec,
        out_shape=out_shape,
        scratch_shapes=scratch,
        compiler_params=pltpu.CompilerParams(vmem_limit_bytes=ROOM),
        cost_estimate=SMALL,
    )(*operands)


def place_kernel(order_ref, ids_ref, raw_ref, out_ref):
    count, choices = ids_ref.shape[1:]
    lanes = out_ref.shape[2]
    names = 128
    ids = ids_ref[0]
    raw = raw_ref[0]
    shares = raw / jnp.sum(raw, axis=1, keepdims=True)
    name = lax.broadcasted_iota(jnp.int32, (count, names), 1)
    mask = jnp.zeros((count, names), jnp.float32)
    weight = jnp.zeros((count, names), jnp.float32)
    for choice in range(choices):
        hit = ids[:, choice : choice + 1] == name
        mask = mask + jnp.where(hit, 1.0, 0.0)
        weight = weight + jnp.where(hit, shares[:, choice : choice + 1], 0.0)
    row = lax.broadcasted_iota(jnp.int32, (count, count), 0)
    column = lax.broadcasted_iota(jnp.int32, (count, count), 1)
    before = jnp.where(column < row, 1.0, 0.0).astype(jnp.bfloat16)
    place = jnp.dot(before, mask.astype(jnp.bfloat16), preferred_element_type=jnp.float32)
    place = jnp.where(mask > 0.0, place, 255.0).astype(jnp.bfloat16)
    high = weight.astype(jnp.bfloat16)
    low = (weight - high.astype(jnp.float32)).astype(jnp.bfloat16)
    stacked = jnp.concatenate([place, high, low], axis=0)
    span = lanes // PARTS
    for part in range(PARTS):
        lane = lax.broadcasted_iota(jnp.int32, (names, span), 1)
        device = lane // CAP
        expert = (device // 4 * 4 + order_ref[part]) * 4 + device % 4
        spread = jnp.where(
            lax.broadcasted_iota(jnp.int32, (names, span), 0) == expert, 1.0, 0.0
        ).astype(jnp.bfloat16)
        wide = jnp.dot(stacked, spread, preferred_element_type=jnp.float32)
        slot = (lax.broadcasted_iota(jnp.int32, (count, span), 1) % CAP).astype(jnp.float32)
        here = wide[:count] == slot
        at = slice(part * span, (part + 1) * span)
        out_ref[0, :count, at] = jnp.where(here, wide[count : 2 * count], 0.0).astype(jnp.bfloat16)
        out_ref[0, count:, at] = jnp.where(here, wide[2 * count :], 0.0).astype(jnp.bfloat16)


def place_rows(order, ids, raw, lanes):
    steps, count, choices = ids.shape
    return pl.pallas_call(
        place_kernel,
        grid_spec=pltpu.PrefetchScalarGridSpec(
            num_scalar_prefetch=1,
            grid=(steps,),
            in_specs=[pl.BlockSpec((1, count, choices), lambda i, w: (i, 0, 0))] * 2,
            out_specs=pl.BlockSpec((1, 2 * count, lanes), lambda i, w: (i, 0, 0)),
        ),
        out_shape=jax.ShapeDtypeStruct((steps, 2 * count, lanes), jnp.bfloat16),
        compiler_params=pltpu.CompilerParams(vmem_limit_bytes=ROOM),
        cost_estimate=SMALL,
    )(order, ids, raw)


def mix_kernel(first, place_ref, *refs):
    out_ref = refs[-1]
    steps, count, _ = out_ref.shape
    for step in range(steps):
        part, total = first, None
        for ref in refs[:-1]:
            if len(ref.shape) == len(out_ref.shape):
                total = total + ref[step]
                continue
            cores, devices, slots, _, rows, strip = ref.shape
            span = devices * rows
            for slot in range(slots):
                arrived = jnp.concatenate(
                    [ref[core, :, slot, step].reshape(span, strip) for core in range(cores)], axis=1
                )
                piece = jnp.dot(
                    place_ref[step, :, part * span : (part + 1) * span],
                    arrived,
                    preferred_element_type=jnp.float32,
                )
                piece = piece[:count] + piece[count:]
                total = piece if total is None else total + piece
                part += 1
        out_ref[step] = total.astype(out_ref.dtype)


def swap(value, offset):
    high, low = lax.axis_size("zh"), lax.axis_size("zl")
    pairs = []
    for z in range(offset, high * low + offset, low):
        a, b = [(at % low) * high + at // low % high for at in (z, z + 1)]
        pairs += [(a, b), (b, a)]
    return lax.ppermute(value, ("zl", "zh"), pairs)


def swap_cores(value):
    return lax.ppermute(value, "core", [(0, 1), (1, 0)])


def per_device(master, first_moment, second_moment, gradient, tokens, expert_ids, router_scores):
    steps, token_count, depth = tokens.shape
    quarters = lax.axis_size("x")
    cores = lax.axis_size("core")
    owners = lax.axis_size("zh")
    ys = lax.axis_size("y")
    groups = cores * ys
    z_low, z_high = lax.axis_index("zl"), lax.axis_index("zh")
    x_at = lax.axis_index("x")

    turn = jnp.where(z_low == 0, 1, -1)
    order = jnp.mod(jnp.stack([z_high, z_high - turn, z_high + turn, z_high + 2]), owners)
    names = quarters * (jnp.arange(ys)[:, None] * owners + order[None, :]) + x_at
    where = jnp.concatenate([z_low[None], names.reshape(-1)]).astype(jnp.int32)
    order = order.astype(jnp.int32)
    core = lax.axis_index("core").reshape(1).astype(jnp.int32)

    new_master, blocks = adam(master, first_moment, second_moment, gradient, cores)
    rows, width = master.shape[1:]
    part = width // cores
    strip = width // (quarters * cores)

    hold = lax.optimization_barrier
    blocks, tokens = hold((blocks.reshape(-1, rows, part), tokens))
    own = lax.all_to_all(blocks, ("core", "x"), split_axis=0, concat_axis=0, tiled=True)
    picked = pick_rows(where, expert_ids.transpose(0, 2, 1), tokens, ys)
    own, picked = hold((own, picked))
    near = lax.all_to_all(picked, "y", split_axis=0, concat_axis=0, tiled=True)
    own = own.reshape(-1, part)
    cut = own.shape[0] // 2
    own_a, own_b = own[:cut], own[cut:]
    a1_a, c1_a = swap(own_a, 0), swap(own_a, 1)
    a1_b, c1_b = swap(own_b, 0), swap(own_b, 1)
    placed = place_rows(order, expert_ids, router_scores, PARTS * quarters * ys * CAP)
    a1_a, c1_a = hold((a1_a, c1_a))
    a2_a, c2_a = swap(c1_a, 0), swap(a1_a, 1)
    a1_b, c1_b, placed, used_1 = hold((a1_b, c1_b, placed, a1_a))
    a2_b, c2_b = swap(c1_b, 0), swap(a1_b, 1)
    a2_a, c2_a = hold((a2_a, c2_a))
    a3_a, c3_a = swap(c2_a, 0), swap(a2_a, 1)
    a2_b, c2_b, used_2, near = hold((a2_b, c2_b, a2_a, near))
    a3_b, c3_b = swap(c2_b, 0), swap(a2_b, 1)
    sides = (near, swap_cores(near))
    double = jax.ShapeDtypeStruct((groups, quarters, 2, steps * CAP, strip), jnp.bfloat16)
    single = jax.ShapeDtypeStruct((groups, quarters, 1, steps * CAP, strip), jnp.bfloat16)
    start = jax.ShapeDtypeStruct((groups * steps * CAP, part), jnp.float32)

    def send_back(value):
        slots = value.shape[2]
        value = value.reshape(groups * quarters, slots * steps * CAP, strip)
        back = lax.all_to_all(value, ("core", "y", "x"), split_axis=0, concat_axis=0, tiled=True)
        return back.reshape(cores, ys * quarters, slots, steps, CAP, strip)

    early = [own_a, own_b, used_1, a1_b, c2_a, c2_b, c1_a, c1_b]
    early = run(early_kernel, early, double, sides, core, 2)
    a3_a, c3_a = hold((a3_a, c3_a))
    z4_a = swap(c3_a, 0)
    a3_b, c3_b, early, used_3 = hold((a3_b, c3_b, early, a3_a))
    early = send_back(early)
    z4_b = swap(a3_b, 1)
    later = send_back(run(later_kernel, [used_2, a2_b, used_3, a3_b], single, sides, core))
    begun = run(begin_kernel, [c3_a, c3_b], start, sides, core)
    mixed_shape = (steps, token_count, cores * strip)
    half_mixed = jax.ShapeDtypeStruct(mixed_shape, jnp.float32)
    half_mixed = run(functools.partial(mix_kernel, 0), [placed, early], half_mixed)
    z4_a, z4_b, begun, half_mixed = hold((z4_a, z4_b, begun, half_mixed))
    final = send_back(run(last_kernel, [z4_a, z4_b, begun], single, sides, core))
    mixed = jax.ShapeDtypeStruct(mixed_shape, jnp.bfloat16)
    mixed = run(functools.partial(mix_kernel, 2), [placed, later, final, half_mixed], mixed)
    return (new_master, mixed)


def solution(mesh):
    grid = Mesh(mesh.devices.reshape(2, 2, 4, 4, 4), ("zl", "core", "y", "zh", "x"))
    owner, part, group = ("y", "zh"), ("zl", "core", "x"), ("zl", "core", "y", "zh")
    weights = P(owner, part, None)
    routed = P(None, group, None)
    return jax.shard_map(
        per_device,
        mesh=grid,
        in_specs=(weights,) * 4 + (routed,) * 3,
        out_specs=(weights, P(None, group, "x")),
        check_vma=False,
    )
```

time: 195 us -> 172 us (0.88)
  starting transfers between devices: 62.7 us -> 44.6 us
  local copies, waits for them, and re-layouts: 15.8 us -> 6.48 us
  waiting for transfers between devices: 68.5 us -> 72.1 us
  Pallas kernels: 29.6 us -> 31.6 us
    unnamed x38 -> x16, local copies, waits for them, and re-layouts: 15.8 us -> 5.09 us
    all_to_all x2, waiting for transfers between devices: 4.43 us -> 12 us  [send_back(): lax.all_to_all(value, ('core', 'y', 'x'), split_axis=0, concat_axis=0, ti...]
    ppermute x6 -> x0, starting transfers between devices: 7.28 us -> none  [from_y(): lax.ppermute(value, 'y', [((at + away) % size, at) for at in range(size)])]
    ppermute x14, waiting for transfers between devices: 43.6 us -> 50.7 us  [swap(): return lax.ppermute(value, ('zl', 'zh'), pairs)]
    pallas_call x6, Pallas kernels: 14 us -> 19.8 us  [run(): pl.pallas_call(body, in_specs=in_specs, out_specs=spec, out_shape=out_sha...]
    all_to_all x2, waiting for transfers between devices: 14.7 us -> 9.44 us  [the longest x1 9.44 us: per_device(): lax.all_to_all(blocks, ('core', 'x'), split_axis=0, concat_axis=0, tiled=...]
    all_to_all x2, starting transfers between devices: 16.9 us -> 12 us  [send_back(): lax.all_to_all(value, ('core', 'y', 'x'), split_axis=0, concat_axis=0, ti...]
    ppermute x6 -> x0, waiting for transfers between devices: 4.57 us -> none  [from_y(): lax.ppermute(value, 'y', [((at + away) % size, at) for at in range(size)])]
  transfers between devices with their start and end apart: 29 -> 19, of which waited for: 15 -> 15; matrix products, arithmetic and copies ran while one was open for 0% -> 1% of each run, Pallas kernels for 14% -> 14%
where the time goes in v5:
time: 172 us; the launch traced here: 171 us
  waiting for transfers between devices  72.1 us (42%)
  starting transfers between devices  44.6 us (26%)
  Pallas kernels  31.6 us (18%)
  blocking collectives  15.1 us (9%)
  local copies, waits for them, and re-layouts  6.48 us (4%)
    ppermute x14, waiting for transfers between devices, swap(): return lax.ppermute(value, ('zl', 'zh'), pairs)  50.7 us
    pallas_call x6, Pallas kernels, run(): pl.pallas_call(body, in_specs=in_specs, out_specs=spec, out_shape=out_sha...  19.8 us
    ppermute x14, starting transfers between devices, swap(): return lax.ppermute(value, ('zl', 'zh'), pairs)  19.7 us
    all_to_all x1, blocking collectives, send_back(): lax.all_to_all(value, ('core', 'y', 'x'), split_axis=0, concat_axis=0, ti...  15.1 us
    all_to_all x2, starting transfers between devices, send_back(): lax.all_to_all(value, ('core', 'y', 'x'), split_axis=0, concat_axis=0, ti...  12 us
    all_to_all x2, waiting for transfers between devices, send_back(): lax.all_to_all(value, ('core', 'y', 'x'), split_axis=0, concat_axis=0, ti...  12 us
    all_to_all x1, waiting for transfers between devices, per_device(): lax.all_to_all(blocks, ('core', 'x'), split_axis=0, concat_axis=0, tiled=...  9.44 us
    all_to_all x1, starting transfers between devices, per_device(): lax.all_to_all(blocks, ('core', 'x'), split_axis=0, concat_axis=0, tiled=...  6.86 us
  transfers between devices with their start and end apart: 19, of which 15 were waited for; matrix products, arithmetic and copies ran while one was open for 1% of the time, Pallas kernels for 14%

profile of v5, /device:TPU:1, one launch (start us, length us, event | category | flops | bytes accessed | tf_op | source)
XLA Modules:
  0.0 170.8 jit_solution(4010978592343517074)
XLA Ops:
  0.6 5.8 %shard_map.86 = (f32[4,128,1024]{2,1,0:T(8,128)}, bf16[2,4,128,512]{3,2,1,0:T(8,128)(2,1)}) custom-call(f32[4,128,1024]{2,1,0:T(8,128)} %master_ref.1, f32[4,128,1024]{2,1,0:T(8,128)} %first_ref.1, f32[4,128,1024]{2,1,0:T(8,128)} %second_ref.1, bf16[4,128,1024]{2,1,0:T(8,128)(2,1)} %gradient_ref.1), custom_call_target="tpu_custom_call" | custom-call | flops 8388608 | bytes 10485760 | tf_op jit(solution)/shard_map/pallas_call | solution.py:48
  6.5 6.9 %all-to-all-start = ((bf16[8,128,512]{2,1,0:T(8,128)(2,1)}), bf16[8,128,512]{2,1,0:T(8,128)(2,1)S(1)}, u32[]{:S(2)}, u32[]{:S(2)}) async-start(bf16[8,128,512]{2,1,0:T(8,128)(2,1)} %bitcast.28), calls=%async_computation | async-start | bytes 2097152 | tf_op jit(solution)/shard_map/all_to_all | solution.py:320
  13.6 3.2 %shard_map.87 = bf16[4,4,64,2048]{3,2,1,0:T(8,128)(2,1)S(1)} custom-call(s32[17]{0:T(128)S(1)} %pad_add_fusion.where_ref, s32[2,8,128]{2,1,0:T(8,128)S(1)} %bitcast.27, bf16[2,128,2048]{2,1,0:T(8,128)(2,1)S(1)} %copy-done.3), custom_call_target="tpu_custom_call" | custom-call | flops 1 | bytes 1 | tf_op jit(solution)/shard_map/pallas_call | solution.py:92
  18.9 9.4 %all-to-all-done = bf16[8,128,512]{2,1,0:T(8,128)(2,1)S(1)} async-done(((bf16[8,128,512]{2,1,0:T(8,128)(2,1)}), bf16[8,128,512]{2,1,0:T(8,128)(2,1)S(1)}, u32[]{:S(2)}, u32[]{:S(2)}) %all-to-all-start) | async-done | bytes 1048608 | tf_op jit(solution)/shard_map/all_to_all | solution.py:320
  29.3 4.8 %all-to-all-start.1 = ((bf16[4,4,64,2048]{3,2,1,0:T(8,128)(2,1)}), bf16[4,4,64,2048]{3,2,1,0:T(8,128)(2,1)}, u32[]{:S(2)}, u32[]{:S(2)}) async-start(bf16[4,4,64,2048]{3,2,1,0:T(8,128)(2,1)} %copy-done), calls=%async_computation.1 | async-start | bytes 8388608 | tf_op jit(solution)/shard_map/all_to_all | solution.py:323
  36.3 4.7 %collective-permute-start.3 = (bf16[512,512]{1,0:T(8,128)(2,1)S(1)}, bf16[512,512]{1,0:T(8,128)(2,1)}, u32[]{:S(2)}, u32[]{:S(2)}) collective-permute-start(bf16[512,512]{1,0:T(8,128)(2,1)S(1)} %bitcast.22), channel_id=1, source_target_pairs={{128,4},{4,128},{132,8},{8,132},{136,12},{12,136},{140,0},{0,140},... | collective-permute-start | bytes 1572872 | tf_op jit(solution)/shard_map/ppermute | solution.py:289
  45.5 3.3 %collective-permute-done.2.refs_2_ = bf16[512,512]{1,0:T(8,128)(2,1)} collective-permute-done((bf16[512,512]{1,0:T(8,128)(2,1)S(1)}, bf16[512,512]{1,0:T(8,128)(2,1)}, u32[]{:S(2)}, u32[]{:S(2)}) %collective-permute-start.2) | collective-permute-done | bytes 524320 | tf_op jit(solution)/shard_map/ppermute | solution.py:289
  48.9 3.9 %collective-permute-done.3.refs_6_ = bf16[512,512]{1,0:T(8,128)(2,1)} collective-permute-done((bf16[512,512]{1,0:T(8,128)(2,1)S(1)}, bf16[512,512]{1,0:T(8,128)(2,1)}, u32[]{:S(2)}, u32[]{:S(2)}) %collective-permute-start.3) | collective-permute-done | bytes 524320 | tf_op jit(solution)/shard_map/ppermute | solution.py:289
  55.1 4.9 %collective-permute-done.refs_3_ = bf16[512,512]{1,0:T(8,128)(2,1)} collective-permute-done((bf16[512,512]{1,0:T(8,128)(2,1)S(1)}, bf16[512,512]{1,0:T(8,128)(2,1)}, u32[]{:S(2)}, u32[]{:S(2)}) %collective-permute-start) | collective-permute-done | bytes 524320 | tf_op jit(solution)/shard_map/ppermute | solution.py:289
  60.1 3.9 %collective-permute-done.1.refs_7_ = bf16[512,512]{1,0:T(8,128)(2,1)} collective-permute-done((bf16[512,512]{1,0:T(8,128)(2,1)S(1)}, bf16[512,512]{1,0:T(8,128)(2,1)}, u32[]{:S(2)}, u32[]{:S(2)}) %collective-permute-start.1) | collective-permute-done | bytes 524320 | tf_op jit(solution)/shard_map/ppermute | solution.py:289
  66.4 4.9 %collective-permute-done.6.refs_0_ = bf16[512,512]{1,0:T(8,128)(2,1)} collective-permute-done((bf16[512,512]{1,0:T(8,128)(2,1)}, bf16[512,512]{1,0:T(8,128)(2,1)}, u32[]{:S(2)}, u32[]{:S(2)}) %collective-permute-start.6) | collective-permute-done | bytes 524320 | tf_op jit(solution)/shard_map/ppermute | solution.py:289
  71.3 3.9 %collective-permute-done.7.refs_4_ = bf16[512,512]{1,0:T(8,128)(2,1)} collective-permute-done((bf16[512,512]{1,0:T(8,128)(2,1)}, bf16[512,512]{1,0:T(8,128)(2,1)}, u32[]{:S(2)}, u32[]{:S(2)}) %collective-permute-start.7) | collective-permute-done | bytes 524320 | tf_op jit(solution)/shard_map/ppermute | solution.py:289
  75.3 7.3 %collective-permute-done.4.refs_1_ = bf16[512,512]{1,0:T(8,128)(2,1)} collective-permute-done((bf16[512,512]{1,0:T(8,128)(2,1)}, bf16[512,512]{1,0:T(8,128)(2,1)}, u32[]{:S(2)}, u32[]{:S(2)}) %collective-permute-start.4) | collective-permute-done | bytes 524320 | tf_op jit(solution)/shard_map/ppermute | solution.py:289
  82.6 3.9 %collective-permute-done.5.refs_5_ = bf16[512,512]{1,0:T(8,128)(2,1)} collective-permute-done((bf16[512,512]{1,0:T(8,128)(2,1)}, bf16[512,512]{1,0:T(8,128)(2,1)}, u32[]{:S(2)}, u32[]{:S(2)}) %collective-permute-start.5) | collective-permute-done | bytes 524320 | tf_op jit(solution)/shard_map/ppermute | solution.py:289
  92.6 9.0 %collective-permute-done.11.refs_2_ = bf16[512,512]{1,0:T(8,128)(2,1)} collective-permute-done((bf16[512,512]{1,0:T(8,128)(2,1)}, bf16[512,512]{1,0:T(8,128)(2,1)}, u32[]{:S(2)}, u32[]{:S(2)}) %collective-permute-start.11) | collective-permute-done | bytes 524320 | tf_op jit(solution)/shard_map/ppermute | solution.py:289
  102.7 5.9 %shard_map.89 = bf16[8,4,2,64,128]{4,3,2,1,0:T(8,128)(2,1)S(1)} custom-call(s32[1]{0:T(128)} %bitcast.9.core_ref, bf16[4,4,64,2048]{3,2,1,0:T(8,128)(2,1)} %all-to-all-done.1.near, bf16[4,4,64,2048]{3,2,1,0:T(8,128)(2,1)} %collective-permute-done.8.far, bf16[512,512]{1,0:T(8,128)(2,1)S(1)} %bitcast.23, bf16[512,512]{1,0:T(8,128)(2,1)S(1)} %bitcast.26, ...), custom_call_target="tpu_custom_call" | custom-call | flops 1 | bytes 1 | tf_op jit(solution)/shard_map/pallas_call | solution.py:192
  113.9 6.2 %all-to-all-start.3 = ((bf16[32,128,128]{2,1,0:T(8,128)(2,1)}), bf16[32,128,128]{2,1,0:T(8,128)(2,1)S(1)}, u32[]{:S(2)}, u32[]{:S(2)}) async-start(bf16[32,128,128]{2,1,0:T(8,128)(2,1)} %bitcast.17), calls=%async_computation.3 | async-start | bytes 2097152 | tf_op jit(solution)/shard_map/all_to_all | solution.py:346
  123.3 4.3 %shard_map.90 = bf16[8,4,1,64,128]{4,3,2,1,0:T(8,128)(2,1)S(1)} custom-call(s32[1]{0:T(128)} %bitcast.9.core_ref, bf16[4,4,64,2048]{3,2,1,0:T(8,128)(2,1)} %all-to-all-done.1.near, bf16[4,4,64,2048]{3,2,1,0:T(8,128)(2,1)} %collective-permute-done.8.far, bf16[512,512]{1,0:T(8,128)(2,1)} %collective-permute-done.6.refs_0_, ...), custom_call_target="tpu_custom_call" | custom-call | flops 1 | bytes 1 | tf_op jit(solution)/shard_map/pallas_call | solution.py:192
  128.5 8.2 %all-to-all-done.3 = bf16[32,128,128]{2,1,0:T(8,128)(2,1)S(1)} async-done(((bf16[32,128,128]{2,1,0:T(8,128)(2,1)}), bf16[32,128,128]{2,1,0:T(8,128)(2,1)S(1)}, u32[]{:S(2)}, u32[]{:S(2)}) %all-to-all-start.3) | async-done | bytes 1048608 | tf_op jit(solution)/shard_map/all_to_all | solution.py:346
  136.7 5.8 %all-to-all-start.2 = ((bf16[32,64,128]{2,1,0:T(8,128)(2,1)}), bf16[32,64,128]{2,1,0:T(8,128)(2,1)}, u32[]{:S(2)}, u32[]{:S(2)}) async-start(bf16[32,64,128]{2,1,0:T(8,128)(2,1)} %bitcast.18), calls=%async_computation.2 | async-start | bytes 1048576 | tf_op jit(solution)/shard_map/all_to_all | solution.py:346
  142.5 3.5 %shard_map.91.start_ref = f32[512,512]{1,0:T(8,128)S(1)} custom-call(s32[1]{0:T(128)} %bitcast.9.core_ref, bf16[4,4,64,2048]{3,2,1,0:T(8,128)(2,1)} %all-to-all-done.1.near, bf16[4,4,64,2048]{3,2,1,0:T(8,128)(2,1)} %collective-permute-done.8.far, bf16[512,512]{1,0:T(8,128)(2,1)} %collective-permute-done.12.c3_a, bf16[512,512]{1,0:T(8,128)(2,1)} %collective-permute-done.10.c3_b), custom_call_target="tpu_custom_call" | custom-call | flops 1 | bytes 1 | tf_op jit(solution)/shard_map/pallas_call | solution.py:192
  146.4 3.5 %shard_map.93 = bf16[8,4,1,64,128]{4,3,2,1,0:T(8,128)(2,1)S(1)} custom-call(s32[1]{0:T(128)} %bitcast.9.core_ref, bf16[4,4,64,2048]{3,2,1,0:T(8,128)(2,1)} %all-to-all-done.1.near, bf16[4,4,64,2048]{3,2,1,0:T(8,128)(2,1)} %collective-permute-done.8.far, bf16[512,512]{1,0:T(8,128)(2,1)} %collective-permute-done.13.z4_a, ...), custom_call_target="tpu_custom_call" | custom-call | flops 1 | bytes 1 | tf_op jit(solution)/shard_map/pallas_call | solution.py:192
  149.9 3.7 %all-to-all-done.2 = bf16[32,64,128]{2,1,0:T(8,128)(2,1)} async-done(((bf16[32,64,128]{2,1,0:T(8,128)(2,1)}), bf16[32,64,128]{2,1,0:T(8,128)(2,1)}, u32[]{:S(2)}, u32[]{:S(2)}) %all-to-all-start.2) | async-done | bytes 524320 | tf_op jit(solution)/shard_map/all_to_all | solution.py:346
  153.6 15.1 %all_to_all.25 = bf16[32,64,128]{2,1,0:T(8,128)(2,1)S(1)} all-to-all(bf16[32,64,128]{2,1,0:T(8,128)(2,1)S(1)} %bitcast.19), channel_id=1, replica_groups=mesh['zl'=2,'core'=2,'y'=4,'zh'=4,'x'=4] {'core','y','x'}, dimensions={0} | all-to-all | bytes 1048576 | tf_op jit(solution)/shard_map/all_to_all | solution.py:346
  (45 shorter events, 33.7 us)
Async XLA Ops:
  6.4 7.2 %copy-start.3 = (bf16[2,128,2048]{2,1,0:T(8,128)(2,1)S(1)}, bf16[2,128,2048]{2,1,0:T(8,128)(2,1)}, u32[]{:S(2)}) copy-start(bf16[2,128,2048]{2,1,0:T(8,128)(2,1)} %tokens_ref) | copy-start | bytes 3145732
  6.4 7.2 %copy-start.4 = (s32[2,128,8]{1,2,0:T(8,128)S(1)}, s32[2,128,8]{1,2,0:T(8,128)}, u32[]{:S(2)}) copy-start(s32[2,128,8]{1,2,0:T(8,128)} %param.12) | copy-start | bytes 24580
  6.5 21.9 %all-to-all-start = ((bf16[8,128,512]{2,1,0:T(8,128)(2,1)}), bf16[8,128,512]{2,1,0:T(8,128)(2,1)S(1)}, u32[]{:S(2)}, u32[]{:S(2)}) async-start(bf16[8,128,512]{2,1,0:T(8,128)(2,1)} %bitcast.28), calls=%async_computation | async-start | bytes 2097152 | tf_op jit(solution)/shard_map/all_to_all | solution.py:320
  16.9 2.0 %copy-start = (bf16[4,4,64,2048]{3,2,1,0:T(8,128)(2,1)}, bf16[4,4,64,2048]{3,2,1,0:T(8,128)(2,1)S(1)}, u32[]{:S(2)}) copy-start(bf16[4,4,64,2048]{3,2,1,0:T(8,128)(2,1)S(1)} %shard_map.87) | copy-start | bytes 12582916
  29.3 57.2 %all-to-all-start.1 = ((bf16[4,4,64,2048]{3,2,1,0:T(8,128)(2,1)}), bf16[4,4,64,2048]{3,2,1,0:T(8,128)(2,1)}, u32[]{:S(2)}, u32[]{:S(2)}) async-start(bf16[4,4,64,2048]{3,2,1,0:T(8,128)(2,1)} %copy-done), calls=%async_computation.1 | async-start | bytes 8388608 | tf_op jit(solution)/shard_map/all_to_all | solution.py:323
  34.2 8.4 %copy-start.6 = (f32[2,128,8]{1,2,0:T(8,128)S(1)}, f32[2,128,8]{1,2,0:T(8,128)}, u32[]{:S(2)}) copy-start(f32[2,128,8]{1,2,0:T(8,128)} %param.13) | copy-start | bytes 24580
  35.5 13.3 %collective-permute-start.2 = (bf16[512,512]{1,0:T(8,128)(2,1)S(1)}, bf16[512,512]{1,0:T(8,128)(2,1)}, u32[]{:S(2)}, u32[]{:S(2)}) collective-permute-start(bf16[512,512]{1,0:T(8,128)(2,1)S(1)} %bitcast.21), channel_id=1, source_target_pairs={{0,128},{128,0},{4,132},{132,4},{8,136},{136,8},{12,140},{140,12},... | collective-permute-start | bytes 1572872 | tf_op jit(solution)/shard_map/ppermute | solution.py:289
  36.3 16.5 %collective-permute-start.3 = (bf16[512,512]{1,0:T(8,128)(2,1)S(1)}, bf16[512,512]{1,0:T(8,128)(2,1)}, u32[]{:S(2)}, u32[]{:S(2)}) collective-permute-start(bf16[512,512]{1,0:T(8,128)(2,1)S(1)} %bitcast.22), channel_id=1, source_target_pairs={{128,4},{4,128},{132,8},{8,132},{136,12},{12,136},{140,0},{0,140},... | collective-permute-start | bytes 1572872 | tf_op jit(solution)/shard_map/ppermute | solution.py:289
  41.0 19.1 %collective-permute-start = (bf16[512,512]{1,0:T(8,128)(2,1)S(1)}, bf16[512,512]{1,0:T(8,128)(2,1)}, u32[]{:S(2)}, u32[]{:S(2)}) collective-permute-start(bf16[512,512]{1,0:T(8,128)(2,1)S(1)} %bitcast.24), channel_id=1, source_target_pairs={{0,128},{128,0},{4,132},{132,4},{8,136},{136,8},{12,140},{140,12},... | collective-permute-start | bytes 1572872 | tf_op jit(solution)/shard_map/ppermute | solution.py:289
  41.0 23.0 %collective-permute-start.1 = (bf16[512,512]{1,0:T(8,128)(2,1)S(1)}, bf16[512,512]{1,0:T(8,128)(2,1)}, u32[]{:S(2)}, u32[]{:S(2)}) collective-permute-start(bf16[512,512]{1,0:T(8,128)(2,1)S(1)} %bitcast.25), channel_id=1, source_target_pairs={{128,4},{4,128},{132,8},{8,132},{136,12},{12,136},{140,0},{0,140},... | collective-permute-start | bytes 1572872 | tf_op jit(solution)/shard_map/ppermute | solution.py:289
  52.8 18.5 %collective-permute-start.6 = (bf16[512,512]{1,0:T(8,128)(2,1)}, bf16[512,512]{1,0:T(8,128)(2,1)}, u32[]{:S(2)}, u32[]{:S(2)}) collective-permute-start(bf16[512,512]{1,0:T(8,128)(2,1)} %collective-permute-done.3.refs_6_), channel_id=1, source_target_pairs={{0,128},{128,0},{4,132},{132,4},{8,136},{136,8},{12,140},{140,12},... | collective-permute-start | bytes 1572872 | tf_op jit(solution)/shard_map/ppermute | solution.py:289
  52.8 22.5 %collective-permute-start.7 = (bf16[512,512]{1,0:T(8,128)(2,1)}, bf16[512,512]{1,0:T(8,128)(2,1)}, u32[]{:S(2)}, u32[]{:S(2)}) collective-permute-start(bf16[512,512]{1,0:T(8,128)(2,1)} %collective-permute-done.2.refs_2_), channel_id=1, source_target_pairs={{128,4},{4,128},{132,8},{8,132},{136,12},{12,136},{140,0},{0,140},... | collective-permute-start | bytes 1572872 | tf_op jit(solution)/shard_map/ppermute | solution.py:289
  64.0 18.5 %collective-permute-start.4 = (bf16[512,512]{1,0:T(8,128)(2,1)}, bf16[512,512]{1,0:T(8,128)(2,1)}, u32[]{:S(2)}, u32[]{:S(2)}) collective-permute-start(bf16[512,512]{1,0:T(8,128)(2,1)} %collective-permute-done.1.refs_7_), channel_id=1, source_target_pairs={{0,128},{128,0},{4,132},{132,4},{8,136},{136,8},{12,140},{140,12},... | collective-permute-start | bytes 1572872 | tf_op jit(solution)/shard_map/ppermute | solution.py:289
  64.0 22.5 %collective-permute-start.5 = (bf16[512,512]{1,0:T(8,128)(2,1)}, bf16[512,512]{1,0:T(8,128)(2,1)}, u32[]{:S(2)}, u32[]{:S(2)}) collective-permute-start(bf16[512,512]{1,0:T(8,128)(2,1)} %collective-permute-done.refs_3_), channel_id=1, source_target_pairs={{128,4},{4,128},{132,8},{8,132},{136,12},{12,136},{140,0},{0,140},... | collective-permute-start | bytes 1572872 | tf_op jit(solution)/shard_map/ppermute | solution.py:289
  86.5 16.2 %collective-permute-start.8 = (bf16[4,4,64,2048]{3,2,1,0:T(8,128)(2,1)}, bf16[4,4,64,2048]{3,2,1,0:T(8,128)(2,1)}, u32[]{:S(2)}, u32[]{:S(2)}) collective-permute-start(bf16[4,4,64,2048]{3,2,1,0:T(8,128)(2,1)} %all-to-all-done.1.near), channel_id=1, source_target_pairs={{0,64},{64,0},{1,65},{65,1},{2,66},{66,2},{3,67},{67,3},{4,68},{68... | collective-permute-start | bytes 12582920 | tf_op jit(solution)/shard_map/ppermute | solution.py:293
  87.7 13.9 %collective-permute-start.11 = (bf16[512,512]{1,0:T(8,128)(2,1)}, bf16[512,512]{1,0:T(8,128)(2,1)}, u32[]{:S(2)}, u32[]{:S(2)}) collective-permute-start(bf16[512,512]{1,0:T(8,128)(2,1)} %collective-permute-done.7.refs_4_), channel_id=1, source_target_pairs={{0,128},{128,0},{4,132},{132,4},{8,136},{136,8},{12,140},{140,12},... | collective-permute-start | bytes 1572872 | tf_op jit(solution)/shard_map/ppermute | solution.py:289
  87.7 15.0 %collective-permute-start.12 = (bf16[512,512]{1,0:T(8,128)(2,1)}, bf16[512,512]{1,0:T(8,128)(2,1)}, u32[]{:S(2)}, u32[]{:S(2)}) collective-permute-start(bf16[512,512]{1,0:T(8,128)(2,1)} %collective-permute-done.6.refs_0_), channel_id=1, source_target_pairs={{128,4},{4,128},{132,8},{8,132},{136,12},{12,136},{140,0},{0,140},... | collective-permute-start | bytes 1572872 | tf_op jit(solution)/shard_map/ppermute | solution.py:289
  90.4 22.4 %collective-permute-start.9 = (bf16[512,512]{1,0:T(8,128)(2,1)}, bf16[512,512]{1,0:T(8,128)(2,1)}, u32[]{:S(2)}, u32[]{:S(2)}) collective-permute-start(bf16[512,512]{1,0:T(8,128)(2,1)} %collective-permute-done.5.refs_5_), channel_id=1, source_target_pairs={{0,128},{128,0},{4,132},{132,4},{8,136},{136,8},{12,140},{140,12},... | collective-permute-start | bytes 1572872 | tf_op jit(solution)/shard_map/ppermute | solution.py:289
  90.4 23.6 %collective-permute-start.10 = (bf16[512,512]{1,0:T(8,128)(2,1)}, bf16[512,512]{1,0:T(8,128)(2,1)}, u32[]{:S(2)}, u32[]{:S(2)}) collective-permute-start(bf16[512,512]{1,0:T(8,128)(2,1)} %collective-permute-done.4.refs_1_), channel_id=1, source_target_pairs={{128,4},{4,128},{132,8},{8,132},{136,12},{12,136},{140,0},{0,140},... | collective-permute-start | bytes 1572872 | tf_op jit(solution)/shard_map/ppermute | solution.py:289
  108.6 1.0 copy-start.1
  113.9 22.8 %all-to-all-start.3 = ((bf16[32,128,128]{2,1,0:T(8,128)(2,1)}), bf16[32,128,128]{2,1,0:T(8,128)(2,1)S(1)}, u32[]{:S(2)}, u32[]{:S(2)}) async-start(bf16[32,128,128]{2,1,0:T(8,128)(2,1)} %bitcast.17), calls=%async_computation.3 | async-start | bytes 2097152 | tf_op jit(solution)/shard_map/all_to_all | solution.py:346
  120.2 26.2 %collective-permute-start.13 = (bf16[512,512]{1,0:T(8,128)(2,1)}, bf16[512,512]{1,0:T(8,128)(2,1)}, u32[]{:S(2)}, u32[]{:S(2)}) collective-permute-start(bf16[512,512]{1,0:T(8,128)(2,1)} %collective-permute-done.12.c3_a), channel_id=1, source_target_pairs={{0,128},{128,0},{4,132},{132,4},{8,136},{136,8},{12,140},{140,12},... | collective-permute-start | bytes 1572872 | tf_op jit(solution)/shard_map/ppermute | solution.py:289
  120.7 25.7 %collective-permute-start.14 = (bf16[512,512]{1,0:T(8,128)(2,1)}, bf16[512,512]{1,0:T(8,128)(2,1)}, u32[]{:S(2)}, u32[]{:S(2)}) collective-permute-start(bf16[512,512]{1,0:T(8,128)(2,1)} %collective-permute-done.9.refs_3_), channel_id=1, source_target_pairs={{128,4},{4,128},{132,8},{8,132},{136,12},{12,136},{140,0},{0,140},... | collective-permute-start | bytes 1572872 | tf_op jit(solution)/shard_map/ppermute | solution.py:289
  136.7 16.9 %all-to-all-start.2 = ((bf16[32,64,128]{2,1,0:T(8,128)(2,1)}), bf16[32,64,128]{2,1,0:T(8,128)(2,1)}, u32[]{:S(2)}, u32[]{:S(2)}) async-start(bf16[32,64,128]{2,1,0:T(8,128)(2,1)} %bitcast.18), calls=%async_computation.2 | async-start | bytes 1048576 | tf_op jit(solution)/shard_map/all_to_all | solution.py:346
  (2 other events, 1.8 us)

commit v6 on v3

--- a/solution.py
+++ b/solution.py
@@ -19,7 +19,10 @@
 PARTS = 4
 CHUNKS = 2
 STRIP = 128
-ROOM = 20 * 2**20
+ROOM = 12 * 2**20
+WIDE = 56 * 2**20
+PICK = 44 * 2**20
+SMALL = pl.CostEstimate(flops=1, bytes_accessed=1, transcendentals=0)
 
 
 def adam_kernel(master_ref, first_ref, second_ref, gradient_ref, new_ref, *chunk_refs):
@@ -42,23 +45,24 @@
 def adam(master, first_moment, second_moment, gradient, cores):
     experts, rows, width = master.shape
     part = width // (cores * CHUNKS)
-    whole = pl.BlockSpec((1, rows, width), lambda i: (i, 0, 0))
-    block = pl.BlockSpec((cores, 1, rows, part), lambda i: (0, i, 0, 0))
+    cut = rows // 2
+    whole = pl.BlockSpec((1, cut, width), lambda i, j: (i, j, 0))
+    block = pl.BlockSpec((cores, 1, cut, part), lambda i, j: (0, i, j, 0))
     chunk = jax.ShapeDtypeStruct((cores, experts, rows, part), jnp.bfloat16)
     return pl.pallas_call(
         adam_kernel,
-        grid=(experts,),
+        grid=(experts, 2),
         in_specs=[whole] * 4,
         out_specs=[whole] + [block] * CHUNKS,
         out_shape=[jax.ShapeDtypeStruct(master.shape, jnp.float32)] + [chunk] * CHUNKS,
-        compiler_params=pltpu.CompilerParams(vmem_limit_bytes=ROOM),
+        compiler_params=pltpu.CompilerParams(vmem_limit_bytes=WIDE),
         cost_estimate=pl.CostEstimate(
             flops=16 * master.size, bytes_accessed=20 * master.size, transcendentals=master.size
         ),
     )(master, first_moment, second_moment, gradient)
 
 
-def pick_kernel(where_ref, ids_ref, low_ref, high_ref, out_ref):
+def pick_kernel(where_ref, ids_ref, low_ref, high_ref, *out_refs):
     steps, _, count = ids_ref.shape[2:]
     half = low_ref.shape[1]
     earlier = lax.broadcasted_iota(jnp.int32, (count, count), 0)
@@ -85,7 +89,7 @@
             picked = jnp.dot(chosen, ref[rows, :], preferred_element_type=jnp.float32)
             picked = picked.astype(jnp.bfloat16)
             for part in range(PARTS):
-                out_ref[part, step * CAP : (step + 1) * CAP, at : at + half] = picked[
+                out_refs[part][step * CAP : (step + 1) * CAP, at : at + half] = picked[
                     part * CAP : (part + 1) * CAP
                 ]
 
@@ -108,22 +112,22 @@
                 pl.BlockSpec((group_rows, half), lambda i, w: (i, w[0])),
                 pl.BlockSpec((group_rows, half), lambda i, w: (i, 1 - w[0])),
             ],
-            out_specs=pl.BlockSpec((PARTS, steps * CAP, depth), lambda i, w: (0, i, 0)),
-        ),
-        out_shape=jax.ShapeDtypeStruct((PARTS, groups * steps * CAP, depth), jnp.bfloat16),
-        compiler_params=pltpu.CompilerParams(vmem_limit_bytes=ROOM),
+            out_specs=[pl.BlockSpec((steps * CAP, depth), lambda i, w: (i, 0))] * PARTS,
+        ),
+        out_shape=[jax.ShapeDtypeStruct((groups * steps * CAP, depth), jnp.bfloat16)] * PARTS,
+        compiler_params=pltpu.CompilerParams(vmem_limit_bytes=PICK),
         cost_estimate=pl.CostEstimate(
             flops=8 * total * 128 * depth, bytes_accessed=4 * total * depth, transcendentals=0
         ),
     )(where, all_ids, all_tokens, all_tokens)
 
 
-def halves(picked_ref, part, even, odd):
-    half = picked_ref.shape[2] // 2
+def halves(rows_ref, even, odd):
+    half = rows_ref.shape[1] // 2
     total = None
     for at, weight in ((0, even), (half, odd)):
         if weight is not None:
-            rows = picked_ref[part, :, at : at + half]
+            rows = rows_ref[:, at : at + half]
             piece = jnp.dot(rows, weight[...], preferred_element_type=jnp.float32)
             total = piece if total is None else total + piece
     return total
@@ -140,39 +144,38 @@
             ]
 
 
-def early_kernel(picked_ref, own_a, own_b, a1_a, a1_b, c2_a, c2_b, c1_a, c1_b, out_ref):
+def early_kernel(rows_0, rows_1, own_a, own_b, a1_a, a1_b, c2_a, c2_b, c1_a, c1_b, out_ref):
     for chunk, (even, odd) in enumerate(((own_a, a1_a), (own_b, a1_b))):
-        act(out_ref, 0, chunk, halves(picked_ref, 0, even, odd))
+        act(out_ref, 0, chunk, halves(rows_0, even, odd))
     for chunk, (even, odd) in enumerate(((c2_a, c1_a), (c2_b, c1_b))):
-        act(out_ref, 1, chunk, halves(picked_ref, 1, even, odd))
-
-
-def later_kernel(picked_ref, a2_a, a2_b, a3_a, a3_b, c3_a, c3_b, out_ref, start_ref):
+        act(out_ref, 1, chunk, halves(rows_1, even, odd))
+
+
+def later_kernel(rows_2, a2_a, a2_b, a3_a, a3_b, out_ref):
     for chunk, (even, odd) in enumerate(((a2_a, a3_a), (a2_b, a3_b))):
-        act(out_ref, 0, chunk, halves(picked_ref, 2, even, odd))
+        act(out_ref, 0, chunk, halves(rows_2, even, odd))
+
+
+def begin_kernel(rows_3, c3_a, c3_b, start_ref):
     for chunk, odd in enumerate((c3_a, c3_b)):
-        start_ref[chunk] = halves(picked_ref, 3, None, odd)
-
-
-def last_kernel(picked_ref, z4_a, z4_b, acted_ref, start_ref, out_ref):
+        start_ref[chunk] = halves(rows_3, None, odd)
+
+
+def last_kernel(rows_3, z4_a, z4_b, start_ref, acted_ref, out_ref):
     out_ref[:, :, :1] = acted_ref[...]
     for chunk, even in enumerate((z4_a, z4_b)):
-        act(out_ref, 1, chunk, start_ref[chunk] + halves(picked_ref, 3, even, None))
-
-
-def run(body, operands, out_shape, flops):
+        act(out_ref, 1, chunk, start_ref[chunk] + halves(rows_3, even, None))
+
+
+def run(body, operands, out_shape):
     spec = pl.BlockSpec(memory_space=pltpu.VMEM)
     return pl.pallas_call(
         body,
         in_specs=[spec] * len(operands),
-        out_specs=jax.tree.map(lambda _: spec, out_shape),
+        out_specs=spec,
         out_shape=out_shape,
         compiler_params=pltpu.CompilerParams(vmem_limit_bytes=ROOM),
-        cost_estimate=pl.CostEstimate(
-            flops=flops,
-            bytes_accessed=sum(2 * x.size for x in operands),
-            transcendentals=0,
-        ),
+        cost_estimate=SMALL,
     )(*operands)
 
 
@@ -234,27 +237,29 @@
     )(order, ids, raw)
 
 
-def mix_kernel(first, final, place_ref, returned_ref, *refs):
+def mix_kernel(first, place_ref, *refs):
     out_ref = refs[-1]
     steps, count, _ = out_ref.shape
-    cores, devices, slots, _, rows, strip = returned_ref.shape
-    span = devices * rows
     for step in range(steps):
-        total = None
-        for slot in range(slots):
-            part = first + slot
-            arrived = jnp.concatenate(
-                [returned_ref[c, :, slot, step].reshape(span, strip) for c in range(cores)], axis=1
-            )
-            piece = jnp.dot(
-                place_ref[step, :, part * span : (part + 1) * span],
-                arrived,
-                preferred_element_type=jnp.float32,
-            )
-            total = piece if total is None else total + piece
-        total = total[:count] + total[count:]
-        if final:
-            total = total + refs[0][step]
+        part, total = first, None
+        for ref in refs[:-1]:
+            if len(ref.shape) == len(out_ref.shape):
+                total = total + ref[step]
+                continue
+            cores, devices, slots, _, rows, strip = ref.shape
+            span = devices * rows
+            for slot in range(slots):
+                arrived = jnp.concatenate(
+                    [ref[core, :, slot, step].reshape(span, strip) for core in range(cores)], axis=1
+                )
+                piece = jnp.dot(
+                    place_ref[step, :, part * span : (part + 1) * span],
+                    arrived,
+                    preferred_element_type=jnp.float32,
+                )
+                piece = piece[:count] + piece[count:]
+                total = piece if total is None else total + piece
+                part += 1
         out_ref[step] = total.astype(out_ref.dtype)
 
 
@@ -322,47 +327,38 @@
     a2_a, c2_a = swap(c1_a, 0), swap(a1_a, 1)
     a1_b, c1_b, placed = hold((a1_b, c1_b, placed))
     a2_b, c2_b = swap(c1_b, 0), swap(a1_b, 1)
-    picked = pick_rows(where, all_ids, all_tokens, steps * token_count)
+    rows = pick_rows(where, all_ids, all_tokens, steps * token_count)
     a2_a, c2_a = hold((a2_a, c2_a))
     a3_a, c3_a = swap(c2_a, 0), swap(a2_a, 1)
-    a2_b, c2_b, picked = hold((a2_b, c2_b, picked))
+    a2_b, c2_b, *rows = hold((a2_b, c2_b, *rows))
     a3_b, c3_b = swap(c2_b, 0), swap(a2_b, 1)
-    flops = 2 * picked.shape[1] * depth * width // cores
-    acted = jax.ShapeDtypeStruct((groups, quarters, 2, steps * CAP, strip), jnp.bfloat16)
+    count = groups * steps * CAP
+    double = jax.ShapeDtypeStruct((groups, quarters, 2, steps * CAP, strip), jnp.bfloat16)
     single = jax.ShapeDtypeStruct((groups, quarters, 1, steps * CAP, strip), jnp.bfloat16)
-    start = jax.ShapeDtypeStruct((CHUNKS, picked.shape[1], part), jnp.float32)
+    start = jax.ShapeDtypeStruct((CHUNKS, count, part), jnp.float32)
 
     def send_back(value):
-        value = value.reshape(groups * quarters, 2 * steps * CAP, strip)
+        slots = value.shape[2]
+        value = value.reshape(groups * quarters, slots * steps * CAP, strip)
         back = lax.all_to_all(value, ("core", "y", "x"), split_axis=0, concat_axis=0, tiled=True)
-        return back.reshape(cores, ys * quarters, 2, steps, CAP, strip)
-
-    early = run(
-        early_kernel, [picked, own_a, own_b, a1_a, a1_b, c2_a, c2_b, c1_a, c1_b], acted, 2 * flops
-    )
+        return back.reshape(cores, ys * quarters, slots, steps, CAP, strip)
+
+    early = [rows[0], rows[1], own_a, own_b, a1_a, a1_b, c2_a, c2_b, c1_a, c1_b]
+    early = run(early_kernel, early, double)
     a3_a, c3_a = hold((a3_a, c3_a))
     z4_a = swap(c3_a, 0)
     a3_b, c3_b, early = hold((a3_b, c3_b, early))
     early = send_back(early)
     z4_b = swap(a3_b, 1)
-    later, begun = run(
-        later_kernel, [picked, a2_a, a2_b, a3_a, a3_b, c3_a, c3_b], [single, start], 3 * flops // 2
-    )
+    later = run(later_kernel, [rows[2], a2_a, a2_b, a3_a, a3_b], single)
+    begun = run(begin_kernel, [rows[3], c3_a, c3_b], start)
     mixed_shape = (steps, token_count, cores * strip)
-    half_mixed = run(
-        functools.partial(mix_kernel, 0, False),
-        [placed, early],
-        jax.ShapeDtypeStruct(mixed_shape, jnp.float32),
-        2 * placed.size * cores * strip // 2,
-    )
+    half_mixed = jax.ShapeDtypeStruct(mixed_shape, jnp.float32)
+    half_mixed = run(functools.partial(mix_kernel, 0), [placed, early], half_mixed)
     z4_a, z4_b, later, begun, half_mixed = hold((z4_a, z4_b, later, begun, half_mixed))
-    final = send_back(run(last_kernel, [picked, z4_a, z4_b, later, begun], acted, flops // 2))
-    mixed = run(
-        functools.partial(mix_kernel, 2, True),
-        [placed, final, half_mixed],
-        jax.ShapeDtypeStruct(mixed_shape, jnp.bfloat16),
-        2 * placed.size * cores * strip // 2,
-    )
+    final = send_back(run(last_kernel, [rows[3], z4_a, z4_b, begun, later], double))
+    mixed = jax.ShapeDtypeStruct(mixed_shape, jnp.bfloat16)
+    mixed = run(functools.partial(mix_kernel, 2), [placed, final, half_mixed], mixed)
     return (new_master, mixed)
 
 

time: 164 us -> 161 us (0.982)
  local copies, waits for them, and re-layouts: 21.8 us -> 7.98 us
  Pallas kernels: 24.2 us -> 32.8 us
    unnamed x36 -> x28, local copies, waits for them, and re-layouts: 21.8 us -> 7.98 us
    pallas_call x6 -> x7, Pallas kernels: 14.2 us -> 20.9 us  [the longest x6 13.4 us: run(): pl.pallas_call(body, in_specs=[spec] * len(operands), out_specs=spec, out...]
    pallas_call x1, Pallas kernels: 7.2 us -> 9.09 us  [pick_rows(): pl.pallas_call(pick_kernel, grid_spec=pltpu.PrefetchScalarGridSpec(num_sc...]
  transfers between devices with their start and end apart: 22 -> 22, of which waited for: 11 -> 11; matrix products, arithmetic and copies ran while one was open for 0% -> 0% of each run, Pallas kernels for 13% -> 19%
where the time goes in v6:
time: 161 us; the launch traced here: 160 us
  starting transfers between devices  46.6 us (29%)
  waiting for transfers between devices  35.2 us (22%)
  Pallas kernels  32.8 us (20%)
  blocking collectives  22.8 us (14%)
  between operations  14.3 us (9%)
  local copies, waits for them, and re-layouts  7.98 us (5%)
    ppermute x14, starting transfers between devices, swap(): return lax.ppermute(value, ('zl', 'zh'), pairs)  24.1 us
    all_to_all x1, blocking collectives, send_back(): lax.all_to_all(value, ('core', 'y', 'x'), split_axis=0, concat_axis=0, ti...  22.8 us
    ppermute x14, waiting for transfers between devices, swap(): return lax.ppermute(value, ('zl', 'zh'), pairs)  19.9 us
    pallas_call x6, Pallas kernels, run(): pl.pallas_call(body, in_specs=[spec] * len(operands), out_specs=spec, out...  13.4 us
    all_to_all x2, starting transfers between devices, share_out(): lax.all_to_all(chunk, ('core', 'x'), split_axis=0, concat_axis=0, tiled=T...  10.2 us
    all_to_all x1, starting transfers between devices, send_back(): lax.all_to_all(value, ('core', 'y', 'x'), split_axis=0, concat_axis=0, ti...  9.15 us
    pallas_call x1, Pallas kernels, pick_rows(): pl.pallas_call(pick_kernel, grid_spec=pltpu.PrefetchScalarGridSpec(num_sc...  9.09 us
    unnamed x28, local copies, waits for them, and re-layouts  7.98 us
  transfers between devices with their start and end apart: 22, of which 11 were waited for; matrix products, arithmetic and copies ran while one was open for 0% of the time, Pallas kernels for 19%

profile of v6, /device:TPU:1, one launch (start us, length us, event | category | flops | bytes accessed | tf_op | source)
XLA Modules:
  0.0 159.7 jit_solution(14615144303552286456)
XLA Ops:
  7.9 7.5 %shard_map.86 = (f32[4,128,1024]{2,1,0:T(8,128)}, bf16[2,4,128,256]{3,2,1,0:T(8,128)(2,1)}, bf16[2,4,128,256]{3,2,1,0:T(8,128)(2,1)}) custom-call(f32[4,128,1024]{2,1,0:T(8,128)} %master_ref.1, f32[4,128,1024]{2,1,0:T(8,128)} %first_ref.1, f32[4,128,1024]{2,1,0:T(8,128)} %second_ref.1, bf16[4,128,1024]{2,1,0:T(8,128)(2,1)} %gradient_ref.1), custom_call_target="tpu_custom_call" | custom-call | flops 8388608 | bytes 10485760 | tf_op jit(solution)/shard_map/pallas_call | solution.py:52
  15.4 6.8 %all-to-all-start = ((bf16[8,128,256]{2,1,0:T(8,128)(2,1)}), bf16[8,128,256]{2,1,0:T(8,128)(2,1)S(1)}, u32[]{:S(2)}, u32[]{:S(2)}) async-start(bf16[8,128,256]{2,1,0:T(8,128)(2,1)} %bitcast.35), calls=%async_computation | async-start | bytes 1048576 | tf_op jit(solution)/shard_map/all_to_all | solution.py:312
  25.1 3.3 %collective-permute-done.5 = s32[2,8,128]{2,1,0:T(8,128)S(1)} collective-permute-done((s32[2,8,128]{2,1,0:T(8,128)S(1)}, s32[2,8,128]{2,1,0:T(8,128)S(1)}, u32[]{:S(2)}, u32[]{:S(2)}) %collective-permute-start.5) | collective-permute-done | bytes 8224 | tf_op jit(solution)/shard_map/ppermute | solution.py:280
  28.5 3.5 %all-to-all-done = bf16[8,128,256]{2,1,0:T(8,128)(2,1)S(1)} async-done(((bf16[8,128,256]{2,1,0:T(8,128)(2,1)}), bf16[8,128,256]{2,1,0:T(8,128)(2,1)S(1)}, u32[]{:S(2)}, u32[]{:S(2)}) %all-to-all-start) | async-done | bytes 524320 | tf_op jit(solution)/shard_map/all_to_all | solution.py:312
  32.0 3.4 %all-to-all-start.1 = ((bf16[8,128,256]{2,1,0:T(8,128)(2,1)}), bf16[8,128,256]{2,1,0:T(8,128)(2,1)S(1)}, u32[]{:S(2)}, u32[]{:S(2)}) async-start(bf16[8,128,256]{2,1,0:T(8,128)(2,1)} %bitcast.34), calls=%async_computation.1 | async-start | bytes 1048576 | tf_op jit(solution)/shard_map/all_to_all | solution.py:312
  36.4 4.7 %collective-permute-start.1 = (bf16[1024,256]{1,0:T(8,128)(2,1)S(1)}, bf16[1024,256]{1,0:T(8,128)(2,1)}, u32[]{:S(2)}, u32[]{:S(2)}) collective-permute-start(bf16[1024,256]{1,0:T(8,128)(2,1)S(1)} %bitcast.28), channel_id=1, source_target_pairs={{128,4},{4,128},{132,8},{8,132},{136,12},{12,136},{140,0},{0,140},... | collective-permute-start | bytes 1572872 | tf_op jit(solution)/shard_map/ppermute | solution.py:272
  41.1 4.0 %all-to-all-done.1 = bf16[8,128,256]{2,1,0:T(8,128)(2,1)S(1)} async-done(((bf16[8,128,256]{2,1,0:T(8,128)(2,1)}), bf16[8,128,256]{2,1,0:T(8,128)(2,1)S(1)}, u32[]{:S(2)}, u32[]{:S(2)}) %all-to-all-start.1) | async-done | bytes 524320 | tf_op jit(solution)/shard_map/all_to_all | solution.py:312
  46.1 4.7 %collective-permute-start.9 = (bf16[1024,256]{1,0:T(8,128)(2,1)S(1)}, bf16[1024,256]{1,0:T(8,128)(2,1)}, u32[]{:S(2)}, u32[]{:S(2)}) collective-permute-start(bf16[1024,256]{1,0:T(8,128)(2,1)S(1)} %bitcast.31), channel_id=1, source_target_pairs={{128,4},{4,128},{132,8},{8,132},{136,12},{12,136},{140,0},{0,140},... | collective-permute-start | bytes 1572872 | tf_op jit(solution)/shard_map/ppermute | solution.py:272
  51.1 2.8 %shard_map.87.place_ref = bf16[2,256,2048]{2,1,0:T(8,128)(2,1)S(1)} custom-call(s32[4]{0:T(128)S(1)} %get-tuple-element.71.order_ref, s32[2,128,8]{2,1,0:T(8,128)S(1)} %copy.9.ids_ref, f32[2,128,8]{2,1,0:T(8,128)S(1)} %copy.10.raw_ref), custom_call_target="tpu_custom_call" | custom-call | flops 402653184 | bytes 2097152 | tf_op jit(solution)/shard_map/pallas_call | solution.py:222
  55.6 4.5 %collective-permute-done.8.a1_a = bf16[1024,256]{1,0:T(8,128)(2,1)} collective-permute-done((bf16[1024,256]{1,0:T(8,128)(2,1)S(1)}, bf16[1024,256]{1,0:T(8,128)(2,1)}, u32[]{:S(2)}, u32[]{:S(2)}) %collective-permute-start.8) | collective-permute-done | bytes 524320 | tf_op jit(solution)/shard_map/ppermute | solution.py:272
  60.0 4.0 %collective-permute-done.9.c1_a = bf16[1024,256]{1,0:T(8,128)(2,1)} collective-permute-done((bf16[1024,256]{1,0:T(8,128)(2,1)S(1)}, bf16[1024,256]{1,0:T(8,128)(2,1)}, u32[]{:S(2)}, u32[]{:S(2)}) %collective-permute-start.9) | collective-permute-done | bytes 524320 | tf_op jit(solution)/shard_map/ppermute | solution.py:272
  64.0 2.4 %collective-permute-start.11 = (bf16[1024,256]{1,0:T(8,128)(2,1)}, bf16[1024,256]{1,0:T(8,128)(2,1)}, u32[]{:S(2)}, u32[]{:S(2)}) collective-permute-start(bf16[1024,256]{1,0:T(8,128)(2,1)} %collective-permute-done.8.a1_a), channel_id=1, source_target_pairs={{128,4},{4,128},{132,8},{8,132},{136,12},{12,136},{140,0},{0,140},... | collective-permute-start | bytes 1572872 | tf_op jit(solution)/shard_map/ppermute | solution.py:272
  66.4 9.1 %shard_map.88 = (bf16[512,2048]{1,0:T(8,128)(2,1)S(1)}, bf16[512,2048]{1,0:T(8,128)(2,1)S(1)}, bf16[512,2048]{1,0:T(8,128)(2,1)S(1)}, bf16[512,2048]{1,0:T(8,128)(2,1)S(1)}) custom-call(s32[7]{0:T(128)S(1)} %pad_add_fusion.2.where_ref, s32[2,4,2,8,128]{4,3,2,1,0:T(8,128)S(1)} %pad_add_fusion.ids_ref, ...), custom_call_target="tpu_custom_call" | custom-call | flops 4294967296 | bytes 16777216 | tf_op jit(solution)/shard_map/pallas_call | solution.py:102
  76.9 3.0 %collective-permute-start.16 = (bf16[1024,256]{1,0:T(8,128)(2,1)}, bf16[1024,256]{1,0:T(8,128)(2,1)S(1)}, u32[]{:S(2)}, u32[]{:S(2)}) collective-permute-start(bf16[1024,256]{1,0:T(8,128)(2,1)} %collective-permute-done.2.a2_b), channel_id=1, source_target_pairs={{128,4},{4,128},{132,8},{8,132},{136,12},{12,136},{140,0},{0,140},... | collective-permute-start | bytes 1572872 | tf_op jit(solution)/shard_map/ppermute | solution.py:272
  79.9 2.6 %collective-permute-done.10.a2_a = bf16[1024,256]{1,0:T(8,128)(2,1)} collective-permute-done((bf16[1024,256]{1,0:T(8,128)(2,1)}, bf16[1024,256]{1,0:T(8,128)(2,1)}, u32[]{:S(2)}, u32[]{:S(2)}) %collective-permute-start.10) | collective-permute-done | bytes 524320 | tf_op jit(solution)/shard_map/ppermute | solution.py:272
  82.5 4.0 %collective-permute-done.11.c2_a = bf16[1024,256]{1,0:T(8,128)(2,1)} collective-permute-done((bf16[1024,256]{1,0:T(8,128)(2,1)}, bf16[1024,256]{1,0:T(8,128)(2,1)}, u32[]{:S(2)}, u32[]{:S(2)}) %collective-permute-start.11) | collective-permute-done | bytes 524320 | tf_op jit(solution)/shard_map/ppermute | solution.py:272
  86.5 2.4 %collective-permute-start.13 = (bf16[1024,256]{1,0:T(8,128)(2,1)}, bf16[1024,256]{1,0:T(8,128)(2,1)}, u32[]{:S(2)}, u32[]{:S(2)}) collective-permute-start(bf16[1024,256]{1,0:T(8,128)(2,1)} %collective-permute-done.10.a2_a), channel_id=1, source_target_pairs={{128,4},{4,128},{132,8},{8,132},{136,12},{12,136},{140,0},{0,140},... | collective-permute-start | bytes 1572872 | tf_op jit(solution)/shard_map/ppermute | solution.py:272
  88.8 5.2 %shard_map.89 = bf16[8,4,2,64,128]{4,3,2,1,0:T(8,128)(2,1)} custom-call(bf16[512,2048]{1,0:T(8,128)(2,1)S(1)} %get-tuple-element.58.rows_0, bf16[512,2048]{1,0:T(8,128)(2,1)S(1)} %get-tuple-element.59.rows_1, bf16[1024,256]{1,0:T(8,128)(2,1)S(1)} %bitcast.32, bf16[1024,256]{1,0:T(8,128)(2,1)S(1)} %bitcast.29, bf16[1024,256]{1,0:T(8,128)(2,1)} %collective-permute-done.8.a1_a, ...), custom_call_target="tpu_custom_call" | custom-call | flops 1 | bytes 1 | tf_op jit(solution)/shard_map/pallas_call | solution.py:172
  94.1 3.6 %collective-permute-done.16.c3_b = bf16[1024,256]{1,0:T(8,128)(2,1)S(1)} collective-permute-done((bf16[1024,256]{1,0:T(8,128)(2,1)}, bf16[1024,256]{1,0:T(8,128)(2,1)S(1)}, u32[]{:S(2)}, u32[]{:S(2)}) %collective-permute-start.16) | collective-permute-done | bytes 524320 | tf_op jit(solution)/shard_map/ppermute | solution.py:272
  98.4 9.1 %all-to-all-start.2 = ((bf16[32,128,128]{2,1,0:T(8,128)(2,1)}), bf16[32,128,128]{2,1,0:T(8,128)(2,1)S(1)}, u32[]{:S(2)}, u32[]{:S(2)}) async-start(bf16[32,128,128]{2,1,0:T(8,128)(2,1)} %bitcast.19), calls=%async_computation.2 | async-start | bytes 2097152 | tf_op jit(solution)/shard_map/all_to_all | solution.py:343
  109.0 2.4 %collective-permute-start.17 = (bf16[1024,256]{1,0:T(8,128)(2,1)}, bf16[1024,256]{1,0:T(8,128)(2,1)}, u32[]{:S(2)}, u32[]{:S(2)}) collective-permute-start(bf16[1024,256]{1,0:T(8,128)(2,1)} %collective-permute-done.15.a3_b), channel_id=1, source_target_pairs={{128,4},{4,128},{132,8},{8,132},{136,12},{12,136},{140,0},{0,140},... | collective-permute-start | bytes 1572872 | tf_op jit(solution)/shard_map/ppermute | solution.py:272
  116.8 2.8 %shard_map.90.acted_ref = bf16[8,4,1,64,128]{4,3,2,1,0:T(8,128)(2,1)S(1)} custom-call(bf16[512,2048]{1,0:T(8,128)(2,1)S(1)} %copy-done.6, bf16[1024,256]{1,0:T(8,128)(2,1)} %collective-permute-done.10.a2_a, bf16[1024,256]{1,0:T(8,128)(2,1)} %collective-permute-done.2.a2_b, bf16[1024,256]{1,0:T(8,128)(2,1)} %collective-permute-done.12.a3_a, ...), custom_call_target="tpu_custom_call" | custom-call | flops 1 | bytes 1 | tf_op jit(solution)/shard_map/pallas_call | solution.py:172
  120.5 3.6 %all-to-all-done.2 = bf16[32,128,128]{2,1,0:T(8,128)(2,1)S(1)} async-done(((bf16[32,128,128]{2,1,0:T(8,128)(2,1)}), bf16[32,128,128]{2,1,0:T(8,128)(2,1)S(1)}, u32[]{:S(2)}, u32[]{:S(2)}) %all-to-all-start.2) | async-done | bytes 1048608 | tf_op jit(solution)/shard_map/all_to_all | solution.py:343
  129.0 22.8 %all_to_all.20 = bf16[32,128,128]{2,1,0:T(8,128)(2,1)S(1)} all-to-all(bf16[32,128,128]{2,1,0:T(8,128)(2,1)S(1)} %bitcast.26), channel_id=1, replica_groups=mesh['zl'=2,'core'=2,'y'=4,'zh'=4,'x'=4] {'core','y','x'}, dimensions={0} | all-to-all | bytes 2097152 | tf_op jit(solution)/shard_map/all_to_all | solution.py:343
  (63 shorter events, 23.5 us)
Async XLA Ops:
  7.2 59.2 %all-gather.2.cloned.1.call-start = ((), (), s32[]{:S(2)}) async-start(), calls=%async_computation.4 | async-start | bytes 9437184 | tf_op jit(solution)/shard_map/all_gather | solution.py:294
  15.4 35.5 %copy-start.12 = (f32[2,128,8]{1,2,0:T(8,128)S(1)}, f32[2,128,8]{1,2,0:T(8,128)}, u32[]{:S(2)}) copy-start(f32[2,128,8]{1,2,0:T(8,128)} %param.13) | copy-start | bytes 24580
  15.4 16.6 %all-to-all-start = ((bf16[8,128,256]{2,1,0:T(8,128)(2,1)}), bf16[8,128,256]{2,1,0:T(8,128)(2,1)S(1)}, u32[]{:S(2)}, u32[]{:S(2)}) async-start(bf16[8,128,256]{2,1,0:T(8,128)(2,1)} %bitcast.35), calls=%async_computation | async-start | bytes 1048576 | tf_op jit(solution)/shard_map/all_to_all | solution.py:312
  22.2 2.9 %collective-permute-start.4 = (s32[2,8,128]{2,1,0:T(8,128)S(1)}, s32[2,8,128]{2,1,0:T(8,128)S(1)}, u32[]{:S(2)}, u32[]{:S(2)}) collective-permute-start(s32[2,8,128]{2,1,0:T(8,128)S(1)} %bitcast.38), channel_id=1, source_target_pairs={{16,0},{32,16},{48,32},{0,48},{17,1},{33,17},{49,33},{1,49},{18,2}... | collective-permute-start | bytes 24584 | tf_op jit(solution)/shard_map/ppermute | solution.py:280
  24.1 4.3 %collective-permute-start.5 = (s32[2,8,128]{2,1,0:T(8,128)S(1)}, s32[2,8,128]{2,1,0:T(8,128)S(1)}, u32[]{:S(2)}, u32[]{:S(2)}) collective-permute-start(s32[2,8,128]{2,1,0:T(8,128)S(1)} %bitcast.39), channel_id=1, source_target_pairs={{32,0},{48,16},{0,32},{16,48},{33,1},{49,17},{1,33},{17,49},{34,2}... | collective-permute-start | bytes 24584 | tf_op jit(solution)/shard_map/ppermute | solution.py:280
  24.4 4.1 %collective-permute-start.6 = (s32[2,8,128]{2,1,0:T(8,128)S(1)}, s32[2,8,128]{2,1,0:T(8,128)S(1)}, u32[]{:S(2)}, u32[]{:S(2)}) collective-permute-start(s32[2,8,128]{2,1,0:T(8,128)S(1)} %bitcast.40), channel_id=1, source_target_pairs={{48,0},{0,16},{16,32},{32,48},{49,1},{1,17},{17,33},{33,49},{50,2}... | collective-permute-start | bytes 24584 | tf_op jit(solution)/shard_map/ppermute | solution.py:280
  32.0 13.2 %all-to-all-start.1 = ((bf16[8,128,256]{2,1,0:T(8,128)(2,1)}), bf16[8,128,256]{2,1,0:T(8,128)(2,1)S(1)}, u32[]{:S(2)}, u32[]{:S(2)}) async-start(bf16[8,128,256]{2,1,0:T(8,128)(2,1)} %bitcast.34), calls=%async_computation.1 | async-start | bytes 1048576 | tf_op jit(solution)/shard_map/all_to_all | solution.py:312
  35.4 5.6 %collective-permute-start.7 = (s32[4,2,8,128]{3,2,1,0:T(8,128)S(1)}, s32[4,2,8,128]{3,2,1,0:T(8,128)S(1)}, u32[]{:S(2)}, u32[]{:S(2)}) collective-permute-start(s32[4,2,8,128]{3,2,1,0:T(8,128)S(1)} %pad_add_fusion.1), channel_id=1, source_target_pairs={{0,64},{64,0},{1,65},{65,1},{2,66},{66,2},{3,67},{67,3},{4,68},{68... | collective-permute-start | bytes 98312 | tf_op jit(solution)/shard_map/ppermute | solution.py:318
  35.5 18.4 %collective-permute-start = (bf16[1024,256]{1,0:T(8,128)(2,1)S(1)}, bf16[1024,256]{1,0:T(8,128)(2,1)}, u32[]{:S(2)}, u32[]{:S(2)}) collective-permute-start(bf16[1024,256]{1,0:T(8,128)(2,1)S(1)} %bitcast.27), channel_id=1, source_target_pairs={{0,128},{128,0},{4,132},{132,4},{8,136},{136,8},{12,140},{140,12},... | collective-permute-start | bytes 1572872 | tf_op jit(solution)/shard_map/ppermute | solution.py:272
  36.4 17.6 %collective-permute-start.1 = (bf16[1024,256]{1,0:T(8,128)(2,1)S(1)}, bf16[1024,256]{1,0:T(8,128)(2,1)}, u32[]{:S(2)}, u32[]{:S(2)}) collective-permute-start(bf16[1024,256]{1,0:T(8,128)(2,1)S(1)} %bitcast.28), channel_id=1, source_target_pairs={{128,4},{4,128},{132,8},{8,132},{136,12},{12,136},{140,0},{0,140},... | collective-permute-start | bytes 1572872 | tf_op jit(solution)/shard_map/ppermute | solution.py:272
  45.1 14.9 %collective-permute-start.8 = (bf16[1024,256]{1,0:T(8,128)(2,1)S(1)}, bf16[1024,256]{1,0:T(8,128)(2,1)}, u32[]{:S(2)}, u32[]{:S(2)}) collective-permute-start(bf16[1024,256]{1,0:T(8,128)(2,1)S(1)} %bitcast.30), channel_id=1, source_target_pairs={{0,128},{128,0},{4,132},{132,4},{8,136},{136,8},{12,140},{140,12},... | collective-permute-start | bytes 1572872 | tf_op jit(solution)/shard_map/ppermute | solution.py:272
  46.1 17.9 %collective-permute-start.9 = (bf16[1024,256]{1,0:T(8,128)(2,1)S(1)}, bf16[1024,256]{1,0:T(8,128)(2,1)}, u32[]{:S(2)}, u32[]{:S(2)}) collective-permute-start(bf16[1024,256]{1,0:T(8,128)(2,1)S(1)} %bitcast.31), channel_id=1, source_target_pairs={{128,4},{4,128},{132,8},{8,132},{136,12},{12,136},{140,0},{0,140},... | collective-permute-start | bytes 1572872 | tf_op jit(solution)/shard_map/ppermute | solution.py:272
  53.9 21.6 %collective-permute-start.2 = (bf16[1024,256]{1,0:T(8,128)(2,1)}, bf16[1024,256]{1,0:T(8,128)(2,1)}, u32[]{:S(2)}, u32[]{:S(2)}) collective-permute-start(bf16[1024,256]{1,0:T(8,128)(2,1)} %collective-permute-done.1.c1_b), channel_id=1, source_target_pairs={{0,128},{128,0},{4,132},{132,4},{8,136},{136,8},{12,140},{140,12},... | collective-permute-start | bytes 1572872 | tf_op jit(solution)/shard_map/ppermute | solution.py:272
  54.1 21.5 %collective-permute-start.3 = (bf16[1024,256]{1,0:T(8,128)(2,1)}, bf16[1024,256]{1,0:T(8,128)(2,1)}, u32[]{:S(2)}, u32[]{:S(2)}) collective-permute-start(bf16[1024,256]{1,0:T(8,128)(2,1)} %collective-permute-done.a1_b), channel_id=1, source_target_pairs={{128,4},{4,128},{132,8},{8,132},{136,12},{12,136},{140,0},{0,140},... | collective-permute-start | bytes 1572872 | tf_op jit(solution)/shard_map/ppermute | solution.py:272
  64.0 18.5 %collective-permute-start.10 = (bf16[1024,256]{1,0:T(8,128)(2,1)}, bf16[1024,256]{1,0:T(8,128)(2,1)}, u32[]{:S(2)}, u32[]{:S(2)}) collective-permute-start(bf16[1024,256]{1,0:T(8,128)(2,1)} %collective-permute-done.9.c1_a), channel_id=1, source_target_pairs={{0,128},{128,0},{4,132},{132,4},{8,136},{136,8},{12,140},{140,12},... | collective-permute-start | bytes 1572872 | tf_op jit(solution)/shard_map/ppermute | solution.py:272
  64.0 22.5 %collective-permute-start.11 = (bf16[1024,256]{1,0:T(8,128)(2,1)}, bf16[1024,256]{1,0:T(8,128)(2,1)}, u32[]{:S(2)}, u32[]{:S(2)}) collective-permute-start(bf16[1024,256]{1,0:T(8,128)(2,1)} %collective-permute-done.8.a1_a), channel_id=1, source_target_pairs={{128,4},{4,128},{132,8},{8,132},{136,12},{12,136},{140,0},{0,140},... | collective-permute-start | bytes 1572872 | tf_op jit(solution)/shard_map/ppermute | solution.py:272
  75.5 18.5 %copy-start = (bf16[512,2048]{1,0:T(8,128)(2,1)}, bf16[512,2048]{1,0:T(8,128)(2,1)S(1)}, u32[]{:S(2)}) copy-start(bf16[512,2048]{1,0:T(8,128)(2,1)S(1)} %get-tuple-element.49.rows_3) | copy-start | bytes 6291460
  75.6 18.5 %collective-permute-start.15 = (bf16[1024,256]{1,0:T(8,128)(2,1)}, bf16[1024,256]{1,0:T(8,128)(2,1)}, u32[]{:S(2)}, u32[]{:S(2)}) collective-permute-start(bf16[1024,256]{1,0:T(8,128)(2,1)} %collective-permute-done.3.c2_b), channel_id=1, source_target_pairs={{0,128},{128,0},{4,132},{132,4},{8,136},{136,8},{12,140},{140,12},... | collective-permute-start | bytes 1572872 | tf_op jit(solution)/shard_map/ppermute | solution.py:272
  76.9 20.7 %collective-permute-start.16 = (bf16[1024,256]{1,0:T(8,128)(2,1)}, bf16[1024,256]{1,0:T(8,128)(2,1)S(1)}, u32[]{:S(2)}, u32[]{:S(2)}) collective-permute-start(bf16[1024,256]{1,0:T(8,128)(2,1)} %collective-permute-done.2.a2_b), channel_id=1, source_target_pairs={{128,4},{4,128},{132,8},{8,132},{136,12},{12,136},{140,0},{0,140},... | collective-permute-start | bytes 1572872 | tf_op jit(solution)/shard_map/ppermute | solution.py:272
  86.5 21.1 %collective-permute-start.12 = (bf16[1024,256]{1,0:T(8,128)(2,1)}, bf16[1024,256]{1,0:T(8,128)(2,1)}, u32[]{:S(2)}, u32[]{:S(2)}) collective-permute-start(bf16[1024,256]{1,0:T(8,128)(2,1)} %collective-permute-done.11.c2_a), channel_id=1, source_target_pairs={{0,128},{128,0},{4,132},{132,4},{8,136},{136,8},{12,140},{140,12},... | collective-permute-start | bytes 1572872 | tf_op jit(solution)/shard_map/ppermute | solution.py:272
  86.5 22.5 %collective-permute-start.13 = (bf16[1024,256]{1,0:T(8,128)(2,1)}, bf16[1024,256]{1,0:T(8,128)(2,1)}, u32[]{:S(2)}, u32[]{:S(2)}) collective-permute-start(bf16[1024,256]{1,0:T(8,128)(2,1)} %collective-permute-done.10.a2_a), channel_id=1, source_target_pairs={{128,4},{4,128},{132,8},{8,132},{136,12},{12,136},{140,0},{0,140},... | collective-permute-start | bytes 1572872 | tf_op jit(solution)/shard_map/ppermute | solution.py:272
  98.4 25.7 %all-to-all-start.2 = ((bf16[32,128,128]{2,1,0:T(8,128)(2,1)}), bf16[32,128,128]{2,1,0:T(8,128)(2,1)S(1)}, u32[]{:S(2)}, u32[]{:S(2)}) async-start(bf16[32,128,128]{2,1,0:T(8,128)(2,1)} %bitcast.19), calls=%async_computation.2 | async-start | bytes 2097152 | tf_op jit(solution)/shard_map/all_to_all | solution.py:343
  108.9 15.6 %collective-permute-start.14 = (bf16[1024,256]{1,0:T(8,128)(2,1)}, bf16[1024,256]{1,0:T(8,128)(2,1)}, u32[]{:S(2)}, u32[]{:S(2)}) collective-permute-start(bf16[1024,256]{1,0:T(8,128)(2,1)} %collective-permute-done.13.c3_a), channel_id=1, source_target_pairs={{0,128},{128,0},{4,132},{132,4},{8,136},{136,8},{12,140},{140,12},... | collective-permute-start | bytes 1572872 | tf_op jit(solution)/shard_map/ppermute | solution.py:272
  109.0 15.6 %collective-permute-start.17 = (bf16[1024,256]{1,0:T(8,128)(2,1)}, bf16[1024,256]{1,0:T(8,128)(2,1)}, u32[]{:S(2)}, u32[]{:S(2)}) collective-permute-start(bf16[1024,256]{1,0:T(8,128)(2,1)} %collective-permute-done.15.a3_b), channel_id=1, source_target_pairs={{128,4},{4,128},{132,8},{8,132},{136,12},{12,136},{140,0},{0,140},... | collective-permute-start | bytes 1572872 | tf_op jit(solution)/shard_map/ppermute | solution.py:272
  (11 other events, 45.5 us)
Sparse Core Ops, SparseCore 0:
  9.9 56.5 all-gather.1

commit v7 on v6

--- a/solution.py
+++ b/solution.py
@@ -45,13 +45,13 @@
 def adam(master, first_moment, second_moment, gradient, cores):
     experts, rows, width = master.shape
     part = width // (cores * CHUNKS)
-    cut = rows // 2
+    cut = rows
     whole = pl.BlockSpec((1, cut, width), lambda i, j: (i, j, 0))
     block = pl.BlockSpec((cores, 1, cut, part), lambda i, j: (0, i, j, 0))
     chunk = jax.ShapeDtypeStruct((cores, experts, rows, part), jnp.bfloat16)
     return pl.pallas_call(
         adam_kernel,
-        grid=(experts, 2),
+        grid=(experts, 1),
         in_specs=[whole] * 4,
         out_specs=[whole] + [block] * CHUNKS,
         out_shape=[jax.ShapeDtypeStruct(master.shape, jnp.float32)] + [chunk] * CHUNKS,
@@ -347,7 +347,7 @@
     early = run(early_kernel, early, double)
     a3_a, c3_a = hold((a3_a, c3_a))
     z4_a = swap(c3_a, 0)
-    a3_b, c3_b, early = hold((a3_b, c3_b, early))
+    a3_b, c3_b, acted = hold((a3_b, c3_b, early))
     early = send_back(early)
     z4_b = swap(a3_b, 1)
     later = run(later_kernel, [rows[2], a2_a, a2_b, a3_a, a3_b], single)
@@ -355,7 +355,7 @@
     mixed_shape = (steps, token_count, cores * strip)
     half_mixed = jax.ShapeDtypeStruct(mixed_shape, jnp.float32)
     half_mixed = run(functools.partial(mix_kernel, 0), [placed, early], half_mixed)
-    z4_a, z4_b, later, begun, half_mixed = hold((z4_a, z4_b, later, begun, half_mixed))
+    z4_a, z4_b, later, begun = hold((z4_a, z4_b, later, begun))
     final = send_back(run(last_kernel, [rows[3], z4_a, z4_b, begun, later], double))
     mixed = jax.ShapeDtypeStruct(mixed_shape, jnp.bfloat16)
     mixed = run(functools.partial(mix_kernel, 2), [placed, final, half_mixed], mixed)

time: 161 us -> 162 us (level)
  blocking collectives: 22.8 us -> 0 us
  waiting for transfers between devices: 35.2 us -> 54.6 us
  starting transfers between devices: 46.6 us -> 55.5 us
  Pallas kernels: 32.8 us -> 30.1 us
  local copies, waits for them, and re-layouts: 7.98 us -> 6.35 us
    all_to_all x1 -> x0, blocking collectives: 22.8 us -> none  [send_back(): lax.all_to_all(value, ('core', 'y', 'x'), split_axis=0, concat_axis=0, ti...]
    all_to_all x1 -> x2, waiting for transfers between devices: 3.63 us -> 14.9 us  [send_back(): lax.all_to_all(value, ('core', 'y', 'x'), split_axis=0, concat_axis=0, ti...]
    all_to_all x1 -> x2, starting transfers between devices: 9.15 us -> 17.1 us  [send_back(): lax.all_to_all(value, ('core', 'y', 'x'), split_axis=0, concat_axis=0, ti...]
    ppermute x14, waiting for transfers between devices: 19.9 us -> 26 us  [swap(): return lax.ppermute(value, ('zl', 'zh'), pairs)]
    all_to_all x2, waiting for transfers between devices: 7.52 us -> 13 us  [share_out(): lax.all_to_all(chunk, ('core', 'x'), split_axis=0, concat_axis=0, tiled=T...]
    ppermute x3, waiting for transfers between devices: 3.36 us -> 0.01 us  [along_y(): lax.ppermute(own, 'y', [((at + away) % size, at) for at in range(size)])]
    ppermute x3, starting transfers between devices: 2.94 us -> 4.68 us  [along_y(): lax.ppermute(own, 'y', [((at + away) % size, at) for at in range(size)])]
    pallas_call x1, Pallas kernels: 7.5 us -> 5.77 us  [adam(): pl.pallas_call(adam_kernel, grid=(experts, 1), in_specs=[whole] * 4, out_...]
  transfers between devices with their start and end apart: 22 -> 23, of which waited for: 11 -> 11; matrix products, arithmetic and copies ran while one was open for 0% -> 0% of each run, Pallas kernels for 19% -> 18%
where the time goes in v7:
time: 162 us; the launch traced here: 161 us
  starting transfers between devices  55.5 us (34%)
  waiting for transfers between devices  54.6 us (34%)
  Pallas kernels  30.1 us (19%)
  between operations  14.3 us (9%)
  local copies, waits for them, and re-layouts  6.35 us (4%)
    ppermute x14, waiting for transfers between devices, swap(): return lax.ppermute(value, ('zl', 'zh'), pairs)  26 us
    ppermute x14, starting transfers between devices, swap(): return lax.ppermute(value, ('zl', 'zh'), pairs)  24.5 us
    all_to_all x2, starting transfers between devices, send_back(): lax.all_to_all(value, ('core', 'y', 'x'), split_axis=0, concat_axis=0, ti...  17.1 us
    all_to_all x2, waiting for transfers between devices, send_back(): lax.all_to_all(value, ('core', 'y', 'x'), split_axis=0, concat_axis=0, ti...  14.9 us
    all_to_all x2, waiting for transfers between devices, share_out(): lax.all_to_all(chunk, ('core', 'x'), split_axis=0, concat_axis=0, tiled=T...  13 us
    pallas_call x6, Pallas kernels, run(): pl.pallas_call(body, in_specs=[spec] * len(operands), out_specs=spec, out...  12.4 us
    all_to_all x2, starting transfers between devices, share_out(): lax.all_to_all(chunk, ('core', 'x'), split_axis=0, concat_axis=0, tiled=T...  9.27 us
    pallas_call x1, Pallas kernels, pick_rows(): pl.pallas_call(pick_kernel, grid_spec=pltpu.PrefetchScalarGridSpec(num_sc...  9.1 us
  transfers between devices with their start and end apart: 23, of which 11 were waited for; matrix products, arithmetic and copies ran while one was open for 0% of the time, Pallas kernels for 18%

profile of v7, /device:TPU:1, one launch (start us, length us, event | category | flops | bytes accessed | tf_op | source)
XLA Modules:
  0.0 161.0 jit_solution(12985025073671144871)
XLA Ops:
  7.9 3.6 %collective-permute-start.4 = (s32[2,8,128]{2,1,0:T(8,128)}, s32[2,8,128]{2,1,0:T(8,128)S(1)}, u32[]{:S(2)}, u32[]{:S(2)}) collective-permute-start(s32[2,8,128]{2,1,0:T(8,128)} %bitcast.38), channel_id=1, source_target_pairs={{16,0},{32,16},{48,32},{0,48},{17,1},{33,17},{49,33},{1,49},{18,2}... | collective-permute-start | bytes 24584 | tf_op jit(solution)/shard_map/ppermute | solution.py:280
  12.6 5.8 %shard_map.86 = (f32[4,128,1024]{2,1,0:T(8,128)}, bf16[2,4,128,256]{3,2,1,0:T(8,128)(2,1)}, bf16[2,4,128,256]{3,2,1,0:T(8,128)(2,1)}) custom-call(f32[4,128,1024]{2,1,0:T(8,128)} %master_ref.1, f32[4,128,1024]{2,1,0:T(8,128)} %first_ref.1, f32[4,128,1024]{2,1,0:T(8,128)} %second_ref.1, bf16[4,128,1024]{2,1,0:T(8,128)(2,1)} %gradient_ref.1), custom_call_target="tpu_custom_call" | custom-call | flops 8388608 | bytes 10485760 | tf_op jit(solution)/shard_map/pallas_call | solution.py:52
  18.4 5.8 %all-to-all-start.1 = ((bf16[8,128,256]{2,1,0:T(8,128)(2,1)}), bf16[8,128,256]{2,1,0:T(8,128)(2,1)S(1)}, u32[]{:S(2)}, u32[]{:S(2)}) async-start(bf16[8,128,256]{2,1,0:T(8,128)(2,1)} %bitcast.35), calls=%async_computation.1 | async-start | bytes 1048576 | tf_op jit(solution)/shard_map/all_to_all | solution.py:312
  24.2 9.8 %all-to-all-done.1 = bf16[8,128,256]{2,1,0:T(8,128)(2,1)S(1)} async-done(((bf16[8,128,256]{2,1,0:T(8,128)(2,1)}), bf16[8,128,256]{2,1,0:T(8,128)(2,1)S(1)}, u32[]{:S(2)}, u32[]{:S(2)}) %all-to-all-start.1) | async-done | bytes 524320 | tf_op jit(solution)/shard_map/all_to_all | solution.py:312
  34.0 3.4 %all-to-all-start = ((bf16[8,128,256]{2,1,0:T(8,128)(2,1)}), bf16[8,128,256]{2,1,0:T(8,128)(2,1)S(1)}, u32[]{:S(2)}, u32[]{:S(2)}) async-start(bf16[8,128,256]{2,1,0:T(8,128)(2,1)} %bitcast.34), calls=%async_computation | async-start | bytes 1048576 | tf_op jit(solution)/shard_map/all_to_all | solution.py:312
  39.2 4.7 %collective-permute-start.9 = (bf16[1024,256]{1,0:T(8,128)(2,1)S(1)}, bf16[1024,256]{1,0:T(8,128)(2,1)}, u32[]{:S(2)}, u32[]{:S(2)}) collective-permute-start(bf16[1024,256]{1,0:T(8,128)(2,1)S(1)} %bitcast.28), channel_id=1, source_target_pairs={{128,4},{4,128},{132,8},{8,132},{136,12},{12,136},{140,0},{0,140},... | collective-permute-start | bytes 1572872 | tf_op jit(solution)/shard_map/ppermute | solution.py:272
  43.9 3.3 %all-to-all-done = bf16[8,128,256]{2,1,0:T(8,128)(2,1)S(1)} async-done(((bf16[8,128,256]{2,1,0:T(8,128)(2,1)}), bf16[8,128,256]{2,1,0:T(8,128)(2,1)S(1)}, u32[]{:S(2)}, u32[]{:S(2)}) %all-to-all-start) | async-done | bytes 524320 | tf_op jit(solution)/shard_map/all_to_all | solution.py:312
  48.8 4.7 %collective-permute-start.1 = (bf16[1024,256]{1,0:T(8,128)(2,1)S(1)}, bf16[1024,256]{1,0:T(8,128)(2,1)}, u32[]{:S(2)}, u32[]{:S(2)}) collective-permute-start(bf16[1024,256]{1,0:T(8,128)(2,1)S(1)} %bitcast.31), channel_id=1, source_target_pairs={{128,4},{4,128},{132,8},{8,132},{136,12},{12,136},{140,0},{0,140},... | collective-permute-start | bytes 1572872 | tf_op jit(solution)/shard_map/ppermute | solution.py:272
  53.5 2.6 %collective-permute-done.9.c1_a = bf16[1024,256]{1,0:T(8,128)(2,1)} collective-permute-done((bf16[1024,256]{1,0:T(8,128)(2,1)S(1)}, bf16[1024,256]{1,0:T(8,128)(2,1)}, u32[]{:S(2)}, u32[]{:S(2)}) %collective-permute-start.9) | collective-permute-done | bytes 524320 | tf_op jit(solution)/shard_map/ppermute | solution.py:272
  56.1 2.4 %collective-permute-start.11 = (bf16[1024,256]{1,0:T(8,128)(2,1)}, bf16[1024,256]{1,0:T(8,128)(2,1)}, u32[]{:S(2)}, u32[]{:S(2)}) collective-permute-start(bf16[1024,256]{1,0:T(8,128)(2,1)} %collective-permute-done.8.a1_a), channel_id=1, source_target_pairs={{128,4},{4,128},{132,8},{8,132},{136,12},{12,136},{140,0},{0,140},... | collective-permute-start | bytes 1572872 | tf_op jit(solution)/shard_map/ppermute | solution.py:272
  58.8 2.8 %shard_map.87.place_ref = bf16[2,256,2048]{2,1,0:T(8,128)(2,1)S(1)} custom-call(s32[4]{0:T(128)S(1)} %get-tuple-element.67.order_ref, s32[2,128,8]{2,1,0:T(8,128)S(1)} %copy.9.ids_ref, f32[2,128,8]{2,1,0:T(8,128)S(1)} %copy.10.raw_ref), custom_call_target="tpu_custom_call" | custom-call | flops 402653184 | bytes 2097152 | tf_op jit(solution)/shard_map/pallas_call | solution.py:222
  62.7 4.6 %collective-permute-done.1.c1_b = bf16[1024,256]{1,0:T(8,128)(2,1)} collective-permute-done((bf16[1024,256]{1,0:T(8,128)(2,1)S(1)}, bf16[1024,256]{1,0:T(8,128)(2,1)}, u32[]{:S(2)}, u32[]{:S(2)}) %collective-permute-start.1) | collective-permute-done | bytes 524320 | tf_op jit(solution)/shard_map/ppermute | solution.py:272
  67.3 2.4 %collective-permute-start.3 = (bf16[1024,256]{1,0:T(8,128)(2,1)}, bf16[1024,256]{1,0:T(8,128)(2,1)}, u32[]{:S(2)}, u32[]{:S(2)}) collective-permute-start(bf16[1024,256]{1,0:T(8,128)(2,1)} %collective-permute-done.a1_b), channel_id=1, source_target_pairs={{128,4},{4,128},{132,8},{8,132},{136,12},{12,136},{140,0},{0,140},... | collective-permute-start | bytes 1572872 | tf_op jit(solution)/shard_map/ppermute | solution.py:272
  69.7 4.2 %collective-permute-done.10.a2_a = bf16[1024,256]{1,0:T(8,128)(2,1)} collective-permute-done((bf16[1024,256]{1,0:T(8,128)(2,1)}, bf16[1024,256]{1,0:T(8,128)(2,1)}, u32[]{:S(2)}, u32[]{:S(2)}) %collective-permute-start.10) | collective-permute-done | bytes 524320 | tf_op jit(solution)/shard_map/ppermute | solution.py:272
  74.0 4.6 %collective-permute-done.11.c2_a = bf16[1024,256]{1,0:T(8,128)(2,1)} collective-permute-done((bf16[1024,256]{1,0:T(8,128)(2,1)}, bf16[1024,256]{1,0:T(8,128)(2,1)}, u32[]{:S(2)}, u32[]{:S(2)}) %collective-permute-start.11) | collective-permute-done | bytes 524320 | tf_op jit(solution)/shard_map/ppermute | solution.py:272
  78.5 2.4 %collective-permute-start.13 = (bf16[1024,256]{1,0:T(8,128)(2,1)}, bf16[1024,256]{1,0:T(8,128)(2,1)}, u32[]{:S(2)}, u32[]{:S(2)}) collective-permute-start(bf16[1024,256]{1,0:T(8,128)(2,1)} %collective-permute-done.10.a2_a), channel_id=1, source_target_pairs={{128,4},{4,128},{132,8},{8,132},{136,12},{12,136},{140,0},{0,140},... | collective-permute-start | bytes 1572872 | tf_op jit(solution)/shard_map/ppermute | solution.py:272
  80.9 9.1 %shard_map.88 = (bf16[512,2048]{1,0:T(8,128)(2,1)S(1)}, bf16[512,2048]{1,0:T(8,128)(2,1)S(1)}, bf16[512,2048]{1,0:T(8,128)(2,1)S(1)}, bf16[512,2048]{1,0:T(8,128)(2,1)S(1)}) custom-call(s32[7]{0:T(128)S(1)} %pad_add_fusion.2.where_ref, s32[2,4,2,8,128]{4,3,2,1,0:T(8,128)S(1)} %pad_add_fusion.ids_ref, ...), custom_call_target="tpu_custom_call" | custom-call | flops 4294967296 | bytes 16777216 | tf_op jit(solution)/shard_map/pallas_call | solution.py:102
  93.6 5.2 %shard_map.89 = bf16[8,4,2,64,128]{4,3,2,1,0:T(8,128)(2,1)} custom-call(bf16[512,2048]{1,0:T(8,128)(2,1)S(1)} %get-tuple-element.56.rows_0, bf16[512,2048]{1,0:T(8,128)(2,1)S(1)} %get-tuple-element.57.rows_1, bf16[1024,256]{1,0:T(8,128)(2,1)S(1)} %bitcast.29, bf16[1024,256]{1,0:T(8,128)(2,1)S(1)} %bitcast.32, bf16[1024,256]{1,0:T(8,128)(2,1)} %collective-permute-done.8.a1_a, ...), custom_call_target="tpu_custom_call" | custom-call | flops 1 | bytes 1 | tf_op jit(solution)/shard_map/pallas_call | solution.py:172
  98.8 9.5 %all-to-all-start.3 = ((bf16[32,128,128]{2,1,0:T(8,128)(2,1)}), bf16[32,128,128]{2,1,0:T(8,128)(2,1)S(1)}, u32[]{:S(2)}, u32[]{:S(2)}) async-start(bf16[32,128,128]{2,1,0:T(8,128)(2,1)} %bitcast.21), calls=%async_computation.3 | async-start | bytes 2097152 | tf_op jit(solution)/shard_map/all_to_all | solution.py:343
  108.5 3.7 %collective-permute-done.16.c3_b = bf16[1024,256]{1,0:T(8,128)(2,1)} collective-permute-done((bf16[1024,256]{1,0:T(8,128)(2,1)}, bf16[1024,256]{1,0:T(8,128)(2,1)}, u32[]{:S(2)}, u32[]{:S(2)}) %collective-permute-start.16) | collective-permute-done | bytes 524320 | tf_op jit(solution)/shard_map/ppermute | solution.py:272
  118.3 2.9 %shard_map.90.acted_ref = bf16[8,4,1,64,128]{4,3,2,1,0:T(8,128)(2,1)S(1)} custom-call(bf16[512,2048]{1,0:T(8,128)(2,1)S(1)} %copy-done.7, bf16[1024,256]{1,0:T(8,128)(2,1)} %collective-permute-done.10.a2_a, bf16[1024,256]{1,0:T(8,128)(2,1)} %collective-permute-done.2.a2_b, bf16[1024,256]{1,0:T(8,128)(2,1)} %collective-permute-done.12.a3_a, ...), custom_call_target="tpu_custom_call" | custom-call | flops 1 | bytes 1 | tf_op jit(solution)/shard_map/pallas_call | solution.py:172
  122.0 4.3 %collective-permute-done.17.z4_b = bf16[1024,256]{1,0:T(8,128)(2,1)S(1)} collective-permute-done((bf16[1024,256]{1,0:T(8,128)(2,1)}, bf16[1024,256]{1,0:T(8,128)(2,1)S(1)}, u32[]{:S(2)}, u32[]{:S(2)}) %collective-permute-start.17) | collective-permute-done | bytes 524320 | tf_op jit(solution)/shard_map/ppermute | solution.py:272
  129.0 7.5 %all-to-all-start.2 = ((bf16[32,128,128]{2,1,0:T(8,128)(2,1)}), bf16[32,128,128]{2,1,0:T(8,128)(2,1)S(1)}, u32[]{:S(2)}, u32[]{:S(2)}) async-start(bf16[32,128,128]{2,1,0:T(8,128)(2,1)} %bitcast.26), calls=%async_computation.2 | async-start | bytes 2097152 | tf_op jit(solution)/shard_map/all_to_all | solution.py:343
  138.2 14.9 %all-to-all-done.2 = bf16[32,128,128]{2,1,0:T(8,128)(2,1)S(1)} async-done(((bf16[32,128,128]{2,1,0:T(8,128)(2,1)}), bf16[32,128,128]{2,1,0:T(8,128)(2,1)S(1)}, u32[]{:S(2)}, u32[]{:S(2)}) %all-to-all-start.2) | async-done | bytes 1048608 | tf_op jit(solution)/shard_map/all_to_all | solution.py:343
  (58 shorter events, 22.7 us)
Async XLA Ops:
  7.2 73.7 %all-gather.2.cloned.1.call-start = ((), (), s32[]{:S(2)}) async-start(), calls=%async_computation.4 | async-start | bytes 9437184 | tf_op jit(solution)/shard_map/all_gather | solution.py:294
  7.9 10.5 %collective-permute-start.4 = (s32[2,8,128]{2,1,0:T(8,128)}, s32[2,8,128]{2,1,0:T(8,128)S(1)}, u32[]{:S(2)}, u32[]{:S(2)}) collective-permute-start(s32[2,8,128]{2,1,0:T(8,128)} %bitcast.38), channel_id=1, source_target_pairs={{16,0},{32,16},{48,32},{0,48},{17,1},{33,17},{49,33},{1,49},{18,2}... | collective-permute-start | bytes 24584 | tf_op jit(solution)/shard_map/ppermute | solution.py:280
  11.6 6.8 %collective-permute-start.5 = (s32[2,8,128]{2,1,0:T(8,128)}, s32[2,8,128]{2,1,0:T(8,128)S(1)}, u32[]{:S(2)}, u32[]{:S(2)}) collective-permute-start(s32[2,8,128]{2,1,0:T(8,128)} %bitcast.39), channel_id=1, source_target_pairs={{32,0},{48,16},{0,32},{16,48},{33,1},{49,17},{1,33},{17,49},{34,2}... | collective-permute-start | bytes 24584 | tf_op jit(solution)/shard_map/ppermute | solution.py:280
  11.9 6.5 %collective-permute-start.6 = (s32[2,8,128]{2,1,0:T(8,128)}, s32[2,8,128]{2,1,0:T(8,128)S(1)}, u32[]{:S(2)}, u32[]{:S(2)}) collective-permute-start(s32[2,8,128]{2,1,0:T(8,128)} %bitcast.40), channel_id=1, source_target_pairs={{48,0},{0,16},{16,32},{32,48},{49,1},{1,17},{17,33},{33,49},{50,2}... | collective-permute-start | bytes 24584 | tf_op jit(solution)/shard_map/ppermute | solution.py:280
  18.4 40.2 %copy-start.9 = (f32[2,128,8]{1,2,0:T(8,128)S(1)}, f32[2,128,8]{1,2,0:T(8,128)}, u32[]{:S(2)}) copy-start(f32[2,128,8]{1,2,0:T(8,128)} %param.13) | copy-start | bytes 24580
  18.4 15.6 %all-to-all-start.1 = ((bf16[8,128,256]{2,1,0:T(8,128)(2,1)}), bf16[8,128,256]{2,1,0:T(8,128)(2,1)S(1)}, u32[]{:S(2)}, u32[]{:S(2)}) async-start(bf16[8,128,256]{2,1,0:T(8,128)(2,1)} %bitcast.35), calls=%async_computation.1 | async-start | bytes 1048576 | tf_op jit(solution)/shard_map/all_to_all | solution.py:312
  24.2 13.2 %collective-permute-start.7 = (s32[4,2,8,128]{3,2,1,0:T(8,128)S(1)}, s32[4,2,8,128]{3,2,1,0:T(8,128)S(1)}, u32[]{:S(2)}, u32[]{:S(2)}) collective-permute-start(s32[4,2,8,128]{3,2,1,0:T(8,128)S(1)} %pad_add_fusion.1), channel_id=1, source_target_pairs={{0,64},{64,0},{1,65},{65,1},{2,66},{66,2},{3,67},{67,3},{4,68},{68... | collective-permute-start | bytes 98312 | tf_op jit(solution)/shard_map/ppermute | solution.py:318
  34.0 13.1 %all-to-all-start = ((bf16[8,128,256]{2,1,0:T(8,128)(2,1)}), bf16[8,128,256]{2,1,0:T(8,128)(2,1)S(1)}, u32[]{:S(2)}, u32[]{:S(2)}) async-start(bf16[8,128,256]{2,1,0:T(8,128)(2,1)} %bitcast.34), calls=%async_computation | async-start | bytes 1048576 | tf_op jit(solution)/shard_map/all_to_all | solution.py:312
  37.5 16.0 %collective-permute-start.8 = (bf16[1024,256]{1,0:T(8,128)(2,1)S(1)}, bf16[1024,256]{1,0:T(8,128)(2,1)}, u32[]{:S(2)}, u32[]{:S(2)}) collective-permute-start(bf16[1024,256]{1,0:T(8,128)(2,1)S(1)} %bitcast.27), channel_id=1, source_target_pairs={{0,128},{128,0},{4,132},{132,4},{8,136},{136,8},{12,140},{140,12},... | collective-permute-start | bytes 1572872 | tf_op jit(solution)/shard_map/ppermute | solution.py:272
  39.2 16.9 %collective-permute-start.9 = (bf16[1024,256]{1,0:T(8,128)(2,1)S(1)}, bf16[1024,256]{1,0:T(8,128)(2,1)}, u32[]{:S(2)}, u32[]{:S(2)}) collective-permute-start(bf16[1024,256]{1,0:T(8,128)(2,1)S(1)} %bitcast.28), channel_id=1, source_target_pairs={{128,4},{4,128},{132,8},{8,132},{136,12},{12,136},{140,0},{0,140},... | collective-permute-start | bytes 1572872 | tf_op jit(solution)/shard_map/ppermute | solution.py:272
  47.2 15.6 %collective-permute-start = (bf16[1024,256]{1,0:T(8,128)(2,1)S(1)}, bf16[1024,256]{1,0:T(8,128)(2,1)}, u32[]{:S(2)}, u32[]{:S(2)}) collective-permute-start(bf16[1024,256]{1,0:T(8,128)(2,1)S(1)} %bitcast.30), channel_id=1, source_target_pairs={{0,128},{128,0},{4,132},{132,4},{8,136},{136,8},{12,140},{140,12},... | collective-permute-start | bytes 1572872 | tf_op jit(solution)/shard_map/ppermute | solution.py:272
  48.8 18.5 %collective-permute-start.1 = (bf16[1024,256]{1,0:T(8,128)(2,1)S(1)}, bf16[1024,256]{1,0:T(8,128)(2,1)}, u32[]{:S(2)}, u32[]{:S(2)}) collective-permute-start(bf16[1024,256]{1,0:T(8,128)(2,1)S(1)} %bitcast.31), channel_id=1, source_target_pairs={{128,4},{4,128},{132,8},{8,132},{136,12},{12,136},{140,0},{0,140},... | collective-permute-start | bytes 1572872 | tf_op jit(solution)/shard_map/ppermute | solution.py:272
  56.1 17.9 %collective-permute-start.10 = (bf16[1024,256]{1,0:T(8,128)(2,1)}, bf16[1024,256]{1,0:T(8,128)(2,1)}, u32[]{:S(2)}, u32[]{:S(2)}) collective-permute-start(bf16[1024,256]{1,0:T(8,128)(2,1)} %collective-permute-done.9.c1_a), channel_id=1, source_target_pairs={{0,128},{128,0},{4,132},{132,4},{8,136},{136,8},{12,140},{140,12},... | collective-permute-start | bytes 1572872 | tf_op jit(solution)/shard_map/ppermute | solution.py:272
  56.1 22.5 %collective-permute-start.11 = (bf16[1024,256]{1,0:T(8,128)(2,1)}, bf16[1024,256]{1,0:T(8,128)(2,1)}, u32[]{:S(2)}, u32[]{:S(2)}) collective-permute-start(bf16[1024,256]{1,0:T(8,128)(2,1)} %collective-permute-done.8.a1_a), channel_id=1, source_target_pairs={{128,4},{4,128},{132,8},{8,132},{136,12},{12,136},{140,0},{0,140},... | collective-permute-start | bytes 1572872 | tf_op jit(solution)/shard_map/ppermute | solution.py:272
  67.3 24.1 %collective-permute-start.2 = (bf16[1024,256]{1,0:T(8,128)(2,1)}, bf16[1024,256]{1,0:T(8,128)(2,1)}, u32[]{:S(2)}, u32[]{:S(2)}) collective-permute-start(bf16[1024,256]{1,0:T(8,128)(2,1)} %collective-permute-done.1.c1_b), channel_id=1, source_target_pairs={{0,128},{128,0},{4,132},{132,4},{8,136},{136,8},{12,140},{140,12},... | collective-permute-start | bytes 1572872 | tf_op jit(solution)/shard_map/ppermute | solution.py:272
  67.3 24.1 %collective-permute-start.3 = (bf16[1024,256]{1,0:T(8,128)(2,1)}, bf16[1024,256]{1,0:T(8,128)(2,1)}, u32[]{:S(2)}, u32[]{:S(2)}) collective-permute-start(bf16[1024,256]{1,0:T(8,128)(2,1)} %collective-permute-done.a1_b), channel_id=1, source_target_pairs={{128,4},{4,128},{132,8},{8,132},{136,12},{12,136},{140,0},{0,140},... | collective-permute-start | bytes 1572872 | tf_op jit(solution)/shard_map/ppermute | solution.py:272
  78.5 29.8 %collective-permute-start.12 = (bf16[1024,256]{1,0:T(8,128)(2,1)}, bf16[1024,256]{1,0:T(8,128)(2,1)}, u32[]{:S(2)}, u32[]{:S(2)}) collective-permute-start(bf16[1024,256]{1,0:T(8,128)(2,1)} %collective-permute-done.11.c2_a), channel_id=1, source_target_pairs={{0,128},{128,0},{4,132},{132,4},{8,136},{136,8},{12,140},{140,12},... | collective-permute-start | bytes 1572872 | tf_op jit(solution)/shard_map/ppermute | solution.py:272
  78.5 29.9 %collective-permute-start.13 = (bf16[1024,256]{1,0:T(8,128)(2,1)}, bf16[1024,256]{1,0:T(8,128)(2,1)}, u32[]{:S(2)}, u32[]{:S(2)}) collective-permute-start(bf16[1024,256]{1,0:T(8,128)(2,1)} %collective-permute-done.10.a2_a), channel_id=1, source_target_pairs={{128,4},{4,128},{132,8},{8,132},{136,12},{12,136},{140,0},{0,140},... | collective-permute-start | bytes 1572872 | tf_op jit(solution)/shard_map/ppermute | solution.py:272
  91.4 17.1 %collective-permute-start.15 = (bf16[1024,256]{1,0:T(8,128)(2,1)}, bf16[1024,256]{1,0:T(8,128)(2,1)}, u32[]{:S(2)}, u32[]{:S(2)}) collective-permute-start(bf16[1024,256]{1,0:T(8,128)(2,1)} %collective-permute-done.3.c2_b), channel_id=1, source_target_pairs={{0,128},{128,0},{4,132},{132,4},{8,136},{136,8},{12,140},{140,12},... | collective-permute-start | bytes 1572872 | tf_op jit(solution)/shard_map/ppermute | solution.py:272
  91.5 20.8 %collective-permute-start.16 = (bf16[1024,256]{1,0:T(8,128)(2,1)}, bf16[1024,256]{1,0:T(8,128)(2,1)}, u32[]{:S(2)}, u32[]{:S(2)}) collective-permute-start(bf16[1024,256]{1,0:T(8,128)(2,1)} %collective-permute-done.2.a2_b), channel_id=1, source_target_pairs={{128,4},{4,128},{132,8},{8,132},{136,12},{12,136},{140,0},{0,140},... | collective-permute-start | bytes 1572872 | tf_op jit(solution)/shard_map/ppermute | solution.py:272
  98.8 29.3 %all-to-all-start.3 = ((bf16[32,128,128]{2,1,0:T(8,128)(2,1)}), bf16[32,128,128]{2,1,0:T(8,128)(2,1)S(1)}, u32[]{:S(2)}, u32[]{:S(2)}) async-start(bf16[32,128,128]{2,1,0:T(8,128)(2,1)} %bitcast.21), calls=%async_computation.3 | async-start | bytes 2097152 | tf_op jit(solution)/shard_map/all_to_all | solution.py:343
  108.4 13.6 %collective-permute-start.14 = (bf16[1024,256]{1,0:T(8,128)(2,1)}, bf16[1024,256]{1,0:T(8,128)(2,1)S(1)}, u32[]{:S(2)}, u32[]{:S(2)}) collective-permute-start(bf16[1024,256]{1,0:T(8,128)(2,1)} %collective-permute-done.13.c3_a), channel_id=1, source_target_pairs={{0,128},{128,0},{4,132},{132,4},{8,136},{136,8},{12,140},{140,12},... | collective-permute-start | bytes 1572872 | tf_op jit(solution)/shard_map/ppermute | solution.py:272
  112.2 14.1 %collective-permute-start.17 = (bf16[1024,256]{1,0:T(8,128)(2,1)}, bf16[1024,256]{1,0:T(8,128)(2,1)S(1)}, u32[]{:S(2)}, u32[]{:S(2)}) collective-permute-start(bf16[1024,256]{1,0:T(8,128)(2,1)} %collective-permute-done.15.a3_b), channel_id=1, source_target_pairs={{128,4},{4,128},{132,8},{8,132},{136,12},{12,136},{140,0},{0,140},... | collective-permute-start | bytes 1572872 | tf_op jit(solution)/shard_map/ppermute | solution.py:272
  129.0 24.1 %all-to-all-start.2 = ((bf16[32,128,128]{2,1,0:T(8,128)(2,1)}), bf16[32,128,128]{2,1,0:T(8,128)(2,1)S(1)}, u32[]{:S(2)}, u32[]{:S(2)}) async-start(bf16[32,128,128]{2,1,0:T(8,128)(2,1)} %bitcast.26), calls=%async_computation.2 | async-start | bytes 2097152 | tf_op jit(solution)/shard_map/all_to_all | solution.py:343
  (9 other events, 34.2 us)
Sparse Core Ops, SparseCore 0:
  9.9 56.5 all-gather.1

commit v8 on v7

--- a/solution.py
+++ b/solution.py
@@ -347,7 +347,7 @@
     early = run(early_kernel, early, double)
     a3_a, c3_a = hold((a3_a, c3_a))
     z4_a = swap(c3_a, 0)
-    a3_b, c3_b, acted = hold((a3_b, c3_b, early))
+    a3_b, c3_b, early = hold((a3_b, c3_b, early))
     early = send_back(early)
     z4_b = swap(a3_b, 1)
     later = run(later_kernel, [rows[2], a2_a, a2_b, a3_a, a3_b], single)

time: 162 us -> 159 us (0.981)
  waiting for transfers between devices: 54.6 us -> 48.7 us
  local copies, waits for them, and re-layouts: 6.35 us -> 8.19 us
    all_to_all x2, waiting for transfers between devices: 13 us -> 7.13 us  [share_out(): lax.all_to_all(chunk, ('core', 'x'), split_axis=0, concat_axis=0, tiled=T...]
    ppermute x14, waiting for transfers between devices: 26 us -> 20.9 us  [swap(): return lax.ppermute(value, ('zl', 'zh'), pairs)]
    ppermute x3, waiting for transfers between devices: 0.01 us -> 3.35 us  [along_y(): lax.ppermute(own, 'y', [((at + away) % size, at) for at in range(size)])]
    all_to_all x2, starting transfers between devices: 17.1 us -> 19 us  [send_back(): lax.all_to_all(value, ('core', 'y', 'x'), split_axis=0, concat_axis=0, ti...]
    unnamed x22 -> x26, local copies, waits for them, and re-layouts: 6.35 us -> 8.19 us
    all_gather x1, waiting for transfers between devices: 0.01 us -> 1.77 us  [per_device(): lax.all_gather(tokens.reshape(steps * token_count, depth), ('core', 'y'),...]
    ppermute x3, starting transfers between devices: 4.68 us -> 2.94 us  [along_y(): lax.ppermute(own, 'y', [((at + away) % size, at) for at in range(size)])]
  transfers between devices with their start and end apart: 23 -> 23, of which waited for: 11 -> 13; matrix products, arithmetic and copies ran while one was open for 0% -> 0% of each run, Pallas kernels for 18% -> 18%
where the time goes in v8:
time: 159 us; the launch traced here: 158 us
  starting transfers between devices  56.6 us (36%)
  waiting for transfers between devices  48.7 us (31%)
  Pallas kernels  29.9 us (19%)
  between operations  14.2 us (9%)
  local copies, waits for them, and re-layouts  8.19 us (5%)
    ppermute x14, starting transfers between devices, swap(): return lax.ppermute(value, ('zl', 'zh'), pairs)  23.9 us
    ppermute x14, waiting for transfers between devices, swap(): return lax.ppermute(value, ('zl', 'zh'), pairs)  20.9 us
    all_to_all x2, starting transfers between devices, send_back(): lax.all_to_all(value, ('core', 'y', 'x'), split_axis=0, concat_axis=0, ti...  19 us
    all_to_all x2, waiting for transfers between devices, send_back(): lax.all_to_all(value, ('core', 'y', 'x'), split_axis=0, concat_axis=0, ti...  14.9 us
    pallas_call x6, Pallas kernels, run(): pl.pallas_call(body, in_specs=[spec] * len(operands), out_specs=spec, out...  12.3 us
    all_to_all x2, starting transfers between devices, share_out(): lax.all_to_all(chunk, ('core', 'x'), split_axis=0, concat_axis=0, tiled=T...  10.6 us
    pallas_call x1, Pallas kernels, pick_rows(): pl.pallas_call(pick_kernel, grid_spec=pltpu.PrefetchScalarGridSpec(num_sc...  9.09 us
    unnamed x26, local copies, waits for them, and re-layouts  8.19 us
  transfers between devices with their start and end apart: 23, of which 13 were waited for; matrix products, arithmetic and copies ran while one was open for 0% of the time, Pallas kernels for 18%

profile of v8, /device:TPU:1, one launch (start us, length us, event | category | flops | bytes accessed | tf_op | source)
XLA Modules:
  0.0 157.8 jit_solution(17414742691886773247)
XLA Ops:
  7.9 5.8 %shard_map.86 = (f32[4,128,1024]{2,1,0:T(8,128)}, bf16[2,4,128,256]{3,2,1,0:T(8,128)(2,1)}, bf16[2,4,128,256]{3,2,1,0:T(8,128)(2,1)}) custom-call(f32[4,128,1024]{2,1,0:T(8,128)} %master_ref.1, f32[4,128,1024]{2,1,0:T(8,128)} %first_ref.1, f32[4,128,1024]{2,1,0:T(8,128)} %second_ref.1, bf16[4,128,1024]{2,1,0:T(8,128)(2,1)} %gradient_ref.1), custom_call_target="tpu_custom_call" | custom-call | flops 8388608 | bytes 10485760 | tf_op jit(solution)/shard_map/pallas_call | solution.py:52
  13.7 6.8 %all-to-all-start = ((bf16[8,128,256]{2,1,0:T(8,128)(2,1)}), bf16[8,128,256]{2,1,0:T(8,128)(2,1)S(1)}, u32[]{:S(2)}, u32[]{:S(2)}) async-start(bf16[8,128,256]{2,1,0:T(8,128)(2,1)} %bitcast.35), calls=%async_computation | async-start | bytes 1048576 | tf_op jit(solution)/shard_map/all_to_all | solution.py:312
  23.4 3.3 %collective-permute-done.5 = s32[2,8,128]{2,1,0:T(8,128)S(1)} collective-permute-done((s32[2,8,128]{2,1,0:T(8,128)S(1)}, s32[2,8,128]{2,1,0:T(8,128)S(1)}, u32[]{:S(2)}, u32[]{:S(2)}) %collective-permute-start.5) | collective-permute-done | bytes 8224 | tf_op jit(solution)/shard_map/ppermute | solution.py:280
  26.8 3.1 %all-to-all-done = bf16[8,128,256]{2,1,0:T(8,128)(2,1)S(1)} async-done(((bf16[8,128,256]{2,1,0:T(8,128)(2,1)}), bf16[8,128,256]{2,1,0:T(8,128)(2,1)S(1)}, u32[]{:S(2)}, u32[]{:S(2)}) %all-to-all-start) | async-done | bytes 524320 | tf_op jit(solution)/shard_map/all_to_all | solution.py:312
  29.8 3.8 %all-to-all-start.1 = ((bf16[8,128,256]{2,1,0:T(8,128)(2,1)}), bf16[8,128,256]{2,1,0:T(8,128)(2,1)S(1)}, u32[]{:S(2)}, u32[]{:S(2)}) async-start(bf16[8,128,256]{2,1,0:T(8,128)(2,1)} %bitcast.34), calls=%async_computation.1 | async-start | bytes 1048576 | tf_op jit(solution)/shard_map/all_to_all | solution.py:312
  34.6 4.7 %collective-permute-start.1 = (bf16[1024,256]{1,0:T(8,128)(2,1)S(1)}, bf16[1024,256]{1,0:T(8,128)(2,1)}, u32[]{:S(2)}, u32[]{:S(2)}) collective-permute-start(bf16[1024,256]{1,0:T(8,128)(2,1)S(1)} %bitcast.28), channel_id=1, source_target_pairs={{128,4},{4,128},{132,8},{8,132},{136,12},{12,136},{140,0},{0,140},... | collective-permute-start | bytes 1572872 | tf_op jit(solution)/shard_map/ppermute | solution.py:272
  39.3 4.1 %all-to-all-done.1 = bf16[8,128,256]{2,1,0:T(8,128)(2,1)S(1)} async-done(((bf16[8,128,256]{2,1,0:T(8,128)(2,1)}), bf16[8,128,256]{2,1,0:T(8,128)(2,1)S(1)}, u32[]{:S(2)}, u32[]{:S(2)}) %all-to-all-start.1) | async-done | bytes 524320 | tf_op jit(solution)/shard_map/all_to_all | solution.py:312
  44.3 4.7 %collective-permute-start.9 = (bf16[1024,256]{1,0:T(8,128)(2,1)S(1)}, bf16[1024,256]{1,0:T(8,128)(2,1)}, u32[]{:S(2)}, u32[]{:S(2)}) collective-permute-start(bf16[1024,256]{1,0:T(8,128)(2,1)S(1)} %bitcast.31), channel_id=1, source_target_pairs={{128,4},{4,128},{132,8},{8,132},{136,12},{12,136},{140,0},{0,140},... | collective-permute-start | bytes 1572872 | tf_op jit(solution)/shard_map/ppermute | solution.py:272
  49.4 2.8 %shard_map.87.place_ref = bf16[2,256,2048]{2,1,0:T(8,128)(2,1)S(1)} custom-call(s32[4]{0:T(128)S(1)} %get-tuple-element.69.order_ref, s32[2,128,8]{2,1,0:T(8,128)S(1)} %copy.9.ids_ref, f32[2,128,8]{2,1,0:T(8,128)S(1)} %copy.10.raw_ref), custom_call_target="tpu_custom_call" | custom-call | flops 402653184 | bytes 2097152 | tf_op jit(solution)/shard_map/pallas_call | solution.py:222
  53.8 4.5 %collective-permute-done.8.a1_a = bf16[1024,256]{1,0:T(8,128)(2,1)} collective-permute-done((bf16[1024,256]{1,0:T(8,128)(2,1)S(1)}, bf16[1024,256]{1,0:T(8,128)(2,1)}, u32[]{:S(2)}, u32[]{:S(2)}) %collective-permute-start.8) | collective-permute-done | bytes 524320 | tf_op jit(solution)/shard_map/ppermute | solution.py:272
  58.3 4.0 %collective-permute-done.9.c1_a = bf16[1024,256]{1,0:T(8,128)(2,1)} collective-permute-done((bf16[1024,256]{1,0:T(8,128)(2,1)S(1)}, bf16[1024,256]{1,0:T(8,128)(2,1)}, u32[]{:S(2)}, u32[]{:S(2)}) %collective-permute-start.9) | collective-permute-done | bytes 524320 | tf_op jit(solution)/shard_map/ppermute | solution.py:272
  62.3 2.4 %collective-permute-start.11 = (bf16[1024,256]{1,0:T(8,128)(2,1)}, bf16[1024,256]{1,0:T(8,128)(2,1)}, u32[]{:S(2)}, u32[]{:S(2)}) collective-permute-start(bf16[1024,256]{1,0:T(8,128)(2,1)} %collective-permute-done.8.a1_a), channel_id=1, source_target_pairs={{128,4},{4,128},{132,8},{8,132},{136,12},{12,136},{140,0},{0,140},... | collective-permute-start | bytes 1572872 | tf_op jit(solution)/shard_map/ppermute | solution.py:272
  66.4 9.1 %shard_map.88 = (bf16[512,2048]{1,0:T(8,128)(2,1)S(1)}, bf16[512,2048]{1,0:T(8,128)(2,1)S(1)}, bf16[512,2048]{1,0:T(8,128)(2,1)S(1)}, bf16[512,2048]{1,0:T(8,128)(2,1)S(1)}) custom-call(s32[7]{0:T(128)S(1)} %pad_add_fusion.2.where_ref, s32[2,4,2,8,128]{4,3,2,1,0:T(8,128)S(1)} %pad_add_fusion.ids_ref, ...), custom_call_target="tpu_custom_call" | custom-call | flops 4294967296 | bytes 16777216 | tf_op jit(solution)/shard_map/pallas_call | solution.py:102
  78.2 2.8 %collective-permute-start.16 = (bf16[1024,256]{1,0:T(8,128)(2,1)}, bf16[1024,256]{1,0:T(8,128)(2,1)S(1)}, u32[]{:S(2)}, u32[]{:S(2)}) collective-permute-start(bf16[1024,256]{1,0:T(8,128)(2,1)} %collective-permute-done.2.a2_b), channel_id=1, source_target_pairs={{128,4},{4,128},{132,8},{8,132},{136,12},{12,136},{140,0},{0,140},... | collective-permute-start | bytes 1572872 | tf_op jit(solution)/shard_map/ppermute | solution.py:272
  81.1 3.7 %collective-permute-done.11.c2_a = bf16[1024,256]{1,0:T(8,128)(2,1)} collective-permute-done((bf16[1024,256]{1,0:T(8,128)(2,1)}, bf16[1024,256]{1,0:T(8,128)(2,1)}, u32[]{:S(2)}, u32[]{:S(2)}) %collective-permute-start.11) | collective-permute-done | bytes 524320 | tf_op jit(solution)/shard_map/ppermute | solution.py:272
  84.8 2.4 %collective-permute-start.13 = (bf16[1024,256]{1,0:T(8,128)(2,1)}, bf16[1024,256]{1,0:T(8,128)(2,1)}, u32[]{:S(2)}, u32[]{:S(2)}) collective-permute-start(bf16[1024,256]{1,0:T(8,128)(2,1)} %collective-permute-done.10.a2_a), channel_id=1, source_target_pairs={{128,4},{4,128},{132,8},{8,132},{136,12},{12,136},{140,0},{0,140},... | collective-permute-start | bytes 1572872 | tf_op jit(solution)/shard_map/ppermute | solution.py:272
  87.1 5.2 %shard_map.89 = bf16[8,4,2,64,128]{4,3,2,1,0:T(8,128)(2,1)} custom-call(bf16[512,2048]{1,0:T(8,128)(2,1)S(1)} %get-tuple-element.57.rows_0, bf16[512,2048]{1,0:T(8,128)(2,1)S(1)} %get-tuple-element.58.rows_1, bf16[1024,256]{1,0:T(8,128)(2,1)S(1)} %bitcast.32, bf16[1024,256]{1,0:T(8,128)(2,1)S(1)} %bitcast.29, bf16[1024,256]{1,0:T(8,128)(2,1)} %collective-permute-done.8.a1_a, ...), custom_call_target="tpu_custom_call" | custom-call | flops 1 | bytes 1 | tf_op jit(solution)/shard_map/pallas_call | solution.py:172
  92.3 3.6 %collective-permute-done.16.c3_b = bf16[1024,256]{1,0:T(8,128)(2,1)S(1)} collective-permute-done((bf16[1024,256]{1,0:T(8,128)(2,1)}, bf16[1024,256]{1,0:T(8,128)(2,1)S(1)}, u32[]{:S(2)}, u32[]{:S(2)}) %collective-permute-start.16) | collective-permute-done | bytes 524320 | tf_op jit(solution)/shard_map/ppermute | solution.py:272
  96.7 9.1 %all-to-all-start.3 = ((bf16[32,128,128]{2,1,0:T(8,128)(2,1)}), bf16[32,128,128]{2,1,0:T(8,128)(2,1)S(1)}, u32[]{:S(2)}, u32[]{:S(2)}) async-start(bf16[32,128,128]{2,1,0:T(8,128)(2,1)} %bitcast.21), calls=%async_computation.3 | async-start | bytes 2097152 | tf_op jit(solution)/shard_map/all_to_all | solution.py:343
  107.2 2.4 %collective-permute-start.17 = (bf16[1024,256]{1,0:T(8,128)(2,1)}, bf16[1024,256]{1,0:T(8,128)(2,1)S(1)}, u32[]{:S(2)}, u32[]{:S(2)}) collective-permute-start(bf16[1024,256]{1,0:T(8,128)(2,1)} %collective-permute-done.15.a3_b), channel_id=1, source_target_pairs={{128,4},{4,128},{132,8},{8,132},{136,12},{12,136},{140,0},{0,140},... | collective-permute-start | bytes 1572872 | tf_op jit(solution)/shard_map/ppermute | solution.py:272
  114.1 2.9 %shard_map.90.acted_ref = bf16[8,4,1,64,128]{4,3,2,1,0:T(8,128)(2,1)S(1)} custom-call(bf16[512,2048]{1,0:T(8,128)(2,1)S(1)} %copy-done.7, bf16[1024,256]{1,0:T(8,128)(2,1)} %collective-permute-done.10.a2_a, bf16[1024,256]{1,0:T(8,128)(2,1)} %collective-permute-done.2.a2_b, bf16[1024,256]{1,0:T(8,128)(2,1)} %collective-permute-done.12.a3_a, ...), custom_call_target="tpu_custom_call" | custom-call | flops 1 | bytes 1 | tf_op jit(solution)/shard_map/pallas_call | solution.py:172
  117.1 2.5 %collective-permute-done.14.z4_a = bf16[1024,256]{1,0:T(8,128)(2,1)S(1)} collective-permute-done((bf16[1024,256]{1,0:T(8,128)(2,1)}, bf16[1024,256]{1,0:T(8,128)(2,1)S(1)}, u32[]{:S(2)}, u32[]{:S(2)}) %collective-permute-start.14) | collective-permute-done | bytes 524320 | tf_op jit(solution)/shard_map/ppermute | solution.py:272
  123.5 9.8 %all-to-all-start.2 = ((bf16[32,128,128]{2,1,0:T(8,128)(2,1)}), bf16[32,128,128]{2,1,0:T(8,128)(2,1)S(1)}, u32[]{:S(2)}, u32[]{:S(2)}) async-start(bf16[32,128,128]{2,1,0:T(8,128)(2,1)} %bitcast.26), calls=%async_computation.2 | async-start | bytes 2097152 | tf_op jit(solution)/shard_map/all_to_all | solution.py:343
  135.0 14.9 %all-to-all-done.2 = bf16[32,128,128]{2,1,0:T(8,128)(2,1)S(1)} async-done(((bf16[32,128,128]{2,1,0:T(8,128)(2,1)}), bf16[32,128,128]{2,1,0:T(8,128)(2,1)S(1)}, u32[]{:S(2)}, u32[]{:S(2)}) %all-to-all-start.2) | async-done | bytes 1048608 | tf_op jit(solution)/shard_map/all_to_all | solution.py:343
  (62 shorter events, 25.5 us)
Async XLA Ops:
  7.2 59.2 %all-gather.2.cloned.1.call-start = ((), (), s32[]{:S(2)}) async-start(), calls=%async_computation.4 | async-start | bytes 9437184 | tf_op jit(solution)/shard_map/all_gather | solution.py:294
  13.7 35.5 %copy-start.11 = (f32[2,128,8]{1,2,0:T(8,128)S(1)}, f32[2,128,8]{1,2,0:T(8,128)}, u32[]{:S(2)}) copy-start(f32[2,128,8]{1,2,0:T(8,128)} %param.13) | copy-start | bytes 24580
  13.7 16.2 %all-to-all-start = ((bf16[8,128,256]{2,1,0:T(8,128)(2,1)}), bf16[8,128,256]{2,1,0:T(8,128)(2,1)S(1)}, u32[]{:S(2)}, u32[]{:S(2)}) async-start(bf16[8,128,256]{2,1,0:T(8,128)(2,1)} %bitcast.35), calls=%async_computation | async-start | bytes 1048576 | tf_op jit(solution)/shard_map/all_to_all | solution.py:312
  20.5 2.9 %collective-permute-start.4 = (s32[2,8,128]{2,1,0:T(8,128)S(1)}, s32[2,8,128]{2,1,0:T(8,128)S(1)}, u32[]{:S(2)}, u32[]{:S(2)}) collective-permute-start(s32[2,8,128]{2,1,0:T(8,128)S(1)} %bitcast.38), channel_id=1, source_target_pairs={{16,0},{32,16},{48,32},{0,48},{17,1},{33,17},{49,33},{1,49},{18,2}... | collective-permute-start | bytes 24584 | tf_op jit(solution)/shard_map/ppermute | solution.py:280
  22.4 4.3 %collective-permute-start.5 = (s32[2,8,128]{2,1,0:T(8,128)S(1)}, s32[2,8,128]{2,1,0:T(8,128)S(1)}, u32[]{:S(2)}, u32[]{:S(2)}) collective-permute-start(s32[2,8,128]{2,1,0:T(8,128)S(1)} %bitcast.39), channel_id=1, source_target_pairs={{32,0},{48,16},{0,32},{16,48},{33,1},{49,17},{1,33},{17,49},{34,2}... | collective-permute-start | bytes 24584 | tf_op jit(solution)/shard_map/ppermute | solution.py:280
  22.7 4.0 %collective-permute-start.6 = (s32[2,8,128]{2,1,0:T(8,128)S(1)}, s32[2,8,128]{2,1,0:T(8,128)S(1)}, u32[]{:S(2)}, u32[]{:S(2)}) collective-permute-start(s32[2,8,128]{2,1,0:T(8,128)S(1)} %bitcast.40), channel_id=1, source_target_pairs={{48,0},{0,16},{16,32},{32,48},{49,1},{1,17},{17,33},{33,49},{50,2}... | collective-permute-start | bytes 24584 | tf_op jit(solution)/shard_map/ppermute | solution.py:280
  29.8 13.6 %all-to-all-start.1 = ((bf16[8,128,256]{2,1,0:T(8,128)(2,1)}), bf16[8,128,256]{2,1,0:T(8,128)(2,1)S(1)}, u32[]{:S(2)}, u32[]{:S(2)}) async-start(bf16[8,128,256]{2,1,0:T(8,128)(2,1)} %bitcast.34), calls=%async_computation.1 | async-start | bytes 1048576 | tf_op jit(solution)/shard_map/all_to_all | solution.py:312
  33.6 5.7 %collective-permute-start.7 = (s32[4,2,8,128]{3,2,1,0:T(8,128)S(1)}, s32[4,2,8,128]{3,2,1,0:T(8,128)S(1)}, u32[]{:S(2)}, u32[]{:S(2)}) collective-permute-start(s32[4,2,8,128]{3,2,1,0:T(8,128)S(1)} %pad_add_fusion.1), channel_id=1, source_target_pairs={{0,64},{64,0},{1,65},{65,1},{2,66},{66,2},{3,67},{67,3},{4,68},{68... | collective-permute-start | bytes 98312 | tf_op jit(solution)/shard_map/ppermute | solution.py:318
  33.8 18.4 %collective-permute-start = (bf16[1024,256]{1,0:T(8,128)(2,1)S(1)}, bf16[1024,256]{1,0:T(8,128)(2,1)}, u32[]{:S(2)}, u32[]{:S(2)}) collective-permute-start(bf16[1024,256]{1,0:T(8,128)(2,1)S(1)} %bitcast.27), channel_id=1, source_target_pairs={{0,128},{128,0},{4,132},{132,4},{8,136},{136,8},{12,140},{140,12},... | collective-permute-start | bytes 1572872 | tf_op jit(solution)/shard_map/ppermute | solution.py:272
  34.6 17.6 %collective-permute-start.1 = (bf16[1024,256]{1,0:T(8,128)(2,1)S(1)}, bf16[1024,256]{1,0:T(8,128)(2,1)}, u32[]{:S(2)}, u32[]{:S(2)}) collective-permute-start(bf16[1024,256]{1,0:T(8,128)(2,1)S(1)} %bitcast.28), channel_id=1, source_target_pairs={{128,4},{4,128},{132,8},{8,132},{136,12},{12,136},{140,0},{0,140},... | collective-permute-start | bytes 1572872 | tf_op jit(solution)/shard_map/ppermute | solution.py:272
  43.4 14.9 %collective-permute-start.8 = (bf16[1024,256]{1,0:T(8,128)(2,1)S(1)}, bf16[1024,256]{1,0:T(8,128)(2,1)}, u32[]{:S(2)}, u32[]{:S(2)}) collective-permute-start(bf16[1024,256]{1,0:T(8,128)(2,1)S(1)} %bitcast.30), channel_id=1, source_target_pairs={{0,128},{128,0},{4,132},{132,4},{8,136},{136,8},{12,140},{140,12},... | collective-permute-start | bytes 1572872 | tf_op jit(solution)/shard_map/ppermute | solution.py:272
  44.3 17.9 %collective-permute-start.9 = (bf16[1024,256]{1,0:T(8,128)(2,1)S(1)}, bf16[1024,256]{1,0:T(8,128)(2,1)}, u32[]{:S(2)}, u32[]{:S(2)}) collective-permute-start(bf16[1024,256]{1,0:T(8,128)(2,1)S(1)} %bitcast.31), channel_id=1, source_target_pairs={{128,4},{4,128},{132,8},{8,132},{136,12},{12,136},{140,0},{0,140},... | collective-permute-start | bytes 1572872 | tf_op jit(solution)/shard_map/ppermute | solution.py:272
  52.2 24.6 %collective-permute-start.2 = (bf16[1024,256]{1,0:T(8,128)(2,1)}, bf16[1024,256]{1,0:T(8,128)(2,1)}, u32[]{:S(2)}, u32[]{:S(2)}) collective-permute-start(bf16[1024,256]{1,0:T(8,128)(2,1)} %collective-permute-done.1.c1_b), channel_id=1, source_target_pairs={{0,128},{128,0},{4,132},{132,4},{8,136},{136,8},{12,140},{140,12},... | collective-permute-start | bytes 1572872 | tf_op jit(solution)/shard_map/ppermute | solution.py:272
  52.3 24.5 %collective-permute-start.3 = (bf16[1024,256]{1,0:T(8,128)(2,1)}, bf16[1024,256]{1,0:T(8,128)(2,1)}, u32[]{:S(2)}, u32[]{:S(2)}) collective-permute-start(bf16[1024,256]{1,0:T(8,128)(2,1)} %collective-permute-done.a1_b), channel_id=1, source_target_pairs={{128,4},{4,128},{132,8},{8,132},{136,12},{12,136},{140,0},{0,140},... | collective-permute-start | bytes 1572872 | tf_op jit(solution)/shard_map/ppermute | solution.py:272
  62.3 18.8 %collective-permute-start.10 = (bf16[1024,256]{1,0:T(8,128)(2,1)}, bf16[1024,256]{1,0:T(8,128)(2,1)}, u32[]{:S(2)}, u32[]{:S(2)}) collective-permute-start(bf16[1024,256]{1,0:T(8,128)(2,1)} %collective-permute-done.9.c1_a), channel_id=1, source_target_pairs={{0,128},{128,0},{4,132},{132,4},{8,136},{136,8},{12,140},{140,12},... | collective-permute-start | bytes 1572872 | tf_op jit(solution)/shard_map/ppermute | solution.py:272
  62.3 22.5 %collective-permute-start.11 = (bf16[1024,256]{1,0:T(8,128)(2,1)}, bf16[1024,256]{1,0:T(8,128)(2,1)}, u32[]{:S(2)}, u32[]{:S(2)}) collective-permute-start(bf16[1024,256]{1,0:T(8,128)(2,1)} %collective-permute-done.8.a1_a), channel_id=1, source_target_pairs={{128,4},{4,128},{132,8},{8,132},{136,12},{12,136},{140,0},{0,140},... | collective-permute-start | bytes 1572872 | tf_op jit(solution)/shard_map/ppermute | solution.py:272
  76.9 15.4 %collective-permute-start.15 = (bf16[1024,256]{1,0:T(8,128)(2,1)}, bf16[1024,256]{1,0:T(8,128)(2,1)}, u32[]{:S(2)}, u32[]{:S(2)}) collective-permute-start(bf16[1024,256]{1,0:T(8,128)(2,1)} %collective-permute-done.3.c2_b), channel_id=1, source_target_pairs={{0,128},{128,0},{4,132},{132,4},{8,136},{136,8},{12,140},{140,12},... | collective-permute-start | bytes 1572872 | tf_op jit(solution)/shard_map/ppermute | solution.py:272
  78.2 17.7 %collective-permute-start.16 = (bf16[1024,256]{1,0:T(8,128)(2,1)}, bf16[1024,256]{1,0:T(8,128)(2,1)S(1)}, u32[]{:S(2)}, u32[]{:S(2)}) collective-permute-start(bf16[1024,256]{1,0:T(8,128)(2,1)} %collective-permute-done.2.a2_b), channel_id=1, source_target_pairs={{128,4},{4,128},{132,8},{8,132},{136,12},{12,136},{140,0},{0,140},... | collective-permute-start | bytes 1572872 | tf_op jit(solution)/shard_map/ppermute | solution.py:272
  84.8 21.1 %collective-permute-start.12 = (bf16[1024,256]{1,0:T(8,128)(2,1)}, bf16[1024,256]{1,0:T(8,128)(2,1)}, u32[]{:S(2)}, u32[]{:S(2)}) collective-permute-start(bf16[1024,256]{1,0:T(8,128)(2,1)} %collective-permute-done.11.c2_a), channel_id=1, source_target_pairs={{0,128},{128,0},{4,132},{132,4},{8,136},{136,8},{12,140},{140,12},... | collective-permute-start | bytes 1572872 | tf_op jit(solution)/shard_map/ppermute | solution.py:272
  84.8 22.5 %collective-permute-start.13 = (bf16[1024,256]{1,0:T(8,128)(2,1)}, bf16[1024,256]{1,0:T(8,128)(2,1)}, u32[]{:S(2)}, u32[]{:S(2)}) collective-permute-start(bf16[1024,256]{1,0:T(8,128)(2,1)} %collective-permute-done.10.a2_a), channel_id=1, source_target_pairs={{128,4},{4,128},{132,8},{8,132},{136,12},{12,136},{140,0},{0,140},... | collective-permute-start | bytes 1572872 | tf_op jit(solution)/shard_map/ppermute | solution.py:272
  96.7 25.9 %all-to-all-start.3 = ((bf16[32,128,128]{2,1,0:T(8,128)(2,1)}), bf16[32,128,128]{2,1,0:T(8,128)(2,1)S(1)}, u32[]{:S(2)}, u32[]{:S(2)}) async-start(bf16[32,128,128]{2,1,0:T(8,128)(2,1)} %bitcast.21), calls=%async_computation.3 | async-start | bytes 2097152 | tf_op jit(solution)/shard_map/all_to_all | solution.py:343
  107.2 12.4 %collective-permute-start.14 = (bf16[1024,256]{1,0:T(8,128)(2,1)}, bf16[1024,256]{1,0:T(8,128)(2,1)S(1)}, u32[]{:S(2)}, u32[]{:S(2)}) collective-permute-start(bf16[1024,256]{1,0:T(8,128)(2,1)} %collective-permute-done.13.c3_a), channel_id=1, source_target_pairs={{0,128},{128,0},{4,132},{132,4},{8,136},{136,8},{12,140},{140,12},... | collective-permute-start | bytes 1572872 | tf_op jit(solution)/shard_map/ppermute | solution.py:272
  107.2 13.6 %collective-permute-start.17 = (bf16[1024,256]{1,0:T(8,128)(2,1)}, bf16[1024,256]{1,0:T(8,128)(2,1)S(1)}, u32[]{:S(2)}, u32[]{:S(2)}) collective-permute-start(bf16[1024,256]{1,0:T(8,128)(2,1)} %collective-permute-done.15.a3_b), channel_id=1, source_target_pairs={{128,4},{4,128},{132,8},{8,132},{136,12},{12,136},{140,0},{0,140},... | collective-permute-start | bytes 1572872 | tf_op jit(solution)/shard_map/ppermute | solution.py:272
  123.5 26.4 %all-to-all-start.2 = ((bf16[32,128,128]{2,1,0:T(8,128)(2,1)}), bf16[32,128,128]{2,1,0:T(8,128)(2,1)S(1)}, u32[]{:S(2)}, u32[]{:S(2)}) async-start(bf16[32,128,128]{2,1,0:T(8,128)(2,1)} %bitcast.26), calls=%async_computation.2 | async-start | bytes 2097152 | tf_op jit(solution)/shard_map/all_to_all | solution.py:343
  (11 other events, 44.6 us)
Sparse Core Ops, SparseCore 0:
  9.9 56.5 all-gather.1

commit v9 on v8

--- a/solution.py
+++ b/solution.py
@@ -29,8 +29,9 @@
     grad_full = gradient_ref[0].astype(jnp.float32)
     new_first = beta_one * first_ref[0] + (1.0 - beta_one) * grad_full
     new_second = beta_two * second_ref[0] + (1.0 - beta_two) * grad_full * grad_full
-    update = new_first / correct_one / (jnp.sqrt(new_second / correct_two) + epsilon)
-    updated = master_ref[0] * (1.0 - learn_rate * decay_rate) - learn_rate * update
+    scale = jnp.sqrt(new_second * (1.0 / correct_two)) + epsilon
+    update = new_first * (learn_rate / correct_one) / scale
+    updated = master_ref[0] * (1.0 - learn_rate * decay_rate) - update
     new_ref[0] = updated
     lowered = updated.astype(jnp.bfloat16)
     cores, _, _, part = chunk_refs[0].shape

time: 159 us -> 159 us (level)
  no operation moved by 1% of the time
where the time goes in v9:
time: 159 us; the launch traced here: 158 us
  starting transfers between devices  56.6 us (36%)
  waiting for transfers between devices  48.7 us (31%)
  Pallas kernels  29.9 us (19%)
  between operations  14.2 us (9%)
  local copies, waits for them, and re-layouts  8.19 us (5%)
    ppermute x14, starting transfers between devices, swap(): return lax.ppermute(value, ('zl', 'zh'), pairs)  23.9 us
    ppermute x14, waiting for transfers between devices, swap(): return lax.ppermute(value, ('zl', 'zh'), pairs)  20.9 us
    all_to_all x2, starting transfers between devices, send_back(): lax.all_to_all(value, ('core', 'y', 'x'), split_axis=0, concat_axis=0, ti...  19 us
    all_to_all x2, waiting for transfers between devices, send_back(): lax.all_to_all(value, ('core', 'y', 'x'), split_axis=0, concat_axis=0, ti...  14.9 us
    pallas_call x6, Pallas kernels, run(): pl.pallas_call(body, in_specs=[spec] * len(operands), out_specs=spec, out...  12.3 us
    all_to_all x2, starting transfers between devices, share_out(): lax.all_to_all(chunk, ('core', 'x'), split_axis=0, concat_axis=0, tiled=T...  10.6 us
    pallas_call x1, Pallas kernels, pick_rows(): pl.pallas_call(pick_kernel, grid_spec=pltpu.PrefetchScalarGridSpec(num_sc...  9.09 us
    unnamed x26, local copies, waits for them, and re-layouts  8.19 us
  transfers between devices with their start and end apart: 23, of which 13 were waited for; matrix products, arithmetic and copies ran while one was open for 0% of the time, Pallas kernels for 18%

profile of v9, /device:TPU:1, one launch (start us, length us, event | category | flops | bytes accessed | tf_op | source)
XLA Modules:
  0.0 157.8 jit_solution(9741091443311126935)
XLA Ops:
  7.9 5.7 %shard_map.86 = (f32[4,128,1024]{2,1,0:T(8,128)}, bf16[2,4,128,256]{3,2,1,0:T(8,128)(2,1)}, bf16[2,4,128,256]{3,2,1,0:T(8,128)(2,1)}) custom-call(f32[4,128,1024]{2,1,0:T(8,128)} %master_ref.1, f32[4,128,1024]{2,1,0:T(8,128)} %first_ref.1, f32[4,128,1024]{2,1,0:T(8,128)} %second_ref.1, bf16[4,128,1024]{2,1,0:T(8,128)(2,1)} %gradient_ref.1), custom_call_target="tpu_custom_call" | custom-call | flops 8388608 | bytes 10485760 | tf_op jit(solution)/shard_map/pallas_call | solution.py:53
  13.7 6.8 %all-to-all-start = ((bf16[8,128,256]{2,1,0:T(8,128)(2,1)}), bf16[8,128,256]{2,1,0:T(8,128)(2,1)S(1)}, u32[]{:S(2)}, u32[]{:S(2)}) async-start(bf16[8,128,256]{2,1,0:T(8,128)(2,1)} %bitcast.35), calls=%async_computation | async-start | bytes 1048576 | tf_op jit(solution)/shard_map/all_to_all | solution.py:313
  23.4 3.3 %collective-permute-done.5 = s32[2,8,128]{2,1,0:T(8,128)S(1)} collective-permute-done((s32[2,8,128]{2,1,0:T(8,128)S(1)}, s32[2,8,128]{2,1,0:T(8,128)S(1)}, u32[]{:S(2)}, u32[]{:S(2)}) %collective-permute-start.5) | collective-permute-done | bytes 8224 | tf_op jit(solution)/shard_map/ppermute | solution.py:281
  26.7 3.1 %all-to-all-done = bf16[8,128,256]{2,1,0:T(8,128)(2,1)S(1)} async-done(((bf16[8,128,256]{2,1,0:T(8,128)(2,1)}), bf16[8,128,256]{2,1,0:T(8,128)(2,1)S(1)}, u32[]{:S(2)}, u32[]{:S(2)}) %all-to-all-start) | async-done | bytes 524320 | tf_op jit(solution)/shard_map/all_to_all | solution.py:313
  29.8 3.8 %all-to-all-start.1 = ((bf16[8,128,256]{2,1,0:T(8,128)(2,1)}), bf16[8,128,256]{2,1,0:T(8,128)(2,1)S(1)}, u32[]{:S(2)}, u32[]{:S(2)}) async-start(bf16[8,128,256]{2,1,0:T(8,128)(2,1)} %bitcast.34), calls=%async_computation.1 | async-start | bytes 1048576 | tf_op jit(solution)/shard_map/all_to_all | solution.py:313
  34.6 4.7 %collective-permute-start.1 = (bf16[1024,256]{1,0:T(8,128)(2,1)S(1)}, bf16[1024,256]{1,0:T(8,128)(2,1)}, u32[]{:S(2)}, u32[]{:S(2)}) collective-permute-start(bf16[1024,256]{1,0:T(8,128)(2,1)S(1)} %bitcast.28), channel_id=1, source_target_pairs={{128,4},{4,128},{132,8},{8,132},{136,12},{12,136},{140,0},{0,140},... | collective-permute-start | bytes 1572872 | tf_op jit(solution)/shard_map/ppermute | solution.py:273
  39.3 4.1 %all-to-all-done.1 = bf16[8,128,256]{2,1,0:T(8,128)(2,1)S(1)} async-done(((bf16[8,128,256]{2,1,0:T(8,128)(2,1)}), bf16[8,128,256]{2,1,0:T(8,128)(2,1)S(1)}, u32[]{:S(2)}, u32[]{:S(2)}) %all-to-all-start.1) | async-done | bytes 524320 | tf_op jit(solution)/shard_map/all_to_all | solution.py:313
  44.3 4.7 %collective-permute-start.9 = (bf16[1024,256]{1,0:T(8,128)(2,1)S(1)}, bf16[1024,256]{1,0:T(8,128)(2,1)}, u32[]{:S(2)}, u32[]{:S(2)}) collective-permute-start(bf16[1024,256]{1,0:T(8,128)(2,1)S(1)} %bitcast.31), channel_id=1, source_target_pairs={{128,4},{4,128},{132,8},{8,132},{136,12},{12,136},{140,0},{0,140},... | collective-permute-start | bytes 1572872 | tf_op jit(solution)/shard_map/ppermute | solution.py:273
  49.3 2.8 %shard_map.87.place_ref = bf16[2,256,2048]{2,1,0:T(8,128)(2,1)S(1)} custom-call(s32[4]{0:T(128)S(1)} %get-tuple-element.69.order_ref, s32[2,128,8]{2,1,0:T(8,128)S(1)} %copy.9.ids_ref, f32[2,128,8]{2,1,0:T(8,128)S(1)} %copy.10.raw_ref), custom_call_target="tpu_custom_call" | custom-call | flops 402653184 | bytes 2097152 | tf_op jit(solution)/shard_map/pallas_call | solution.py:223
  53.8 4.5 %collective-permute-done.8.a1_a = bf16[1024,256]{1,0:T(8,128)(2,1)} collective-permute-done((bf16[1024,256]{1,0:T(8,128)(2,1)S(1)}, bf16[1024,256]{1,0:T(8,128)(2,1)}, u32[]{:S(2)}, u32[]{:S(2)}) %collective-permute-start.8) | collective-permute-done | bytes 524320 | tf_op jit(solution)/shard_map/ppermute | solution.py:273
  58.3 4.0 %collective-permute-done.9.c1_a = bf16[1024,256]{1,0:T(8,128)(2,1)} collective-permute-done((bf16[1024,256]{1,0:T(8,128)(2,1)S(1)}, bf16[1024,256]{1,0:T(8,128)(2,1)}, u32[]{:S(2)}, u32[]{:S(2)}) %collective-permute-start.9) | collective-permute-done | bytes 524320 | tf_op jit(solution)/shard_map/ppermute | solution.py:273
  62.3 2.4 %collective-permute-start.11 = (bf16[1024,256]{1,0:T(8,128)(2,1)}, bf16[1024,256]{1,0:T(8,128)(2,1)}, u32[]{:S(2)}, u32[]{:S(2)}) collective-permute-start(bf16[1024,256]{1,0:T(8,128)(2,1)} %collective-permute-done.8.a1_a), channel_id=1, source_target_pairs={{128,4},{4,128},{132,8},{8,132},{136,12},{12,136},{140,0},{0,140},... | collective-permute-start | bytes 1572872 | tf_op jit(solution)/shard_map/ppermute | solution.py:273
  66.4 9.1 %shard_map.88 = (bf16[512,2048]{1,0:T(8,128)(2,1)S(1)}, bf16[512,2048]{1,0:T(8,128)(2,1)S(1)}, bf16[512,2048]{1,0:T(8,128)(2,1)S(1)}, bf16[512,2048]{1,0:T(8,128)(2,1)S(1)}) custom-call(s32[7]{0:T(128)S(1)} %pad_add_fusion.2.where_ref, s32[2,4,2,8,128]{4,3,2,1,0:T(8,128)S(1)} %pad_add_fusion.ids_ref, ...), custom_call_target="tpu_custom_call" | custom-call | flops 4294967296 | bytes 16777216 | tf_op jit(solution)/shard_map/pallas_call | solution.py:103
  78.2 2.8 %collective-permute-start.16 = (bf16[1024,256]{1,0:T(8,128)(2,1)}, bf16[1024,256]{1,0:T(8,128)(2,1)S(1)}, u32[]{:S(2)}, u32[]{:S(2)}) collective-permute-start(bf16[1024,256]{1,0:T(8,128)(2,1)} %collective-permute-done.2.a2_b), channel_id=1, source_target_pairs={{128,4},{4,128},{132,8},{8,132},{136,12},{12,136},{140,0},{0,140},... | collective-permute-start | bytes 1572872 | tf_op jit(solution)/shard_map/ppermute | solution.py:273
  81.1 3.7 %collective-permute-done.11.c2_a = bf16[1024,256]{1,0:T(8,128)(2,1)} collective-permute-done((bf16[1024,256]{1,0:T(8,128)(2,1)}, bf16[1024,256]{1,0:T(8,128)(2,1)}, u32[]{:S(2)}, u32[]{:S(2)}) %collective-permute-start.11) | collective-permute-done | bytes 524320 | tf_op jit(solution)/shard_map/ppermute | solution.py:273
  84.7 2.4 %collective-permute-start.13 = (bf16[1024,256]{1,0:T(8,128)(2,1)}, bf16[1024,256]{1,0:T(8,128)(2,1)}, u32[]{:S(2)}, u32[]{:S(2)}) collective-permute-start(bf16[1024,256]{1,0:T(8,128)(2,1)} %collective-permute-done.10.a2_a), channel_id=1, source_target_pairs={{128,4},{4,128},{132,8},{8,132},{136,12},{12,136},{140,0},{0,140},... | collective-permute-start | bytes 1572872 | tf_op jit(solution)/shard_map/ppermute | solution.py:273
  87.1 5.2 %shard_map.89 = bf16[8,4,2,64,128]{4,3,2,1,0:T(8,128)(2,1)} custom-call(bf16[512,2048]{1,0:T(8,128)(2,1)S(1)} %get-tuple-element.57.rows_0, bf16[512,2048]{1,0:T(8,128)(2,1)S(1)} %get-tuple-element.58.rows_1, bf16[1024,256]{1,0:T(8,128)(2,1)S(1)} %bitcast.32, bf16[1024,256]{1,0:T(8,128)(2,1)S(1)} %bitcast.29, bf16[1024,256]{1,0:T(8,128)(2,1)} %collective-permute-done.8.a1_a, ...), custom_call_target="tpu_custom_call" | custom-call | flops 1 | bytes 1 | tf_op jit(solution)/shard_map/pallas_call | solution.py:173
  92.3 3.6 %collective-permute-done.16.c3_b = bf16[1024,256]{1,0:T(8,128)(2,1)S(1)} collective-permute-done((bf16[1024,256]{1,0:T(8,128)(2,1)}, bf16[1024,256]{1,0:T(8,128)(2,1)S(1)}, u32[]{:S(2)}, u32[]{:S(2)}) %collective-permute-start.16) | collective-permute-done | bytes 524320 | tf_op jit(solution)/shard_map/ppermute | solution.py:273
  96.7 9.1 %all-to-all-start.3 = ((bf16[32,128,128]{2,1,0:T(8,128)(2,1)}), bf16[32,128,128]{2,1,0:T(8,128)(2,1)S(1)}, u32[]{:S(2)}, u32[]{:S(2)}) async-start(bf16[32,128,128]{2,1,0:T(8,128)(2,1)} %bitcast.21), calls=%async_computation.3 | async-start | bytes 2097152 | tf_op jit(solution)/shard_map/all_to_all | solution.py:344
  107.2 2.4 %collective-permute-start.17 = (bf16[1024,256]{1,0:T(8,128)(2,1)}, bf16[1024,256]{1,0:T(8,128)(2,1)S(1)}, u32[]{:S(2)}, u32[]{:S(2)}) collective-permute-start(bf16[1024,256]{1,0:T(8,128)(2,1)} %collective-permute-done.15.a3_b), channel_id=1, source_target_pairs={{128,4},{4,128},{132,8},{8,132},{136,12},{12,136},{140,0},{0,140},... | collective-permute-start | bytes 1572872 | tf_op jit(solution)/shard_map/ppermute | solution.py:273
  114.1 2.9 %shard_map.90.acted_ref = bf16[8,4,1,64,128]{4,3,2,1,0:T(8,128)(2,1)S(1)} custom-call(bf16[512,2048]{1,0:T(8,128)(2,1)S(1)} %copy-done.7, bf16[1024,256]{1,0:T(8,128)(2,1)} %collective-permute-done.10.a2_a, bf16[1024,256]{1,0:T(8,128)(2,1)} %collective-permute-done.2.a2_b, bf16[1024,256]{1,0:T(8,128)(2,1)} %collective-permute-done.12.a3_a, ...), custom_call_target="tpu_custom_call" | custom-call | flops 1 | bytes 1 | tf_op jit(solution)/shard_map/pallas_call | solution.py:173
  117.0 2.5 %collective-permute-done.14.z4_a = bf16[1024,256]{1,0:T(8,128)(2,1)S(1)} collective-permute-done((bf16[1024,256]{1,0:T(8,128)(2,1)}, bf16[1024,256]{1,0:T(8,128)(2,1)S(1)}, u32[]{:S(2)}, u32[]{:S(2)}) %collective-permute-start.14) | collective-permute-done | bytes 524320 | tf_op jit(solution)/shard_map/ppermute | solution.py:273
  123.5 9.8 %all-to-all-start.2 = ((bf16[32,128,128]{2,1,0:T(8,128)(2,1)}), bf16[32,128,128]{2,1,0:T(8,128)(2,1)S(1)}, u32[]{:S(2)}, u32[]{:S(2)}) async-start(bf16[32,128,128]{2,1,0:T(8,128)(2,1)} %bitcast.26), calls=%async_computation.2 | async-start | bytes 2097152 | tf_op jit(solution)/shard_map/all_to_all | solution.py:344
  135.0 14.9 %all-to-all-done.2 = bf16[32,128,128]{2,1,0:T(8,128)(2,1)S(1)} async-done(((bf16[32,128,128]{2,1,0:T(8,128)(2,1)}), bf16[32,128,128]{2,1,0:T(8,128)(2,1)S(1)}, u32[]{:S(2)}, u32[]{:S(2)}) %all-to-all-start.2) | async-done | bytes 1048608 | tf_op jit(solution)/shard_map/all_to_all | solution.py:344
  (62 shorter events, 25.5 us)
Async XLA Ops:
  7.2 59.2 %all-gather.2.cloned.1.call-start = ((), (), s32[]{:S(2)}) async-start(), calls=%async_computation.4 | async-start | bytes 9437184 | tf_op jit(solution)/shard_map/all_gather | solution.py:295
  13.7 35.5 %copy-start.11 = (f32[2,128,8]{1,2,0:T(8,128)S(1)}, f32[2,128,8]{1,2,0:T(8,128)}, u32[]{:S(2)}) copy-start(f32[2,128,8]{1,2,0:T(8,128)} %param.13) | copy-start | bytes 24580
  13.7 16.2 %all-to-all-start = ((bf16[8,128,256]{2,1,0:T(8,128)(2,1)}), bf16[8,128,256]{2,1,0:T(8,128)(2,1)S(1)}, u32[]{:S(2)}, u32[]{:S(2)}) async-start(bf16[8,128,256]{2,1,0:T(8,128)(2,1)} %bitcast.35), calls=%async_computation | async-start | bytes 1048576 | tf_op jit(solution)/shard_map/all_to_all | solution.py:313
  20.4 2.9 %collective-permute-start.4 = (s32[2,8,128]{2,1,0:T(8,128)S(1)}, s32[2,8,128]{2,1,0:T(8,128)S(1)}, u32[]{:S(2)}, u32[]{:S(2)}) collective-permute-start(s32[2,8,128]{2,1,0:T(8,128)S(1)} %bitcast.38), channel_id=1, source_target_pairs={{16,0},{32,16},{48,32},{0,48},{17,1},{33,17},{49,33},{1,49},{18,2}... | collective-permute-start | bytes 24584 | tf_op jit(solution)/shard_map/ppermute | solution.py:281
  22.3 4.3 %collective-permute-start.5 = (s32[2,8,128]{2,1,0:T(8,128)S(1)}, s32[2,8,128]{2,1,0:T(8,128)S(1)}, u32[]{:S(2)}, u32[]{:S(2)}) collective-permute-start(s32[2,8,128]{2,1,0:T(8,128)S(1)} %bitcast.39), channel_id=1, source_target_pairs={{32,0},{48,16},{0,32},{16,48},{33,1},{49,17},{1,33},{17,49},{34,2}... | collective-permute-start | bytes 24584 | tf_op jit(solution)/shard_map/ppermute | solution.py:281
  22.7 4.0 %collective-permute-start.6 = (s32[2,8,128]{2,1,0:T(8,128)S(1)}, s32[2,8,128]{2,1,0:T(8,128)S(1)}, u32[]{:S(2)}, u32[]{:S(2)}) collective-permute-start(s32[2,8,128]{2,1,0:T(8,128)S(1)} %bitcast.40), channel_id=1, source_target_pairs={{48,0},{0,16},{16,32},{32,48},{49,1},{1,17},{17,33},{33,49},{50,2}... | collective-permute-start | bytes 24584 | tf_op jit(solution)/shard_map/ppermute | solution.py:281
  29.8 13.6 %all-to-all-start.1 = ((bf16[8,128,256]{2,1,0:T(8,128)(2,1)}), bf16[8,128,256]{2,1,0:T(8,128)(2,1)S(1)}, u32[]{:S(2)}, u32[]{:S(2)}) async-start(bf16[8,128,256]{2,1,0:T(8,128)(2,1)} %bitcast.34), calls=%async_computation.1 | async-start | bytes 1048576 | tf_op jit(solution)/shard_map/all_to_all | solution.py:313
  33.6 5.7 %collective-permute-start.7 = (s32[4,2,8,128]{3,2,1,0:T(8,128)S(1)}, s32[4,2,8,128]{3,2,1,0:T(8,128)S(1)}, u32[]{:S(2)}, u32[]{:S(2)}) collective-permute-start(s32[4,2,8,128]{3,2,1,0:T(8,128)S(1)} %pad_add_fusion.1), channel_id=1, source_target_pairs={{0,64},{64,0},{1,65},{65,1},{2,66},{66,2},{3,67},{67,3},{4,68},{68... | collective-permute-start | bytes 98312 | tf_op jit(solution)/shard_map/ppermute | solution.py:319
  33.8 18.4 %collective-permute-start = (bf16[1024,256]{1,0:T(8,128)(2,1)S(1)}, bf16[1024,256]{1,0:T(8,128)(2,1)}, u32[]{:S(2)}, u32[]{:S(2)}) collective-permute-start(bf16[1024,256]{1,0:T(8,128)(2,1)S(1)} %bitcast.27), channel_id=1, source_target_pairs={{0,128},{128,0},{4,132},{132,4},{8,136},{136,8},{12,140},{140,12},... | collective-permute-start | bytes 1572872 | tf_op jit(solution)/shard_map/ppermute | solution.py:273
  34.6 17.6 %collective-permute-start.1 = (bf16[1024,256]{1,0:T(8,128)(2,1)S(1)}, bf16[1024,256]{1,0:T(8,128)(2,1)}, u32[]{:S(2)}, u32[]{:S(2)}) collective-permute-start(bf16[1024,256]{1,0:T(8,128)(2,1)S(1)} %bitcast.28), channel_id=1, source_target_pairs={{128,4},{4,128},{132,8},{8,132},{136,12},{12,136},{140,0},{0,140},... | collective-permute-start | bytes 1572872 | tf_op jit(solution)/shard_map/ppermute | solution.py:273
  43.4 14.9 %collective-permute-start.8 = (bf16[1024,256]{1,0:T(8,128)(2,1)S(1)}, bf16[1024,256]{1,0:T(8,128)(2,1)}, u32[]{:S(2)}, u32[]{:S(2)}) collective-permute-start(bf16[1024,256]{1,0:T(8,128)(2,1)S(1)} %bitcast.30), channel_id=1, source_target_pairs={{0,128},{128,0},{4,132},{132,4},{8,136},{136,8},{12,140},{140,12},... | collective-permute-start | bytes 1572872 | tf_op jit(solution)/shard_map/ppermute | solution.py:273
  44.3 17.9 %collective-permute-start.9 = (bf16[1024,256]{1,0:T(8,128)(2,1)S(1)}, bf16[1024,256]{1,0:T(8,128)(2,1)}, u32[]{:S(2)}, u32[]{:S(2)}) collective-permute-start(bf16[1024,256]{1,0:T(8,128)(2,1)S(1)} %bitcast.31), channel_id=1, source_target_pairs={{128,4},{4,128},{132,8},{8,132},{136,12},{12,136},{140,0},{0,140},... | collective-permute-start | bytes 1572872 | tf_op jit(solution)/shard_map/ppermute | solution.py:273
  52.2 24.7 %collective-permute-start.2 = (bf16[1024,256]{1,0:T(8,128)(2,1)}, bf16[1024,256]{1,0:T(8,128)(2,1)}, u32[]{:S(2)}, u32[]{:S(2)}) collective-permute-start(bf16[1024,256]{1,0:T(8,128)(2,1)} %collective-permute-done.1.c1_b), channel_id=1, source_target_pairs={{0,128},{128,0},{4,132},{132,4},{8,136},{136,8},{12,140},{140,12},... | collective-permute-start | bytes 1572872 | tf_op jit(solution)/shard_map/ppermute | solution.py:273
  52.3 24.6 %collective-permute-start.3 = (bf16[1024,256]{1,0:T(8,128)(2,1)}, bf16[1024,256]{1,0:T(8,128)(2,1)}, u32[]{:S(2)}, u32[]{:S(2)}) collective-permute-start(bf16[1024,256]{1,0:T(8,128)(2,1)} %collective-permute-done.a1_b), channel_id=1, source_target_pairs={{128,4},{4,128},{132,8},{8,132},{136,12},{12,136},{140,0},{0,140},... | collective-permute-start | bytes 1572872 | tf_op jit(solution)/shard_map/ppermute | solution.py:273
  62.3 18.8 %collective-permute-start.10 = (bf16[1024,256]{1,0:T(8,128)(2,1)}, bf16[1024,256]{1,0:T(8,128)(2,1)}, u32[]{:S(2)}, u32[]{:S(2)}) collective-permute-start(bf16[1024,256]{1,0:T(8,128)(2,1)} %collective-permute-done.9.c1_a), channel_id=1, source_target_pairs={{0,128},{128,0},{4,132},{132,4},{8,136},{136,8},{12,140},{140,12},... | collective-permute-start | bytes 1572872 | tf_op jit(solution)/shard_map/ppermute | solution.py:273
  62.3 22.5 %collective-permute-start.11 = (bf16[1024,256]{1,0:T(8,128)(2,1)}, bf16[1024,256]{1,0:T(8,128)(2,1)}, u32[]{:S(2)}, u32[]{:S(2)}) collective-permute-start(bf16[1024,256]{1,0:T(8,128)(2,1)} %collective-permute-done.8.a1_a), channel_id=1, source_target_pairs={{128,4},{4,128},{132,8},{8,132},{136,12},{12,136},{140,0},{0,140},... | collective-permute-start | bytes 1572872 | tf_op jit(solution)/shard_map/ppermute | solution.py:273
  76.9 15.4 %collective-permute-start.15 = (bf16[1024,256]{1,0:T(8,128)(2,1)}, bf16[1024,256]{1,0:T(8,128)(2,1)}, u32[]{:S(2)}, u32[]{:S(2)}) collective-permute-start(bf16[1024,256]{1,0:T(8,128)(2,1)} %collective-permute-done.3.c2_b), channel_id=1, source_target_pairs={{0,128},{128,0},{4,132},{132,4},{8,136},{136,8},{12,140},{140,12},... | collective-permute-start | bytes 1572872 | tf_op jit(solution)/shard_map/ppermute | solution.py:273
  78.2 17.6 %collective-permute-start.16 = (bf16[1024,256]{1,0:T(8,128)(2,1)}, bf16[1024,256]{1,0:T(8,128)(2,1)S(1)}, u32[]{:S(2)}, u32[]{:S(2)}) collective-permute-start(bf16[1024,256]{1,0:T(8,128)(2,1)} %collective-permute-done.2.a2_b), channel_id=1, source_target_pairs={{128,4},{4,128},{132,8},{8,132},{136,12},{12,136},{140,0},{0,140},... | collective-permute-start | bytes 1572872 | tf_op jit(solution)/shard_map/ppermute | solution.py:273
  84.7 21.1 %collective-permute-start.12 = (bf16[1024,256]{1,0:T(8,128)(2,1)}, bf16[1024,256]{1,0:T(8,128)(2,1)}, u32[]{:S(2)}, u32[]{:S(2)}) collective-permute-start(bf16[1024,256]{1,0:T(8,128)(2,1)} %collective-permute-done.11.c2_a), channel_id=1, source_target_pairs={{0,128},{128,0},{4,132},{132,4},{8,136},{136,8},{12,140},{140,12},... | collective-permute-start | bytes 1572872 | tf_op jit(solution)/shard_map/ppermute | solution.py:273
  84.7 22.5 %collective-permute-start.13 = (bf16[1024,256]{1,0:T(8,128)(2,1)}, bf16[1024,256]{1,0:T(8,128)(2,1)}, u32[]{:S(2)}, u32[]{:S(2)}) collective-permute-start(bf16[1024,256]{1,0:T(8,128)(2,1)} %collective-permute-done.10.a2_a), channel_id=1, source_target_pairs={{128,4},{4,128},{132,8},{8,132},{136,12},{12,136},{140,0},{0,140},... | collective-permute-start | bytes 1572872 | tf_op jit(solution)/shard_map/ppermute | solution.py:273
  96.7 25.9 %all-to-all-start.3 = ((bf16[32,128,128]{2,1,0:T(8,128)(2,1)}), bf16[32,128,128]{2,1,0:T(8,128)(2,1)S(1)}, u32[]{:S(2)}, u32[]{:S(2)}) async-start(bf16[32,128,128]{2,1,0:T(8,128)(2,1)} %bitcast.21), calls=%async_computation.3 | async-start | bytes 2097152 | tf_op jit(solution)/shard_map/all_to_all | solution.py:344
  107.2 12.4 %collective-permute-start.14 = (bf16[1024,256]{1,0:T(8,128)(2,1)}, bf16[1024,256]{1,0:T(8,128)(2,1)S(1)}, u32[]{:S(2)}, u32[]{:S(2)}) collective-permute-start(bf16[1024,256]{1,0:T(8,128)(2,1)} %collective-permute-done.13.c3_a), channel_id=1, source_target_pairs={{0,128},{128,0},{4,132},{132,4},{8,136},{136,8},{12,140},{140,12},... | collective-permute-start | bytes 1572872 | tf_op jit(solution)/shard_map/ppermute | solution.py:273
  107.2 13.6 %collective-permute-start.17 = (bf16[1024,256]{1,0:T(8,128)(2,1)}, bf16[1024,256]{1,0:T(8,128)(2,1)S(1)}, u32[]{:S(2)}, u32[]{:S(2)}) collective-permute-start(bf16[1024,256]{1,0:T(8,128)(2,1)} %collective-permute-done.15.a3_b), channel_id=1, source_target_pairs={{128,4},{4,128},{132,8},{8,132},{136,12},{12,136},{140,0},{0,140},... | collective-permute-start | bytes 1572872 | tf_op jit(solution)/shard_map/ppermute | solution.py:273
  123.5 26.4 %all-to-all-start.2 = ((bf16[32,128,128]{2,1,0:T(8,128)(2,1)}), bf16[32,128,128]{2,1,0:T(8,128)(2,1)S(1)}, u32[]{:S(2)}, u32[]{:S(2)}) async-start(bf16[32,128,128]{2,1,0:T(8,128)(2,1)} %bitcast.26), calls=%async_computation.2 | async-start | bytes 2097152 | tf_op jit(solution)/shard_map/all_to_all | solution.py:344
  (11 other events, 44.5 us)
Sparse Core Ops, SparseCore 0:
  9.9 56.5 all-gather.1

commit v10 on v5

--- a/solution.py
+++ b/solution.py
@@ -167,10 +167,12 @@
     start_ref[...] = multiply(held.at[0], [c3_a, c3_b], near.shape[3] // 2)
 
 
-def last_kernel(core_ref, near, far, z4_a, z4_b, start_ref, out_ref, held, sems):
-    wait(fetch(near, far, 3, held, sems))
+def last_kernel(core_ref, near, far, z4_a, z4_b, start_ref, acted_ref, out_ref, held, sems):
+    copies = fetch(near, far, 3, held, sems)
+    out_ref[:, :, :1] = acted_ref[...]
+    wait(copies)
     product = start_ref[...] + multiply(held.at[0], [z4_a, z4_b])
-    act(out_ref, around(core_ref, near.shape[0]), 0, product)
+    act(out_ref, around(core_ref, near.shape[0]), 1, product)
 
 
 def run(body, operands, out_shape, rows=None, core=None, slots=1):
@@ -346,22 +348,22 @@
         back = lax.all_to_all(value, ("core", "y", "x"), split_axis=0, concat_axis=0, tiled=True)
         return back.reshape(cores, ys * quarters, slots, steps, CAP, strip)
 
+    a3_a, c3_a, own_a = hold((a3_a, c3_a, own_a))
     early = [own_a, own_b, used_1, a1_b, c2_a, c2_b, c1_a, c1_b]
     early = run(early_kernel, early, double, sides, core, 2)
-    a3_a, c3_a = hold((a3_a, c3_a))
     z4_a = swap(c3_a, 0)
-    a3_b, c3_b, early, used_3 = hold((a3_b, c3_b, early, a3_a))
     early = send_back(early)
+    a3_b, c3_b, used_3 = hold((a3_b, c3_b, a3_a))
     z4_b = swap(a3_b, 1)
-    later = send_back(run(later_kernel, [used_2, a2_b, used_3, a3_b], single, sides, core))
+    later = run(later_kernel, [used_2, a2_b, used_3, a3_b], single, sides, core)
     begun = run(begin_kernel, [c3_a, c3_b], start, sides, core)
     mixed_shape = (steps, token_count, cores * strip)
     half_mixed = jax.ShapeDtypeStruct(mixed_shape, jnp.float32)
     half_mixed = run(functools.partial(mix_kernel, 0), [placed, early], half_mixed)
-    z4_a, z4_b, begun, half_mixed = hold((z4_a, z4_b, begun, half_mixed))
-    final = send_back(run(last_kernel, [z4_a, z4_b, begun], single, sides, core))
+    z4_a, z4_b, begun, later = hold((z4_a, z4_b, begun, later))
+    final = send_back(run(last_kernel, [z4_a, z4_b, begun, later], double, sides, core))
     mixed = jax.ShapeDtypeStruct(mixed_shape, jnp.bfloat16)
-    mixed = run(functools.partial(mix_kernel, 2), [placed, later, final, half_mixed], mixed)
+    mixed = run(functools.partial(mix_kernel, 2), [placed, final, half_mixed], mixed)
     return (new_master, mixed)
 
 

time: 172 us -> 164 us (0.953)
  blocking collectives: 15.1 us -> 0 us
  waiting for transfers between devices: 72.1 us -> 78.6 us
    all_to_all x1 -> x0, blocking collectives: 15.1 us -> none  [send_back(): lax.all_to_all(value, ('core', 'y', 'x'), split_axis=0, concat_axis=0, ti...]
    ppermute x14, waiting for transfers between devices: 50.7 us -> 54.3 us  [swap(): return lax.ppermute(value, ('zl', 'zh'), pairs)]
    all_to_all x2, starting transfers between devices: 12 us -> 15.2 us  [send_back(): lax.all_to_all(value, ('core', 'y', 'x'), split_axis=0, concat_axis=0, ti...]
    all_to_all x2, waiting for transfers between devices: 12 us -> 14.9 us  [send_back(): lax.all_to_all(value, ('core', 'y', 'x'), split_axis=0, concat_axis=0, ti...]
    ppermute x14, starting transfers between devices: 19.7 us -> 17 us  [swap(): return lax.ppermute(value, ('zl', 'zh'), pairs)]
    unnamed x16 -> x18, local copies, waits for them, and re-layouts: 5.09 us -> 6.51 us
  transfers between devices with their start and end apart: 19 -> 19, of which waited for: 15 -> 14; matrix products, arithmetic and copies ran while one was open for 1% -> 1% of each run, Pallas kernels for 14% -> 14%
where the time goes in v10:
time: 164 us; the launch traced here: 163 us
  waiting for transfers between devices  78.6 us (48%)
  starting transfers between devices  45.2 us (28%)
  Pallas kernels  30.4 us (19%)
  local copies, waits for them, and re-layouts  7.9 us (5%)
    ppermute x14, waiting for transfers between devices, swap(): return lax.ppermute(value, ('zl', 'zh'), pairs)  54.3 us
    pallas_call x6, Pallas kernels, run(): pl.pallas_call(body, in_specs=in_specs, out_specs=spec, out_shape=out_sha...  18.6 us
    ppermute x14, starting transfers between devices, swap(): return lax.ppermute(value, ('zl', 'zh'), pairs)  17 us
    all_to_all x2, starting transfers between devices, send_back(): lax.all_to_all(value, ('core', 'y', 'x'), split_axis=0, concat_axis=0, ti...  15.2 us
    all_to_all x2, waiting for transfers between devices, send_back(): lax.all_to_all(value, ('core', 'y', 'x'), split_axis=0, concat_axis=0, ti...  14.9 us
    all_to_all x1, waiting for transfers between devices, per_device(): lax.all_to_all(blocks, ('core', 'x'), split_axis=0, concat_axis=0, tiled=...  9.43 us
    all_to_all x1, starting transfers between devices, per_device(): lax.all_to_all(blocks, ('core', 'x'), split_axis=0, concat_axis=0, tiled=...  6.86 us
    unnamed x18, local copies, waits for them, and re-layouts  6.51 us
  transfers between devices with their start and end apart: 19, of which 14 were waited for; matrix products, arithmetic and copies ran while one was open for 1% of the time, Pallas kernels for 14%

profile of v10, /device:TPU:1, one launch (start us, length us, event | category | flops | bytes accessed | tf_op | source)
XLA Modules:
  0.0 163.1 jit_solution(5322503310783373293)
XLA Ops:
  0.6 5.8 %shard_map.86 = (f32[4,128,1024]{2,1,0:T(8,128)}, bf16[2,4,128,512]{3,2,1,0:T(8,128)(2,1)}) custom-call(f32[4,128,1024]{2,1,0:T(8,128)} %master_ref.1, f32[4,128,1024]{2,1,0:T(8,128)} %first_ref.1, f32[4,128,1024]{2,1,0:T(8,128)} %second_ref.1, bf16[4,128,1024]{2,1,0:T(8,128)(2,1)} %gradient_ref.1), custom_call_target="tpu_custom_call" | custom-call | flops 8388608 | bytes 10485760 | tf_op jit(solution)/shard_map/pallas_call | solution.py:48
  6.4 6.9 %all-to-all-start = ((bf16[8,128,512]{2,1,0:T(8,128)(2,1)}), bf16[8,128,512]{2,1,0:T(8,128)(2,1)S(1)}, u32[]{:S(2)}, u32[]{:S(2)}) async-start(bf16[8,128,512]{2,1,0:T(8,128)(2,1)} %bitcast.24), calls=%async_computation | async-start | bytes 2097152 | tf_op jit(solution)/shard_map/all_to_all | solution.py:322
  13.6 3.2 %shard_map.87 = bf16[4,4,64,2048]{3,2,1,0:T(8,128)(2,1)S(1)} custom-call(s32[17]{0:T(128)S(1)} %pad_add_fusion.where_ref, s32[2,8,128]{2,1,0:T(8,128)S(1)} %bitcast.23, bf16[2,128,2048]{2,1,0:T(8,128)(2,1)S(1)} %copy-done.4), custom_call_target="tpu_custom_call" | custom-call | flops 1 | bytes 1 | tf_op jit(solution)/shard_map/pallas_call | solution.py:92
  18.9 9.4 %all-to-all-done = bf16[8,128,512]{2,1,0:T(8,128)(2,1)S(1)} async-done(((bf16[8,128,512]{2,1,0:T(8,128)(2,1)}), bf16[8,128,512]{2,1,0:T(8,128)(2,1)S(1)}, u32[]{:S(2)}, u32[]{:S(2)}) %all-to-all-start) | async-done | bytes 1048608 | tf_op jit(solution)/shard_map/all_to_all | solution.py:322
  29.3 4.8 %all-to-all-start.1 = ((bf16[4,4,64,2048]{3,2,1,0:T(8,128)(2,1)}), bf16[4,4,64,2048]{3,2,1,0:T(8,128)(2,1)}, u32[]{:S(2)}, u32[]{:S(2)}) async-start(bf16[4,4,64,2048]{3,2,1,0:T(8,128)(2,1)} %copy-done), calls=%async_computation.1 | async-start | bytes 8388608 | tf_op jit(solution)/shard_map/all_to_all | solution.py:325
  36.3 4.7 %collective-permute-start.3 = (bf16[512,512]{1,0:T(8,128)(2,1)S(1)}, bf16[512,512]{1,0:T(8,128)(2,1)}, u32[]{:S(2)}, u32[]{:S(2)}) collective-permute-start(bf16[512,512]{1,0:T(8,128)(2,1)S(1)} %bitcast.18), channel_id=1, source_target_pairs={{128,4},{4,128},{132,8},{8,132},{136,12},{12,136},{140,0},{0,140},... | collective-permute-start | bytes 1572872 | tf_op jit(solution)/shard_map/ppermute | solution.py:291
  42.7 2.8 %shard_map.88.place_ref = bf16[2,256,2048]{2,1,0:T(8,128)(2,1)S(1)} custom-call(s32[4]{0:T(128)S(1)} %get-tuple-element.60.order_ref, s32[2,128,8]{2,1,0:T(8,128)S(1)} %copy.9.ids_ref, f32[2,128,8]{2,1,0:T(8,128)S(1)} %copy.10.raw_ref), custom_call_target="tpu_custom_call" | custom-call | flops 1 | bytes 1 | tf_op jit(solution)/shard_map/pallas_call | solution.py:245
  45.5 3.3 %collective-permute-done.2.refs_2_ = bf16[512,512]{1,0:T(8,128)(2,1)} collective-permute-done((bf16[512,512]{1,0:T(8,128)(2,1)S(1)}, bf16[512,512]{1,0:T(8,128)(2,1)}, u32[]{:S(2)}, u32[]{:S(2)}) %collective-permute-start.2) | collective-permute-done | bytes 524320 | tf_op jit(solution)/shard_map/ppermute | solution.py:291
  48.8 3.9 %collective-permute-done.3.refs_6_ = bf16[512,512]{1,0:T(8,128)(2,1)} collective-permute-done((bf16[512,512]{1,0:T(8,128)(2,1)S(1)}, bf16[512,512]{1,0:T(8,128)(2,1)}, u32[]{:S(2)}, u32[]{:S(2)}) %collective-permute-start.3) | collective-permute-done | bytes 524320 | tf_op jit(solution)/shard_map/ppermute | solution.py:291
  55.1 4.9 %collective-permute-done.refs_3_ = bf16[512,512]{1,0:T(8,128)(2,1)} collective-permute-done((bf16[512,512]{1,0:T(8,128)(2,1)S(1)}, bf16[512,512]{1,0:T(8,128)(2,1)}, u32[]{:S(2)}, u32[]{:S(2)}) %collective-permute-start) | collective-permute-done | bytes 524320 | tf_op jit(solution)/shard_map/ppermute | solution.py:291
  60.1 3.9 %collective-permute-done.1.refs_7_ = bf16[512,512]{1,0:T(8,128)(2,1)} collective-permute-done((bf16[512,512]{1,0:T(8,128)(2,1)S(1)}, bf16[512,512]{1,0:T(8,128)(2,1)}, u32[]{:S(2)}, u32[]{:S(2)}) %collective-permute-start.1) | collective-permute-done | bytes 524320 | tf_op jit(solution)/shard_map/ppermute | solution.py:291
  66.3 4.9 %collective-permute-done.6.refs_0_ = bf16[512,512]{1,0:T(8,128)(2,1)} collective-permute-done((bf16[512,512]{1,0:T(8,128)(2,1)}, bf16[512,512]{1,0:T(8,128)(2,1)}, u32[]{:S(2)}, u32[]{:S(2)}) %collective-permute-start.6) | collective-permute-done | bytes 524320 | tf_op jit(solution)/shard_map/ppermute | solution.py:291
  71.3 3.9 %collective-permute-done.7.refs_4_ = bf16[512,512]{1,0:T(8,128)(2,1)} collective-permute-done((bf16[512,512]{1,0:T(8,128)(2,1)}, bf16[512,512]{1,0:T(8,128)(2,1)}, u32[]{:S(2)}, u32[]{:S(2)}) %collective-permute-start.7) | collective-permute-done | bytes 524320 | tf_op jit(solution)/shard_map/ppermute | solution.py:291
  75.2 7.3 %collective-permute-done.4.refs_1_ = bf16[512,512]{1,0:T(8,128)(2,1)} collective-permute-done((bf16[512,512]{1,0:T(8,128)(2,1)}, bf16[512,512]{1,0:T(8,128)(2,1)}, u32[]{:S(2)}, u32[]{:S(2)}) %collective-permute-start.4) | collective-permute-done | bytes 524320 | tf_op jit(solution)/shard_map/ppermute | solution.py:291
  82.5 3.9 %collective-permute-done.5.refs_5_ = bf16[512,512]{1,0:T(8,128)(2,1)} collective-permute-done((bf16[512,512]{1,0:T(8,128)(2,1)}, bf16[512,512]{1,0:T(8,128)(2,1)}, u32[]{:S(2)}, u32[]{:S(2)}) %collective-permute-start.5) | collective-permute-done | bytes 524320 | tf_op jit(solution)/shard_map/ppermute | solution.py:291
  91.8 10.9 %collective-permute-done.10.c3_a = bf16[512,512]{1,0:T(8,128)(2,1)} collective-permute-done((bf16[512,512]{1,0:T(8,128)(2,1)}, bf16[512,512]{1,0:T(8,128)(2,1)}, u32[]{:S(2)}, u32[]{:S(2)}) %collective-permute-start.10) | collective-permute-done | bytes 524320 | tf_op jit(solution)/shard_map/ppermute | solution.py:291
  103.9 5.9 %shard_map.92 = bf16[8,4,2,64,128]{4,3,2,1,0:T(8,128)(2,1)S(1)} custom-call(s32[1]{0:T(128)} %bitcast.9.core_ref, bf16[4,4,64,2048]{3,2,1,0:T(8,128)(2,1)} %all-to-all-done.1.near, bf16[4,4,64,2048]{3,2,1,0:T(8,128)(2,1)} %collective-permute-done.8.far, bf16[512,512]{1,0:T(8,128)(2,1)S(1)} %bitcast.19, bf16[512,512]{1,0:T(8,128)(2,1)S(1)} %bitcast.22, ...), custom_call_target="tpu_custom_call" | custom-call | flops 1 | bytes 1 | tf_op jit(solution)/shard_map/pallas_call | solution.py:194
  110.8 7.2 %all-to-all-start.3 = ((bf16[32,128,128]{2,1,0:T(8,128)(2,1)}), bf16[32,128,128]{2,1,0:T(8,128)(2,1)S(1)}, u32[]{:S(2)}, u32[]{:S(2)}) async-start(bf16[32,128,128]{2,1,0:T(8,128)(2,1)} %bitcast.16), calls=%async_computation.3 | async-start | bytes 2097152 | tf_op jit(solution)/shard_map/all_to_all | solution.py:348
  119.3 3.5 %shard_map.89.start_ref = f32[512,512]{1,0:T(8,128)S(1)} custom-call(s32[1]{0:T(128)} %bitcast.9.core_ref, bf16[4,4,64,2048]{3,2,1,0:T(8,128)(2,1)} %all-to-all-done.1.near, bf16[4,4,64,2048]{3,2,1,0:T(8,128)(2,1)} %collective-permute-done.8.far, bf16[512,512]{1,0:T(8,128)(2,1)} %collective-permute-done.10.c3_a, bf16[512,512]{1,0:T(8,128)(2,1)} %collective-permute-done.13.c3_b), custom_call_target="tpu_custom_call" | custom-call | flops 1 | bytes 1 | tf_op jit(solution)/shard_map/pallas_call | solution.py:194
  122.8 4.3 %shard_map.90.acted_ref = bf16[8,4,1,64,128]{4,3,2,1,0:T(8,128)(2,1)S(1)} custom-call(s32[1]{0:T(128)} %bitcast.9.core_ref, bf16[4,4,64,2048]{3,2,1,0:T(8,128)(2,1)} %all-to-all-done.1.near, bf16[4,4,64,2048]{3,2,1,0:T(8,128)(2,1)} %collective-permute-done.8.far, bf16[512,512]{1,0:T(8,128)(2,1)} %collective-permute-done.6.refs_0_, ...), custom_call_target="tpu_custom_call" | custom-call | flops 1 | bytes 1 | tf_op jit(solution)/shard_map/pallas_call | solution.py:194
  127.1 4.7 %collective-permute-done.11.z4_a = bf16[512,512]{1,0:T(8,128)(2,1)S(1)} collective-permute-done((bf16[512,512]{1,0:T(8,128)(2,1)}, bf16[512,512]{1,0:T(8,128)(2,1)S(1)}, u32[]{:S(2)}, u32[]{:S(2)}) %collective-permute-start.11) | collective-permute-done | bytes 524320 | tf_op jit(solution)/shard_map/ppermute | solution.py:291
  133.1 3.3 %shard_map.91 = bf16[8,4,2,64,128]{4,3,2,1,0:T(8,128)(2,1)} custom-call(s32[1]{0:T(128)} %bitcast.9.core_ref, bf16[4,4,64,2048]{3,2,1,0:T(8,128)(2,1)} %all-to-all-done.1.near, bf16[4,4,64,2048]{3,2,1,0:T(8,128)(2,1)} %collective-permute-done.8.far, bf16[512,512]{1,0:T(8,128)(2,1)S(1)} %collective-permute-done.11.z4_a, ...), custom_call_target="tpu_custom_call" | custom-call | flops 1 | bytes 1 | tf_op jit(solution)/shard_map/pallas_call | solution.py:194
  137.4 8.1 %all-to-all-start.2 = ((bf16[32,128,128]{2,1,0:T(8,128)(2,1)}), bf16[32,128,128]{2,1,0:T(8,128)(2,1)S(1)}, u32[]{:S(2)}, u32[]{:S(2)}) async-start(bf16[32,128,128]{2,1,0:T(8,128)(2,1)} %bitcast.10), calls=%async_computation.2 | async-start | bytes 2097152 | tf_op jit(solution)/shard_map/all_to_all | solution.py:348
  147.2 14.9 %all-to-all-done.2 = bf16[32,128,128]{2,1,0:T(8,128)(2,1)S(1)} async-done(((bf16[32,128,128]{2,1,0:T(8,128)(2,1)}), bf16[32,128,128]{2,1,0:T(8,128)(2,1)S(1)}, u32[]{:S(2)}, u32[]{:S(2)}) %all-to-all-start.2) | async-done | bytes 1048608 | tf_op jit(solution)/shard_map/all_to_all | solution.py:348
  (46 shorter events, 25.7 us)
Async XLA Ops:
  6.4 7.2 %copy-start.4 = (bf16[2,128,2048]{2,1,0:T(8,128)(2,1)S(1)}, bf16[2,128,2048]{2,1,0:T(8,128)(2,1)}, u32[]{:S(2)}) copy-start(bf16[2,128,2048]{2,1,0:T(8,128)(2,1)} %tokens_ref) | copy-start | bytes 3145732
  6.4 7.2 %copy-start.5 = (s32[2,128,8]{1,2,0:T(8,128)S(1)}, s32[2,128,8]{1,2,0:T(8,128)}, u32[]{:S(2)}) copy-start(s32[2,128,8]{1,2,0:T(8,128)} %param.12) | copy-start | bytes 24580
  6.4 21.9 %all-to-all-start = ((bf16[8,128,512]{2,1,0:T(8,128)(2,1)}), bf16[8,128,512]{2,1,0:T(8,128)(2,1)S(1)}, u32[]{:S(2)}, u32[]{:S(2)}) async-start(bf16[8,128,512]{2,1,0:T(8,128)(2,1)} %bitcast.24), calls=%async_computation | async-start | bytes 2097152 | tf_op jit(solution)/shard_map/all_to_all | solution.py:322
  16.8 2.0 %copy-start = (bf16[4,4,64,2048]{3,2,1,0:T(8,128)(2,1)}, bf16[4,4,64,2048]{3,2,1,0:T(8,128)(2,1)S(1)}, u32[]{:S(2)}) copy-start(bf16[4,4,64,2048]{3,2,1,0:T(8,128)(2,1)S(1)} %shard_map.87) | copy-start | bytes 12582916
  29.3 57.1 %all-to-all-start.1 = ((bf16[4,4,64,2048]{3,2,1,0:T(8,128)(2,1)}), bf16[4,4,64,2048]{3,2,1,0:T(8,128)(2,1)}, u32[]{:S(2)}, u32[]{:S(2)}) async-start(bf16[4,4,64,2048]{3,2,1,0:T(8,128)(2,1)} %copy-done), calls=%async_computation.1 | async-start | bytes 8388608 | tf_op jit(solution)/shard_map/all_to_all | solution.py:325
  34.2 8.4 %copy-start.7 = (f32[2,128,8]{1,2,0:T(8,128)S(1)}, f32[2,128,8]{1,2,0:T(8,128)}, u32[]{:S(2)}) copy-start(f32[2,128,8]{1,2,0:T(8,128)} %param.13) | copy-start | bytes 24580
  35.5 13.3 %collective-permute-start.2 = (bf16[512,512]{1,0:T(8,128)(2,1)S(1)}, bf16[512,512]{1,0:T(8,128)(2,1)}, u32[]{:S(2)}, u32[]{:S(2)}) collective-permute-start(bf16[512,512]{1,0:T(8,128)(2,1)S(1)} %bitcast.17), channel_id=1, source_target_pairs={{0,128},{128,0},{4,132},{132,4},{8,136},{136,8},{12,140},{140,12},... | collective-permute-start | bytes 1572872 | tf_op jit(solution)/shard_map/ppermute | solution.py:291
  36.3 16.5 %collective-permute-start.3 = (bf16[512,512]{1,0:T(8,128)(2,1)S(1)}, bf16[512,512]{1,0:T(8,128)(2,1)}, u32[]{:S(2)}, u32[]{:S(2)}) collective-permute-start(bf16[512,512]{1,0:T(8,128)(2,1)S(1)} %bitcast.18), channel_id=1, source_target_pairs={{128,4},{4,128},{132,8},{8,132},{136,12},{12,136},{140,0},{0,140},... | collective-permute-start | bytes 1572872 | tf_op jit(solution)/shard_map/ppermute | solution.py:291
  41.0 19.1 %collective-permute-start = (bf16[512,512]{1,0:T(8,128)(2,1)S(1)}, bf16[512,512]{1,0:T(8,128)(2,1)}, u32[]{:S(2)}, u32[]{:S(2)}) collective-permute-start(bf16[512,512]{1,0:T(8,128)(2,1)S(1)} %bitcast.20), channel_id=1, source_target_pairs={{0,128},{128,0},{4,132},{132,4},{8,136},{136,8},{12,140},{140,12},... | collective-permute-start | bytes 1572872 | tf_op jit(solution)/shard_map/ppermute | solution.py:291
  41.0 23.0 %collective-permute-start.1 = (bf16[512,512]{1,0:T(8,128)(2,1)S(1)}, bf16[512,512]{1,0:T(8,128)(2,1)}, u32[]{:S(2)}, u32[]{:S(2)}) collective-permute-start(bf16[512,512]{1,0:T(8,128)(2,1)S(1)} %bitcast.21), channel_id=1, source_target_pairs={{128,4},{4,128},{132,8},{8,132},{136,12},{12,136},{140,0},{0,140},... | collective-permute-start | bytes 1572872 | tf_op jit(solution)/shard_map/ppermute | solution.py:291
  52.8 18.5 %collective-permute-start.6 = (bf16[512,512]{1,0:T(8,128)(2,1)}, bf16[512,512]{1,0:T(8,128)(2,1)}, u32[]{:S(2)}, u32[]{:S(2)}) collective-permute-start(bf16[512,512]{1,0:T(8,128)(2,1)} %collective-permute-done.3.refs_6_), channel_id=1, source_target_pairs={{0,128},{128,0},{4,132},{132,4},{8,136},{136,8},{12,140},{140,12},... | collective-permute-start | bytes 1572872 | tf_op jit(solution)/shard_map/ppermute | solution.py:291
  52.8 22.5 %collective-permute-start.7 = (bf16[512,512]{1,0:T(8,128)(2,1)}, bf16[512,512]{1,0:T(8,128)(2,1)}, u32[]{:S(2)}, u32[]{:S(2)}) collective-permute-start(bf16[512,512]{1,0:T(8,128)(2,1)} %collective-permute-done.2.refs_2_), channel_id=1, source_target_pairs={{128,4},{4,128},{132,8},{8,132},{136,12},{12,136},{140,0},{0,140},... | collective-permute-start | bytes 1572872 | tf_op jit(solution)/shard_map/ppermute | solution.py:291
  64.0 18.5 %collective-permute-start.4 = (bf16[512,512]{1,0:T(8,128)(2,1)}, bf16[512,512]{1,0:T(8,128)(2,1)}, u32[]{:S(2)}, u32[]{:S(2)}) collective-permute-start(bf16[512,512]{1,0:T(8,128)(2,1)} %collective-permute-done.1.refs_7_), channel_id=1, source_target_pairs={{0,128},{128,0},{4,132},{132,4},{8,136},{136,8},{12,140},{140,12},... | collective-permute-start | bytes 1572872 | tf_op jit(solution)/shard_map/ppermute | solution.py:291
  64.0 22.5 %collective-permute-start.5 = (bf16[512,512]{1,0:T(8,128)(2,1)}, bf16[512,512]{1,0:T(8,128)(2,1)}, u32[]{:S(2)}, u32[]{:S(2)}) collective-permute-start(bf16[512,512]{1,0:T(8,128)(2,1)} %collective-permute-done.refs_3_), channel_id=1, source_target_pairs={{128,4},{4,128},{132,8},{8,132},{136,12},{12,136},{140,0},{0,140},... | collective-permute-start | bytes 1572872 | tf_op jit(solution)/shard_map/ppermute | solution.py:291
  86.5 17.4 %collective-permute-start.8 = (bf16[4,4,64,2048]{3,2,1,0:T(8,128)(2,1)}, bf16[4,4,64,2048]{3,2,1,0:T(8,128)(2,1)}, u32[]{:S(2)}, u32[]{:S(2)}) collective-permute-start(bf16[4,4,64,2048]{3,2,1,0:T(8,128)(2,1)} %all-to-all-done.1.near), channel_id=1, source_target_pairs={{0,64},{64,0},{1,65},{65,1},{2,66},{66,2},{3,67},{67,3},{4,68},{68... | collective-permute-start | bytes 12582920 | tf_op jit(solution)/shard_map/ppermute | solution.py:295
  87.7 15.1 %collective-permute-start.10 = (bf16[512,512]{1,0:T(8,128)(2,1)}, bf16[512,512]{1,0:T(8,128)(2,1)}, u32[]{:S(2)}, u32[]{:S(2)}) collective-permute-start(bf16[512,512]{1,0:T(8,128)(2,1)} %collective-permute-done.6.refs_0_), channel_id=1, source_target_pairs={{128,4},{4,128},{132,8},{8,132},{136,12},{12,136},{140,0},{0,140},... | collective-permute-start | bytes 1572872 | tf_op jit(solution)/shard_map/ppermute | solution.py:291
  90.3 13.6 %collective-permute-start.9 = (bf16[512,512]{1,0:T(8,128)(2,1)}, bf16[512,512]{1,0:T(8,128)(2,1)}, u32[]{:S(2)}, u32[]{:S(2)}) collective-permute-start(bf16[512,512]{1,0:T(8,128)(2,1)} %collective-permute-done.7.refs_4_), channel_id=1, source_target_pairs={{0,128},{128,0},{4,132},{132,4},{8,136},{136,8},{12,140},{140,12},... | collective-permute-start | bytes 1572872 | tf_op jit(solution)/shard_map/ppermute | solution.py:291
  90.3 28.0 %collective-permute-start.12 = (bf16[512,512]{1,0:T(8,128)(2,1)}, bf16[512,512]{1,0:T(8,128)(2,1)}, u32[]{:S(2)}, u32[]{:S(2)}) collective-permute-start(bf16[512,512]{1,0:T(8,128)(2,1)} %collective-permute-done.5.refs_5_), channel_id=1, source_target_pairs={{0,128},{128,0},{4,132},{132,4},{8,136},{136,8},{12,140},{140,12},... | collective-permute-start | bytes 1572872 | tf_op jit(solution)/shard_map/ppermute | solution.py:291
  91.8 26.5 %collective-permute-start.13 = (bf16[512,512]{1,0:T(8,128)(2,1)}, bf16[512,512]{1,0:T(8,128)(2,1)}, u32[]{:S(2)}, u32[]{:S(2)}) collective-permute-start(bf16[512,512]{1,0:T(8,128)(2,1)} %collective-permute-done.4.refs_1_), channel_id=1, source_target_pairs={{128,4},{4,128},{132,8},{8,132},{136,12},{12,136},{140,0},{0,140},... | collective-permute-start | bytes 1572872 | tf_op jit(solution)/shard_map/ppermute | solution.py:291
  110.8 25.6 %all-to-all-start.3 = ((bf16[32,128,128]{2,1,0:T(8,128)(2,1)}), bf16[32,128,128]{2,1,0:T(8,128)(2,1)S(1)}, u32[]{:S(2)}, u32[]{:S(2)}) async-start(bf16[32,128,128]{2,1,0:T(8,128)(2,1)} %bitcast.16), calls=%async_computation.3 | async-start | bytes 2097152 | tf_op jit(solution)/shard_map/all_to_all | solution.py:348
  118.0 13.8 %collective-permute-start.11 = (bf16[512,512]{1,0:T(8,128)(2,1)}, bf16[512,512]{1,0:T(8,128)(2,1)S(1)}, u32[]{:S(2)}, u32[]{:S(2)}) collective-permute-start(bf16[512,512]{1,0:T(8,128)(2,1)} %collective-permute-done.10.c3_a), channel_id=1, source_target_pairs={{0,128},{128,0},{4,132},{132,4},{8,136},{136,8},{12,140},{140,12},... | collective-permute-start | bytes 1572872 | tf_op jit(solution)/shard_map/ppermute | solution.py:291
  118.3 14.8 %collective-permute-start.14 = (bf16[512,512]{1,0:T(8,128)(2,1)}, bf16[512,512]{1,0:T(8,128)(2,1)S(1)}, u32[]{:S(2)}, u32[]{:S(2)}) collective-permute-start(bf16[512,512]{1,0:T(8,128)(2,1)} %collective-permute-done.12.refs_3_), channel_id=1, source_target_pairs={{128,4},{4,128},{132,8},{8,132},{136,12},{12,136},{140,0},{0,140},... | collective-permute-start | bytes 1572872 | tf_op jit(solution)/shard_map/ppermute | solution.py:291
  137.4 24.6 %all-to-all-start.2 = ((bf16[32,128,128]{2,1,0:T(8,128)(2,1)}), bf16[32,128,128]{2,1,0:T(8,128)(2,1)S(1)}, u32[]{:S(2)}, u32[]{:S(2)}) async-start(bf16[32,128,128]{2,1,0:T(8,128)(2,1)} %bitcast.10), calls=%async_computation.2 | async-start | bytes 2097152 | tf_op jit(solution)/shard_map/all_to_all | solution.py:348
  145.5 1.2 copy-start.2
  (3 other events, 3.0 us)

commit v11 on v8

--- a/solution.py
+++ b/solution.py
@@ -19,7 +19,7 @@
 PARTS = 4
 CHUNKS = 2
 STRIP = 128
-ROOM = 12 * 2**20
+ROOM = 6 * 2**20
 WIDE = 56 * 2**20
 PICK = 44 * 2**20
 SMALL = pl.CostEstimate(flops=1, bytes_accessed=1, transcendentals=0)

time: 159 us -> 159 us (level)
  no operation moved by 1% of the time
where the time goes in v11:
time: 159 us; the launch traced here: 158 us
  starting transfers between devices  56.6 us (36%)
  waiting for transfers between devices  48.7 us (31%)
  Pallas kernels  29.9 us (19%)
  between operations  14.2 us (9%)
  local copies, waits for them, and re-layouts  8.19 us (5%)
    ppermute x14, starting transfers between devices, swap(): return lax.ppermute(value, ('zl', 'zh'), pairs)  23.9 us
    ppermute x14, waiting for transfers between devices, swap(): return lax.ppermute(value, ('zl', 'zh'), pairs)  20.9 us
    all_to_all x2, starting transfers between devices, send_back(): lax.all_to_all(value, ('core', 'y', 'x'), split_axis=0, concat_axis=0, ti...  19 us
    all_to_all x2, waiting for transfers between devices, send_back(): lax.all_to_all(value, ('core', 'y', 'x'), split_axis=0, concat_axis=0, ti...  14.9 us
    pallas_call x6, Pallas kernels, run(): pl.pallas_call(body, in_specs=[spec] * len(operands), out_specs=spec, out...  12.3 us
    all_to_all x2, starting transfers between devices, share_out(): lax.all_to_all(chunk, ('core', 'x'), split_axis=0, concat_axis=0, tiled=T...  10.6 us
    pallas_call x1, Pallas kernels, pick_rows(): pl.pallas_call(pick_kernel, grid_spec=pltpu.PrefetchScalarGridSpec(num_sc...  9.09 us
    unnamed x26, local copies, waits for them, and re-layouts  8.19 us
  transfers between devices with their start and end apart: 23, of which 13 were waited for; matrix products, arithmetic and copies ran while one was open for 0% of the time, Pallas kernels for 18%

profile of v11, /device:TPU:1, one launch (start us, length us, event | category | flops | bytes accessed | tf_op | source)
XLA Modules:
  0.0 157.8 jit_solution(2741300279071327452)
XLA Ops:
  7.9 5.8 %shard_map.86 = (f32[4,128,1024]{2,1,0:T(8,128)}, bf16[2,4,128,256]{3,2,1,0:T(8,128)(2,1)}, bf16[2,4,128,256]{3,2,1,0:T(8,128)(2,1)}) custom-call(f32[4,128,1024]{2,1,0:T(8,128)} %master_ref.1, f32[4,128,1024]{2,1,0:T(8,128)} %first_ref.1, f32[4,128,1024]{2,1,0:T(8,128)} %second_ref.1, bf16[4,128,1024]{2,1,0:T(8,128)(2,1)} %gradient_ref.1), custom_call_target="tpu_custom_call" | custom-call | flops 8388608 | bytes 10485760 | tf_op jit(solution)/shard_map/pallas_call | solution.py:52
  13.7 6.8 %all-to-all-start = ((bf16[8,128,256]{2,1,0:T(8,128)(2,1)}), bf16[8,128,256]{2,1,0:T(8,128)(2,1)S(1)}, u32[]{:S(2)}, u32[]{:S(2)}) async-start(bf16[8,128,256]{2,1,0:T(8,128)(2,1)} %bitcast.35), calls=%async_computation | async-start | bytes 1048576 | tf_op jit(solution)/shard_map/all_to_all | solution.py:312
  23.4 3.3 %collective-permute-done.5 = s32[2,8,128]{2,1,0:T(8,128)S(1)} collective-permute-done((s32[2,8,128]{2,1,0:T(8,128)S(1)}, s32[2,8,128]{2,1,0:T(8,128)S(1)}, u32[]{:S(2)}, u32[]{:S(2)}) %collective-permute-start.5) | collective-permute-done | bytes 8224 | tf_op jit(solution)/shard_map/ppermute | solution.py:280
  26.8 3.1 %all-to-all-done = bf16[8,128,256]{2,1,0:T(8,128)(2,1)S(1)} async-done(((bf16[8,128,256]{2,1,0:T(8,128)(2,1)}), bf16[8,128,256]{2,1,0:T(8,128)(2,1)S(1)}, u32[]{:S(2)}, u32[]{:S(2)}) %all-to-all-start) | async-done | bytes 524320 | tf_op jit(solution)/shard_map/all_to_all | solution.py:312
  29.8 3.8 %all-to-all-start.1 = ((bf16[8,128,256]{2,1,0:T(8,128)(2,1)}), bf16[8,128,256]{2,1,0:T(8,128)(2,1)S(1)}, u32[]{:S(2)}, u32[]{:S(2)}) async-start(bf16[8,128,256]{2,1,0:T(8,128)(2,1)} %bitcast.34), calls=%async_computation.1 | async-start | bytes 1048576 | tf_op jit(solution)/shard_map/all_to_all | solution.py:312
  34.6 4.7 %collective-permute-start.1 = (bf16[1024,256]{1,0:T(8,128)(2,1)S(1)}, bf16[1024,256]{1,0:T(8,128)(2,1)}, u32[]{:S(2)}, u32[]{:S(2)}) collective-permute-start(bf16[1024,256]{1,0:T(8,128)(2,1)S(1)} %bitcast.28), channel_id=1, source_target_pairs={{128,4},{4,128},{132,8},{8,132},{136,12},{12,136},{140,0},{0,140},... | collective-permute-start | bytes 1572872 | tf_op jit(solution)/shard_map/ppermute | solution.py:272
  39.3 4.1 %all-to-all-done.1 = bf16[8,128,256]{2,1,0:T(8,128)(2,1)S(1)} async-done(((bf16[8,128,256]{2,1,0:T(8,128)(2,1)}), bf16[8,128,256]{2,1,0:T(8,128)(2,1)S(1)}, u32[]{:S(2)}, u32[]{:S(2)}) %all-to-all-start.1) | async-done | bytes 524320 | tf_op jit(solution)/shard_map/all_to_all | solution.py:312
  44.3 4.7 %collective-permute-start.9 = (bf16[1024,256]{1,0:T(8,128)(2,1)S(1)}, bf16[1024,256]{1,0:T(8,128)(2,1)}, u32[]{:S(2)}, u32[]{:S(2)}) collective-permute-start(bf16[1024,256]{1,0:T(8,128)(2,1)S(1)} %bitcast.31), channel_id=1, source_target_pairs={{128,4},{4,128},{132,8},{8,132},{136,12},{12,136},{140,0},{0,140},... | collective-permute-start | bytes 1572872 | tf_op jit(solution)/shard_map/ppermute | solution.py:272
  49.4 2.8 %shard_map.87.place_ref = bf16[2,256,2048]{2,1,0:T(8,128)(2,1)S(1)} custom-call(s32[4]{0:T(128)S(1)} %get-tuple-element.69.order_ref, s32[2,128,8]{2,1,0:T(8,128)S(1)} %copy.9.ids_ref, f32[2,128,8]{2,1,0:T(8,128)S(1)} %copy.10.raw_ref), custom_call_target="tpu_custom_call" | custom-call | flops 402653184 | bytes 2097152 | tf_op jit(solution)/shard_map/pallas_call | solution.py:222
  53.8 4.5 %collective-permute-done.8.a1_a = bf16[1024,256]{1,0:T(8,128)(2,1)} collective-permute-done((bf16[1024,256]{1,0:T(8,128)(2,1)S(1)}, bf16[1024,256]{1,0:T(8,128)(2,1)}, u32[]{:S(2)}, u32[]{:S(2)}) %collective-permute-start.8) | collective-permute-done | bytes 524320 | tf_op jit(solution)/shard_map/ppermute | solution.py:272
  58.3 4.0 %collective-permute-done.9.c1_a = bf16[1024,256]{1,0:T(8,128)(2,1)} collective-permute-done((bf16[1024,256]{1,0:T(8,128)(2,1)S(1)}, bf16[1024,256]{1,0:T(8,128)(2,1)}, u32[]{:S(2)}, u32[]{:S(2)}) %collective-permute-start.9) | collective-permute-done | bytes 524320 | tf_op jit(solution)/shard_map/ppermute | solution.py:272
  62.3 2.4 %collective-permute-start.11 = (bf16[1024,256]{1,0:T(8,128)(2,1)}, bf16[1024,256]{1,0:T(8,128)(2,1)}, u32[]{:S(2)}, u32[]{:S(2)}) collective-permute-start(bf16[1024,256]{1,0:T(8,128)(2,1)} %collective-permute-done.8.a1_a), channel_id=1, source_target_pairs={{128,4},{4,128},{132,8},{8,132},{136,12},{12,136},{140,0},{0,140},... | collective-permute-start | bytes 1572872 | tf_op jit(solution)/shard_map/ppermute | solution.py:272
  66.4 9.1 %shard_map.88 = (bf16[512,2048]{1,0:T(8,128)(2,1)S(1)}, bf16[512,2048]{1,0:T(8,128)(2,1)S(1)}, bf16[512,2048]{1,0:T(8,128)(2,1)S(1)}, bf16[512,2048]{1,0:T(8,128)(2,1)S(1)}) custom-call(s32[7]{0:T(128)S(1)} %pad_add_fusion.2.where_ref, s32[2,4,2,8,128]{4,3,2,1,0:T(8,128)S(1)} %pad_add_fusion.ids_ref, ...), custom_call_target="tpu_custom_call" | custom-call | flops 4294967296 | bytes 16777216 | tf_op jit(solution)/shard_map/pallas_call | solution.py:102
  78.2 2.8 %collective-permute-start.16 = (bf16[1024,256]{1,0:T(8,128)(2,1)}, bf16[1024,256]{1,0:T(8,128)(2,1)S(1)}, u32[]{:S(2)}, u32[]{:S(2)}) collective-permute-start(bf16[1024,256]{1,0:T(8,128)(2,1)} %collective-permute-done.2.a2_b), channel_id=1, source_target_pairs={{128,4},{4,128},{132,8},{8,132},{136,12},{12,136},{140,0},{0,140},... | collective-permute-start | bytes 1572872 | tf_op jit(solution)/shard_map/ppermute | solution.py:272
  81.1 3.7 %collective-permute-done.11.c2_a = bf16[1024,256]{1,0:T(8,128)(2,1)} collective-permute-done((bf16[1024,256]{1,0:T(8,128)(2,1)}, bf16[1024,256]{1,0:T(8,128)(2,1)}, u32[]{:S(2)}, u32[]{:S(2)}) %collective-permute-start.11) | collective-permute-done | bytes 524320 | tf_op jit(solution)/shard_map/ppermute | solution.py:272
  84.8 2.4 %collective-permute-start.13 = (bf16[1024,256]{1,0:T(8,128)(2,1)}, bf16[1024,256]{1,0:T(8,128)(2,1)}, u32[]{:S(2)}, u32[]{:S(2)}) collective-permute-start(bf16[1024,256]{1,0:T(8,128)(2,1)} %collective-permute-done.10.a2_a), channel_id=1, source_target_pairs={{128,4},{4,128},{132,8},{8,132},{136,12},{12,136},{140,0},{0,140},... | collective-permute-start | bytes 1572872 | tf_op jit(solution)/shard_map/ppermute | solution.py:272
  87.1 5.2 %shard_map.89 = bf16[8,4,2,64,128]{4,3,2,1,0:T(8,128)(2,1)} custom-call(bf16[512,2048]{1,0:T(8,128)(2,1)S(1)} %get-tuple-element.57.rows_0, bf16[512,2048]{1,0:T(8,128)(2,1)S(1)} %get-tuple-element.58.rows_1, bf16[1024,256]{1,0:T(8,128)(2,1)S(1)} %bitcast.32, bf16[1024,256]{1,0:T(8,128)(2,1)S(1)} %bitcast.29, bf16[1024,256]{1,0:T(8,128)(2,1)} %collective-permute-done.8.a1_a, ...), custom_call_target="tpu_custom_call" | custom-call | flops 1 | bytes 1 | tf_op jit(solution)/shard_map/pallas_call | solution.py:172
  92.3 3.6 %collective-permute-done.16.c3_b = bf16[1024,256]{1,0:T(8,128)(2,1)S(1)} collective-permute-done((bf16[1024,256]{1,0:T(8,128)(2,1)}, bf16[1024,256]{1,0:T(8,128)(2,1)S(1)}, u32[]{:S(2)}, u32[]{:S(2)}) %collective-permute-start.16) | collective-permute-done | bytes 524320 | tf_op jit(solution)/shard_map/ppermute | solution.py:272
  96.7 9.1 %all-to-all-start.3 = ((bf16[32,128,128]{2,1,0:T(8,128)(2,1)}), bf16[32,128,128]{2,1,0:T(8,128)(2,1)S(1)}, u32[]{:S(2)}, u32[]{:S(2)}) async-start(bf16[32,128,128]{2,1,0:T(8,128)(2,1)} %bitcast.21), calls=%async_computation.3 | async-start | bytes 2097152 | tf_op jit(solution)/shard_map/all_to_all | solution.py:343
  107.2 2.4 %collective-permute-start.17 = (bf16[1024,256]{1,0:T(8,128)(2,1)}, bf16[1024,256]{1,0:T(8,128)(2,1)S(1)}, u32[]{:S(2)}, u32[]{:S(2)}) collective-permute-start(bf16[1024,256]{1,0:T(8,128)(2,1)} %collective-permute-done.15.a3_b), channel_id=1, source_target_pairs={{128,4},{4,128},{132,8},{8,132},{136,12},{12,136},{140,0},{0,140},... | collective-permute-start | bytes 1572872 | tf_op jit(solution)/shard_map/ppermute | solution.py:272
  114.1 2.9 %shard_map.90.acted_ref = bf16[8,4,1,64,128]{4,3,2,1,0:T(8,128)(2,1)S(1)} custom-call(bf16[512,2048]{1,0:T(8,128)(2,1)S(1)} %copy-done.7, bf16[1024,256]{1,0:T(8,128)(2,1)} %collective-permute-done.10.a2_a, bf16[1024,256]{1,0:T(8,128)(2,1)} %collective-permute-done.2.a2_b, bf16[1024,256]{1,0:T(8,128)(2,1)} %collective-permute-done.12.a3_a, ...), custom_call_target="tpu_custom_call" | custom-call | flops 1 | bytes 1 | tf_op jit(solution)/shard_map/pallas_call | solution.py:172
  117.1 2.5 %collective-permute-done.14.z4_a = bf16[1024,256]{1,0:T(8,128)(2,1)S(1)} collective-permute-done((bf16[1024,256]{1,0:T(8,128)(2,1)}, bf16[1024,256]{1,0:T(8,128)(2,1)S(1)}, u32[]{:S(2)}, u32[]{:S(2)}) %collective-permute-start.14) | collective-permute-done | bytes 524320 | tf_op jit(solution)/shard_map/ppermute | solution.py:272
  123.5 9.8 %all-to-all-start.2 = ((bf16[32,128,128]{2,1,0:T(8,128)(2,1)}), bf16[32,128,128]{2,1,0:T(8,128)(2,1)S(1)}, u32[]{:S(2)}, u32[]{:S(2)}) async-start(bf16[32,128,128]{2,1,0:T(8,128)(2,1)} %bitcast.26), calls=%async_computation.2 | async-start | bytes 2097152 | tf_op jit(solution)/shard_map/all_to_all | solution.py:343
  135.0 14.9 %all-to-all-done.2 = bf16[32,128,128]{2,1,0:T(8,128)(2,1)S(1)} async-done(((bf16[32,128,128]{2,1,0:T(8,128)(2,1)}), bf16[32,128,128]{2,1,0:T(8,128)(2,1)S(1)}, u32[]{:S(2)}, u32[]{:S(2)}) %all-to-all-start.2) | async-done | bytes 1048608 | tf_op jit(solution)/shard_map/all_to_all | solution.py:343
  (62 shorter events, 25.5 us)
Async XLA Ops:
  7.2 59.2 %all-gather.2.cloned.1.call-start = ((), (), s32[]{:S(2)}) async-start(), calls=%async_computation.4 | async-start | bytes 9437184 | tf_op jit(solution)/shard_map/all_gather | solution.py:294
  13.7 35.5 %copy-start.11 = (f32[2,128,8]{1,2,0:T(8,128)S(1)}, f32[2,128,8]{1,2,0:T(8,128)}, u32[]{:S(2)}) copy-start(f32[2,128,8]{1,2,0:T(8,128)} %param.13) | copy-start | bytes 24580
  13.7 16.2 %all-to-all-start = ((bf16[8,128,256]{2,1,0:T(8,128)(2,1)}), bf16[8,128,256]{2,1,0:T(8,128)(2,1)S(1)}, u32[]{:S(2)}, u32[]{:S(2)}) async-start(bf16[8,128,256]{2,1,0:T(8,128)(2,1)} %bitcast.35), calls=%async_computation | async-start | bytes 1048576 | tf_op jit(solution)/shard_map/all_to_all | solution.py:312
  20.5 2.9 %collective-permute-start.4 = (s32[2,8,128]{2,1,0:T(8,128)S(1)}, s32[2,8,128]{2,1,0:T(8,128)S(1)}, u32[]{:S(2)}, u32[]{:S(2)}) collective-permute-start(s32[2,8,128]{2,1,0:T(8,128)S(1)} %bitcast.38), channel_id=1, source_target_pairs={{16,0},{32,16},{48,32},{0,48},{17,1},{33,17},{49,33},{1,49},{18,2}... | collective-permute-start | bytes 24584 | tf_op jit(solution)/shard_map/ppermute | solution.py:280
  22.4 4.3 %collective-permute-start.5 = (s32[2,8,128]{2,1,0:T(8,128)S(1)}, s32[2,8,128]{2,1,0:T(8,128)S(1)}, u32[]{:S(2)}, u32[]{:S(2)}) collective-permute-start(s32[2,8,128]{2,1,0:T(8,128)S(1)} %bitcast.39), channel_id=1, source_target_pairs={{32,0},{48,16},{0,32},{16,48},{33,1},{49,17},{1,33},{17,49},{34,2}... | collective-permute-start | bytes 24584 | tf_op jit(solution)/shard_map/ppermute | solution.py:280
  22.7 4.0 %collective-permute-start.6 = (s32[2,8,128]{2,1,0:T(8,128)S(1)}, s32[2,8,128]{2,1,0:T(8,128)S(1)}, u32[]{:S(2)}, u32[]{:S(2)}) collective-permute-start(s32[2,8,128]{2,1,0:T(8,128)S(1)} %bitcast.40), channel_id=1, source_target_pairs={{48,0},{0,16},{16,32},{32,48},{49,1},{1,17},{17,33},{33,49},{50,2}... | collective-permute-start | bytes 24584 | tf_op jit(solution)/shard_map/ppermute | solution.py:280
  29.8 13.6 %all-to-all-start.1 = ((bf16[8,128,256]{2,1,0:T(8,128)(2,1)}), bf16[8,128,256]{2,1,0:T(8,128)(2,1)S(1)}, u32[]{:S(2)}, u32[]{:S(2)}) async-start(bf16[8,128,256]{2,1,0:T(8,128)(2,1)} %bitcast.34), calls=%async_computation.1 | async-start | bytes 1048576 | tf_op jit(solution)/shard_map/all_to_all | solution.py:312
  33.6 5.7 %collective-permute-start.7 = (s32[4,2,8,128]{3,2,1,0:T(8,128)S(1)}, s32[4,2,8,128]{3,2,1,0:T(8,128)S(1)}, u32[]{:S(2)}, u32[]{:S(2)}) collective-permute-start(s32[4,2,8,128]{3,2,1,0:T(8,128)S(1)} %pad_add_fusion.1), channel_id=1, source_target_pairs={{0,64},{64,0},{1,65},{65,1},{2,66},{66,2},{3,67},{67,3},{4,68},{68... | collective-permute-start | bytes 98312 | tf_op jit(solution)/shard_map/ppermute | solution.py:318
  33.8 18.4 %collective-permute-start = (bf16[1024,256]{1,0:T(8,128)(2,1)S(1)}, bf16[1024,256]{1,0:T(8,128)(2,1)}, u32[]{:S(2)}, u32[]{:S(2)}) collective-permute-start(bf16[1024,256]{1,0:T(8,128)(2,1)S(1)} %bitcast.27), channel_id=1, source_target_pairs={{0,128},{128,0},{4,132},{132,4},{8,136},{136,8},{12,140},{140,12},... | collective-permute-start | bytes 1572872 | tf_op jit(solution)/shard_map/ppermute | solution.py:272
  34.6 17.6 %collective-permute-start.1 = (bf16[1024,256]{1,0:T(8,128)(2,1)S(1)}, bf16[1024,256]{1,0:T(8,128)(2,1)}, u32[]{:S(2)}, u32[]{:S(2)}) collective-permute-start(bf16[1024,256]{1,0:T(8,128)(2,1)S(1)} %bitcast.28), channel_id=1, source_target_pairs={{128,4},{4,128},{132,8},{8,132},{136,12},{12,136},{140,0},{0,140},... | collective-permute-start | bytes 1572872 | tf_op jit(solution)/shard_map/ppermute | solution.py:272
  43.4 14.9 %collective-permute-start.8 = (bf16[1024,256]{1,0:T(8,128)(2,1)S(1)}, bf16[1024,256]{1,0:T(8,128)(2,1)}, u32[]{:S(2)}, u32[]{:S(2)}) collective-permute-start(bf16[1024,256]{1,0:T(8,128)(2,1)S(1)} %bitcast.30), channel_id=1, source_target_pairs={{0,128},{128,0},{4,132},{132,4},{8,136},{136,8},{12,140},{140,12},... | collective-permute-start | bytes 1572872 | tf_op jit(solution)/shard_map/ppermute | solution.py:272
  44.3 17.9 %collective-permute-start.9 = (bf16[1024,256]{1,0:T(8,128)(2,1)S(1)}, bf16[1024,256]{1,0:T(8,128)(2,1)}, u32[]{:S(2)}, u32[]{:S(2)}) collective-permute-start(bf16[1024,256]{1,0:T(8,128)(2,1)S(1)} %bitcast.31), channel_id=1, source_target_pairs={{128,4},{4,128},{132,8},{8,132},{136,12},{12,136},{140,0},{0,140},... | collective-permute-start | bytes 1572872 | tf_op jit(solution)/shard_map/ppermute | solution.py:272
  52.2 24.6 %collective-permute-start.2 = (bf16[1024,256]{1,0:T(8,128)(2,1)}, bf16[1024,256]{1,0:T(8,128)(2,1)}, u32[]{:S(2)}, u32[]{:S(2)}) collective-permute-start(bf16[1024,256]{1,0:T(8,128)(2,1)} %collective-permute-done.1.c1_b), channel_id=1, source_target_pairs={{0,128},{128,0},{4,132},{132,4},{8,136},{136,8},{12,140},{140,12},... | collective-permute-start | bytes 1572872 | tf_op jit(solution)/shard_map/ppermute | solution.py:272
  52.3 24.5 %collective-permute-start.3 = (bf16[1024,256]{1,0:T(8,128)(2,1)}, bf16[1024,256]{1,0:T(8,128)(2,1)}, u32[]{:S(2)}, u32[]{:S(2)}) collective-permute-start(bf16[1024,256]{1,0:T(8,128)(2,1)} %collective-permute-done.a1_b), channel_id=1, source_target_pairs={{128,4},{4,128},{132,8},{8,132},{136,12},{12,136},{140,0},{0,140},... | collective-permute-start | bytes 1572872 | tf_op jit(solution)/shard_map/ppermute | solution.py:272
  62.3 18.8 %collective-permute-start.10 = (bf16[1024,256]{1,0:T(8,128)(2,1)}, bf16[1024,256]{1,0:T(8,128)(2,1)}, u32[]{:S(2)}, u32[]{:S(2)}) collective-permute-start(bf16[1024,256]{1,0:T(8,128)(2,1)} %collective-permute-done.9.c1_a), channel_id=1, source_target_pairs={{0,128},{128,0},{4,132},{132,4},{8,136},{136,8},{12,140},{140,12},... | collective-permute-start | bytes 1572872 | tf_op jit(solution)/shard_map/ppermute | solution.py:272
  62.3 22.5 %collective-permute-start.11 = (bf16[1024,256]{1,0:T(8,128)(2,1)}, bf16[1024,256]{1,0:T(8,128)(2,1)}, u32[]{:S(2)}, u32[]{:S(2)}) collective-permute-start(bf16[1024,256]{1,0:T(8,128)(2,1)} %collective-permute-done.8.a1_a), channel_id=1, source_target_pairs={{128,4},{4,128},{132,8},{8,132},{136,12},{12,136},{140,0},{0,140},... | collective-permute-start | bytes 1572872 | tf_op jit(solution)/shard_map/ppermute | solution.py:272
  76.9 15.4 %collective-permute-start.15 = (bf16[1024,256]{1,0:T(8,128)(2,1)}, bf16[1024,256]{1,0:T(8,128)(2,1)}, u32[]{:S(2)}, u32[]{:S(2)}) collective-permute-start(bf16[1024,256]{1,0:T(8,128)(2,1)} %collective-permute-done.3.c2_b), channel_id=1, source_target_pairs={{0,128},{128,0},{4,132},{132,4},{8,136},{136,8},{12,140},{140,12},... | collective-permute-start | bytes 1572872 | tf_op jit(solution)/shard_map/ppermute | solution.py:272
  78.2 17.7 %collective-permute-start.16 = (bf16[1024,256]{1,0:T(8,128)(2,1)}, bf16[1024,256]{1,0:T(8,128)(2,1)S(1)}, u32[]{:S(2)}, u32[]{:S(2)}) collective-permute-start(bf16[1024,256]{1,0:T(8,128)(2,1)} %collective-permute-done.2.a2_b), channel_id=1, source_target_pairs={{128,4},{4,128},{132,8},{8,132},{136,12},{12,136},{140,0},{0,140},... | collective-permute-start | bytes 1572872 | tf_op jit(solution)/shard_map/ppermute | solution.py:272
  84.8 21.1 %collective-permute-start.12 = (bf16[1024,256]{1,0:T(8,128)(2,1)}, bf16[1024,256]{1,0:T(8,128)(2,1)}, u32[]{:S(2)}, u32[]{:S(2)}) collective-permute-start(bf16[1024,256]{1,0:T(8,128)(2,1)} %collective-permute-done.11.c2_a), channel_id=1, source_target_pairs={{0,128},{128,0},{4,132},{132,4},{8,136},{136,8},{12,140},{140,12},... | collective-permute-start | bytes 1572872 | tf_op jit(solution)/shard_map/ppermute | solution.py:272
  84.8 22.5 %collective-permute-start.13 = (bf16[1024,256]{1,0:T(8,128)(2,1)}, bf16[1024,256]{1,0:T(8,128)(2,1)}, u32[]{:S(2)}, u32[]{:S(2)}) collective-permute-start(bf16[1024,256]{1,0:T(8,128)(2,1)} %collective-permute-done.10.a2_a), channel_id=1, source_target_pairs={{128,4},{4,128},{132,8},{8,132},{136,12},{12,136},{140,0},{0,140},... | collective-permute-start | bytes 1572872 | tf_op jit(solution)/shard_map/ppermute | solution.py:272
  96.7 25.9 %all-to-all-start.3 = ((bf16[32,128,128]{2,1,0:T(8,128)(2,1)}), bf16[32,128,128]{2,1,0:T(8,128)(2,1)S(1)}, u32[]{:S(2)}, u32[]{:S(2)}) async-start(bf16[32,128,128]{2,1,0:T(8,128)(2,1)} %bitcast.21), calls=%async_computation.3 | async-start | bytes 2097152 | tf_op jit(solution)/shard_map/all_to_all | solution.py:343
  107.2 12.4 %collective-permute-start.14 = (bf16[1024,256]{1,0:T(8,128)(2,1)}, bf16[1024,256]{1,0:T(8,128)(2,1)S(1)}, u32[]{:S(2)}, u32[]{:S(2)}) collective-permute-start(bf16[1024,256]{1,0:T(8,128)(2,1)} %collective-permute-done.13.c3_a), channel_id=1, source_target_pairs={{0,128},{128,0},{4,132},{132,4},{8,136},{136,8},{12,140},{140,12},... | collective-permute-start | bytes 1572872 | tf_op jit(solution)/shard_map/ppermute | solution.py:272
  107.2 13.6 %collective-permute-start.17 = (bf16[1024,256]{1,0:T(8,128)(2,1)}, bf16[1024,256]{1,0:T(8,128)(2,1)S(1)}, u32[]{:S(2)}, u32[]{:S(2)}) collective-permute-start(bf16[1024,256]{1,0:T(8,128)(2,1)} %collective-permute-done.15.a3_b), channel_id=1, source_target_pairs={{128,4},{4,128},{132,8},{8,132},{136,12},{12,136},{140,0},{0,140},... | collective-permute-start | bytes 1572872 | tf_op jit(solution)/shard_map/ppermute | solution.py:272
  123.5 26.4 %all-to-all-start.2 = ((bf16[32,128,128]{2,1,0:T(8,128)(2,1)}), bf16[32,128,128]{2,1,0:T(8,128)(2,1)S(1)}, u32[]{:S(2)}, u32[]{:S(2)}) async-start(bf16[32,128,128]{2,1,0:T(8,128)(2,1)} %bitcast.26), calls=%async_computation.2 | async-start | bytes 2097152 | tf_op jit(solution)/shard_map/all_to_all | solution.py:343
  (11 other events, 44.6 us)
Sparse Core Ops, SparseCore 0:
  9.9 56.5 all-gather.1
